TPU v7x, 32 devices: a whole 2x2x4 slice. The times are simulated.
32 devices in a mesh: bx: 8 (over z, x), by: 4 (over y, core).
Axes of the slice: x: 2, y: 2, z: 4, core: 2. Of those that a mesh axis runs over, the one named last changes fastest.
Arguments:
- scalar_field: float32 [64, 256, 512], P(None, 'bx', 'by'), may hold values from -8 to 8
- transfer_in: bfloat16 [16, 8], replicated, may hold values from -2 to 2
- transfer_out: bfloat16 [16, 16], replicated, may hold values from -1.5 to 1.5
Outputs:
- view_x: float32 [2, 8, 64, 512], P(None, None, 'bx', 'by')
- view_y: float32 [2, 8, 64, 256], P(None, None, 'by', 'bx')
All inputs are finite; a program needn't handle non-finite values.
Results may differ from a plain program's by a relative error of at most 0.00035.
Values sent between devices are 32-bit elements; how exact they have to be, the bound alone decides.
No kernel may reach another device: no remote copies, remote signals or barrier semaphores. Data moves between devices by JAX's collectives and lax.ppermute only.
A program may use at most 64 MiB of HBM per device.

v0:
```python
import jax
import jax.numpy as jnp
from jax import lax
from jax.sharding import PartitionSpec as P


def extended_2(shard, sides, width):
    for axis, dim in sides:
        peers, length = (lax.axis_size(axis), shard.shape[dim])
        up = [(i, (i + 1) % peers) for i in range(peers - 1)]
        down = [(j, i) for i, j in up]
        last = lax.slice_in_dim(shard, length - width, length, axis=dim)
        initial = lax.slice_in_dim(shard, 0, width, axis=dim)
        before = lax.ppermute(last, axis, up)
        after = lax.ppermute(initial, axis, down)
        shard = jnp.concatenate([before, shard, after], axis=dim)
    return shard


def smooth_inner(extended):
    centre = extended[:, 1:-1, 1:-1]
    padded_z = jnp.pad(centre, ((1, 1), (0, 0), (0, 0)))
    nearby = (
        extended[:, 2:, 1:-1]
        + extended[:, :-2, 1:-1]
        + extended[:, 1:-1, 2:]
        + extended[:, 1:-1, :-2]
    )
    nearby = nearby + padded_z[2:] + padded_z[:-2]
    return 0.4 * centre + 0.1 * nearby


def plain_rim(values):
    return extended_2(values, (("bx", 1), ("by", 2)), 1)


def upper_ones(length):
    rows_at = lax.broadcasted_iota(jnp.int32, (length, length), 0)
    cols_at = lax.broadcasted_iota(jnp.int32, (length, length), 1)
    return (rows_at <= cols_at).astype(jnp.float32)


def gradients(padded):
    diff_x = padded[:, 2:, :] - padded[:, :-2, :]
    grad_x = (
        2.0 * diff_x[1:-1, :, 1:-1]
        + diff_x[:-2, :, 1:-1]
        + diff_x[2:, :, 1:-1]
        + diff_x[1:-1, :, :-2]
        + diff_x[1:-1, :, 2:]
    ) / 12.0
    diff_y = padded[:, :, 2:] - padded[:, :, :-2]
    grad_y = (
        2.0 * diff_y[1:-1, 1:-1]
        + diff_y[:-2, 1:-1]
        + diff_y[2:, 1:-1]
        + diff_y[1:-1, :-2]
        + diff_y[1:-1, 2:]
    ) / 12.0
    diff_z = padded[2:] - padded[:-2]
    grad_z = (
        2.0 * diff_z[:, 1:-1, 1:-1]
        + diff_z[:, :-2, 1:-1]
        + diff_z[:, 2:, 1:-1]
        + diff_z[:, 1:-1, :-2]
        + diff_z[:, 1:-1, 2:]
    ) / 12.0
    return (padded[1:-1, 1:-1, 1:-1], grad_x, grad_y, grad_z)


def transfer(padded, transfer_in, transfer_out, bands):
    centre, grad_x, grad_y, grad_z = gradients(padded)
    scaled_x = 4.0 * grad_x
    scaled_y = 4.0 * grad_y
    scaled_z = 4.0 * grad_z
    magnitude = jnp.sqrt(1.0 + scaled_x * scaled_x + scaled_y * scaled_y + scaled_z * scaled_z)
    features = jnp.stack(
        [
            centre,
            scaled_x,
            scaled_y,
            scaled_z,
            magnitude,
            centre * magnitude,
            centre * centre,
            jnp.ones_like(centre),
        ]
    ).astype(jnp.bfloat16)
    hidden = jax.nn.silu(
        jnp.einsum("hf,fzxy->hzxy", transfer_in, features, preferred_element_type=jnp.float32)
    ).astype(jnp.bfloat16)
    channels = jnp.einsum("ch,hzxy->czxy", transfer_out, hidden, preferred_element_type=jnp.float32)
    return (jax.nn.softplus(channels[:bands]), jax.nn.softplus(channels[bands:]))


def fold_bricks(pieces):
    clearance = pieces[:, 1]
    leading = jnp.ones_like(clearance[:1])
    shading = jnp.cumprod(jnp.concatenate([leading, clearance[:-1]], axis=0), axis=0)
    colour = jnp.sum(shading * pieces[:, 0], axis=0)
    return jnp.stack([colour, shading[-1] * clearance[-1]])


def body(scalar_field, transfer_in, transfer_out):
    layers, local_x, local_y = scalar_field.shape
    bands = transfer_out.shape[0] // 2
    count_x = lax.axis_size("bx")
    count_y = lax.axis_size("by")
    full_x = local_x * count_x
    full_y = local_y * count_y
    smoothed_once = smooth_inner(plain_rim(scalar_field))
    smoothed = smooth_inner(plain_rim(smoothed_once))
    margined = extended_2(smoothed, (("bx", 1), ("by", 2)), 1)
    padded = jnp.pad(margined, ((1, 1), (0, 0), (0, 0)))
    planes = 8
    step_x = 2.0 / full_x
    step_y = 2.0 / full_y
    upper_x = upper_ones(planes)
    upper_y = upper_ones(local_y)

    def advance(carried, index):
        colour, optical = carried
        window = lax.dynamic_slice_in_dim(padded, index * planes, planes + 2, 1)
        emission, absorption = transfer(window, transfer_in, transfer_out, bands)
        thickness = absorption * step_x
        running = jnp.einsum("bzxy,xw->bzwy", thickness, upper_x, precision=lax.Precision.HIGHEST)
        visible = jnp.exp(-(optical[:, :, None, :] + running - thickness))
        colour = colour + jnp.sum(visible * -jnp.expm1(-thickness) * emission, axis=2)
        optical = optical + running[:, :, -1, :]
        thickness_y = absorption * step_y
        running_y = jnp.einsum(
            "bzxy,yw->bzxw", thickness_y, upper_y, precision=lax.Precision.HIGHEST
        )
        colour_y = jnp.sum(
            jnp.exp(-(running_y - thickness_y)) * -jnp.expm1(-thickness_y) * emission, axis=3
        )
        clear_y = jnp.exp(-running_y[..., -1])
        return ((colour, optical), jnp.stack([colour_y, clear_y]))

    blank = jnp.zeros((bands, layers, local_y), jnp.float32)
    (colour, optical), images = lax.scan(
        advance, (blank, blank), jnp.arange(local_x // planes, dtype=jnp.int32)
    )
    clear_x = jnp.exp(-optical)
    image_y = jnp.transpose(images, (1, 2, 3, 0, 4)).reshape(2, bands, layers, local_x)
    pieces_y = lax.all_to_all(image_y[None], "by", split_axis=3, concat_axis=0, tiled=True)
    view_y = fold_bricks(pieces_y)
    pieces_x = lax.all_to_all(
        jnp.stack([colour, clear_x])[None], "bx", split_axis=3, concat_axis=0, tiled=True
    )
    view_x = fold_bricks(pieces_x)
    return (view_x, view_y)


def solution(mesh):
    return jax.shard_map(
        body,
        mesh=mesh,
        in_specs=(P(None, "bx", "by"), P(), P()),
        out_specs=(P(None, None, "bx", "by"), P(None, None, "by", "bx")),
        check_vma=False,
    )
```

profile of v0, /device:TPU:0, one launch (start us, length us, event | category | flops | bytes accessed | tf_op | source)
XLA Modules:
  0.0 344.5 jit_solution(15846746393467379719)
XLA Ops:
  3.8 5.5 %collective-permute-start.1 = (f32[64,1,128]{0,2,1:T(8,128)S(1)}, f32[64,1,128]{0,2,1:T(8,128)S(1)}, u32[]{:S(2)}, u32[]{:S(2)}) collective-permute-start(f32[64,1,128]{0,2,1:T(8,128)S(1)} %get-tuple-element.262), channel_id=1, source_target_pairs={{0,4},{4,8},{8,12},{12,16},{16,20},{20,24},{24,28},{1,5},{5,9},{9,... | collective-permute-start | bytes 98312 | tf_op jit(solution)/shard_map/ppermute | solution.py:14
  12.7 3.0 collective-permute-start.3
  16.5 4.2 %fusion.44 = f32[64,32,128]{0,2,1:T(8,128)S(1)} fusion(f32[64,34,1]{0,2,1:T(1,128)S(1)} %collective-permute-done.3, f32[64,1,128]{0,2,1:T(8,128)S(1)} %collective-permute-done, f32[64,32,128]{0,2,1:T(8,128)S(1)} %copy.216, f32[64,1,128]{0,2,1:T(8,128)S(1)} %collective-permute-done.1, f32[64,34,1]{0,2,1:T(1,128)S(1)} %collective-permute-done.2), kind=kLoop, calls=%fused_computation.102 | loop fusion | flops 4194304 | bytes 2180096 | tf_op jit(solution)/shard_map/add | solution.py:30
  22.0 5.3 %collective-permute-start.5 = (f32[64,1,128]{0,2,1:T(8,128)S(1)}, f32[64,1,128]{0,2,1:T(8,128)S(1)}, u32[]{:S(2)}, u32[]{:S(2)}) collective-permute-start(f32[64,1,128]{0,2,1:T(8,128)S(1)} %get-tuple-element.260), channel_id=1, source_target_pairs={{0,4},{4,8},{8,12},{12,16},{16,20},{20,24},{24,28},{1,5},{5,9},{9,... | collective-permute-start | bytes 98312 | tf_op jit(solution)/shard_map/ppermute | solution.py:14
  31.8 3.0 collective-permute-start.7
  35.7 4.2 %fusion.37 = f32[64,32,128]{0,2,1:T(8,128)S(1)} fusion(f32[64,34,1]{0,2,1:T(1,128)S(1)} %collective-permute-done.7, f32[64,1,128]{0,2,1:T(8,128)S(1)} %collective-permute-done.4, f32[64,32,128]{0,2,1:T(8,128)S(1)} %fusion.44, f32[64,1,128]{0,2,1:T(8,128)S(1)} %collective-permute-done.5, f32[64,34,1]{0,2,1:T(1,128)S(1)} %collective-permute-done.6), kind=kLoop, calls=%fused_computation.87 | loop fusion | flops 4194304 | bytes 2180096 | tf_op jit(solution)/shard_map/add | solution.py:30
  39.9 4.4 %collective-permute-start.8 = (f32[64,1,128]{0,2,1:T(8,128)S(1)}, f32[64,1,128]{0,2,1:T(8,128)S(1)}, u32[]{:S(2)}, u32[]{:S(2)}) collective-permute-start(f32[64,1,128]{0,2,1:T(8,128)S(1)} %get-tuple-element.258), channel_id=1, source_target_pairs={{0,4},{4,8},{8,12},{12,16},{16,20},{20,24},{24,28},{1,5},{5,9},{9,... | collective-permute-start | bytes 98312 | tf_op jit(solution)/shard_map/ppermute | solution.py:14
  46.2 5.5 %collective-permute-done.9 = f32[64,1,128]{0,2,1:T(8,128)S(1)} collective-permute-done((f32[64,1,128]{0,2,1:T(8,128)S(1)}, f32[64,1,128]{0,2,1:T(8,128)S(1)}, u32[]{:S(2)}, u32[]{:S(2)}) %collective-permute-start.9) | collective-permute-done | bytes 32800 | tf_op jit(solution)/shard_map/ppermute | solution.py:15
  51.7 3.3 collective-permute-start.10
  56.4 4.7 %collective-permute-done.11 = f32[64,34,1]{0,2,1:T(1,128)S(1)} collective-permute-done((f32[64,34,1]{0,2,1:T(1,128)S(1)}, f32[64,34,1]{0,2,1:T(1,128)S(1)}, u32[]{:S(2)}, u32[]{:S(2)}) %collective-permute-start.11) | collective-permute-done | bytes 8736 | tf_op jit(solution)/shard_map/ppermute | solution.py:15
  63.5 248.9 %while.18 = (s32[]{:T(128)}, f32[8,64,128]{2,0,1:T(8,128)}, f32[8,64,128]{2,0,1:T(8,128)}, f32[4,2,8,64,8]{3,4,0,2,1:T(8,128)}, s32[4]{0:T(128)S(1)}, /*index=5*...) while((s32[]{:T(128)}, f32[8,64,128]{2,0,1:T(8,128)}, ...), condition=%wide.region_3.4_spmd.clone, body=%wide.region_0.3_spmd.clone.sunk | while | flops 933641152 | bytes 96002440 | solution.py:141
  69.2 2.9 copy.323
  72.0 2.9 copy.324
  86.9 3.2 fusion.82
  91.9 3.2 stack.120
  95.2 3.7 %convolution_bitcast_fusion.2 = f32[16,64,8,128]{3,0,2,1:T(8,128)} fusion(bf16[8,64,8,128]{3,0,2,1:T(8,128)(2,1)S(1)} %stack.120, bf16[16,16]{1,0:T(8,128)(2,1)S(1)} %get-tuple-element.398, bf16[16,8]{0,1:T(8,128)(2,1)S(1)} %get-tuple-element.397), kind=kOutput, calls=%fused_computation.10.clone.1 | convolution fusion | flops 55574528 | bytes 5243648 | tf_op jit(solution)/shard_map/while/body/eval_jaxpr/ch,hzxy->czxy/dot_general | solution.py:92
  98.9 4.2 %broadcast_multiply_fusion.3 = (f32[8,64,8,128]{3,0,2,1:T(8,128)S(1)}, f32[8,64,8,128]{3,0,2,1:T(8,128)}) fusion(f32[16,64,8,128]{3,0,2,1:T(8,128)} %convolution_bitcast_fusion.2), kind=kLoop, calls=%fused_computation.24.clone.2 | loop fusion | flops 4194304 | bytes 6291456 | tf_op jit(solution)/shard_map/while/body/eval_jaxpr/mul | solution.py:125
  108.8 3.6 %fusion.83 = f32[8,64,8,128]{3,2,1,0:T(8,128)S(1)} fusion(f32[8,64,8,128]{3,0,2,1:T(8,128)} %get-tuple-element.355), kind=kOutput, calls=%fused_computation.17.clone.1 | convolution fusion | flops 805339136 | bytes 4194304 | tf_op jit(solution)/shard_map/while/body/eval_jaxpr/bzxy,yw->bzxw/dot_general | solution.py:131
  112.5 5.7 %fusion.86 = (f32[8,64,8]{0,2,1:T(8,128)S(1)}, f32[8,64,128]{2,0,1:T(8,128)S(1)}) fusion(f32[8,64,8,128]{3,2,1,0:T(8,128)S(1)} %fusion.83, f32[16,64,8,128]{3,0,2,1:T(8,128)S(1)} %copy-done.3, f32[8,64,128,8]{2,3,1,0:T(8,128)S(1)} %fusion.84, f32[8,64,128]{2,0,1:T(8,128)S(1)} %get-tuple-element.357), kind=kLoop, calls=%fused_computation.16.clone.1 | loop fusion | flops 15134720 | bytes 8929280 | tf_op jit(solution)/shard_map/while/body/eval_jaxpr/reduce_sum | solution.py:134
  118.4 3.6 %slice.497 = f32[8,64,8,1]{3,2,1,0:T(8,128)} slice(f32[8,64,8,128]{3,2,1,0:T(8,128)} %copy-done), slice={[0:8], [0:64], [0:8], [127:128]} | slice | bytes 32768 | tf_op jit(solution)/shard_map/while/body/eval_jaxpr/slice | solution.py:137
  131.3 2.9 copy.323
  149.1 3.2 fusion.82
  154.1 3.2 stack.120
  157.3 3.8 %convolution_bitcast_fusion.2 = f32[16,64,8,128]{3,0,2,1:T(8,128)} fusion(bf16[8,64,8,128]{3,0,2,1:T(8,128)(2,1)S(1)} %stack.120, bf16[16,16]{1,0:T(8,128)(2,1)S(1)} %get-tuple-element.398, bf16[16,8]{0,1:T(8,128)(2,1)S(1)} %get-tuple-element.397), kind=kOutput, calls=%fused_computation.10.clone.1 | convolution fusion | flops 55574528 | bytes 5243648 | tf_op jit(solution)/shard_map/while/body/eval_jaxpr/ch,hzxy->czxy/dot_general | solution.py:92
  161.1 4.2 %broadcast_multiply_fusion.3 = (f32[8,64,8,128]{3,0,2,1:T(8,128)S(1)}, f32[8,64,8,128]{3,0,2,1:T(8,128)}) fusion(f32[16,64,8,128]{3,0,2,1:T(8,128)} %convolution_bitcast_fusion.2), kind=kLoop, calls=%fused_computation.24.clone.2 | loop fusion | flops 4194304 | bytes 6291456 | tf_op jit(solution)/shard_map/while/body/eval_jaxpr/mul | solution.py:125
  171.0 3.6 %fusion.83 = f32[8,64,8,128]{3,2,1,0:T(8,128)S(1)} fusion(f32[8,64,8,128]{3,0,2,1:T(8,128)} %get-tuple-element.355), kind=kOutput, calls=%fused_computation.17.clone.1 | convolution fusion | flops 805339136 | bytes 4194304 | tf_op jit(solution)/shard_map/while/body/eval_jaxpr/bzxy,yw->bzxw/dot_general | solution.py:131
  174.7 5.7 %fusion.86 = (f32[8,64,8]{0,2,1:T(8,128)S(1)}, f32[8,64,128]{2,0,1:T(8,128)S(1)}) fusion(f32[8,64,8,128]{3,2,1,0:T(8,128)S(1)} %fusion.83, f32[16,64,8,128]{3,0,2,1:T(8,128)S(1)} %copy-done.3, f32[8,64,128,8]{2,3,1,0:T(8,128)S(1)} %fusion.84, f32[8,64,128]{2,0,1:T(8,128)S(1)} %get-tuple-element.357), kind=kLoop, calls=%fused_computation.16.clone.1 | loop fusion | flops 15134720 | bytes 8929280 | tf_op jit(solution)/shard_map/while/body/eval_jaxpr/reduce_sum | solution.py:134
  180.6 3.6 %slice.497 = f32[8,64,8,1]{3,2,1,0:T(8,128)} slice(f32[8,64,8,128]{3,2,1,0:T(8,128)} %copy-done), slice={[0:8], [0:64], [0:8], [127:128]} | slice | bytes 32768 | tf_op jit(solution)/shard_map/while/body/eval_jaxpr/slice | solution.py:137
  193.5 2.9 copy.323
  211.2 3.2 fusion.82
  216.3 3.2 stack.120
  219.5 3.8 %convolution_bitcast_fusion.2 = f32[16,64,8,128]{3,0,2,1:T(8,128)} fusion(bf16[8,64,8,128]{3,0,2,1:T(8,128)(2,1)S(1)} %stack.120, bf16[16,16]{1,0:T(8,128)(2,1)S(1)} %get-tuple-element.398, bf16[16,8]{0,1:T(8,128)(2,1)S(1)} %get-tuple-element.397), kind=kOutput, calls=%fused_computation.10.clone.1 | convolution fusion | flops 55574528 | bytes 5243648 | tf_op jit(solution)/shard_map/while/body/eval_jaxpr/ch,hzxy->czxy/dot_general | solution.py:92
  223.2 4.2 %broadcast_multiply_fusion.3 = (f32[8,64,8,128]{3,0,2,1:T(8,128)S(1)}, f32[8,64,8,128]{3,0,2,1:T(8,128)}) fusion(f32[16,64,8,128]{3,0,2,1:T(8,128)} %convolution_bitcast_fusion.2), kind=kLoop, calls=%fused_computation.24.clone.2 | loop fusion | flops 4194304 | bytes 6291456 | tf_op jit(solution)/shard_map/while/body/eval_jaxpr/mul | solution.py:125
  233.2 3.6 %fusion.83 = f32[8,64,8,128]{3,2,1,0:T(8,128)S(1)} fusion(f32[8,64,8,128]{3,0,2,1:T(8,128)} %get-tuple-element.355), kind=kOutput, calls=%fused_computation.17.clone.1 | convolution fusion | flops 805339136 | bytes 4194304 | tf_op jit(solution)/shard_map/while/body/eval_jaxpr/bzxy,yw->bzxw/dot_general | solution.py:131
  236.9 5.7 %fusion.86 = (f32[8,64,8]{0,2,1:T(8,128)S(1)}, f32[8,64,128]{2,0,1:T(8,128)S(1)}) fusion(f32[8,64,8,128]{3,2,1,0:T(8,128)S(1)} %fusion.83, f32[16,64,8,128]{3,0,2,1:T(8,128)S(1)} %copy-done.3, f32[8,64,128,8]{2,3,1,0:T(8,128)S(1)} %fusion.84, f32[8,64,128]{2,0,1:T(8,128)S(1)} %get-tuple-element.357), kind=kLoop, calls=%fused_computation.16.clone.1 | loop fusion | flops 15134720 | bytes 8929280 | tf_op jit(solution)/shard_map/while/body/eval_jaxpr/reduce_sum | solution.py:134
  242.7 3.6 %slice.497 = f32[8,64,8,1]{3,2,1,0:T(8,128)} slice(f32[8,64,8,128]{3,2,1,0:T(8,128)} %copy-done), slice={[0:8], [0:64], [0:8], [127:128]} | slice | bytes 32768 | tf_op jit(solution)/shard_map/while/body/eval_jaxpr/slice | solution.py:137
  255.7 2.9 copy.323
  258.5 2.9 copy.324
  273.4 3.2 fusion.82
  278.4 3.2 stack.120
  281.7 3.8 %convolution_bitcast_fusion.2 = f32[16,64,8,128]{3,0,2,1:T(8,128)} fusion(bf16[8,64,8,128]{3,0,2,1:T(8,128)(2,1)S(1)} %stack.120, bf16[16,16]{1,0:T(8,128)(2,1)S(1)} %get-tuple-element.398, bf16[16,8]{0,1:T(8,128)(2,1)S(1)} %get-tuple-element.397), kind=kOutput, calls=%fused_computation.10.clone.1 | convolution fusion | flops 55574528 | bytes 5243648 | tf_op jit(solution)/shard_map/while/body/eval_jaxpr/ch,hzxy->czxy/dot_general | solution.py:92
  285.4 4.2 %broadcast_multiply_fusion.3 = (f32[8,64,8,128]{3,0,2,1:T(8,128)S(1)}, f32[8,64,8,128]{3,0,2,1:T(8,128)}) fusion(f32[16,64,8,128]{3,0,2,1:T(8,128)} %convolution_bitcast_fusion.2), kind=kLoop, calls=%fused_computation.24.clone.2 | loop fusion | flops 4194304 | bytes 6291456 | tf_op jit(solution)/shard_map/while/body/eval_jaxpr/mul | solution.py:125
  295.3 3.6 %fusion.83 = f32[8,64,8,128]{3,2,1,0:T(8,128)S(1)} fusion(f32[8,64,8,128]{3,0,2,1:T(8,128)} %get-tuple-element.355), kind=kOutput, calls=%fused_computation.17.clone.1 | convolution fusion | flops 805339136 | bytes 4194304 | tf_op jit(solution)/shard_map/while/body/eval_jaxpr/bzxy,yw->bzxw/dot_general | solution.py:131
  299.0 5.7 %fusion.86 = (f32[8,64,8]{0,2,1:T(8,128)S(1)}, f32[8,64,128]{2,0,1:T(8,128)S(1)}) fusion(f32[8,64,8,128]{3,2,1,0:T(8,128)S(1)} %fusion.83, f32[16,64,8,128]{3,0,2,1:T(8,128)S(1)} %copy-done.3, f32[8,64,128,8]{2,3,1,0:T(8,128)S(1)} %fusion.84, f32[8,64,128]{2,0,1:T(8,128)S(1)} %get-tuple-element.357), kind=kLoop, calls=%fused_computation.16.clone.1 | loop fusion | flops 15134720 | bytes 8929280 | tf_op jit(solution)/shard_map/while/body/eval_jaxpr/reduce_sum | solution.py:134
  304.9 3.6 %slice.497 = f32[8,64,8,1]{3,2,1,0:T(8,128)} slice(f32[8,64,8,128]{3,2,1,0:T(8,128)} %copy-done), slice={[0:8], [0:64], [0:8], [127:128]} | slice | bytes 32768 | tf_op jit(solution)/shard_map/while/body/eval_jaxpr/slice | solution.py:137
  314.5 3.8 %all-to-all-start.1 = ((f32[4,1,8192]{2,1,0:T(1,128)}), f32[4,1,8192]{2,1,0:T(1,128)S(1)}, u32[]{:S(2)}, u32[]{:S(2)}) async-start(f32[4,1,8192]{2,1,0:T(1,128)} %reshape.38), calls=%async_computation.1 | async-start | bytes 262144 | tf_op jit(solution)/shard_map/all_to_all | solution.py:146
  322.9 6.2 %all-to-all-start = ((f32[1,2,8,64,128]{4,2,1,0,3:T(8,128)}), f32[1,2,8,64,128]{4,2,1,0,3:T(8,128)S(1)}, u32[]{:S(2)}, u32[]{:S(2)}) async-start(f32[1,2,8,64,128]{4,2,1,0,3:T(8,128)} %maximum_bitcast_fusion.1), calls=%async_computation | async-start | bytes 1048576 | tf_op jit(solution)/shard_map/all_to_all | solution.py:148
  332.1 11.3 %all-to-all-done = f32[1,2,8,64,128]{4,2,1,0,3:T(8,128)S(1)} async-done(((f32[1,2,8,64,128]{4,2,1,0,3:T(8,128)}), f32[1,2,8,64,128]{4,2,1,0,3:T(8,128)S(1)}, u32[]{:S(2)}, u32[]{:S(2)}) %all-to-all-start) | async-done | bytes 524320 | tf_op jit(solution)/shard_map/all_to_all | solution.py:148
  (242 shorter events, 148.7 us)
Async XLA Ops:
  2.5 7.1 %collective-permute-start = (f32[64,1,128]{0,2,1:T(8,128)S(1)}, f32[64,1,128]{0,2,1:T(8,128)S(1)}, u32[]{:S(2)}, u32[]{:S(2)}) collective-permute-start(f32[64,1,128]{0,2,1:T(8,128)S(1)} %get-tuple-element.263), channel_id=1, source_target_pairs={{4,0},{8,4},{12,8},{16,12},{20,16},{24,20},{28,24},{5,1},{9,5},{13... | collective-permute-start | bytes 98312 | tf_op jit(solution)/shard_map/ppermute | solution.py:15
  3.8 7.5 %collective-permute-start.1 = (f32[64,1,128]{0,2,1:T(8,128)S(1)}, f32[64,1,128]{0,2,1:T(8,128)S(1)}, u32[]{:S(2)}, u32[]{:S(2)}) collective-permute-start(f32[64,1,128]{0,2,1:T(8,128)S(1)} %get-tuple-element.262), channel_id=1, source_target_pairs={{0,4},{4,8},{8,12},{12,16},{16,20},{20,24},{24,28},{1,5},{5,9},{9,... | collective-permute-start | bytes 98312 | tf_op jit(solution)/shard_map/ppermute | solution.py:14
  11.4 4.3 %collective-permute-start.2 = (f32[64,34,1]{0,2,1:T(1,128)S(1)}, f32[64,34,1]{0,2,1:T(1,128)S(1)}, u32[]{:S(2)}, u32[]{:S(2)}) collective-permute-start(f32[64,34,1]{0,2,1:T(1,128)S(1)} %get-tuple-element.256), channel_id=1, source_target_pairs={{1,0},{2,1},{3,2},{5,4},{6,5},{7,6},{9,8},{10,9},{11,10},{13,12},{... | collective-permute-start | bytes 26120 | tf_op jit(solution)/shard_map/ppermute | solution.py:15
  12.7 3.9 %collective-permute-start.3 = (f32[64,34,1]{0,2,1:T(1,128)S(1)}, f32[64,34,1]{0,2,1:T(1,128)S(1)}, u32[]{:S(2)}, u32[]{:S(2)}) collective-permute-start(f32[64,34,1]{0,2,1:T(1,128)S(1)} %get-tuple-element.257), channel_id=1, source_target_pairs={{0,1},{1,2},{2,3},{4,5},{5,6},{6,7},{8,9},{9,10},{10,11},{12,13},{... | collective-permute-start | bytes 26120 | tf_op jit(solution)/shard_map/ppermute | solution.py:14
  20.7 7.2 %collective-permute-start.4 = (f32[64,1,128]{0,2,1:T(8,128)S(1)}, f32[64,1,128]{0,2,1:T(8,128)S(1)}, u32[]{:S(2)}, u32[]{:S(2)}) collective-permute-start(f32[64,1,128]{0,2,1:T(8,128)S(1)} %get-tuple-element.261), channel_id=1, source_target_pairs={{4,0},{8,4},{12,8},{16,12},{20,16},{24,20},{28,24},{5,1},{9,5},{13... | collective-permute-start | bytes 98312 | tf_op jit(solution)/shard_map/ppermute | solution.py:15
  22.0 8.5 %collective-permute-start.5 = (f32[64,1,128]{0,2,1:T(8,128)S(1)}, f32[64,1,128]{0,2,1:T(8,128)S(1)}, u32[]{:S(2)}, u32[]{:S(2)}) collective-permute-start(f32[64,1,128]{0,2,1:T(8,128)S(1)} %get-tuple-element.260), channel_id=1, source_target_pairs={{0,4},{4,8},{8,12},{12,16},{16,20},{20,24},{24,28},{1,5},{5,9},{9,... | collective-permute-start | bytes 98312 | tf_op jit(solution)/shard_map/ppermute | solution.py:14
  30.5 4.3 %collective-permute-start.6 = (f32[64,34,1]{0,2,1:T(1,128)S(1)}, f32[64,34,1]{0,2,1:T(1,128)S(1)}, u32[]{:S(2)}, u32[]{:S(2)}) collective-permute-start(f32[64,34,1]{0,2,1:T(1,128)S(1)} %get-tuple-element.254), channel_id=1, source_target_pairs={{1,0},{2,1},{3,2},{5,4},{6,5},{7,6},{9,8},{10,9},{11,10},{13,12},{... | collective-permute-start | bytes 26120 | tf_op jit(solution)/shard_map/ppermute | solution.py:15
  31.8 3.9 %collective-permute-start.7 = (f32[64,34,1]{0,2,1:T(1,128)S(1)}, f32[64,34,1]{0,2,1:T(1,128)S(1)}, u32[]{:S(2)}, u32[]{:S(2)}) collective-permute-start(f32[64,34,1]{0,2,1:T(1,128)S(1)} %get-tuple-element.255), channel_id=1, source_target_pairs={{0,1},{1,2},{2,3},{4,5},{5,6},{6,7},{8,9},{9,10},{10,11},{12,13},{... | collective-permute-start | bytes 26120 | tf_op jit(solution)/shard_map/ppermute | solution.py:14
  39.9 11.8 %copy-start.4 = (f32[64,32,128]{0,2,1:T(8,128)}, f32[64,32,128]{0,2,1:T(8,128)S(1)}, u32[]{:S(2)}) copy-start(f32[64,32,128]{0,2,1:T(8,128)S(1)} %fusion.37) | copy-start | bytes 3145732
  39.9 6.3 %collective-permute-start.8 = (f32[64,1,128]{0,2,1:T(8,128)S(1)}, f32[64,1,128]{0,2,1:T(8,128)S(1)}, u32[]{:S(2)}, u32[]{:S(2)}) collective-permute-start(f32[64,1,128]{0,2,1:T(8,128)S(1)} %get-tuple-element.258), channel_id=1, source_target_pairs={{0,4},{4,8},{8,12},{12,16},{16,20},{20,24},{24,28},{1,5},{5,9},{9,... | collective-permute-start | bytes 98312 | tf_op jit(solution)/shard_map/ppermute | solution.py:14
  44.3 7.4 %collective-permute-start.9 = (f32[64,1,128]{0,2,1:T(8,128)S(1)}, f32[64,1,128]{0,2,1:T(8,128)S(1)}, u32[]{:S(2)}, u32[]{:S(2)}) collective-permute-start(f32[64,1,128]{0,2,1:T(8,128)S(1)} %get-tuple-element.259), channel_id=1, source_target_pairs={{4,0},{8,4},{12,8},{16,12},{20,16},{24,20},{28,24},{5,1},{9,5},{13... | collective-permute-start | bytes 98312 | tf_op jit(solution)/shard_map/ppermute | solution.py:15
  51.7 4.6 %collective-permute-start.10 = (f32[64,34,1]{0,2,1:T(1,128)S(1)}, f32[64,34,1]{0,2,1:T(1,128)S(1)}, u32[]{:S(2)}, u32[]{:S(2)}) collective-permute-start(f32[64,34,1]{0,2,1:T(1,128)S(1)} %get-tuple-element.252), channel_id=1, source_target_pairs={{0,1},{1,2},{2,3},{4,5},{5,6},{6,7},{8,9},{9,10},{10,11},{12,13},{... | collective-permute-start | bytes 26120 | tf_op jit(solution)/shard_map/ppermute | solution.py:14
  55.0 6.0 %collective-permute-start.11 = (f32[64,34,1]{0,2,1:T(1,128)S(1)}, f32[64,34,1]{0,2,1:T(1,128)S(1)}, u32[]{:S(2)}, u32[]{:S(2)}) collective-permute-start(f32[64,34,1]{0,2,1:T(1,128)S(1)} %get-tuple-element.253), channel_id=1, source_target_pairs={{1,0},{2,1},{3,2},{5,4},{6,5},{7,6},{9,8},{10,9},{11,10},{13,12},{... | collective-permute-start | bytes 26120 | tf_op jit(solution)/shard_map/ppermute | solution.py:15
  56.3 7.1 %copy-start.10 = (bf16[16,16]{1,0:T(8,128)(2,1)S(1)}, bf16[16,16]{1,0:T(8,128)(2,1)}, u32[]{:S(2)}) copy-start(bf16[16,16]{1,0:T(8,128)(2,1)} %param.7) | copy-start | bytes 1540
  56.4 7.1 %copy-start.11 = (bf16[16,8]{0,1:T(8,128)(2,1)S(1)}, bf16[16,8]{0,1:T(8,128)(2,1)}, u32[]{:S(2)}) copy-start(bf16[16,8]{0,1:T(8,128)(2,1)} %param.6) | copy-start | bytes 772
  63.7 21.0 %copy-start.1 = (f32[66,34,130]{0,2,1:T(8,128)}, f32[66,34,130]{0,2,1:T(8,128)S(1)}, u32[]{:S(2)}) copy-start(f32[66,34,130]{0,2,1:T(8,128)S(1)} %get-tuple-element.396) | copy-start | bytes 3500644 | tf_op jit(solution)/shard_map/while
  105.2 2.6 copy-start.8
  108.8 3.7 %copy-start.9 = (f32[8,64,128]{2,0,1:T(8,128)}, f32[8,64,128]{2,0,1:T(8,128)S(1)}, u32[]{:S(2)}) copy-start(f32[8,64,128]{2,0,1:T(8,128)S(1)} %get-tuple-element.393) | copy-start | bytes 786436 | tf_op jit(solution)/shard_map/while
  108.8 3.7 %copy-start.3 = (f32[16,64,8,128]{3,0,2,1:T(8,128)S(1)}, f32[16,64,8,128]{3,0,2,1:T(8,128)}, u32[]{:S(2)}) copy-start(f32[16,64,8,128]{3,0,2,1:T(8,128)} %convolution_bitcast_fusion.2) | copy-start | bytes 12582916 | tf_op jit(solution)/shard_map/while
  112.5 5.8 %copy-start = (f32[8,64,8,128]{3,2,1,0:T(8,128)}, f32[8,64,8,128]{3,2,1,0:T(8,128)S(1)}, u32[]{:S(2)}) copy-start(f32[8,64,8,128]{3,2,1,0:T(8,128)S(1)} %fusion.83) | copy-start | bytes 6291460 | tf_op jit(solution)/shard_map/while
  118.4 6.7 %copy-start.5 = (f32[8,64,128]{2,0,1:T(8,128)S(1)}, f32[8,64,128]{2,0,1:T(8,128)}, u32[]{:S(2)}) copy-start(f32[8,64,128]{2,0,1:T(8,128)} %get-tuple-element.377) | copy-start | bytes 786436 | tf_op jit(solution)/shard_map/while
  122.0 3.9 %copy-start.2 = (f32[66,34,130]{0,2,1:T(8,128)S(1)}, f32[66,34,130]{0,2,1:T(8,128)}, u32[]{:S(2)}) copy-start(f32[66,34,130]{0,2,1:T(8,128)} %copy-done.1) | copy-start | bytes 3500644 | tf_op jit(solution)/shard_map/while
  125.1 0.7 copy-start.6
  125.8 21.0 %copy-start.1 = (f32[66,34,130]{0,2,1:T(8,128)}, f32[66,34,130]{0,2,1:T(8,128)S(1)}, u32[]{:S(2)}) copy-start(f32[66,34,130]{0,2,1:T(8,128)S(1)} %get-tuple-element.396) | copy-start | bytes 3500644 | tf_op jit(solution)/shard_map/while
  167.4 2.6 copy-start.8
  171.0 3.7 %copy-start.9 = (f32[8,64,128]{2,0,1:T(8,128)}, f32[8,64,128]{2,0,1:T(8,128)S(1)}, u32[]{:S(2)}) copy-start(f32[8,64,128]{2,0,1:T(8,128)S(1)} %get-tuple-element.393) | copy-start | bytes 786436 | tf_op jit(solution)/shard_map/while
  171.0 3.7 %copy-start.3 = (f32[16,64,8,128]{3,0,2,1:T(8,128)S(1)}, f32[16,64,8,128]{3,0,2,1:T(8,128)}, u32[]{:S(2)}) copy-start(f32[16,64,8,128]{3,0,2,1:T(8,128)} %convolution_bitcast_fusion.2) | copy-start | bytes 12582916 | tf_op jit(solution)/shard_map/while
  174.7 5.8 %copy-start = (f32[8,64,8,128]{3,2,1,0:T(8,128)}, f32[8,64,8,128]{3,2,1,0:T(8,128)S(1)}, u32[]{:S(2)}) copy-start(f32[8,64,8,128]{3,2,1,0:T(8,128)S(1)} %fusion.83) | copy-start | bytes 6291460 | tf_op jit(solution)/shard_map/while
  180.6 6.7 %copy-start.5 = (f32[8,64,128]{2,0,1:T(8,128)S(1)}, f32[8,64,128]{2,0,1:T(8,128)}, u32[]{:S(2)}) copy-start(f32[8,64,128]{2,0,1:T(8,128)} %get-tuple-element.377) | copy-start | bytes 786436 | tf_op jit(solution)/shard_map/while
  184.1 3.9 %copy-start.2 = (f32[66,34,130]{0,2,1:T(8,128)S(1)}, f32[66,34,130]{0,2,1:T(8,128)}, u32[]{:S(2)}) copy-start(f32[66,34,130]{0,2,1:T(8,128)} %copy-done.1) | copy-start | bytes 3500644 | tf_op jit(solution)/shard_map/while
  188.0 21.0 %copy-start.1 = (f32[66,34,130]{0,2,1:T(8,128)}, f32[66,34,130]{0,2,1:T(8,128)S(1)}, u32[]{:S(2)}) copy-start(f32[66,34,130]{0,2,1:T(8,128)S(1)} %get-tuple-element.396) | copy-start | bytes 3500644 | tf_op jit(solution)/shard_map/while
  229.5 2.6 copy-start.8
  233.2 3.7 %copy-start.9 = (f32[8,64,128]{2,0,1:T(8,128)}, f32[8,64,128]{2,0,1:T(8,128)S(1)}, u32[]{:S(2)}) copy-start(f32[8,64,128]{2,0,1:T(8,128)S(1)} %get-tuple-element.393) | copy-start | bytes 786436 | tf_op jit(solution)/shard_map/while
  233.2 3.7 %copy-start.3 = (f32[16,64,8,128]{3,0,2,1:T(8,128)S(1)}, f32[16,64,8,128]{3,0,2,1:T(8,128)}, u32[]{:S(2)}) copy-start(f32[16,64,8,128]{3,0,2,1:T(8,128)} %convolution_bitcast_fusion.2) | copy-start | bytes 12582916 | tf_op jit(solution)/shard_map/while
  236.8 5.8 %copy-start = (f32[8,64,8,128]{3,2,1,0:T(8,128)}, f32[8,64,8,128]{3,2,1,0:T(8,128)S(1)}, u32[]{:S(2)}) copy-start(f32[8,64,8,128]{3,2,1,0:T(8,128)S(1)} %fusion.83) | copy-start | bytes 6291460 | tf_op jit(solution)/shard_map/while
  242.7 6.7 %copy-start.5 = (f32[8,64,128]{2,0,1:T(8,128)S(1)}, f32[8,64,128]{2,0,1:T(8,128)}, u32[]{:S(2)}) copy-start(f32[8,64,128]{2,0,1:T(8,128)} %get-tuple-element.377) | copy-start | bytes 786436 | tf_op jit(solution)/shard_map/while
  246.3 3.9 %copy-start.2 = (f32[66,34,130]{0,2,1:T(8,128)S(1)}, f32[66,34,130]{0,2,1:T(8,128)}, u32[]{:S(2)}) copy-start(f32[66,34,130]{0,2,1:T(8,128)} %copy-done.1) | copy-start | bytes 3500644 | tf_op jit(solution)/shard_map/while
  249.5 0.7 copy-start.6
  250.2 21.0 %copy-start.1 = (f32[66,34,130]{0,2,1:T(8,128)}, f32[66,34,130]{0,2,1:T(8,128)S(1)}, u32[]{:S(2)}) copy-start(f32[66,34,130]{0,2,1:T(8,128)S(1)} %get-tuple-element.396) | copy-start | bytes 3500644 | tf_op jit(solution)/shard_map/while
  291.7 2.6 copy-start.8
  295.3 3.7 %copy-start.9 = (f32[8,64,128]{2,0,1:T(8,128)}, f32[8,64,128]{2,0,1:T(8,128)S(1)}, u32[]{:S(2)}) copy-start(f32[8,64,128]{2,0,1:T(8,128)S(1)} %get-tuple-element.393) | copy-start | bytes 786436 | tf_op jit(solution)/shard_map/while
  295.3 3.7 %copy-start.3 = (f32[16,64,8,128]{3,0,2,1:T(8,128)S(1)}, f32[16,64,8,128]{3,0,2,1:T(8,128)}, u32[]{:S(2)}) copy-start(f32[16,64,8,128]{3,0,2,1:T(8,128)} %convolution_bitcast_fusion.2) | copy-start | bytes 12582916 | tf_op jit(solution)/shard_map/while
  299.0 5.8 %copy-start = (f32[8,64,8,128]{3,2,1,0:T(8,128)}, f32[8,64,8,128]{3,2,1,0:T(8,128)S(1)}, u32[]{:S(2)}) copy-start(f32[8,64,8,128]{3,2,1,0:T(8,128)S(1)} %fusion.83) | copy-start | bytes 6291460 | tf_op jit(solution)/shard_map/while
  304.9 6.7 %copy-start.5 = (f32[8,64,128]{2,0,1:T(8,128)S(1)}, f32[8,64,128]{2,0,1:T(8,128)}, u32[]{:S(2)}) copy-start(f32[8,64,128]{2,0,1:T(8,128)} %get-tuple-element.377) | copy-start | bytes 786436 | tf_op jit(solution)/shard_map/while
  308.5 3.9 %copy-start.2 = (f32[66,34,130]{0,2,1:T(8,128)S(1)}, f32[66,34,130]{0,2,1:T(8,128)}, u32[]{:S(2)}) copy-start(f32[66,34,130]{0,2,1:T(8,128)} %copy-done.1) | copy-start | bytes 3500644 | tf_op jit(solution)/shard_map/while
  312.3 7.0 %copy-start.7 = (f32[8,64,128]{2,0,1:T(8,128)S(1)}, f32[8,64,128]{2,0,1:T(8,128)}, u32[]{:S(2)}) copy-start(f32[8,64,128]{2,0,1:T(8,128)} %get-tuple-element.156) | copy-start | bytes 786436
  314.5 8.4 %all-to-all-start.1 = ((f32[4,1,8192]{2,1,0:T(1,128)}), f32[4,1,8192]{2,1,0:T(1,128)S(1)}, u32[]{:S(2)}, u32[]{:S(2)}) async-start(f32[4,1,8192]{2,1,0:T(1,128)} %reshape.38), calls=%async_computation.1 | async-start | bytes 262144 | tf_op jit(solution)/shard_map/all_to_all | solution.py:146
  322.9 20.4 %all-to-all-start = ((f32[1,2,8,64,128]{4,2,1,0,3:T(8,128)}), f32[1,2,8,64,128]{4,2,1,0,3:T(8,128)S(1)}, u32[]{:S(2)}, u32[]{:S(2)}) async-start(f32[1,2,8,64,128]{4,2,1,0,3:T(8,128)} %maximum_bitcast_fusion.1), calls=%async_computation | async-start | bytes 1048576 | tf_op jit(solution)/shard_map/all_to_all | solution.py:148
  (2 other events, 1.4 us)
where the time goes:
time: 347 us; the launch traced here: 345 us
  local copies, waits for them, and re-layouts  132 us (38%)
  other arithmetic  96.4 us (28%)
  starting transfers between devices  42.2 us (12%)
  matrix products  37.8 us (11%)
  waiting for transfers between devices  31.6 us (9%)
  loops' own time  3.83 us (1%)
    while x96, local copies, waits for them, and re-layouts  65 us
    ppermute x6, starting transfers between devices, extended_2(): before = lax.ppermute(last, axis, up)  24.5 us
    reduce_sum x4, other arithmetic, advance(): jnp.sum(jnp.exp(-(running_y - thickness_y)) * -jnp.expm1(-thickness_y) *...  23 us
    another operation x32, local copies, waits for them, and re-layouts, transfer(): jnp.stack([centre, scaled_x, scaled_y, scaled_z, magnitude, centre * magn...  18.7 us
    mul x4, other arithmetic, advance(): thickness = absorption * step_x  16.9 us
    dot_general x4, matrix products, transfer(): jnp.einsum('ch,hzxy->czxy', transfer_out, hidden, preferred_element_type=...  15 us
    dot_general x4, matrix products, advance(): jnp.einsum('bzxy,yw->bzxw', thickness_y, upper_y, precision=lax.Precision...  14.5 us
    slice x4, local copies, waits for them, and re-layouts, advance(): clear_y = jnp.exp(-running_y[..., -1])  14.3 us
  transfers between devices with their start and end apart: 14, of which 11 were waited for; matrix products, arithmetic and copies ran while one was open for 1% of the time, Pallas kernels for 0%

commit v1 on v0

v1 whole, which is shorter than its diff:
```python
import functools

import jax
import jax.numpy as jnp
from jax import lax
from jax.experimental import pallas as pl
from jax.experimental.pallas import tpu as pltpu
from jax.sharding import PartitionSpec as P

F32 = jnp.float32
LOG2E = 1.4426950408889634
SUB = 8
LANES = 128
REACH = 3
VMEM = pl.BlockSpec(memory_space=pltpu.VMEM)
PARAMS = pltpu.CompilerParams(vmem_limit_bytes=48 * 1024 * 1024)


def strips_kernel(field_ref, low_ref, high_ref):
    length = field_ref.shape[1]
    for k in range(REACH):
        low_ref[k] = field_ref[:, k, :]
        high_ref[k] = field_ref[:, length - REACH + k, :]


def turn_kernel(field_ref, before_ref, after_ref, out_ref, first_ref, last_ref):
    layers, length, width = field_ref.shape
    half = length // 2

    def row(x):
        if x < 0:
            return before_ref[x + REACH]
        if x >= length:
            return after_ref[x - length]
        return field_ref[:, x, :]

    for k in range(half + 2 * REACH):
        x = k - REACH
        turned = jnp.concatenate([row(x), row(x + half)], axis=0).T
        out_ref[k] = turned
        for j in range(REACH):
            first_ref[j, k : k + 1] = turned[j : j + 1]
            last_ref[j, k : k + 1] = turned[width - REACH + j : width - REACH + j + 1]


def over_sublanes(colour, clear):
    for shift in (1, 2, 4):
        rolled_c = pltpu.roll(colour, SUB - shift, axis=0)
        rolled_q = pltpu.roll(clear, SUB - shift, axis=0)
        colour = colour + clear * rolled_c
        clear = clear * rolled_q
    return colour, clear


def march_kernel(
    spans,
    flags,
    steps,
    bands,
    turned_ref,
    before_ref,
    after_ref,
    win_ref,
    wout_ref,
    image_x_ref,
    image_y_ref,
    raw_ref,
    once_ref,
    twice_ref,
    ridge_ref,
    tx_ref,
    cx_ref,
    ty_ref,
    cy_ref,
    rows_ref,
    rows_y_ref,
):
    wide_x, width, _ = turned_ref.shape
    half = wide_x - 2 * REACH
    run = width // SUB
    hidden_units = win_ref.shape[0] // 16
    layers = LANES // 2
    lane = lax.broadcasted_iota(jnp.int32, (SUB, LANES), 1)
    chunk = lax.broadcasted_iota(jnp.int32, (SUB, LANES), 0)
    z = lane % layers
    near = (z > 0).astype(F32)
    far = (z < layers - 1).astype(F32)
    at_x, at_y = lax.axis_index("bx"), lax.axis_index("by")
    count_x, count_y = flags
    mask_x_low = jnp.where((lane < layers) & (at_x == 0), 0.0, 1.0)
    mask_x_high = jnp.where((lane >= layers) & (at_x == count_x - 1), 0.0, 1.0)
    mask_y_low = jnp.where((chunk == 0) & (at_y == 0), 0.0, 1.0)
    mask_y_high = jnp.where((chunk == SUB - 1) & (at_y == count_y - 1), 0.0, 1.0)

    def z_sum(value):
        return pltpu.roll(value, 1, axis=1) * near + pltpu.roll(value, LANES - 1, axis=1) * far

    def fill(k, _):
        raw_ref[k, REACH : REACH + width] = turned_ref[k]
        for j in range(REACH):
            raw_ref[k, j : j + 1] = before_ref[j, pl.ds(k, 1)]
            raw_ref[k, REACH + width + j : REACH + width + j + 1] = after_ref[j, pl.ds(k, 1)]
        return 0

    lax.fori_loop(0, wide_x, fill, 0)

    def raw(k, y):
        return raw_ref[k, pl.ds(y + REACH, SUB, stride=run), :]

    def masked(value, y):
        if y < 0:
            value = value * mask_y_low
        if y >= run:
            value = value * mask_y_high
        return value

    low, high = spans[0][0], spans[-1][1]

    def smooth(centre, others):
        total = z_sum(centre)
        for other in others:
            total = total + other
        return 0.4 * centre + 0.1 * total

    def smooth_once(k, _):
        column = [raw(k + 1, y) for y in range(low - 3, high + 3)]
        for i in range(1, len(column) - 1):
            y = low - 3 + i
            value = smooth(column[i], [column[i - 1], column[i + 1], raw(k, y), raw(k + 2, y)])
            once_ref[k, y + 2] = masked(value, y)
        return 0

    lax.fori_loop(0, half + 4, smooth_once, 0)
    for ref, margin, ys in ((once_ref, 2, range(low - 2, high + 2)),):
        for y in ys:
            for k in (0, 1):
                ref[k, y + margin] = ref[k, y + margin] * mask_x_low
                ref[half + 2 + k, y + margin] = ref[half + 2 + k, y + margin] * mask_x_high

    def smooth_twice(k, _):
        at_low = jnp.where(k == 0, mask_x_low, 1.0)
        at_high = jnp.where(k == half + 1, mask_x_high, 1.0)
        edge = at_low * at_high
        column = [once_ref[k + 1, y + 2] for y in range(low - 2, high + 2)]
        for i in range(1, len(column) - 1):
            y = low - 2 + i
            value = smooth(
                column[i], [column[i - 1], column[i + 1], once_ref[k, y + 2], once_ref[k + 2, y + 2]]
            )
            value = masked(value * edge, y)
            twice_ref[k, y + 1] = value
            ridge_ref[k, y + 1] = 2.0 * value + z_sum(value)
        return 0

    lax.fori_loop(0, half + 2, smooth_twice, 0)

    ones = jnp.ones((16, 2 * LANES), jnp.bfloat16)

    def features(k, y):
        p = lambda a, b: twice_ref[k + 1 + a, y + 1 + b]
        r = lambda a, b: ridge_ref[k + 1 + a, y + 1 + b]
        centre = p(0, 0)
        pp, pm, mp, mm = p(1, 1), p(1, -1), p(-1, 1), p(-1, -1)
        main, cross = pp - mm, pm - mp
        third = 1.0 / 3.0
        gx = (main + cross + (r(1, 0) - r(-1, 0))) * third
        gy = (main - cross + (r(0, 1) - r(0, -1))) * third
        around = 2.0 * centre + ((p(1, 0) + p(-1, 0)) + (p(0, 1) + p(0, -1)))
        gz = (pltpu.roll(around, LANES - 1, axis=1) * far - pltpu.roll(around, 1, axis=1) * near) * third
        m = jnp.sqrt(1.0 + gx * gx + gy * gy + gz * gz)
        return [centre, gx, gy, gz, m, centre * m, centre * centre]

    def square(parts):
        return jnp.concatenate(
            [
                jnp.concatenate([parts[0], parts[1]], axis=1),
                jnp.concatenate([parts[2], parts[3]], axis=1),
            ],
            axis=0,
        )

    def network(x0, y):
        cells = [features(x0 + i, y) for i in range(4)]
        rows = [square([cell[f] for cell in cells]).astype(jnp.bfloat16) for f in range(7)] + [ones]
        packed = jnp.concatenate(rows, axis=0)
        half_v = jnp.dot(win_ref[...], packed, preferred_element_type=F32)
        hidden = (half_v + half_v * jnp.tanh(half_v)).astype(jnp.bfloat16)
        v = jnp.dot(wout_ref[...], hidden, preferred_element_type=F32)
        soft = jnp.maximum(v, jnp.log(1.0 + jnp.exp2(jnp.minimum(v * LOG2E, 126.0))))
        split = bands * 16
        emission = soft[:split]
        clear_y = jnp.exp2(soft[split:] * (-LOG2E * steps[1]))
        return emission, clear_y

    ratio = steps[0] / steps[1]

    def clear_of_x(q):
        if ratio == 1.0:
            return q
        if ratio == 2.0:
            return q * q
        return jnp.exp2(jnp.log(q) * (LOG2E * ratio))

    def cell_of(values, band, i):
        j, h = divmod(i, 2)
        return values[band * 16 + j * 8 : band * 16 + j * 8 + 8, h * LANES : (h + 1) * LANES]

    nys = sum(b - a for a, b in spans)
    zeros = jnp.zeros((SUB, LANES), F32)
    unit = jnp.ones((SUB, LANES), F32)

    def reset(k, _):
        for band in range(bands):
            ty_ref[k, band] = unit
            cy_ref[k, band] = zeros
        return 0

    lax.fori_loop(0, half, reset, 0)
    for k in range(nys):
        for band in range(bands):
            tx_ref[k, band] = unit
            cx_ref[k, band] = zeros

    slot0 = 0
    for first, last in spans:
        for y0 in range(first, last, 4):
            count = min(4, last - y0)

            def block(xb, _, y0=y0, count=count, slot=slot0 + y0 - first):
                x0 = xb * 4
                results = [network(x0, y0 + j) for j in range(count)]
                for band in range(bands):
                    ty = [ty_ref[x0 + i, band] for i in range(4)]
                    cy = [cy_ref[x0 + i, band] for i in range(4)]
                    for j, (emission, clear) in enumerate(results):
                        tx = tx_ref[slot + j, band]
                        cx = cx_ref[slot + j, band]
                        for i in range(4):
                            e = cell_of(emission, band, i)
                            q = cell_of(clear, band, i)
                            later = ty[i] * q
                            cy[i] = cy[i] + (ty[i] - later) * e
                            ty[i] = later
                            later = tx * clear_of_x(q)
                            cx = cx + (tx - later) * e
                            tx = later
                        tx_ref[slot + j, band] = tx
                        cx_ref[slot + j, band] = cx
                    for i in range(4):
                        ty_ref[x0 + i, band] = ty[i]
                        cy_ref[x0 + i, band] = cy[i]
                return 0

            lax.fori_loop(0, half // 4, block, 0)
        slot0 += last - first

    front = lane < layers
    for band in range(bands):
        for k in range(nys):
            colour, clear = cx_ref[k, band], tx_ref[k, band]
            colour = colour + clear * pltpu.roll(colour, layers, axis=1)
            clear = clear * pltpu.roll(clear, layers, axis=1)
            rows_ref[pl.ds(k, SUB, stride=nys), :] = jnp.where(
                front, colour, pltpu.roll(clear, layers, axis=1)
            )
        turned = rows_ref[...].T
        for kind in range(2):
            for d in range(layers // SUB):
                start = kind * layers + d * SUB
                image_x_ref[d, kind, band] = turned[start : start + SUB]

    def fold_y(k, _):
        for band in range(bands):
            colour, clear = over_sublanes(cy_ref[k, band], ty_ref[k, band])
            rows_y_ref[pl.ds(band * half + k, 1), :] = colour[:1]
            rows_y_ref[pl.ds((bands + band) * half + k, 1), :] = clear[:1]
        return 0

    lax.fori_loop(0, half, fold_y, 0)
    for kind in range(2):
        turned = rows_y_ref[kind * LANES : (kind + 1) * LANES].T
        image_y_ref[kind] = turned


def fold_kernel(pieces_ref, out_ref):
    colour, clear = pieces_ref[0, 0], pieces_ref[0, 1]
    for k in range(1, pieces_ref.shape[0]):
        colour = colour + clear * pieces_ref[k, 0]
        clear = clear * pieces_ref[k, 1]
    out_ref[0] = colour
    out_ref[1] = clear


def fold(pieces):
    return pl.pallas_call(
        fold_kernel,
        out_shape=jax.ShapeDtypeStruct(pieces.shape[1:], F32),
        in_specs=[VMEM],
        out_specs=VMEM,
        name="fold",
    )(pieces)


def exchange(last, first, axis):
    peers = lax.axis_size(axis)
    up = [(i, i + 1) for i in range(peers - 1)]
    down = [(j, i) for i, j in up]
    return lax.ppermute(last, axis, up), lax.ppermute(first, axis, down)


def body(scalar_field, transfer_in, transfer_out):
    layers, local_x, local_y = scalar_field.shape
    bands = transfer_out.shape[0] // 2
    count_x = lax.axis_size("bx")
    count_y = lax.axis_size("by")
    steps = (2.0 / (local_x * count_x), 2.0 / (local_y * count_y))
    half = local_x // 2
    wide = half + 2 * REACH
    run = local_y // SUB
    sds = jax.ShapeDtypeStruct
    eye = jnp.eye(16, dtype=jnp.bfloat16)
    win = jnp.kron(transfer_in * jnp.bfloat16(0.5), eye)
    wout = jnp.kron(transfer_out, eye)

    strip = sds((REACH, layers, local_y), F32)
    first, last = pl.pallas_call(
        strips_kernel,
        out_shape=[strip, strip],
        in_specs=[VMEM],
        out_specs=[VMEM, VMEM],
        compiler_params=PARAMS,
        name="strips",
    )(scalar_field)
    before, after = exchange(last, first, "bx")
    edge = sds((REACH, wide, LANES), F32)
    turned, first, last = pl.pallas_call(
        turn_kernel,
        out_shape=[sds((wide, local_y, LANES), F32), edge, edge],
        in_specs=[VMEM] * 3,
        out_specs=[VMEM] * 3,
        compiler_params=PARAMS,
        name="turn",
    )(scalar_field, before, after)
    before, after = exchange(last, first, "by")
    spans = ((0, run),)
    scratch = [
        pltpu.VMEM((wide, local_y + 2 * SUB, LANES), F32),
        pltpu.VMEM((half + 4, run + 4, SUB, LANES), F32),
        pltpu.VMEM((half + 2, run + 2, SUB, LANES), F32),
        pltpu.VMEM((half + 2, run + 2, SUB, LANES), F32),
        pltpu.VMEM((run, bands, SUB, LANES), F32),
        pltpu.VMEM((run, bands, SUB, LANES), F32),
        pltpu.VMEM((half, bands, SUB, LANES), F32),
        pltpu.VMEM((half, bands, SUB, LANES), F32),
        pltpu.VMEM((local_y, LANES), F32),
        pltpu.VMEM((2 * bands * half, LANES), F32),
    ]
    image_x, image_y = pl.pallas_call(
        functools.partial(march_kernel, spans, (count_x, count_y), steps, bands),
        out_shape=[
            sds((layers // SUB, 2, bands, SUB, local_y), F32),
            sds((2, LANES, bands * half), F32),
        ],
        in_specs=[VMEM] * 5,
        out_specs=[VMEM] * 2,
        scratch_shapes=scratch,
        compiler_params=PARAMS,
        name="march",
    )(turned, before, after, win, wout)
    share = layers // count_y
    pieces = image_y.reshape(2, 2, count_y, share, bands * half)
    pieces = jnp.transpose(pieces, (2, 0, 1, 3, 4)).reshape(count_y, 2, 2 * share, bands * half)
    pieces = lax.all_to_all(pieces, "by", split_axis=0, concat_axis=0, tiled=True)
    view_y = fold(pieces)
    view_y = jnp.transpose(
        view_y.reshape(2, 2, share, bands, half), (0, 3, 2, 1, 4)
    ).reshape(2, bands, share, local_x)
    share_x = layers // count_x
    image_x = image_x.reshape(layers // SUB, 2, bands, SUB, local_y)
    if share_x != SUB:
        image_x = jnp.transpose(image_x, (1, 2, 0, 3, 4)).reshape(2, bands, count_x, share_x, local_y)
        image_x = jnp.transpose(image_x, (2, 0, 1, 3, 4))
    pieces = lax.all_to_all(image_x, "bx", split_axis=0, concat_axis=0, tiled=True)
    view_x = fold(pieces)
    return (view_x, view_y)


def solution(mesh):
    return jax.shard_map(
        body,
        mesh=mesh,
        in_specs=(P(None, "bx", "by"), P(), P()),
        out_specs=(P(None, None, "bx", "by"), P(None, None, "by", "bx")),
        check_vma=False,
    )
```

time: 347 us -> 81.6 us (0.24)
  local copies, waits for them, and re-layouts: 132 us -> 6.6 us
  other arithmetic: 96.4 us -> 1.92 us
  matrix products: 37.8 us -> 0 us
  Pallas kernels: 0 us -> 32.9 us
  starting transfers between devices: 42.2 us -> 14.6 us
  waiting for transfers between devices: 31.6 us -> 14.9 us
  blocking collectives: 0 us -> 9.46 us
  loops' own time: 3.83 us -> 0 us
    while x96 -> x0, local copies, waits for them, and re-layouts: 65 us -> none
    dot_general x12 -> x0, matrix products: 37.8 us -> none  [the longest x4 15 us: transfer(): jnp.einsum('ch,hzxy->czxy', transfer_out, hidden, preferred_element_type=...]
    pallas_call x0 -> x5, Pallas kernels: none -> 32.9 us  [the longest x1 28.7 us: body(): pl.pallas_call(functools.partial(march_kernel, spans, (count_x, count_y),...]
    slice x27 -> x0, local copies, waits for them, and re-layouts: 28.7 us -> none  [the longest x4 14.3 us: advance(): clear_y = jnp.exp(-running_y[..., -1])]
    ppermute x12 -> x4, starting transfers between devices: 32.3 us -> 8.86 us  [exchange(): return (lax.ppermute(last, axis, up), lax.ppermute(first, axis, down))]
    reduce_sum x4 -> x0, other arithmetic: 23 us -> none  [advance(): jnp.sum(jnp.exp(-(running_y - thickness_y)) * -jnp.expm1(-thickness_y) *...]
    another operation x41 -> x0, local copies, waits for them, and re-layouts: 21.1 us -> none  [the longest x32 18.7 us: transfer(): jnp.stack([centre, scaled_x, scaled_y, scaled_z, magnitude, centre * magn...]
    sub x12 -> x0, other arithmetic: 20.5 us -> none  [the longest x4 10.9 us: gradients(): diff_z = padded[2:] - padded[:-2]]
  transfers between devices with their start and end apart: 14 -> 5, of which waited for: 11 -> 3; matrix products, arithmetic and copies ran while one was open for 1% -> 8% of each run, Pallas kernels for 0% -> 2%
where the time goes in v1:
time: 81.6 us; the launch traced here: 81.1 us
  Pallas kernels  32.9 us (40%)
  waiting for transfers between devices  14.9 us (18%)
  starting transfers between devices  14.6 us (18%)
  blocking collectives  9.46 us (12%)
  local copies, waits for them, and re-layouts  6.6 us (8%)
  other arithmetic  1.92 us (2%)
    pallas_call x1, Pallas kernels, body(): pl.pallas_call(functools.partial(march_kernel, spans, (count_x, count_y),...  28.7 us
    all_to_all x1, waiting for transfers between devices, body(): lax.all_to_all(image_x, 'bx', split_axis=0, concat_axis=0, tiled=True)  10.7 us
    all_to_all x1, blocking collectives, body(): lax.all_to_all(pieces, 'by', split_axis=0, concat_axis=0, tiled=True)  9.46 us
    ppermute x4, starting transfers between devices, exchange(): return (lax.ppermute(last, axis, up), lax.ppermute(first, axis, down))  8.86 us
    all_to_all x1, starting transfers between devices, body(): lax.all_to_all(image_x, 'bx', split_axis=0, concat_axis=0, tiled=True)  5.75 us
    ppermute x4, waiting for transfers between devices, exchange(): return (lax.ppermute(last, axis, up), lax.ppermute(first, axis, down))  4.17 us
    pallas_call x2, Pallas kernels, fold(): pl.pallas_call(fold_kernel, out_shape=jax.ShapeDtypeStruct(pieces.shape[1...  3.23 us
    mul x1, local copies, waits for them, and re-layouts, body(): wout = jnp.kron(transfer_out, eye)  2.22 us
  transfers between devices with their start and end apart: 5, of which 3 were waited for; matrix products, arithmetic and copies ran while one was open for 8% of the time, Pallas kernels for 2%

profile of v1, /device:TPU:0, one launch (start us, length us, event | category | flops | bytes accessed | tf_op | source)
XLA Modules:
  0.0 81.1 jit_solution(6865826713719447798)
XLA Ops:
  0.6 0.0 copy-start
  0.6 1.2 %copy-done = f32[64,32,128]{2,1,0:T(8,128)S(1)} copy-done((f32[64,32,128]{2,1,0:T(8,128)S(1)}, f32[64,32,128]{2,1,0:T(8,128)}, u32[]{:S(2)}) %copy-start) | copy-done | bytes 1048600
  1.9 0.0 copy-start.3
  1.9 0.0 copy-start.1
  1.9 0.1 strips.1
  2.0 5.0 %collective-permute-start = (f32[3,64,128]{2,1,0:T(8,128)S(1)}, f32[3,64,128]{2,1,0:T(8,128)S(1)}, u32[]{:S(2)}, u32[]{:S(2)}) collective-permute-start(f32[3,64,128]{2,1,0:T(8,128)S(1)} %get-tuple-element.9), channel_id=1, source_target_pairs={{0,4},{4,8},{8,12},{12,16},{16,20},{20,24},{24,28},{1,5},{5,9},{9,... | collective-permute-start | bytes 294920 | tf_op jit(solution)/shard_map/ppermute | solution.py:308
  7.0 1.3 %collective-permute-start.1 = (f32[3,64,128]{2,1,0:T(8,128)S(1)}, f32[3,64,128]{2,1,0:T(8,128)S(1)}, u32[]{:S(2)}, u32[]{:S(2)}) collective-permute-start(f32[3,64,128]{2,1,0:T(8,128)S(1)} %get-tuple-element.10), channel_id=1, source_target_pairs={{4,0},{8,4},{12,8},{16,12},{20,16},{24,20},{28,24},{5,1},{9,5},{13... | collective-permute-start | bytes 294920 | tf_op jit(solution)/shard_map/ppermute | solution.py:308
  8.3 1.8 %broadcast_multiply_fusion = bf16[16,16,16,16]{3,2,1,0:T(8,128)(2,1)} fusion(bf16[16,16]{1,0:T(8,128)(2,1)S(1)} %fusion, bf16[16,16]{1,0:T(8,128)(2,1)} %param.5), kind=kLoop, calls=%fused_computation | loop fusion | flops 65536 | bytes 132096 | tf_op jit(solution)/shard_map/jit(kron)/mul | solution.py:323
  10.1 0.0 copy-done.3
  10.1 0.1 copy.5
  10.2 0.0 collective-permute-done.before_ref
  10.2 3.3 %collective-permute-done.1.after_ref = f32[3,64,128]{2,1,0:T(8,128)S(1)} collective-permute-done((f32[3,64,128]{2,1,0:T(8,128)S(1)}, f32[3,64,128]{2,1,0:T(8,128)S(1)}, u32[]{:S(2)}, u32[]{:S(2)}) %collective-permute-start.1) | collective-permute-done | bytes 98336 | tf_op jit(solution)/shard_map/ppermute | solution.py:308
  13.5 0.0 copy-done.1
  13.5 0.8 turn.1
  14.3 1.3 %collective-permute-start.2 = (f32[3,22,128]{2,1,0:T(8,128)S(1)}, f32[3,22,128]{2,1,0:T(8,128)S(1)}, u32[]{:S(2)}, u32[]{:S(2)}) collective-permute-start(f32[3,22,128]{2,1,0:T(8,128)S(1)} %get-tuple-element.12), channel_id=1, source_target_pairs={{0,1},{1,2},{2,3},{4,5},{5,6},{6,7},{8,9},{9,10},{10,11},{12,13},{... | collective-permute-start | bytes 101384 | tf_op jit(solution)/shard_map/ppermute | solution.py:308
  15.6 1.3 %collective-permute-start.3 = (f32[3,22,128]{2,1,0:T(8,128)S(1)}, f32[3,22,128]{2,1,0:T(8,128)S(1)}, u32[]{:S(2)}, u32[]{:S(2)}) collective-permute-start(f32[3,22,128]{2,1,0:T(8,128)S(1)} %get-tuple-element.13), channel_id=1, source_target_pairs={{1,0},{2,1},{3,2},{5,4},{6,5},{7,6},{9,8},{10,9},{11,10},{13,12},{... | collective-permute-start | bytes 101384 | tf_op jit(solution)/shard_map/ppermute | solution.py:308
  16.9 0.1 broadcast_multiply_fusion.1
  17.0 0.3 mul.59.win_ref
  17.4 2.2 %mul.63.wout_ref = bf16[256,256]{1,0:T(8,128)(2,1)S(1)} reshape(bf16[16,16,16,16]{3,2,1,0:T(8,128)(2,1)} %broadcast_multiply_fusion) | data formatting | bytes 262144 | tf_op jit(solution)/shard_map/jit(kron)/mul | solution.py:323
  19.6 0.0 collective-permute-done.2.before_ref
  19.6 0.9 %collective-permute-done.3.after_ref = f32[3,22,128]{2,1,0:T(8,128)S(1)} collective-permute-done((f32[3,22,128]{2,1,0:T(8,128)S(1)}, f32[3,22,128]{2,1,0:T(8,128)S(1)}, u32[]{:S(2)}, u32[]{:S(2)}) %collective-permute-start.3) | collective-permute-done | bytes 33824 | tf_op jit(solution)/shard_map/ppermute | solution.py:308
  20.5 28.7 %march.1 = (f32[8,2,8,8,128]{4,3,2,1,0:T(8,128)}, f32[2,128,128]{2,1,0:T(8,128)S(1)}) custom-call(f32[22,128,128]{2,1,0:T(8,128)S(1)} %get-tuple-element.11.turned_ref, f32[3,22,128]{2,1,0:T(8,128)S(1)} %collective-permute-done.2.before_ref, f32[3,22,128]{2,1,0:T(8,128)S(1)} %collective-permute-done.3.after_ref, bf16[256,128]{1,0:T(8,128)(2,1)S(1)} %mul.59.win_ref, ...), custom_call_target="tpu_custom_call" | custom-call | tf_op jit(solution)/shard_map/march/pallas_call | solution.py:358
  49.2 9.5 %all_to_all.10.pieces_ref = f32[4,2,32,128]{3,2,1,0:T(8,128)} all-to-all(f32[4,2,32,128]{3,2,1,0:T(8,128)S(1)} %bitcast.11), channel_id=1, replica_groups=mesh['bx'=8,'by'=4] {'by'}, dimensions={0} | all-to-all | bytes 262144 | tf_op jit(solution)/shard_map/all_to_all | solution.py:373
  58.7 5.7 %all-to-all-start = ((f32[8,2,8,8,128]{4,3,2,1,0:T(8,128)}), f32[8,2,8,8,128]{4,3,2,1,0:T(8,128)S(1)}, u32[]{:S(2)}, u32[]{:S(2)}) async-start(f32[8,2,8,8,128]{4,3,2,1,0:T(8,128)} %get-tuple-element.14), calls=%async_computation | async-start | bytes 1048576 | tf_op jit(solution)/shard_map/all_to_all | solution.py:383
  64.4 1.5 %fold.3 = f32[2,32,128]{2,1,0:T(8,128)} custom-call(f32[4,2,32,128]{3,2,1,0:T(8,128)} %all_to_all.10.pieces_ref), custom_call_target="tpu_custom_call" | custom-call | tf_op jit(solution)/shard_map/fold/pallas_call | solution.py:295
  66.0 0.9 %reshape.38 = f32[2,2,16,8,16]{4,3,2,1,0:T(8,128)S(1)} reshape(f32[2,32,128]{2,1,0:T(8,128)} %fold.3) | data formatting | bytes 65536 | tf_op jit(solution)/shard_map/reshape | solution.py:376
  66.8 0.2 copy.7
  67.0 0.8 %reshape.39 = f32[2,8,16,32]{3,2,1,0:T(8,128)} reshape(f32[2,8,16,2,16]{4,3,2,1,0:T(2,128)S(1)} %copy.7) | data formatting | bytes 65536 | tf_op jit(solution)/shard_map/reshape | solution.py:377
  67.9 10.7 %all-to-all-done.pieces_ref = f32[8,2,8,8,128]{4,3,2,1,0:T(8,128)S(1)} async-done(((f32[8,2,8,8,128]{4,3,2,1,0:T(8,128)}), f32[8,2,8,8,128]{4,3,2,1,0:T(8,128)S(1)}, u32[]{:S(2)}, u32[]{:S(2)}) %all-to-all-start) | async-done | bytes 524320 | tf_op jit(solution)/shard_map/all_to_all | solution.py:383
  78.6 0.0 copy-start.2
  78.6 0.8 copy-done.2
  79.4 1.7 %fold.2 = f32[2,8,8,128]{3,2,1,0:T(8,128)} custom-call(f32[8,2,8,8,128]{4,3,2,1,0:T(8,128)} %copy-done.2), custom_call_target="tpu_custom_call" | custom-call | tf_op jit(solution)/shard_map/fold/pallas_call | solution.py:295
  (3 shorter events, 0.0 us)
Async XLA Ops:
  0.6 1.2 %copy-start = (f32[64,32,128]{2,1,0:T(8,128)S(1)}, f32[64,32,128]{2,1,0:T(8,128)}, u32[]{:S(2)}) copy-start(f32[64,32,128]{2,1,0:T(8,128)} %field_ref.3) | copy-start | bytes 3145732
  1.9 8.3 %copy-start.3 = (bf16[16,8]{0,1:T(8,128)(2,1)S(1)}, bf16[16,8]{0,1:T(8,128)(2,1)}, u32[]{:S(2)}) copy-start(bf16[16,8]{0,1:T(8,128)(2,1)} %param.4) | copy-start | bytes 772
  1.9 11.7 %copy-start.1 = (f32[64,32,128]{2,1,0:T(8,128)S(1)}, f32[64,32,128]{2,1,0:T(8,128)}, u32[]{:S(2)}) copy-start(f32[64,32,128]{2,1,0:T(8,128)} %field_ref.3) | copy-start | bytes 3145732
  2.0 8.2 %collective-permute-start = (f32[3,64,128]{2,1,0:T(8,128)S(1)}, f32[3,64,128]{2,1,0:T(8,128)S(1)}, u32[]{:S(2)}, u32[]{:S(2)}) collective-permute-start(f32[3,64,128]{2,1,0:T(8,128)S(1)} %get-tuple-element.9), channel_id=1, source_target_pairs={{0,4},{4,8},{8,12},{12,16},{16,20},{20,24},{24,28},{1,5},{5,9},{9,... | collective-permute-start | bytes 294920 | tf_op jit(solution)/shard_map/ppermute | solution.py:308
  7.0 6.5 %collective-permute-start.1 = (f32[3,64,128]{2,1,0:T(8,128)S(1)}, f32[3,64,128]{2,1,0:T(8,128)S(1)}, u32[]{:S(2)}, u32[]{:S(2)}) collective-permute-start(f32[3,64,128]{2,1,0:T(8,128)S(1)} %get-tuple-element.10), channel_id=1, source_target_pairs={{4,0},{8,4},{12,8},{16,12},{20,16},{24,20},{28,24},{5,1},{9,5},{13... | collective-permute-start | bytes 294920 | tf_op jit(solution)/shard_map/ppermute | solution.py:308
  14.3 5.3 %collective-permute-start.2 = (f32[3,22,128]{2,1,0:T(8,128)S(1)}, f32[3,22,128]{2,1,0:T(8,128)S(1)}, u32[]{:S(2)}, u32[]{:S(2)}) collective-permute-start(f32[3,22,128]{2,1,0:T(8,128)S(1)} %get-tuple-element.12), channel_id=1, source_target_pairs={{0,1},{1,2},{2,3},{4,5},{5,6},{6,7},{8,9},{9,10},{10,11},{12,13},{... | collective-permute-start | bytes 101384 | tf_op jit(solution)/shard_map/ppermute | solution.py:308
  15.6 4.9 %collective-permute-start.3 = (f32[3,22,128]{2,1,0:T(8,128)S(1)}, f32[3,22,128]{2,1,0:T(8,128)S(1)}, u32[]{:S(2)}, u32[]{:S(2)}) collective-permute-start(f32[3,22,128]{2,1,0:T(8,128)S(1)} %get-tuple-element.13), channel_id=1, source_target_pairs={{1,0},{2,1},{3,2},{5,4},{6,5},{7,6},{9,8},{10,9},{11,10},{13,12},{... | collective-permute-start | bytes 101384 | tf_op jit(solution)/shard_map/ppermute | solution.py:308
  58.7 19.9 %all-to-all-start = ((f32[8,2,8,8,128]{4,3,2,1,0:T(8,128)}), f32[8,2,8,8,128]{4,3,2,1,0:T(8,128)S(1)}, u32[]{:S(2)}, u32[]{:S(2)}) async-start(f32[8,2,8,8,128]{4,3,2,1,0:T(8,128)} %get-tuple-element.14), calls=%async_computation | async-start | bytes 1048576 | tf_op jit(solution)/shard_map/all_to_all | solution.py:383
  78.6 0.8 copy-start.2

commit v2 on v0

v2 whole, which is shorter than its diff:
```python
import functools

import jax
import jax.numpy as jnp
from jax import lax
from jax.experimental import pallas as pl
from jax.experimental.pallas import tpu as pltpu
from jax.sharding import PartitionSpec as P

F32 = jnp.float32
BF16 = jnp.bfloat16
LOG2E = 1.4426950408889634
SUB = 8
LANES = 128
CHUNKS = 16
REACH = 3
VMEM = pl.BlockSpec(memory_space=pltpu.VMEM)
PARAMS = pltpu.CompilerParams(vmem_limit_bytes=48 * 1024 * 1024)


def call(kernel, name, outs, count, scratch=()):
    return pl.pallas_call(
        kernel,
        out_shape=outs,
        in_specs=[VMEM] * count,
        out_specs=jax.tree.map(lambda _: VMEM, outs),
        scratch_shapes=scratch,
        compiler_params=PARAMS,
        name=name,
    )


def rows_of(width):
    return -(-(width + 2 * REACH) // 16) * 16


def iota(shape, dim):
    return lax.broadcasted_iota(jnp.int32, shape, dim)


def one_hot(mask):
    return jnp.where(mask, 1.0, 0.0).astype(BF16)


def spread(weights, left, right, mask):
    inner = lax.dot_general(
        left, weights, (((1,), (1,)), ((), ())), preferred_element_type=F32
    ).astype(BF16)
    return jnp.where(mask, jnp.dot(inner, right, preferred_element_type=F32), 0.0)


def turn_kernel(field_ref, in_ref, out_ref, turned_ref, first_ref, last_ref, win_ref, wout_ref):
    layers, length, width = field_ref.shape
    half = length // 2
    for k in range(half):
        turned = jnp.concatenate([field_ref[:, k, :], field_ref[:, k + half, :]], axis=0).T
        turned_ref[k, REACH : REACH + width] = turned
        for j in range(REACH):
            first_ref[j, k : k + 1] = turned[j : j + 1]
            last_ref[j, k : k + 1] = turned[width - REACH + j : width - REACH + j + 1]
    units, feats = in_ref.shape
    channels = out_ref.shape[0]
    bands = channels // 2
    rows, cols = feats * CHUNKS, units * CHUNKS
    left = one_hot(iota((rows, feats), 0) // CHUNKS == iota((rows, feats), 1))
    right = one_hot(iota((units, cols), 1) // CHUNKS == iota((units, cols), 0))
    mask = iota((rows, cols), 0) % CHUNKS == iota((rows, cols), 1) % CHUNKS
    win_ref[...] = (0.5 * spread(in_ref[...], left, right, mask)).astype(BF16)
    rows, cols = cols, channels * CHUNKS
    left = one_hot(iota((rows, units), 0) // CHUNKS == iota((rows, units), 1))
    at = iota((channels, cols), 1)
    right = one_hot((at // LANES) * bands + at % bands == iota((channels, cols), 0))
    mask = iota((rows, cols), 0) % CHUNKS == (iota((rows, cols), 1) % LANES) // bands
    wout_ref[...] = spread(out_ref[...], left, right, mask).astype(BF16)


def sides_kernel(rows_in, turned_ref, before_ref, after_ref, wide_ref, first_ref, last_ref):
    half, rows, _ = turned_ref.shape
    width = rows_in
    layers = LANES // 2
    part = rows // 2
    front = iota((part, LANES), 1) < layers
    for k in range(half):
        wide_ref[k, REACH : REACH + width] = turned_ref[k, REACH : REACH + width]
        for j in range(REACH):
            wide_ref[k, j : j + 1] = before_ref[j, k : k + 1]
            wide_ref[k, REACH + width + j : REACH + width + j + 1] = after_ref[j, k : k + 1]
        wide_ref[k, 2 * REACH + width :] = jnp.zeros((rows - 2 * REACH - width, LANES), F32)
    for j in range(REACH):
        top, low = wide_ref[j, :part], wide_ref[j, part:]
        first_ref[j] = jnp.where(front, top, pltpu.roll(low, layers, axis=1))
        k = half - REACH + j
        top, low = wide_ref[k, :part], wide_ref[k, part:]
        last_ref[j] = jnp.where(front, pltpu.roll(top, layers, axis=1), low)


def march_kernel(
    spans,
    block_y,
    counts,
    steps,
    *refs,
):
    (wide_ref, before_ref, after_ref, win_ref, wout_ref, image_x_ref, ty_ref, cy_ref) = refs[:8]
    (raw_ref, once_ref, twice_ref, ridge_ref, tx_ref, cx_ref) = refs[8:]
    half, rows, _ = wide_ref.shape
    run = tx_ref.shape[0]
    layers = LANES // 2
    shape = (CHUNKS, LANES)
    lane, chunk = iota(shape, 1), iota(shape, 0)
    z = lane % layers
    near = (z > 0).astype(F32)
    far = (z < layers - 1).astype(F32)
    at_x, at_y = lax.axis_index("bx"), lax.axis_index("by")
    count_x, count_y = counts
    mask_x_low = jnp.where((lane < layers) & (at_x == 0), 0.0, 1.0)
    mask_x_high = jnp.where((lane >= layers) & (at_x == count_x - 1), 0.0, 1.0)
    mask_y_low = jnp.where((chunk == 0) & (at_y == 0), 0.0, 1.0)
    mask_y_high = jnp.where((chunk == CHUNKS - 1) & (at_y == count_y - 1), 0.0, 1.0)

    def roll(value, shift):
        return pltpu.roll(value, shift % LANES, axis=1)

    def z_sum(value):
        return roll(value, 1) * near + roll(value, -1) * far

    part = rows // 2
    front = iota((part, LANES), 1) < layers
    for j in range(REACH):
        halo, own = before_ref[j], wide_ref[half - REACH + j]
        raw_ref[j, :part] = jnp.where(front, halo, roll(own[:part], layers))
        raw_ref[j, part:] = jnp.where(front, roll(halo, layers), roll(own[part:], layers))
        halo, own = after_ref[j], wide_ref[j]
        k = half + REACH + j
        raw_ref[k, :part] = jnp.where(front, roll(own[:part], layers), roll(halo, layers))
        raw_ref[k, part:] = jnp.where(front, roll(own[part:], layers), halo)

    def copy_in(k, _):
        raw_ref[k + REACH] = wide_ref[k]
        return 0

    lax.fori_loop(0, half, copy_in, 0)

    def raw(k, y):
        return raw_ref[k, pl.ds(y + REACH, CHUNKS, stride=run), :]

    def masked(value, y):
        if y < 0:
            value = value * mask_y_low
        if y >= run:
            value = value * mask_y_high
        return value

    def smooth(centre, others):
        total = z_sum(centre)
        for other in others:
            total = total + other
        return 0.4 * centre + 0.1 * total

    def smooth_once(k, _):
        column = [raw(k + 1, y) for y in range(-3, run + 3)]
        for i in range(1, len(column) - 1):
            y = i - 3
            value = smooth(column[i], [column[i - 1], column[i + 1], raw(k, y), raw(k + 2, y)])
            once_ref[k, y + 2] = masked(value, y)
        return 0

    lax.fori_loop(0, half + 4, smooth_once, 0)
    for y in range(run + 4):
        for k in (0, 1):
            once_ref[k, y] = once_ref[k, y] * mask_x_low
            once_ref[half + 2 + k, y] = once_ref[half + 2 + k, y] * mask_x_high

    def smooth_twice(k, _):
        edge = jnp.where(k == 0, mask_x_low, 1.0) * jnp.where(k == half + 1, mask_x_high, 1.0)
        column = [once_ref[k + 1, y] for y in range(run + 4)]
        for i in range(1, len(column) - 1):
            y = i - 2
            value = smooth(
                column[i], [column[i - 1], column[i + 1], once_ref[k, i], once_ref[k + 2, i]]
            )
            value = masked(value * edge, y)
            twice_ref[k, y + 1] = value
            ridge_ref[k, y + 1] = 2.0 * value + z_sum(value)
        return 0

    lax.fori_loop(0, half + 2, smooth_twice, 0)

    ones = jnp.ones(shape, BF16)

    def features(k, y):
        p = lambda a, b: twice_ref[k + 1 + a, y + 1 + b]
        r = lambda a, b: ridge_ref[k + 1 + a, y + 1 + b]
        centre = p(0, 0)
        main, cross = p(1, 1) - p(-1, -1), p(1, -1) - p(-1, 1)
        third = 1.0 / 3.0
        gx = (main + cross + (r(1, 0) - r(-1, 0))) * third
        gy = (main - cross + (r(0, 1) - r(0, -1))) * third
        around = 2.0 * centre + ((p(1, 0) + p(-1, 0)) + (p(0, 1) + p(0, -1)))
        gz = (roll(around, -1) * far - roll(around, 1) * near) * third
        m = jnp.sqrt(1.0 + gx * gx + gy * gy + gz * gz)
        parts = [centre, gx, gy, gz, m, centre * m, centre * centre]
        packed = [part.astype(BF16) for part in parts] + [ones]
        return jnp.concatenate(packed, axis=0).T

    def network(tiles):
        half_v = jnp.dot(tiles, win_ref[...], preferred_element_type=F32)
        hidden = (half_v + half_v * jnp.tanh(half_v)).astype(BF16)
        v = jnp.dot(hidden, wout_ref[...], preferred_element_type=F32)
        soft = jnp.maximum(v, jnp.log(1.0 + jnp.exp2(jnp.minimum(v * LOG2E, 126.0))))
        return soft[:, :LANES], jnp.exp2(soft[:, LANES:] * (-LOG2E * steps[1]))

    ratio = steps[0] / steps[1]

    def clear_of_x(q):
        if ratio == 1.0:
            return q
        if ratio == 2.0:
            return q * q
        return jnp.exp2(jnp.log(q) * (LOG2E * ratio))

    groups = LANES // SUB

    def reset(k, _):
        ty_ref[k] = jnp.ones((LANES, LANES), F32)
        cy_ref[k] = jnp.zeros((LANES, LANES), F32)
        return 0

    lax.fori_loop(0, half, reset, 0)
    for k in range(run):
        tx_ref[k] = jnp.ones((LANES, LANES), F32)
        cx_ref[k] = jnp.zeros((LANES, LANES), F32)

    def block(x0, y0, many_x, many_y):
        tiles = [features(x0 + i, y0 + j) for j in range(many_y) for i in range(many_x)]
        emission, clear = network(jnp.concatenate(tiles, axis=0))
        for g in range(groups):
            at = pl.ds(g * SUB, SUB)
            ty = [ty_ref[x0 + i, at] for i in range(many_x)]
            cy = [cy_ref[x0 + i, at] for i in range(many_x)]
            for j in range(many_y):
                tx, cx = tx_ref[y0 + j, at], cx_ref[y0 + j, at]
                for i in range(many_x):
                    start = (j * many_x + i) * LANES + g * SUB
                    e, q = emission[start : start + SUB], clear[start : start + SUB]
                    later = ty[i] * q
                    cy[i] = cy[i] + (ty[i] - later) * e
                    ty[i] = later
                    later = tx * clear_of_x(q)
                    cx = cx + (tx - later) * e
                    tx = later
                tx_ref[y0 + j, at], cx_ref[y0 + j, at] = tx, cx
            for i in range(many_x):
                ty_ref[x0 + i, at], cy_ref[x0 + i, at] = ty[i], cy[i]

    for first, last, many_x in spans:

        def over_blocks(step, _, first=first, many_x=many_x):
            x0 = first + (step // (run // block_y)) * many_x
            y0 = (step % (run // block_y)) * block_y
            block(x0, y0, many_x, block_y)
            return 0

        lax.fori_loop(0, (last - first) // many_x * (run // block_y), over_blocks, 0)

    for y in range(run):
        q = tx_ref[y, :layers]
        colour = cx_ref[y, :layers] + q * cx_ref[y, layers:]
        q = q * tx_ref[y, layers:]
        for d in range(layers // SUB):
            image_x_ref[d, 0, y] = colour[d * SUB : (d + 1) * SUB]
            image_x_ref[d, 1, y] = q[d * SUB : (d + 1) * SUB]


def columns_kernel(share, peers, ty_ref, cy_ref, *refs):
    outs, (rows_ref, turned_ref) = refs[:peers], refs[peers:]
    half = ty_ref.shape[0]
    layers = LANES // 2
    for k in range(half):
        colours, clears = cy_ref[k].T, ty_ref[k].T
        colour, clear = colours[:SUB], clears[:SUB]
        for c in range(1, CHUNKS):
            at = slice(c * SUB, (c + 1) * SUB)
            colour = colour + clear * colours[at]
            clear = clear * clears[at]
        rows_ref[0, k * SUB : (k + 1) * SUB] = colour
        rows_ref[1, k * SUB : (k + 1) * SUB] = clear
    me = lax.axis_index("by")
    for kind in range(2):
        turned_ref[kind] = rows_ref[kind].T
        for s in range(peers):
            start = pl.multiple_of(lax.rem(me + s, peers) * share, share)
            for part in range(2):
                outs[s][kind, part] = turned_ref[kind, pl.ds(part * layers + start, share)]


def fold_y_kernel(*refs):
    pieces, out_ref = refs[:-1], refs[-1]
    peers = len(pieces)
    me = lax.axis_index("by")

    def piece(source):
        shift = lax.rem(me - source + peers, peers)
        value = pieces[0][...]
        for s in range(1, peers):
            value = jnp.where(shift == s, pieces[s][...], value)
        return value

    value = piece(0)
    colour, clear = value[0], value[1]
    for source in range(1, peers):
        value = piece(source)
        colour = colour + clear * value[0]
        clear = clear * value[1]
    out_ref[0] = colour
    out_ref[1] = clear


def fold_x_kernel(pieces_ref, out_ref):
    peers, _, run, share, _ = pieces_ref.shape
    lane = iota((share, LANES), 1)
    kinds = [[], []]
    for y in range(run):
        colour, clear = pieces_ref[0, 0, y], pieces_ref[0, 1, y]
        for k in range(1, peers):
            colour = colour + clear * pieces_ref[k, 0, y]
            clear = clear * pieces_ref[k, 1, y]
        kinds[0].append(colour)
        kinds[1].append(clear)
    for kind, values in enumerate(kinds):
        for s in (1, 2, 4):
            for i in range(run):
                if not i & s:
                    a, b = values[i], values[i | s]
                    odd = (lane & s) != 0
                    values[i] = jnp.where(odd, pltpu.roll(b, s, axis=1), a)
                    values[i | s] = jnp.where(odd, b, pltpu.roll(a, LANES - s, axis=1))
        for band, value in enumerate(values):
            out_ref[kind, band] = value


def exchange(last, first, axis):
    peers = lax.axis_size(axis)
    up = [(i, i + 1) for i in range(peers - 1)]
    down = [(j, i) for i, j in up]
    return lax.ppermute(last, axis, up), lax.ppermute(first, axis, down)


def body(scalar_field, transfer_in, transfer_out):
    layers, local_x, local_y = scalar_field.shape
    units, feats = transfer_in.shape
    channels = transfer_out.shape[0]
    bands = channels // 2
    count_x, count_y = lax.axis_size("bx"), lax.axis_size("by")
    steps = (2.0 / (local_x * count_x), 2.0 / (local_y * count_y))
    half, run, rows = local_x // 2, local_y // CHUNKS, rows_of(local_y)
    sds = lambda *shape: jax.ShapeDtypeStruct(shape, F32)
    weights = [
        jax.ShapeDtypeStruct((feats * CHUNKS, units * CHUNKS), BF16),
        jax.ShapeDtypeStruct((units * CHUNKS, channels * CHUNKS), BF16),
    ]

    edge = sds(REACH, half, LANES)
    turned, first, last, win, wout = call(
        turn_kernel, "turn", [sds(half, rows, LANES), edge, edge] + weights, 3
    )(scalar_field, transfer_in, transfer_out)
    before, after = exchange(last, first, "by")
    edge = sds(REACH, rows // 2, LANES)
    wide, first, last = call(functools.partial(sides_kernel, local_y), "sides", [sds(half, rows, LANES), edge, edge], 3)(
        turned, before, after
    )
    before, after = exchange(last, first, "bx")
    state = sds(half, LANES, LANES)
    scratch = [
        pltpu.VMEM((half + 2 * REACH, rows, LANES), F32),
        pltpu.VMEM((half + 4, run + 4, CHUNKS, LANES), F32),
        pltpu.VMEM((half + 2, run + 2, CHUNKS, LANES), F32),
        pltpu.VMEM((half + 2, run + 2, CHUNKS, LANES), F32),
        pltpu.VMEM((run, LANES, LANES), F32),
        pltpu.VMEM((run, LANES, LANES), F32),
    ]
    image_x, clear_y, colour_y = call(
        functools.partial(march_kernel, ((0, half, 4),), 2, (count_x, count_y), steps),
        "march",
        [sds(layers // SUB, 2, run, SUB, LANES), state, state],
        5,
        scratch,
    )(wide, before, after, win, wout)

    share_x = layers // count_x
    if share_x != SUB:
        image_x = jnp.transpose(image_x, (1, 2, 0, 3, 4)).reshape(2, run, count_x, share_x, LANES)
        image_x = jnp.transpose(image_x, (2, 0, 1, 3, 4))
    pieces = lax.all_to_all(image_x, "bx", split_axis=0, concat_axis=0, tiled=True)
    view_x = call(fold_x_kernel, "fold_x", sds(2, bands, share_x, local_y), 1)(pieces)

    share = layers // count_y
    piece = sds(2, 2, share, LANES)
    scratch = [pltpu.VMEM((2, LANES, LANES), F32), pltpu.VMEM((2, LANES, LANES), F32)]
    pieces = call(
        functools.partial(columns_kernel, share, count_y), "columns", [piece] * count_y, 2, scratch
    )(clear_y, colour_y)
    pieces = list(pieces)
    for s in range(1, count_y):
        pairs = [(i, (i + s) % count_y) for i in range(count_y)]
        pieces[s] = lax.ppermute(pieces[s], "by", pairs)
    view_y = call(fold_y_kernel, "fold_y", piece, count_y)(*pieces)
    view_y = view_y.reshape(2, 2, share, half, bands)
    view_y = jnp.transpose(view_y, (0, 4, 2, 1, 3)).reshape(2, bands, share, local_x)
    return (view_x, view_y)


def solution(mesh):
    return jax.shard_map(
        body,
        mesh=mesh,
        in_specs=(P(None, "bx", "by"), P(), P()),
        out_specs=(P(None, None, "bx", "by"), P(None, None, "by", "bx")),
        check_vma=False,
    )
```

time: 347 us -> 67.1 us (0.19)
  local copies, waits for them, and re-layouts: 132 us -> 3.6 us
  other arithmetic: 96.4 us -> 0 us
  matrix products: 37.8 us -> 0 us
  Pallas kernels: 0 us -> 24.7 us
  starting transfers between devices: 42.2 us -> 18.1 us
  waiting for transfers between devices: 31.6 us -> 19.7 us
  loops' own time: 3.83 us -> 0 us
    while x96 -> x0, local copies, waits for them, and re-layouts: 65 us -> none
    dot_general x12 -> x0, matrix products: 37.8 us -> none  [the longest x4 15 us: transfer(): jnp.einsum('ch,hzxy->czxy', transfer_out, hidden, preferred_element_type=...]
    slice x27 -> x0, local copies, waits for them, and re-layouts: 28.7 us -> none  [the longest x4 14.3 us: advance(): clear_y = jnp.exp(-running_y[..., -1])]
    pallas_call x0 -> x6, Pallas kernels: none -> 24.7 us  [the longest x1 22.3 us: body(): call(functools.partial(march_kernel, ((0, half, 4),), 2, (count_x, count_...]
    reduce_sum x4 -> x0, other arithmetic: 23 us -> none  [advance(): jnp.sum(jnp.exp(-(running_y - thickness_y)) * -jnp.expm1(-thickness_y) *...]
    another operation x41 -> x0, local copies, waits for them, and re-layouts: 21.1 us -> none  [the longest x32 18.7 us: transfer(): jnp.stack([centre, scaled_x, scaled_y, scaled_z, magnitude, centre * magn...]
    sub x12 -> x0, other arithmetic: 20.5 us -> none  [the longest x4 10.9 us: gradients(): diff_z = padded[2:] - padded[:-2]]
    ppermute x12 -> x7, starting transfers between devices: 32.3 us -> 12.3 us  [the longest x4 8.34 us: exchange(): return (lax.ppermute(last, axis, up), lax.ppermute(first, axis, down))]
  transfers between devices with their start and end apart: 14 -> 8, of which waited for: 11 -> 6; matrix products, arithmetic and copies ran while one was open for 1% -> 1% of each run, Pallas kernels for 0% -> 1%
where the time goes in v2:
time: 67.1 us; the launch traced here: 66.7 us
  Pallas kernels  24.7 us (37%)
  waiting for transfers between devices  19.7 us (29%)
  starting transfers between devices  18.1 us (27%)
  local copies, waits for them, and re-layouts  3.6 us (5%)
  between operations  0.7 us (1%)
    pallas_call x1, Pallas kernels, body(): call(functools.partial(march_kernel, ((0, half, 4),), 2, (count_x, count_...  22.3 us
    ppermute x4, waiting for transfers between devices, exchange(): return (lax.ppermute(last, axis, up), lax.ppermute(first, axis, down))  9.26 us
    all_to_all x1, waiting for transfers between devices, body(): lax.all_to_all(image_x, 'bx', split_axis=0, concat_axis=0, tiled=True)  8.81 us
    ppermute x4, starting transfers between devices, exchange(): return (lax.ppermute(last, axis, up), lax.ppermute(first, axis, down))  8.34 us
    all_to_all x1, starting transfers between devices, body(): lax.all_to_all(image_x, 'bx', split_axis=0, concat_axis=0, tiled=True)  5.75 us
    ppermute x3, starting transfers between devices, body(): pieces[s] = lax.ppermute(pieces[s], 'by', pairs)  3.97 us
    unnamed x6, local copies, waits for them, and re-layouts  3.48 us
    ppermute x3, waiting for transfers between devices, body(): pieces[s] = lax.ppermute(pieces[s], 'by', pairs)  1.6 us
  transfers between devices with their start and end apart: 8, of which 6 were waited for; matrix products, arithmetic and copies ran while one was open for 1% of the time, Pallas kernels for 1%

profile of v2, /device:TPU:0, one launch (start us, length us, event | category | flops | bytes accessed | tf_op | source)
XLA Modules:
  0.0 66.7 jit_solution(10386137889124704249)
XLA Ops:
  0.6 0.8 %copy.7.in_ref = bf16[16,8]{1,0:T(8,128)(2,1)S(1)} copy(bf16[16,8]{0,1:T(8,128)(2,1)} %param.4) | data formatting | bytes 512 | tf_op args[1]
  1.4 0.0 copy-start
  1.4 1.2 %copy-done = f32[64,32,128]{2,1,0:T(8,128)S(1)} copy-done((f32[64,32,128]{2,1,0:T(8,128)S(1)}, f32[64,32,128]{2,1,0:T(8,128)}, u32[]{:S(2)}) %copy-start) | copy-done | bytes 1048600
  2.6 0.0 copy-start.1
  2.6 0.7 %copy-done.1 = bf16[16,16]{1,0:T(8,128)(2,1)S(1)} copy-done((bf16[16,16]{1,0:T(8,128)(2,1)S(1)}, bf16[16,16]{1,0:T(8,128)(2,1)}, u32[]{:S(2)}) %copy-start.1) | copy-done | bytes 536
  3.3 0.7 %turn.1 = (f32[16,144,128]{2,1,0:T(8,128)S(1)}, f32[3,16,128]{2,1,0:T(8,128)S(1)}, f32[3,16,128]{2,1,0:T(8,128)S(1)}, bf16[128,256]{1,0:T(8,128)(2,1)S(1)}, bf16[256,256]{1,0:T(8,128)(2,1)S(1)}) custom-call(f32[64,32,128]{2,1,0:T(8,128)S(1)} %copy-done, bf16[16,8]{1,0:T(8,128)(2,1)S(1)} %copy.7.in_ref, bf16[16,16]{1,0:T(8,128)(2,1)S(1)} %copy-done.1), custom_call_target="tpu_custom_call" | custom-call | tf_op jit(solution)/shard_map/turn/pallas_call | solution.py:364
  4.0 2.4 %collective-permute-start = (f32[3,16,128]{2,1,0:T(8,128)S(1)}, f32[3,16,128]{2,1,0:T(8,128)S(1)}, u32[]{:S(2)}, u32[]{:S(2)}) collective-permute-start(f32[3,16,128]{2,1,0:T(8,128)S(1)} %get-tuple-element.18), channel_id=1, source_target_pairs={{0,1},{1,2},{2,3},{4,5},{5,6},{6,7},{8,9},{9,10},{10,11},{12,13},{... | collective-permute-start | bytes 73736 | tf_op jit(solution)/shard_map/ppermute | solution.py:346
  6.4 1.3 %collective-permute-start.1 = (f32[3,16,128]{2,1,0:T(8,128)S(1)}, f32[3,16,128]{2,1,0:T(8,128)S(1)}, u32[]{:S(2)}, u32[]{:S(2)}) collective-permute-start(f32[3,16,128]{2,1,0:T(8,128)S(1)} %get-tuple-element.19), channel_id=1, source_target_pairs={{1,0},{2,1},{3,2},{5,4},{6,5},{7,6},{9,8},{10,9},{11,10},{13,12},{... | collective-permute-start | bytes 73736 | tf_op jit(solution)/shard_map/ppermute | solution.py:346
  7.7 0.0 collective-permute-done.before_ref
  7.7 3.9 %collective-permute-done.1.after_ref = f32[3,16,128]{2,1,0:T(8,128)S(1)} collective-permute-done((f32[3,16,128]{2,1,0:T(8,128)S(1)}, f32[3,16,128]{2,1,0:T(8,128)S(1)}, u32[]{:S(2)}, u32[]{:S(2)}) %collective-permute-start.1) | collective-permute-done | bytes 24608 | tf_op jit(solution)/shard_map/ppermute | solution.py:346
  11.6 0.2 sides.1
  11.7 3.4 %collective-permute-start.2 = (f32[3,72,128]{2,1,0:T(8,128)S(1)}, f32[3,72,128]{2,1,0:T(8,128)S(1)}, u32[]{:S(2)}, u32[]{:S(2)}) collective-permute-start(f32[3,72,128]{2,1,0:T(8,128)S(1)} %get-tuple-element.21), channel_id=1, source_target_pairs={{0,4},{4,8},{8,12},{12,16},{16,20},{20,24},{24,28},{1,5},{5,9},{9,... | collective-permute-start | bytes 331784 | tf_op jit(solution)/shard_map/ppermute | solution.py:346
  15.2 1.3 %collective-permute-start.3 = (f32[3,72,128]{2,1,0:T(8,128)S(1)}, f32[3,72,128]{2,1,0:T(8,128)S(1)}, u32[]{:S(2)}, u32[]{:S(2)}) collective-permute-start(f32[3,72,128]{2,1,0:T(8,128)S(1)} %get-tuple-element.22), channel_id=1, source_target_pairs={{4,0},{8,4},{12,8},{16,12},{20,16},{24,20},{28,24},{5,1},{9,5},{13... | collective-permute-start | bytes 331784 | tf_op jit(solution)/shard_map/ppermute | solution.py:346
  16.4 1.0 %collective-permute-done.2.refs_1_ = f32[3,72,128]{2,1,0:T(8,128)S(1)} collective-permute-done((f32[3,72,128]{2,1,0:T(8,128)S(1)}, f32[3,72,128]{2,1,0:T(8,128)S(1)}, u32[]{:S(2)}, u32[]{:S(2)}) %collective-permute-start.2) | collective-permute-done | bytes 110624 | tf_op jit(solution)/shard_map/ppermute | solution.py:346
  17.5 4.3 %collective-permute-done.3.refs_2_ = f32[3,72,128]{2,1,0:T(8,128)S(1)} collective-permute-done((f32[3,72,128]{2,1,0:T(8,128)S(1)}, f32[3,72,128]{2,1,0:T(8,128)S(1)}, u32[]{:S(2)}, u32[]{:S(2)}) %collective-permute-start.3) | collective-permute-done | bytes 110624 | tf_op jit(solution)/shard_map/ppermute | solution.py:346
  21.8 22.3 %march.1 = (f32[8,2,8,8,128]{4,3,2,1,0:T(8,128)}, f32[16,128,128]{2,1,0:T(8,128)S(1)}, f32[16,128,128]{2,1,0:T(8,128)S(1)}) custom-call(f32[16,144,128]{2,1,0:T(8,128)S(1)} %get-tuple-element.20.refs_0_, f32[3,72,128]{2,1,0:T(8,128)S(1)} %collective-permute-done.2.refs_1_, f32[3,72,128]{2,1,0:T(8,128)S(1)} %collective-permute-done.3.refs_2_, ...), custom_call_target="tpu_custom_call" | custom-call | tf_op jit(solution)/shard_map/march/pallas_call | solution.py:382
  44.1 5.7 %all-to-all-start = ((f32[8,2,8,8,128]{4,3,2,1,0:T(8,128)}), f32[8,2,8,8,128]{4,3,2,1,0:T(8,128)S(1)}, u32[]{:S(2)}, u32[]{:S(2)}) async-start(f32[8,2,8,8,128]{4,3,2,1,0:T(8,128)} %get-tuple-element.25), calls=%async_computation | async-start | bytes 1048576 | tf_op jit(solution)/shard_map/all_to_all | solution.py:394
  49.8 0.7 %columns.1 = (f32[2,2,16,128]{3,2,1,0:T(8,128)S(1)}, f32[2,2,16,128]{3,2,1,0:T(8,128)S(1)}, f32[2,2,16,128]{3,2,1,0:T(8,128)S(1)}, f32[2,2,16,128]{3,2,1,0:T(8,128)S(1)}) custom-call(f32[16,128,128]{2,1,0:T(8,128)S(1)} %get-tuple-element.26.ty_ref, f32[16,128,128]{2,1,0:T(8,128)S(1)} %get-tuple-element.27.cy_ref), custom_call_target="tpu_custom_call" | custom-call | tf_op jit(solution)/shard_map/columns/pallas_call | solution.py:400
  50.5 0.9 %collective-permute-start.4 = (f32[2,2,16,128]{3,2,1,0:T(8,128)S(1)}, f32[2,2,16,128]{3,2,1,0:T(8,128)S(1)}, u32[]{:S(2)}, u32[]{:S(2)}) collective-permute-start(f32[2,2,16,128]{3,2,1,0:T(8,128)S(1)} %get-tuple-element.29), channel_id=1, source_target_pairs={{0,1},{1,2},{2,3},{3,0},{4,5},{5,6},{6,7},{7,4},{8,9},{9,10},{10,1... | collective-permute-start | bytes 98312 | tf_op jit(solution)/shard_map/ppermute | solution.py:406
  51.4 1.7 %collective-permute-start.5 = (f32[2,2,16,128]{3,2,1,0:T(8,128)S(1)}, f32[2,2,16,128]{3,2,1,0:T(8,128)S(1)}, u32[]{:S(2)}, u32[]{:S(2)}) collective-permute-start(f32[2,2,16,128]{3,2,1,0:T(8,128)S(1)} %get-tuple-element.30), channel_id=1, source_target_pairs={{0,2},{1,3},{2,0},{3,1},{4,6},{5,7},{6,4},{7,5},{8,10},{9,11},{10,... | collective-permute-start | bytes 98312 | tf_op jit(solution)/shard_map/ppermute | solution.py:406
  53.1 1.4 %collective-permute-start.6 = (f32[2,2,16,128]{3,2,1,0:T(8,128)S(1)}, f32[2,2,16,128]{3,2,1,0:T(8,128)S(1)}, u32[]{:S(2)}, u32[]{:S(2)}) collective-permute-start(f32[2,2,16,128]{3,2,1,0:T(8,128)S(1)} %get-tuple-element.31), channel_id=1, source_target_pairs={{0,3},{1,0},{2,1},{3,2},{4,7},{5,4},{6,5},{7,6},{8,11},{9,8},{10,9... | collective-permute-start | bytes 98312 | tf_op jit(solution)/shard_map/ppermute | solution.py:406
  54.5 0.0 collective-permute-done.4.refs_1_
  54.5 0.8 %collective-permute-done.5.refs_2_ = f32[2,2,16,128]{3,2,1,0:T(8,128)S(1)} collective-permute-done((f32[2,2,16,128]{3,2,1,0:T(8,128)S(1)}, f32[2,2,16,128]{3,2,1,0:T(8,128)S(1)}, u32[]{:S(2)}, u32[]{:S(2)}) %collective-permute-start.5) | collective-permute-done | bytes 32800 | tf_op jit(solution)/shard_map/ppermute | solution.py:406
  55.3 0.8 %collective-permute-done.6.refs_3_ = f32[2,2,16,128]{3,2,1,0:T(8,128)S(1)} collective-permute-done((f32[2,2,16,128]{3,2,1,0:T(8,128)S(1)}, f32[2,2,16,128]{3,2,1,0:T(8,128)S(1)}, u32[]{:S(2)}, u32[]{:S(2)}) %collective-permute-start.6) | collective-permute-done | bytes 32800 | tf_op jit(solution)/shard_map/ppermute | solution.py:406
  56.1 0.1 copy.8
  56.2 0.8 %copy.9 = f32[2,8,16,32]{3,2,1,0:T(8,128)} copy(f32[2,8,16,32]{2,1,3,0:T(8,128)S(1)} %bitcast.5) | data formatting | bytes 65536
  57.0 8.8 %all-to-all-done.pieces_ref = f32[8,2,8,8,128]{4,3,2,1,0:T(8,128)S(1)} async-done(((f32[8,2,8,8,128]{4,3,2,1,0:T(8,128)}), f32[8,2,8,8,128]{4,3,2,1,0:T(8,128)S(1)}, u32[]{:S(2)}, u32[]{:S(2)}) %all-to-all-start) | async-done | bytes 524320 | tf_op jit(solution)/shard_map/all_to_all | solution.py:394
  65.8 0.9 %fold_x.1 = f32[2,8,8,128]{3,2,1,0:T(8,128)} custom-call(f32[8,2,8,8,128]{4,3,2,1,0:T(8,128)S(1)} %all-to-all-done.pieces_ref), custom_call_target="tpu_custom_call" | custom-call | tf_op jit(solution)/shard_map/fold_x/pallas_call | solution.py:395
  (1 shorter events, 0.0 us)
Async XLA Ops:
  1.4 1.2 %copy-start = (f32[64,32,128]{2,1,0:T(8,128)S(1)}, f32[64,32,128]{2,1,0:T(8,128)}, u32[]{:S(2)}) copy-start(f32[64,32,128]{2,1,0:T(8,128)} %field_ref.1) | copy-start | bytes 3145732
  2.6 0.7 %copy-start.1 = (bf16[16,16]{1,0:T(8,128)(2,1)S(1)}, bf16[16,16]{1,0:T(8,128)(2,1)}, u32[]{:S(2)}) copy-start(bf16[16,16]{1,0:T(8,128)(2,1)} %out_ref.1) | copy-start | bytes 1540
  4.0 3.7 %collective-permute-start = (f32[3,16,128]{2,1,0:T(8,128)S(1)}, f32[3,16,128]{2,1,0:T(8,128)S(1)}, u32[]{:S(2)}, u32[]{:S(2)}) collective-permute-start(f32[3,16,128]{2,1,0:T(8,128)S(1)} %get-tuple-element.18), channel_id=1, source_target_pairs={{0,1},{1,2},{2,3},{4,5},{5,6},{6,7},{8,9},{9,10},{10,11},{12,13},{... | collective-permute-start | bytes 73736 | tf_op jit(solution)/shard_map/ppermute | solution.py:346
  6.4 5.2 %collective-permute-start.1 = (f32[3,16,128]{2,1,0:T(8,128)S(1)}, f32[3,16,128]{2,1,0:T(8,128)S(1)}, u32[]{:S(2)}, u32[]{:S(2)}) collective-permute-start(f32[3,16,128]{2,1,0:T(8,128)S(1)} %get-tuple-element.19), channel_id=1, source_target_pairs={{1,0},{2,1},{3,2},{5,4},{6,5},{7,6},{9,8},{10,9},{11,10},{13,12},{... | collective-permute-start | bytes 73736 | tf_op jit(solution)/shard_map/ppermute | solution.py:346
  11.7 5.7 %collective-permute-start.2 = (f32[3,72,128]{2,1,0:T(8,128)S(1)}, f32[3,72,128]{2,1,0:T(8,128)S(1)}, u32[]{:S(2)}, u32[]{:S(2)}) collective-permute-start(f32[3,72,128]{2,1,0:T(8,128)S(1)} %get-tuple-element.21), channel_id=1, source_target_pairs={{0,4},{4,8},{8,12},{12,16},{16,20},{20,24},{24,28},{1,5},{5,9},{9,... | collective-permute-start | bytes 331784 | tf_op jit(solution)/shard_map/ppermute | solution.py:346
  15.2 6.6 %collective-permute-start.3 = (f32[3,72,128]{2,1,0:T(8,128)S(1)}, f32[3,72,128]{2,1,0:T(8,128)S(1)}, u32[]{:S(2)}, u32[]{:S(2)}) collective-permute-start(f32[3,72,128]{2,1,0:T(8,128)S(1)} %get-tuple-element.22), channel_id=1, source_target_pairs={{4,0},{8,4},{12,8},{16,12},{20,16},{24,20},{28,24},{5,1},{9,5},{13... | collective-permute-start | bytes 331784 | tf_op jit(solution)/shard_map/ppermute | solution.py:346
  44.1 21.8 %all-to-all-start = ((f32[8,2,8,8,128]{4,3,2,1,0:T(8,128)}), f32[8,2,8,8,128]{4,3,2,1,0:T(8,128)S(1)}, u32[]{:S(2)}, u32[]{:S(2)}) async-start(f32[8,2,8,8,128]{4,3,2,1,0:T(8,128)} %get-tuple-element.25), calls=%async_computation | async-start | bytes 1048576 | tf_op jit(solution)/shard_map/all_to_all | solution.py:394
  50.5 4.0 %collective-permute-start.4 = (f32[2,2,16,128]{3,2,1,0:T(8,128)S(1)}, f32[2,2,16,128]{3,2,1,0:T(8,128)S(1)}, u32[]{:S(2)}, u32[]{:S(2)}) collective-permute-start(f32[2,2,16,128]{3,2,1,0:T(8,128)S(1)} %get-tuple-element.29), channel_id=1, source_target_pairs={{0,1},{1,2},{2,3},{3,0},{4,5},{5,6},{6,7},{7,4},{8,9},{9,10},{10,1... | collective-permute-start | bytes 98312 | tf_op jit(solution)/shard_map/ppermute | solution.py:406
  51.4 3.9 %collective-permute-start.5 = (f32[2,2,16,128]{3,2,1,0:T(8,128)S(1)}, f32[2,2,16,128]{3,2,1,0:T(8,128)S(1)}, u32[]{:S(2)}, u32[]{:S(2)}) collective-permute-start(f32[2,2,16,128]{3,2,1,0:T(8,128)S(1)} %get-tuple-element.30), channel_id=1, source_target_pairs={{0,2},{1,3},{2,0},{3,1},{4,6},{5,7},{6,4},{7,5},{8,10},{9,11},{10,... | collective-permute-start | bytes 98312 | tf_op jit(solution)/shard_map/ppermute | solution.py:406
  53.1 3.0 %collective-permute-start.6 = (f32[2,2,16,128]{3,2,1,0:T(8,128)S(1)}, f32[2,2,16,128]{3,2,1,0:T(8,128)S(1)}, u32[]{:S(2)}, u32[]{:S(2)}) collective-permute-start(f32[2,2,16,128]{3,2,1,0:T(8,128)S(1)} %get-tuple-element.31), channel_id=1, source_target_pairs={{0,3},{1,0},{2,1},{3,2},{4,7},{5,4},{6,5},{7,6},{8,11},{9,8},{10,9... | collective-permute-start | bytes 98312 | tf_op jit(solution)/shard_map/ppermute | solution.py:406

commit v3 on v2

v3 whole, which is shorter than its diff:
```python
import functools

import jax
import jax.numpy as jnp
from jax import lax
from jax.experimental import pallas as pl
from jax.experimental.pallas import tpu as pltpu
from jax.sharding import PartitionSpec as P

F32 = jnp.float32
BF16 = jnp.bfloat16
LOG2E = 1.4426950408889634
SUB = 8
LANES = 128
CHUNKS = 16
REACH = 3
VMEM = pl.BlockSpec(memory_space=pltpu.VMEM)
PARAMS = pltpu.CompilerParams(vmem_limit_bytes=48 * 1024 * 1024)


def call(kernel, name, outs, count, scratch=()):
    return pl.pallas_call(
        kernel,
        out_shape=outs,
        in_specs=[VMEM] * count,
        out_specs=jax.tree.map(lambda _: VMEM, outs),
        scratch_shapes=scratch,
        compiler_params=PARAMS,
        name=name,
    )


def rows_of(width):
    return -(-(width + 2 * REACH) // 16) * 16


def iota(shape, dim):
    return lax.broadcasted_iota(jnp.int32, shape, dim)


def one_hot(mask):
    return jnp.where(mask, 1.0, 0.0).astype(BF16)


def spread(weights, left, right, mask):
    inner = lax.dot_general(
        left, weights, (((1,), (1,)), ((), ())), preferred_element_type=F32
    ).astype(BF16)
    return jnp.where(mask, jnp.dot(inner, right, preferred_element_type=F32), 0.0)


def turn_kernel(field_ref, turned_ref, first_ref, last_ref):
    layers, length, width = field_ref.shape
    half = length // 2
    for k in range(half):
        turned = jnp.concatenate([field_ref[:, k, :], field_ref[:, k + half, :]], axis=0).T
        turned_ref[k, REACH : REACH + width] = turned
        for j in range(REACH):
            first_ref[j, k : k + 1] = turned[j : j + 1]
            last_ref[j, k : k + 1] = turned[width - REACH + j : width - REACH + j + 1]


def weights_kernel(in_ref, out_ref, after_ref, win_ref, wout_ref):
    del after_ref
    units, feats = in_ref.shape
    channels = out_ref.shape[0]
    bands = channels // 2
    rows, cols = feats * CHUNKS, units * CHUNKS
    left = one_hot(iota((rows, feats), 0) // CHUNKS == iota((rows, feats), 1))
    right = one_hot(iota((units, cols), 1) // CHUNKS == iota((units, cols), 0))
    mask = iota((rows, cols), 0) % CHUNKS == iota((rows, cols), 1) % CHUNKS
    win_ref[...] = (0.5 * spread(in_ref[...], left, right, mask)).astype(BF16)
    rows, cols = cols, channels * CHUNKS
    left = one_hot(iota((rows, units), 0) // CHUNKS == iota((rows, units), 1))
    at = iota((channels, cols), 1)
    right = one_hot((at // LANES) * bands + at % bands == iota((channels, cols), 0))
    mask = iota((rows, cols), 0) % CHUNKS == (iota((rows, cols), 1) % LANES) // bands
    wout_ref[...] = spread(out_ref[...], left, right, mask).astype(BF16)


def sides_kernel(rows_in, turned_ref, before_ref, after_ref, wide_ref, first_ref, last_ref):
    half, rows, _ = turned_ref.shape
    width = rows_in
    layers = LANES // 2
    part = rows // 2
    front = iota((part, LANES), 1) < layers
    for k in range(half):
        wide_ref[k, REACH : REACH + width] = turned_ref[k, REACH : REACH + width]
        for j in range(REACH):
            wide_ref[k, j : j + 1] = before_ref[j, k : k + 1]
            wide_ref[k, REACH + width + j : REACH + width + j + 1] = after_ref[j, k : k + 1]
        wide_ref[k, 2 * REACH + width :] = jnp.zeros((rows - 2 * REACH - width, LANES), F32)
    for j in range(REACH):
        top, low = wide_ref[j, :part], wide_ref[j, part:]
        first_ref[j] = jnp.where(front, top, pltpu.roll(low, layers, axis=1))
        k = half - REACH + j
        top, low = wide_ref[k, :part], wide_ref[k, part:]
        last_ref[j] = jnp.where(front, pltpu.roll(top, layers, axis=1), low)


class Stencil:
    def __init__(self, run, counts):
        self.run = run
        self.layers = layers = LANES // 2
        self.shape = (CHUNKS, LANES)
        lane, chunk = iota(self.shape, 1), iota(self.shape, 0)
        z = lane % layers
        self.near = (z > 0).astype(F32)
        self.far = (z < layers - 1).astype(F32)
        at_x, at_y = lax.axis_index("bx"), lax.axis_index("by")
        count_x, count_y = counts
        self.x_low = jnp.where((lane < layers) & (at_x == 0), 0.0, 1.0)
        self.x_high = jnp.where((lane >= layers) & (at_x == count_x - 1), 0.0, 1.0)
        self.y_low = jnp.where((chunk == 0) & (at_y == 0), 0.0, 1.0)
        self.y_high = jnp.where((chunk == CHUNKS - 1) & (at_y == count_y - 1), 0.0, 1.0)

    def z_sum(self, value):
        return roll(value, 1) * self.near + roll(value, -1) * self.far

    def inside(self, value, y, edge):
        if edge is not None:
            value = value * edge
        if y < 0:
            value = value * self.y_low
        if y >= self.run:
            value = value * self.y_high
        return value

    def smooth(self, centre, others):
        total = self.z_sum(centre)
        for other in others:
            total = total + other
        return 0.4 * centre + 0.1 * total

    def raw(self, ref, k, y):
        return ref[k, pl.ds(y + REACH, CHUNKS, stride=self.run), :]

    def once(self, raw, k, out, at, edge=None):
        column = [self.raw(raw, k, y) for y in range(-3, self.run + 3)]
        for i in range(1, len(column) - 1):
            y = i - 3
            sides = [self.raw(raw, k - 1, y), self.raw(raw, k + 1, y)]
            value = self.smooth(column[i], [column[i - 1], column[i + 1]] + sides)
            out[at, i - 1] = self.inside(value, y, edge)

    def twice(self, once, k, out, ridge, at, edge=None):
        column = [once[k, i] for i in range(self.run + 4)]
        for i in range(1, len(column) - 1):
            sides = [once[k - 1, i], once[k + 1, i]]
            value = self.smooth(column[i], [column[i - 1], column[i + 1]] + sides)
            value = self.inside(value, i - 2, edge)
            out[at, i - 1] = value
            ridge[at, i - 1] = 2.0 * value + self.z_sum(value)

    def features(self, twice, ridge, k, y):
        p = lambda a, b: twice[k + a, y + 1 + b]
        r = lambda a, b: ridge[k + a, y + 1 + b]
        centre = p(0, 0)
        main, cross = p(1, 1) - p(-1, -1), p(1, -1) - p(-1, 1)
        third = 1.0 / 3.0
        gx = (main + cross + (r(1, 0) - r(-1, 0))) * third
        gy = (main - cross + (r(0, 1) - r(0, -1))) * third
        around = 2.0 * centre + ((p(1, 0) + p(-1, 0)) + (p(0, 1) + p(0, -1)))
        gz = (roll(around, -1) * self.far - roll(around, 1) * self.near) * third
        m = jnp.sqrt(1.0 + gx * gx + gy * gy + gz * gz)
        parts = [centre, gx, gy, gz, m, centre * m, centre * centre]
        packed = [part.astype(BF16) for part in parts] + [jnp.ones(self.shape, BF16)]
        return jnp.concatenate(packed, axis=0).T


def roll(value, shift):
    return pltpu.roll(value, shift % LANES, axis=1)


def network(tiles, win_ref, wout_ref, step):
    cells = jnp.concatenate(tiles, axis=0)
    half_v = jnp.dot(cells, win_ref[...], preferred_element_type=F32)
    hidden = (half_v + half_v * jnp.tanh(half_v)).astype(BF16)
    v = jnp.dot(hidden, wout_ref[...], preferred_element_type=F32)
    soft = jnp.maximum(v, jnp.log(1.0 + jnp.exp2(jnp.minimum(v * LOG2E, 126.0))))
    return soft[:, :LANES], jnp.exp2(soft[:, LANES:] * (-LOG2E * step))


def clear_of_x(q, ratio):
    if ratio == 1.0:
        return q
    if ratio == 2.0:
        return q * q
    return jnp.exp2(jnp.log(q) * (LOG2E * ratio))


def step_ray(ray, clear, emission):
    colour, light = ray
    later = light * clear
    return colour + (light - later) * emission, later


def middle_kernel(
    spans,
    counts,
    steps,
    wide_ref,
    win_ref,
    wout_ref,
    once_out_ref,
    twice_out_ref,
    ridge_out_ref,
    cx_ref,
    tx_ref,
    cy_ref,
    ty_ref,
    once_ref,
    twice_ref,
    ridge_ref,
):
    half = wide_ref.shape[0]
    run = cx_ref.shape[0]
    stencil = Stencil(run, counts)
    many_x, many_y = spans
    inner = half - 2 * REACH

    def once(k, _):
        stencil.once(wide_ref, k + 1, once_ref, k)
        return 0

    lax.fori_loop(0, inner + 4, once, 0, unroll=2)

    def twice(k, _):
        stencil.twice(once_ref, k + 1, twice_ref, ridge_ref, k)
        return 0

    lax.fori_loop(0, inner + 2, twice, 0, unroll=2)
    for k in range(4):
        once_out_ref[0, k] = once_ref[k]
        once_out_ref[1, k] = once_ref[inner + k]
    for k in range(2):
        twice_out_ref[0, k] = twice_ref[k]
        twice_out_ref[1, k] = twice_ref[inner + k]
        ridge_out_ref[0, k] = ridge_ref[k]
        ridge_out_ref[1, k] = ridge_ref[inner + k]

    for k in range(run):
        tx_ref[k] = jnp.ones((LANES, LANES), F32)
        cx_ref[k] = jnp.zeros((LANES, LANES), F32)
    for k in range(inner):
        ty_ref[k] = jnp.ones((LANES, LANES), F32)
        cy_ref[k] = jnp.zeros((LANES, LANES), F32)
    ratio = steps[0] / steps[1]
    down = run // many_y

    def block(step, _):
        x0, y0 = (step // down) * many_x, (step % down) * many_y
        tiles = [
            stencil.features(twice_ref, ridge_ref, x0 + i + 1, y0 + j)
            for j in range(many_y)
            for i in range(many_x)
        ]
        emission, clear = network(tiles, win_ref, wout_ref, steps[1])
        for g in range(LANES // SUB):
            at = pl.ds(g * SUB, SUB)
            rays_y = [(cy_ref[x0 + i, at], ty_ref[x0 + i, at]) for i in range(many_x)]
            for j in range(many_y):
                ray_x = cx_ref[y0 + j, at], tx_ref[y0 + j, at]
                for i in range(many_x):
                    start = (j * many_x + i) * LANES + g * SUB
                    e, q = emission[start : start + SUB], clear[start : start + SUB]
                    rays_y[i] = step_ray(rays_y[i], q, e)
                    ray_x = step_ray(ray_x, clear_of_x(q, ratio), e)
                cx_ref[y0 + j, at], tx_ref[y0 + j, at] = ray_x
            for i in range(many_x):
                cy_ref[x0 + i, at], ty_ref[x0 + i, at] = rays_y[i]
        return 0

    lax.fori_loop(0, inner // many_x * down, block, 0)


def ends_kernel(
    many_y,
    counts,
    steps,
    wide_ref,
    before_ref,
    after_ref,
    win_ref,
    wout_ref,
    once_in_ref,
    twice_in_ref,
    ridge_in_ref,
    cx_ref,
    tx_ref,
    image_x_ref,
    cy_ref,
    ty_ref,
    raw_ref,
    once_ref,
    twice_ref,
    ridge_ref,
):
    half, rows, _ = wide_ref.shape
    run = cx_ref.shape[0]
    layers = LANES // 2
    stencil = Stencil(run, counts)
    part = rows // 2
    front = iota((part, LANES), 1) < layers
    for j in range(REACH):
        halo, own = before_ref[j], wide_ref[half - REACH + j]
        raw_ref[0, j, :part] = jnp.where(front, halo, roll(own[:part], layers))
        raw_ref[0, j, part:] = jnp.where(front, roll(halo, layers), roll(own[part:], layers))
        halo, own = after_ref[j], wide_ref[j]
        raw_ref[1, 2 + j, :part] = jnp.where(front, roll(own[:part], layers), roll(halo, layers))
        raw_ref[1, 2 + j, part:] = jnp.where(front, roll(own[part:], layers), halo)
    for j in range(2):
        raw_ref[0, REACH + j] = wide_ref[j]
        raw_ref[1, j] = wide_ref[half - 2 + j]
    for k in range(4):
        once_ref[0, 3 + k] = once_in_ref[0, k]
        once_ref[1, k] = once_in_ref[1, k]
    for k in range(2):
        twice_ref[0, 3 + k] = twice_in_ref[0, k]
        twice_ref[1, k] = twice_in_ref[1, k]
        ridge_ref[0, 3 + k] = ridge_in_ref[0, k]
        ridge_ref[1, k] = ridge_in_ref[1, k]
    for side, edge in enumerate((stencil.x_low, stencil.x_high)):
        outside = (0, 1) if side == 0 else (1, 2)
        for k in range(3):
            kept = edge if k in outside else None
            stencil.once(raw_ref.at[side], k + 1, once_ref.at[side], k + 4 * side, kept)
    for side, edge in enumerate((stencil.x_low, stencil.x_high)):
        for k in range(3):
            kept = edge if k == 2 * side else None
            at = k + 2 * side
            stencil.twice(once_ref.at[side], at + 1, twice_ref.at[side], ridge_ref.at[side], at, kept)

    ratio = steps[0] / steps[1]
    planes = [(0, 1), (0, 2), (0, 3), (1, 1), (1, 2), (1, 3)]
    for k in range(len(planes)):
        ty_ref[k] = jnp.ones((LANES, LANES), F32)
        cy_ref[k] = jnp.zeros((LANES, LANES), F32)

    def block(step, _):
        y0 = step * many_y
        tiles = [
            stencil.features(twice_ref.at[side], ridge_ref.at[side], k, y0 + j)
            for j in range(many_y)
            for side, k in planes
        ]
        emission, clear = network(tiles, win_ref, wout_ref, steps[1])
        images = [[], []]
        for g in range(LANES // SUB):
            at = pl.ds(g * SUB, SUB)
            rays_y = [(cy_ref[i, at], ty_ref[i, at]) for i in range(len(planes))]
            for j in range(many_y):
                ray_x = jnp.zeros((SUB, LANES), F32), jnp.ones((SUB, LANES), F32)
                for i in range(len(planes)):
                    if i == REACH:
                        colour, light = ray_x
                        colour = colour + light * cx_ref[y0 + j, at]
                        ray_x = colour, light * tx_ref[y0 + j, at]
                    start = (j * len(planes) + i) * LANES + g * SUB
                    e, q = emission[start : start + SUB], clear[start : start + SUB]
                    rays_y[i] = step_ray(rays_y[i], q, e)
                    ray_x = step_ray(ray_x, clear_of_x(q, ratio), e)
                images[0].append(ray_x[0])
                images[1].append(ray_x[1])
            for i in range(len(planes)):
                cy_ref[i, at], ty_ref[i, at] = rays_y[i]
        for d in range(layers // SUB):
            for j in range(many_y):
                near, far = d * many_y + j, (d + layers // SUB) * many_y + j
                q = images[1][near]
                image_x_ref[d, 0, y0 + j] = images[0][near] + q * images[0][far]
                image_x_ref[d, 1, y0 + j] = q * images[1][far]
        return 0

    lax.fori_loop(0, run // many_y, block, 0)


def columns_kernel(share, peers, cy_ref, ty_ref, cy_ends_ref, ty_ends_ref, *refs):
    outs, (rows_ref, turned_ref) = refs[:peers], refs[peers:]
    inner = ty_ref.shape[0]
    half = inner + 2 * REACH
    layers = LANES // 2
    for k in range(half):
        if k < REACH:
            colours, clears = cy_ends_ref[k].T, ty_ends_ref[k].T
        elif k < REACH + inner:
            colours, clears = cy_ref[k - REACH].T, ty_ref[k - REACH].T
        else:
            colours, clears = cy_ends_ref[k - inner].T, ty_ends_ref[k - inner].T
        colour, clear = colours[:SUB], clears[:SUB]
        for c in range(1, CHUNKS):
            at = slice(c * SUB, (c + 1) * SUB)
            colour = colour + clear * colours[at]
            clear = clear * clears[at]
        rows_ref[0, k * SUB : (k + 1) * SUB] = colour
        rows_ref[1, k * SUB : (k + 1) * SUB] = clear
    me = lax.axis_index("by")
    for kind in range(2):
        turned_ref[kind] = rows_ref[kind].T
        for s in range(peers):
            start = pl.multiple_of(lax.rem(me + s, peers) * share, share)
            for part in range(2):
                outs[s][kind, part] = turned_ref[kind, pl.ds(part * layers + start, share)]


def fold_y_kernel(*refs):
    pieces, out_ref = refs[:-1], refs[-1]
    peers = len(pieces)
    me = lax.axis_index("by")

    def piece(source):
        shift = lax.rem(me - source + peers, peers)
        value = pieces[0][...]
        for s in range(1, peers):
            value = jnp.where(shift == s, pieces[s][...], value)
        return value

    value = piece(0)
    colour, clear = value[0], value[1]
    for source in range(1, peers):
        value = piece(source)
        colour = colour + clear * value[0]
        clear = clear * value[1]
    out_ref[0] = colour
    out_ref[1] = clear


def fold_x_kernel(pieces_ref, out_ref):
    peers, _, run, share, _ = pieces_ref.shape
    lane = iota((share, LANES), 1)
    kinds = [[], []]
    for y in range(run):
        colour, clear = pieces_ref[0, 0, y], pieces_ref[0, 1, y]
        for k in range(1, peers):
            colour = colour + clear * pieces_ref[k, 0, y]
            clear = clear * pieces_ref[k, 1, y]
        kinds[0].append(colour)
        kinds[1].append(clear)
    for kind, values in enumerate(kinds):
        for s in (1, 2, 4):
            for i in range(run):
                if not i & s:
                    a, b = values[i], values[i | s]
                    odd = (lane & s) != 0
                    values[i] = jnp.where(odd, pltpu.roll(b, s, axis=1), a)
                    values[i | s] = jnp.where(odd, b, pltpu.roll(a, LANES - s, axis=1))
        for band, value in enumerate(values):
            out_ref[kind, band] = value


def exchange(last, first, axis):
    peers = lax.axis_size(axis)
    up = [(i, i + 1) for i in range(peers - 1)]
    down = [(j, i) for i, j in up]
    return lax.ppermute(last, axis, up), lax.ppermute(first, axis, down)


def body(scalar_field, transfer_in, transfer_out):
    layers, local_x, local_y = scalar_field.shape
    units, feats = transfer_in.shape
    channels = transfer_out.shape[0]
    bands = channels // 2
    count_x, count_y = lax.axis_size("bx"), lax.axis_size("by")
    steps = (2.0 / (local_x * count_x), 2.0 / (local_y * count_y))
    half, run, rows = local_x // 2, local_y // CHUNKS, rows_of(local_y)
    sds = lambda *shape: jax.ShapeDtypeStruct(shape, F32)
    weights = [
        jax.ShapeDtypeStruct((feats * CHUNKS, units * CHUNKS), BF16),
        jax.ShapeDtypeStruct((units * CHUNKS, channels * CHUNKS), BF16),
    ]

    edge = sds(REACH, half, LANES)
    turned, first, last = call(turn_kernel, "turn", [sds(half, rows, LANES), edge, edge], 1)(
        scalar_field
    )
    win, wout = call(weights_kernel, "weights", weights, 3)(transfer_in, transfer_out, first)
    before, after = exchange(last, first, "by")
    edge = sds(REACH, rows // 2, LANES)
    wide, first, last = call(
        functools.partial(sides_kernel, local_y), "sides", [sds(half, rows, LANES), edge, edge], 3
    )(turned, before, after)
    before, after = exchange(last, first, "bx")
    inner = half - 2 * REACH
    counts = (count_x, count_y)
    plane = lambda *lead: sds(*lead, CHUNKS, LANES)
    many_x = 5 if inner % 5 == 0 else 1
    many_y = 4 if run % 4 == 0 else 1
    once, twice, ridge, colour_x, clear_x, colour_y, clear_y = call(
        functools.partial(middle_kernel, (many_x, many_y), counts, steps),
        "middle",
        [plane(2, 4, run + 4), plane(2, 2, run + 2), plane(2, 2, run + 2)]
        + [sds(run, LANES, LANES)] * 2
        + [sds(inner, LANES, LANES)] * 2,
        3,
        [
            pltpu.VMEM((inner + 4, run + 4, CHUNKS, LANES), F32),
            pltpu.VMEM((inner + 2, run + 2, CHUNKS, LANES), F32),
            pltpu.VMEM((inner + 2, run + 2, CHUNKS, LANES), F32),
        ],
    )(wide, win, wout)
    image_x, colour_ends, clear_ends = call(
        functools.partial(ends_kernel, many_y, counts, steps),
        "ends",
        [sds(layers // SUB, 2, run, SUB, LANES)] + [sds(2 * REACH, LANES, LANES)] * 2,
        10,
        [
            pltpu.VMEM((2, 5, rows, LANES), F32),
            pltpu.VMEM((2, 7, run + 4, CHUNKS, LANES), F32),
            pltpu.VMEM((2, 5, run + 2, CHUNKS, LANES), F32),
            pltpu.VMEM((2, 5, run + 2, CHUNKS, LANES), F32),
        ],
    )(wide, before, after, win, wout, once, twice, ridge, colour_x, clear_x)

    share_x = layers // count_x
    if share_x != SUB:
        image_x = jnp.transpose(image_x, (1, 2, 0, 3, 4)).reshape(2, run, count_x, share_x, LANES)
        image_x = jnp.transpose(image_x, (2, 0, 1, 3, 4))
    pieces = lax.all_to_all(image_x, "bx", split_axis=0, concat_axis=0, tiled=True)
    view_x = call(fold_x_kernel, "fold_x", sds(2, bands, share_x, local_y), 1)(pieces)

    share = layers // count_y
    piece = sds(2, 2, share, LANES)
    scratch = [pltpu.VMEM((2, LANES, LANES), F32), pltpu.VMEM((2, LANES, LANES), F32)]
    pieces = call(
        functools.partial(columns_kernel, share, count_y), "columns", [piece] * count_y, 4, scratch
    )(colour_y, clear_y, colour_ends, clear_ends)
    pieces = list(pieces)
    for s in range(1, count_y):
        pairs = [(i, (i + s) % count_y) for i in range(count_y)]
        pieces[s] = lax.ppermute(pieces[s], "by", pairs)
    view_y = call(fold_y_kernel, "fold_y", piece, count_y)(*pieces)
    view_y = view_y.reshape(2, 2, share, half, bands)
    view_y = jnp.transpose(view_y, (0, 4, 2, 1, 3)).reshape(2, bands, share, local_x)
    return (view_x, view_y)


def solution(mesh):
    return jax.shard_map(
        body,
        mesh=mesh,
        in_specs=(P(None, "bx", "by"), P(), P()),
        out_specs=(P(None, None, "bx", "by"), P(None, None, "by", "bx")),
        check_vma=False,
    )
```

time: 67.1 us -> 59.6 us (0.89)
  waiting for transfers between devices: 19.7 us -> 13.5 us
  local copies, waits for them, and re-layouts: 3.6 us -> 2.23 us
  Pallas kernels: 24.7 us -> 23.5 us
  starting transfers between devices: 18.1 us -> 19.3 us
    ppermute x4, waiting for transfers between devices: 9.26 us -> 3.92 us  [exchange(): return (lax.ppermute(last, axis, up), lax.ppermute(first, axis, down))]
    unnamed x6 -> x8, local copies, waits for them, and re-layouts: 3.48 us -> 2.11 us
    pallas_call x2 -> x4, Pallas kernels: 23 us -> 21.7 us  [the longest x1 10.7 us: body(): call(functools.partial(middle_kernel, (many_x, many_y), counts, steps), '...]
    all_to_all x1, starting transfers between devices: 5.75 us -> 6.96 us  [body(): lax.all_to_all(image_x, 'bx', split_axis=0, concat_axis=0, tiled=True)]
    all_to_all x1, waiting for transfers between devices: 8.81 us -> 7.62 us  [body(): lax.all_to_all(image_x, 'bx', split_axis=0, concat_axis=0, tiled=True)]
  transfers between devices with their start and end apart: 8 -> 8, of which waited for: 6 -> 3; matrix products, arithmetic and copies ran while one was open for 1% -> 2% of each run, Pallas kernels for 1% -> 20%
where the time goes in v3:
time: 59.6 us; the launch traced here: 59.2 us
  Pallas kernels  23.5 us (39%)
  starting transfers between devices  19.3 us (32%)
  waiting for transfers between devices  13.5 us (23%)
  local copies, waits for them, and re-layouts  2.23 us (4%)
  between operations  0.75 us (1%)
    pallas_call x1, Pallas kernels, body(): call(functools.partial(middle_kernel, (many_x, many_y), counts, steps), '...  10.7 us
    pallas_call x1, Pallas kernels, body(): call(functools.partial(ends_kernel, many_y, counts, steps), 'ends', [sds(...  9.97 us
    ppermute x4, starting transfers between devices, exchange(): return (lax.ppermute(last, axis, up), lax.ppermute(first, axis, down))  8.34 us
    all_to_all x1, waiting for transfers between devices, body(): lax.all_to_all(image_x, 'bx', split_axis=0, concat_axis=0, tiled=True)  7.62 us
    all_to_all x1, starting transfers between devices, body(): lax.all_to_all(image_x, 'bx', split_axis=0, concat_axis=0, tiled=True)  6.96 us
    ppermute x3, starting transfers between devices, body(): pieces[s] = lax.ppermute(pieces[s], 'by', pairs)  3.97 us
    ppermute x4, waiting for transfers between devices, exchange(): return (lax.ppermute(last, axis, up), lax.ppermute(first, axis, down))  3.92 us
    unnamed x8, local copies, waits for them, and re-layouts  2.11 us
  transfers between devices with their start and end apart: 8, of which 3 were waited for; matrix products, arithmetic and copies ran while one was open for 2% of the time, Pallas kernels for 20%

profile of v3, /device:TPU:0, one launch (start us, length us, event | category | flops | bytes accessed | tf_op | source)
XLA Modules:
  0.0 59.2 jit_solution(14471462437897513544)
XLA Ops:
  0.6 0.0 copy-start
  0.6 1.2 %copy-done = f32[64,32,128]{2,1,0:T(8,128)S(1)} copy-done((f32[64,32,128]{2,1,0:T(8,128)S(1)}, f32[64,32,128]{2,1,0:T(8,128)}, u32[]{:S(2)}) %copy-start) | copy-done | bytes 1048600
  1.9 0.0 copy-start.2
  1.9 0.0 copy-start.1
  1.9 0.6 %turn.1 = (f32[16,144,128]{2,1,0:T(8,128)S(1)}, f32[3,16,128]{2,1,0:T(8,128)S(1)}, f32[3,16,128]{2,1,0:T(8,128)S(1)}) custom-call(f32[64,32,128]{2,1,0:T(8,128)S(1)} %copy-done), custom_call_target="tpu_custom_call" | custom-call | tf_op jit(solution)/shard_map/turn/pallas_call | solution.py:473
  2.5 2.4 %collective-permute-start = (f32[3,16,128]{2,1,0:T(8,128)S(1)}, f32[3,16,128]{2,1,0:T(8,128)S(1)}, u32[]{:S(2)}, u32[]{:S(2)}) collective-permute-start(f32[3,16,128]{2,1,0:T(8,128)S(1)} %get-tuple-element.25), channel_id=1, source_target_pairs={{0,1},{1,2},{2,3},{4,5},{5,6},{6,7},{8,9},{9,10},{10,11},{12,13},{... | collective-permute-start | bytes 73736 | tf_op jit(solution)/shard_map/ppermute | solution.py:455
  4.9 1.3 %collective-permute-start.1 = (f32[3,16,128]{2,1,0:T(8,128)S(1)}, f32[3,16,128]{2,1,0:T(8,128)S(1)}, u32[]{:S(2)}, u32[]{:S(2)}) collective-permute-start(f32[3,16,128]{2,1,0:T(8,128)S(1)} %get-tuple-element.26.after_ref), channel_id=1, source_target_pairs={{1,0},{2,1},{3,2},{5,4},{6,5},{7,6},{9,8},{10,9},{11,10},{13,12},{... | collective-permute-start | bytes 73736 | tf_op jit(solution)/shard_map/ppermute | solution.py:455
  6.2 0.0 collective-permute-done.before_ref
  6.2 3.9 %collective-permute-done.1.after_ref = f32[3,16,128]{2,1,0:T(8,128)S(1)} collective-permute-done((f32[3,16,128]{2,1,0:T(8,128)S(1)}, f32[3,16,128]{2,1,0:T(8,128)S(1)}, u32[]{:S(2)}, u32[]{:S(2)}) %collective-permute-start.1) | collective-permute-done | bytes 24608 | tf_op jit(solution)/shard_map/ppermute | solution.py:455
  10.1 0.2 sides.1
  10.3 3.4 %collective-permute-start.2 = (f32[3,72,128]{2,1,0:T(8,128)S(1)}, f32[3,72,128]{2,1,0:T(8,128)S(1)}, u32[]{:S(2)}, u32[]{:S(2)}) collective-permute-start(f32[3,72,128]{2,1,0:T(8,128)S(1)} %get-tuple-element.28), channel_id=1, source_target_pairs={{0,4},{4,8},{8,12},{12,16},{16,20},{20,24},{24,28},{1,5},{5,9},{9,... | collective-permute-start | bytes 331784 | tf_op jit(solution)/shard_map/ppermute | solution.py:455
  13.7 1.3 %collective-permute-start.3 = (f32[3,72,128]{2,1,0:T(8,128)S(1)}, f32[3,72,128]{2,1,0:T(8,128)S(1)}, u32[]{:S(2)}, u32[]{:S(2)}) collective-permute-start(f32[3,72,128]{2,1,0:T(8,128)S(1)} %get-tuple-element.29), channel_id=1, source_target_pairs={{4,0},{8,4},{12,8},{16,12},{20,16},{24,20},{28,24},{5,1},{9,5},{13... | collective-permute-start | bytes 331784 | tf_op jit(solution)/shard_map/ppermute | solution.py:455
  15.0 0.0 copy-done.2
  15.0 0.1 copy.7.in_ref
  15.1 0.0 copy-done.1
  15.1 0.5 weights.1
  15.5 10.7 %middle.1 = (f32[2,4,12,16,128]{4,3,2,1,0:T(8,128)S(1)}, f32[2,2,10,16,128]{4,3,2,1,0:T(8,128)S(1)}, f32[2,2,10,16,128]{4,3,2,1,0:T(8,128)S(1)}, f32[8,128,128]{...) custom-call(f32[16,144,128]{2,1,0:T(8,128)S(1)} %get-tuple-element.27.wide_, ...), custom_call_target="tpu_custom_call" | custom-call | tf_op jit(solution)/shard_map/middle/pallas_call | solution.py:488
  26.2 0.0 collective-permute-done.2.before_ref
  26.2 0.0 collective-permute-done.3.after_ref
  26.2 10.0 %ends.1 = (f32[8,2,8,8,128]{4,3,2,1,0:T(8,128)}, f32[6,128,128]{2,1,0:T(8,128)S(1)}, f32[6,128,128]{2,1,0:T(8,128)S(1)}) custom-call(f32[16,144,128]{2,1,0:T(8,128)S(1)} %get-tuple-element.27.wide_ref, f32[3,72,128]{2,1,0:T(8,128)S(1)} %collective-permute-done.2.before_ref, f32[3,72,128]{2,1,0:T(8,128)S(1)} %collective-permute-done.3.after_ref, ...), custom_call_target="tpu_custom_call" | custom-call | tf_op jit(solution)/shard_map/ends/pallas_call | solution.py:501
  36.2 7.0 %all-to-all-start = ((f32[8,2,8,8,128]{4,3,2,1,0:T(8,128)}), f32[8,2,8,8,128]{4,3,2,1,0:T(8,128)S(1)}, u32[]{:S(2)}, u32[]{:S(2)}) async-start(f32[8,2,8,8,128]{4,3,2,1,0:T(8,128)} %get-tuple-element.37), calls=%async_computation | async-start | bytes 1048576 | tf_op jit(solution)/shard_map/all_to_all | solution.py:518
  43.2 0.7 %columns.1 = (f32[2,2,16,128]{3,2,1,0:T(8,128)S(1)}, f32[2,2,16,128]{3,2,1,0:T(8,128)S(1)}, f32[2,2,16,128]{3,2,1,0:T(8,128)S(1)}, f32[2,2,16,128]{3,2,1,0:T(8,128)S(1)}) custom-call(f32[10,128,128]{2,1,0:T(8,128)S(1)} %get-tuple-element.38.cy_ref, f32[10,128,128]{2,1,0:T(8,128)S(1)} %get-tuple-element.39.ty_ref, ...), custom_call_target="tpu_custom_call" | custom-call | tf_op jit(solution)/shard_map/columns/pallas_call | solution.py:524
  43.8 1.8 %collective-permute-start.4 = (f32[2,2,16,128]{3,2,1,0:T(8,128)S(1)}, f32[2,2,16,128]{3,2,1,0:T(8,128)S(1)}, u32[]{:S(2)}, u32[]{:S(2)}) collective-permute-start(f32[2,2,16,128]{3,2,1,0:T(8,128)S(1)} %get-tuple-element.43), channel_id=1, source_target_pairs={{0,1},{1,2},{2,3},{3,0},{4,5},{5,6},{6,7},{7,4},{8,9},{9,10},{10,1... | collective-permute-start | bytes 98312 | tf_op jit(solution)/shard_map/ppermute | solution.py:530
  45.6 0.8 %collective-permute-start.5 = (f32[2,2,16,128]{3,2,1,0:T(8,128)S(1)}, f32[2,2,16,128]{3,2,1,0:T(8,128)S(1)}, u32[]{:S(2)}, u32[]{:S(2)}) collective-permute-start(f32[2,2,16,128]{3,2,1,0:T(8,128)S(1)} %get-tuple-element.44), channel_id=1, source_target_pairs={{0,2},{1,3},{2,0},{3,1},{4,6},{5,7},{6,4},{7,5},{8,10},{9,11},{10,... | collective-permute-start | bytes 98312 | tf_op jit(solution)/shard_map/ppermute | solution.py:530
  46.4 1.4 %collective-permute-start.6 = (f32[2,2,16,128]{3,2,1,0:T(8,128)S(1)}, f32[2,2,16,128]{3,2,1,0:T(8,128)S(1)}, u32[]{:S(2)}, u32[]{:S(2)}) collective-permute-start(f32[2,2,16,128]{3,2,1,0:T(8,128)S(1)} %get-tuple-element.45), channel_id=1, source_target_pairs={{0,3},{1,0},{2,1},{3,2},{4,7},{5,4},{6,5},{7,6},{8,11},{9,8},{10,9... | collective-permute-start | bytes 98312 | tf_op jit(solution)/shard_map/ppermute | solution.py:530
  47.8 0.0 collective-permute-done.4.refs_1_
  47.8 1.9 %collective-permute-done.5.refs_2_ = f32[2,2,16,128]{3,2,1,0:T(8,128)S(1)} collective-permute-done((f32[2,2,16,128]{3,2,1,0:T(8,128)S(1)}, f32[2,2,16,128]{3,2,1,0:T(8,128)S(1)}, u32[]{:S(2)}, u32[]{:S(2)}) %collective-permute-start.5) | collective-permute-done | bytes 32800 | tf_op jit(solution)/shard_map/ppermute | solution.py:530
  49.8 0.0 collective-permute-done.6.refs_3_
  49.8 0.1 copy.8
  49.9 0.8 %copy.9 = f32[2,8,16,32]{3,2,1,0:T(8,128)} copy(f32[2,8,16,32]{2,1,3,0:T(8,128)S(1)} %bitcast.5) | data formatting | bytes 65536
  50.7 7.6 %all-to-all-done.pieces_ref = f32[8,2,8,8,128]{4,3,2,1,0:T(8,128)S(1)} async-done(((f32[8,2,8,8,128]{4,3,2,1,0:T(8,128)}), f32[8,2,8,8,128]{4,3,2,1,0:T(8,128)S(1)}, u32[]{:S(2)}, u32[]{:S(2)}) %all-to-all-start) | async-done | bytes 524320 | tf_op jit(solution)/shard_map/all_to_all | solution.py:518
  58.3 0.9 %fold_x.1 = f32[2,8,8,128]{3,2,1,0:T(8,128)} custom-call(f32[8,2,8,8,128]{4,3,2,1,0:T(8,128)S(1)} %all-to-all-done.pieces_ref), custom_call_target="tpu_custom_call" | custom-call | tf_op jit(solution)/shard_map/fold_x/pallas_call | solution.py:519
  (1 shorter events, 0.0 us)
Async XLA Ops:
  0.6 1.2 %copy-start = (f32[64,32,128]{2,1,0:T(8,128)S(1)}, f32[64,32,128]{2,1,0:T(8,128)}, u32[]{:S(2)}) copy-start(f32[64,32,128]{2,1,0:T(8,128)} %field_ref.1) | copy-start | bytes 3145732
  1.9 13.1 %copy-start.2 = (bf16[16,8]{0,1:T(8,128)(2,1)S(1)}, bf16[16,8]{0,1:T(8,128)(2,1)}, u32[]{:S(2)}) copy-start(bf16[16,8]{0,1:T(8,128)(2,1)} %param.4) | copy-start | bytes 772
  1.9 13.2 %copy-start.1 = (bf16[16,16]{1,0:T(8,128)(2,1)S(1)}, bf16[16,16]{1,0:T(8,128)(2,1)}, u32[]{:S(2)}) copy-start(bf16[16,16]{1,0:T(8,128)(2,1)} %out_ref.1) | copy-start | bytes 1540
  2.5 3.7 %collective-permute-start = (f32[3,16,128]{2,1,0:T(8,128)S(1)}, f32[3,16,128]{2,1,0:T(8,128)S(1)}, u32[]{:S(2)}, u32[]{:S(2)}) collective-permute-start(f32[3,16,128]{2,1,0:T(8,128)S(1)} %get-tuple-element.25), channel_id=1, source_target_pairs={{0,1},{1,2},{2,3},{4,5},{5,6},{6,7},{8,9},{9,10},{10,11},{12,13},{... | collective-permute-start | bytes 73736 | tf_op jit(solution)/shard_map/ppermute | solution.py:455
  4.9 5.2 %collective-permute-start.1 = (f32[3,16,128]{2,1,0:T(8,128)S(1)}, f32[3,16,128]{2,1,0:T(8,128)S(1)}, u32[]{:S(2)}, u32[]{:S(2)}) collective-permute-start(f32[3,16,128]{2,1,0:T(8,128)S(1)} %get-tuple-element.26.after_ref), channel_id=1, source_target_pairs={{1,0},{2,1},{3,2},{5,4},{6,5},{7,6},{9,8},{10,9},{11,10},{13,12},{... | collective-permute-start | bytes 73736 | tf_op jit(solution)/shard_map/ppermute | solution.py:455
  10.3 16.0 %collective-permute-start.2 = (f32[3,72,128]{2,1,0:T(8,128)S(1)}, f32[3,72,128]{2,1,0:T(8,128)S(1)}, u32[]{:S(2)}, u32[]{:S(2)}) collective-permute-start(f32[3,72,128]{2,1,0:T(8,128)S(1)} %get-tuple-element.28), channel_id=1, source_target_pairs={{0,4},{4,8},{8,12},{12,16},{16,20},{20,24},{24,28},{1,5},{5,9},{9,... | collective-permute-start | bytes 331784 | tf_op jit(solution)/shard_map/ppermute | solution.py:455
  13.7 12.6 %collective-permute-start.3 = (f32[3,72,128]{2,1,0:T(8,128)S(1)}, f32[3,72,128]{2,1,0:T(8,128)S(1)}, u32[]{:S(2)}, u32[]{:S(2)}) collective-permute-start(f32[3,72,128]{2,1,0:T(8,128)S(1)} %get-tuple-element.29), channel_id=1, source_target_pairs={{4,0},{8,4},{12,8},{16,12},{20,16},{24,20},{28,24},{5,1},{9,5},{13... | collective-permute-start | bytes 331784 | tf_op jit(solution)/shard_map/ppermute | solution.py:455
  36.2 22.2 %all-to-all-start = ((f32[8,2,8,8,128]{4,3,2,1,0:T(8,128)}), f32[8,2,8,8,128]{4,3,2,1,0:T(8,128)S(1)}, u32[]{:S(2)}, u32[]{:S(2)}) async-start(f32[8,2,8,8,128]{4,3,2,1,0:T(8,128)} %get-tuple-element.37), calls=%async_computation | async-start | bytes 1048576 | tf_op jit(solution)/shard_map/all_to_all | solution.py:518
  43.8 4.0 %collective-permute-start.4 = (f32[2,2,16,128]{3,2,1,0:T(8,128)S(1)}, f32[2,2,16,128]{3,2,1,0:T(8,128)S(1)}, u32[]{:S(2)}, u32[]{:S(2)}) collective-permute-start(f32[2,2,16,128]{3,2,1,0:T(8,128)S(1)} %get-tuple-element.43), channel_id=1, source_target_pairs={{0,1},{1,2},{2,3},{3,0},{4,5},{5,6},{6,7},{7,4},{8,9},{9,10},{10,1... | collective-permute-start | bytes 98312 | tf_op jit(solution)/shard_map/ppermute | solution.py:530
  45.6 4.2 %collective-permute-start.5 = (f32[2,2,16,128]{3,2,1,0:T(8,128)S(1)}, f32[2,2,16,128]{3,2,1,0:T(8,128)S(1)}, u32[]{:S(2)}, u32[]{:S(2)}) collective-permute-start(f32[2,2,16,128]{3,2,1,0:T(8,128)S(1)} %get-tuple-element.44), channel_id=1, source_target_pairs={{0,2},{1,3},{2,0},{3,1},{4,6},{5,7},{6,4},{7,5},{8,10},{9,11},{10,... | collective-permute-start | bytes 98312 | tf_op jit(solution)/shard_map/ppermute | solution.py:530
  46.4 3.3 %collective-permute-start.6 = (f32[2,2,16,128]{3,2,1,0:T(8,128)S(1)}, f32[2,2,16,128]{3,2,1,0:T(8,128)S(1)}, u32[]{:S(2)}, u32[]{:S(2)}) collective-permute-start(f32[2,2,16,128]{3,2,1,0:T(8,128)S(1)} %get-tuple-element.45), channel_id=1, source_target_pairs={{0,3},{1,0},{2,1},{3,2},{4,7},{5,4},{6,5},{7,6},{8,11},{9,8},{10,9... | collective-permute-start | bytes 98312 | tf_op jit(solution)/shard_map/ppermute | solution.py:530

commit v4 on v3

--- a/solution.py
+++ b/solution.py
@@ -219,17 +219,10 @@
     many_x, many_y = spans
     inner = half - 2 * REACH
 
-    def once(k, _):
+    for k in range(inner + 4):
         stencil.once(wide_ref, k + 1, once_ref, k)
-        return 0
-
-    lax.fori_loop(0, inner + 4, once, 0, unroll=2)
-
-    def twice(k, _):
+    for k in range(inner + 2):
         stencil.twice(once_ref, k + 1, twice_ref, ridge_ref, k)
-        return 0
-
-    lax.fori_loop(0, inner + 2, twice, 0, unroll=2)
     for k in range(4):
         once_out_ref[0, k] = once_ref[k]
         once_out_ref[1, k] = once_ref[inner + k]
@@ -248,7 +241,7 @@
     ratio = steps[0] / steps[1]
     down = run // many_y
 
-    def block(step, _):
+    def block(step):
         x0, y0 = (step // down) * many_x, (step % down) * many_y
         tiles = [
             stencil.features(twice_ref, ridge_ref, x0 + i + 1, y0 + j)
@@ -269,9 +262,9 @@
                 cx_ref[y0 + j, at], tx_ref[y0 + j, at] = ray_x
             for i in range(many_x):
                 cy_ref[x0 + i, at], ty_ref[x0 + i, at] = rays_y[i]
-        return 0
-
-    lax.fori_loop(0, inner // many_x * down, block, 0)
+
+    for step in range(inner // many_x * down):
+        block(step)
 
 
 def ends_kernel(
@@ -337,7 +330,7 @@
         ty_ref[k] = jnp.ones((LANES, LANES), F32)
         cy_ref[k] = jnp.zeros((LANES, LANES), F32)
 
-    def block(step, _):
+    def block(step):
         y0 = step * many_y
         tiles = [
             stencil.features(twice_ref.at[side], ridge_ref.at[side], k, y0 + j)
@@ -370,9 +363,9 @@
                 q = images[1][near]
                 image_x_ref[d, 0, y0 + j] = images[0][near] + q * images[0][far]
                 image_x_ref[d, 1, y0 + j] = q * images[1][far]
-        return 0
-
-    lax.fori_loop(0, run // many_y, block, 0)
+
+    for step in range(run // many_y):
+        block(step)
 
 
 def columns_kernel(share, peers, cy_ref, ty_ref, cy_ends_ref, ty_ends_ref, *refs):
@@ -483,8 +476,7 @@
     inner = half - 2 * REACH
     counts = (count_x, count_y)
     plane = lambda *lead: sds(*lead, CHUNKS, LANES)
-    many_x = 5 if inner % 5 == 0 else 1
-    many_y = 4 if run % 4 == 0 else 1
+    many_x, many_y = inner, 2
     once, twice, ridge, colour_x, clear_x, colour_y, clear_y = call(
         functools.partial(middle_kernel, (many_x, many_y), counts, steps),
         "middle",

time: 59.6 us -> 53.9 us (0.904)
  Pallas kernels: 23.5 us -> 17.7 us
    pallas_call x1, Pallas kernels: 9.97 us -> 6.24 us  [body(): call(functools.partial(ends_kernel, many_y, counts, steps), 'ends', [sds(...]
    pallas_call x1, Pallas kernels: 10.7 us -> 8.65 us  [body(): call(functools.partial(middle_kernel, (many_x, many_y), counts, steps), '...]
  transfers between devices with their start and end apart: 8 -> 8, of which waited for: 3 -> 3; matrix products, arithmetic and copies ran while one was open for 2% -> 2% of each run, Pallas kernels for 20% -> 18%
where the time goes in v4:
time: 53.9 us; the launch traced here: 53.5 us
  starting transfers between devices  19.3 us (36%)
  Pallas kernels  17.7 us (33%)
  waiting for transfers between devices  13.5 us (25%)
  local copies, waits for them, and re-layouts  2.23 us (4%)
  between operations  0.75 us (1%)
    pallas_call x1, Pallas kernels, body(): call(functools.partial(middle_kernel, (many_x, many_y), counts, steps), '...  8.65 us
    ppermute x4, starting transfers between devices, exchange(): return (lax.ppermute(last, axis, up), lax.ppermute(first, axis, down))  8.34 us
    all_to_all x1, waiting for transfers between devices, body(): lax.all_to_all(image_x, 'bx', split_axis=0, concat_axis=0, tiled=True)  7.61 us
    all_to_all x1, starting transfers between devices, body(): lax.all_to_all(image_x, 'bx', split_axis=0, concat_axis=0, tiled=True)  6.95 us
    pallas_call x1, Pallas kernels, body(): call(functools.partial(ends_kernel, many_y, counts, steps), 'ends', [sds(...  6.24 us
    ppermute x3, starting transfers between devices, body(): pieces[s] = lax.ppermute(pieces[s], 'by', pairs)  3.97 us
    ppermute x4, waiting for transfers between devices, exchange(): return (lax.ppermute(last, axis, up), lax.ppermute(first, axis, down))  3.92 us
    unnamed x8, local copies, waits for them, and re-layouts  2.11 us
  transfers between devices with their start and end apart: 8, of which 3 were waited for; matrix products, arithmetic and copies ran while one was open for 2% of the time, Pallas kernels for 18%

profile of v4, /device:TPU:0, one launch (start us, length us, event | category | flops | bytes accessed | tf_op | source)
XLA Modules:
  0.0 53.5 jit_solution(12949854014485052235)
XLA Ops:
  0.6 0.0 copy-start
  0.6 1.2 %copy-done = f32[64,32,128]{2,1,0:T(8,128)S(1)} copy-done((f32[64,32,128]{2,1,0:T(8,128)S(1)}, f32[64,32,128]{2,1,0:T(8,128)}, u32[]{:S(2)}) %copy-start) | copy-done | bytes 1048600
  1.9 0.0 copy-start.2
  1.9 0.0 copy-start.1
  1.9 0.6 %turn.1 = (f32[16,144,128]{2,1,0:T(8,128)S(1)}, f32[3,16,128]{2,1,0:T(8,128)S(1)}, f32[3,16,128]{2,1,0:T(8,128)S(1)}) custom-call(f32[64,32,128]{2,1,0:T(8,128)S(1)} %copy-done), custom_call_target="tpu_custom_call" | custom-call | tf_op jit(solution)/shard_map/turn/pallas_call | solution.py:466
  2.5 2.4 %collective-permute-start = (f32[3,16,128]{2,1,0:T(8,128)S(1)}, f32[3,16,128]{2,1,0:T(8,128)S(1)}, u32[]{:S(2)}, u32[]{:S(2)}) collective-permute-start(f32[3,16,128]{2,1,0:T(8,128)S(1)} %get-tuple-element.25), channel_id=1, source_target_pairs={{0,1},{1,2},{2,3},{4,5},{5,6},{6,7},{8,9},{9,10},{10,11},{12,13},{... | collective-permute-start | bytes 73736 | tf_op jit(solution)/shard_map/ppermute | solution.py:448
  4.9 1.3 %collective-permute-start.1 = (f32[3,16,128]{2,1,0:T(8,128)S(1)}, f32[3,16,128]{2,1,0:T(8,128)S(1)}, u32[]{:S(2)}, u32[]{:S(2)}) collective-permute-start(f32[3,16,128]{2,1,0:T(8,128)S(1)} %get-tuple-element.26.after_ref), channel_id=1, source_target_pairs={{1,0},{2,1},{3,2},{5,4},{6,5},{7,6},{9,8},{10,9},{11,10},{13,12},{... | collective-permute-start | bytes 73736 | tf_op jit(solution)/shard_map/ppermute | solution.py:448
  6.2 0.0 collective-permute-done.before_ref
  6.2 3.9 %collective-permute-done.1.after_ref = f32[3,16,128]{2,1,0:T(8,128)S(1)} collective-permute-done((f32[3,16,128]{2,1,0:T(8,128)S(1)}, f32[3,16,128]{2,1,0:T(8,128)S(1)}, u32[]{:S(2)}, u32[]{:S(2)}) %collective-permute-start.1) | collective-permute-done | bytes 24608 | tf_op jit(solution)/shard_map/ppermute | solution.py:448
  10.1 0.2 sides.1
  10.3 3.4 %collective-permute-start.2 = (f32[3,72,128]{2,1,0:T(8,128)S(1)}, f32[3,72,128]{2,1,0:T(8,128)S(1)}, u32[]{:S(2)}, u32[]{:S(2)}) collective-permute-start(f32[3,72,128]{2,1,0:T(8,128)S(1)} %get-tuple-element.28), channel_id=1, source_target_pairs={{0,4},{4,8},{8,12},{12,16},{16,20},{20,24},{24,28},{1,5},{5,9},{9,... | collective-permute-start | bytes 331784 | tf_op jit(solution)/shard_map/ppermute | solution.py:448
  13.7 1.3 %collective-permute-start.3 = (f32[3,72,128]{2,1,0:T(8,128)S(1)}, f32[3,72,128]{2,1,0:T(8,128)S(1)}, u32[]{:S(2)}, u32[]{:S(2)}) collective-permute-start(f32[3,72,128]{2,1,0:T(8,128)S(1)} %get-tuple-element.29), channel_id=1, source_target_pairs={{4,0},{8,4},{12,8},{16,12},{20,16},{24,20},{28,24},{5,1},{9,5},{13... | collective-permute-start | bytes 331784 | tf_op jit(solution)/shard_map/ppermute | solution.py:448
  15.0 0.0 copy-done.2
  15.0 0.1 copy.7.in_ref
  15.1 0.0 copy-done.1
  15.1 0.5 weights.1
  15.5 8.7 %middle.1 = (f32[2,4,12,16,128]{4,3,2,1,0:T(8,128)S(1)}, f32[2,2,10,16,128]{4,3,2,1,0:T(8,128)S(1)}, f32[2,2,10,16,128]{4,3,2,1,0:T(8,128)S(1)}, f32[8,128,128]{...) custom-call(f32[16,144,128]{2,1,0:T(8,128)S(1)} %get-tuple-element.27.wide_, ...), custom_call_target="tpu_custom_call" | custom-call | tf_op jit(solution)/shard_map/middle/pallas_call | solution.py:480
  24.2 0.0 collective-permute-done.2.before_ref
  24.2 0.0 collective-permute-done.3.after_ref
  24.2 6.2 %ends.1 = (f32[8,2,8,8,128]{4,3,2,1,0:T(8,128)}, f32[6,128,128]{2,1,0:T(8,128)S(1)}, f32[6,128,128]{2,1,0:T(8,128)S(1)}) custom-call(f32[16,144,128]{2,1,0:T(8,128)S(1)} %get-tuple-element.27.wide_ref, f32[3,72,128]{2,1,0:T(8,128)S(1)} %collective-permute-done.2.before_ref, f32[3,72,128]{2,1,0:T(8,128)S(1)} %collective-permute-done.3.after_ref, ...), custom_call_target="tpu_custom_call" | custom-call | tf_op jit(solution)/shard_map/ends/pallas_call | solution.py:493
  30.4 7.0 %all-to-all-start = ((f32[8,2,8,8,128]{4,3,2,1,0:T(8,128)}), f32[8,2,8,8,128]{4,3,2,1,0:T(8,128)S(1)}, u32[]{:S(2)}, u32[]{:S(2)}) async-start(f32[8,2,8,8,128]{4,3,2,1,0:T(8,128)} %get-tuple-element.37), calls=%async_computation | async-start | bytes 1048576 | tf_op jit(solution)/shard_map/all_to_all | solution.py:510
  37.4 0.7 %columns.1 = (f32[2,2,16,128]{3,2,1,0:T(8,128)S(1)}, f32[2,2,16,128]{3,2,1,0:T(8,128)S(1)}, f32[2,2,16,128]{3,2,1,0:T(8,128)S(1)}, f32[2,2,16,128]{3,2,1,0:T(8,128)S(1)}) custom-call(f32[10,128,128]{2,1,0:T(8,128)S(1)} %get-tuple-element.38.cy_ref, f32[10,128,128]{2,1,0:T(8,128)S(1)} %get-tuple-element.39.ty_ref, ...), custom_call_target="tpu_custom_call" | custom-call | tf_op jit(solution)/shard_map/columns/pallas_call | solution.py:516
  38.1 1.8 %collective-permute-start.4 = (f32[2,2,16,128]{3,2,1,0:T(8,128)S(1)}, f32[2,2,16,128]{3,2,1,0:T(8,128)S(1)}, u32[]{:S(2)}, u32[]{:S(2)}) collective-permute-start(f32[2,2,16,128]{3,2,1,0:T(8,128)S(1)} %get-tuple-element.43), channel_id=1, source_target_pairs={{0,1},{1,2},{2,3},{3,0},{4,5},{5,6},{6,7},{7,4},{8,9},{9,10},{10,1... | collective-permute-start | bytes 98312 | tf_op jit(solution)/shard_map/ppermute | solution.py:522
  39.9 0.8 %collective-permute-start.5 = (f32[2,2,16,128]{3,2,1,0:T(8,128)S(1)}, f32[2,2,16,128]{3,2,1,0:T(8,128)S(1)}, u32[]{:S(2)}, u32[]{:S(2)}) collective-permute-start(f32[2,2,16,128]{3,2,1,0:T(8,128)S(1)} %get-tuple-element.44), channel_id=1, source_target_pairs={{0,2},{1,3},{2,0},{3,1},{4,6},{5,7},{6,4},{7,5},{8,10},{9,11},{10,... | collective-permute-start | bytes 98312 | tf_op jit(solution)/shard_map/ppermute | solution.py:522
  40.7 1.4 %collective-permute-start.6 = (f32[2,2,16,128]{3,2,1,0:T(8,128)S(1)}, f32[2,2,16,128]{3,2,1,0:T(8,128)S(1)}, u32[]{:S(2)}, u32[]{:S(2)}) collective-permute-start(f32[2,2,16,128]{3,2,1,0:T(8,128)S(1)} %get-tuple-element.45), channel_id=1, source_target_pairs={{0,3},{1,0},{2,1},{3,2},{4,7},{5,4},{6,5},{7,6},{8,11},{9,8},{10,9... | collective-permute-start | bytes 98312 | tf_op jit(solution)/shard_map/ppermute | solution.py:522
  42.1 0.0 collective-permute-done.4.refs_1_
  42.1 1.9 %collective-permute-done.5.refs_2_ = f32[2,2,16,128]{3,2,1,0:T(8,128)S(1)} collective-permute-done((f32[2,2,16,128]{3,2,1,0:T(8,128)S(1)}, f32[2,2,16,128]{3,2,1,0:T(8,128)S(1)}, u32[]{:S(2)}, u32[]{:S(2)}) %collective-permute-start.5) | collective-permute-done | bytes 32800 | tf_op jit(solution)/shard_map/ppermute | solution.py:522
  44.0 0.0 collective-permute-done.6.refs_3_
  44.0 0.1 copy.8
  44.2 0.8 %copy.9 = f32[2,8,16,32]{3,2,1,0:T(8,128)} copy(f32[2,8,16,32]{2,1,3,0:T(8,128)S(1)} %bitcast.5) | data formatting | bytes 65536
  45.0 7.6 %all-to-all-done.pieces_ref = f32[8,2,8,8,128]{4,3,2,1,0:T(8,128)S(1)} async-done(((f32[8,2,8,8,128]{4,3,2,1,0:T(8,128)}), f32[8,2,8,8,128]{4,3,2,1,0:T(8,128)S(1)}, u32[]{:S(2)}, u32[]{:S(2)}) %all-to-all-start) | async-done | bytes 524320 | tf_op jit(solution)/shard_map/all_to_all | solution.py:510
  52.6 0.9 %fold_x.1 = f32[2,8,8,128]{3,2,1,0:T(8,128)} custom-call(f32[8,2,8,8,128]{4,3,2,1,0:T(8,128)S(1)} %all-to-all-done.pieces_ref), custom_call_target="tpu_custom_call" | custom-call | tf_op jit(solution)/shard_map/fold_x/pallas_call | solution.py:511
  (1 shorter events, 0.0 us)
Async XLA Ops:
  0.6 1.2 %copy-start = (f32[64,32,128]{2,1,0:T(8,128)S(1)}, f32[64,32,128]{2,1,0:T(8,128)}, u32[]{:S(2)}) copy-start(f32[64,32,128]{2,1,0:T(8,128)} %field_ref.1) | copy-start | bytes 3145732
  1.9 13.1 %copy-start.2 = (bf16[16,8]{0,1:T(8,128)(2,1)S(1)}, bf16[16,8]{0,1:T(8,128)(2,1)}, u32[]{:S(2)}) copy-start(bf16[16,8]{0,1:T(8,128)(2,1)} %param.4) | copy-start | bytes 772
  1.9 13.2 %copy-start.1 = (bf16[16,16]{1,0:T(8,128)(2,1)S(1)}, bf16[16,16]{1,0:T(8,128)(2,1)}, u32[]{:S(2)}) copy-start(bf16[16,16]{1,0:T(8,128)(2,1)} %out_ref.1) | copy-start | bytes 1540
  2.5 3.7 %collective-permute-start = (f32[3,16,128]{2,1,0:T(8,128)S(1)}, f32[3,16,128]{2,1,0:T(8,128)S(1)}, u32[]{:S(2)}, u32[]{:S(2)}) collective-permute-start(f32[3,16,128]{2,1,0:T(8,128)S(1)} %get-tuple-element.25), channel_id=1, source_target_pairs={{0,1},{1,2},{2,3},{4,5},{5,6},{6,7},{8,9},{9,10},{10,11},{12,13},{... | collective-permute-start | bytes 73736 | tf_op jit(solution)/shard_map/ppermute | solution.py:448
  4.9 5.2 %collective-permute-start.1 = (f32[3,16,128]{2,1,0:T(8,128)S(1)}, f32[3,16,128]{2,1,0:T(8,128)S(1)}, u32[]{:S(2)}, u32[]{:S(2)}) collective-permute-start(f32[3,16,128]{2,1,0:T(8,128)S(1)} %get-tuple-element.26.after_ref), channel_id=1, source_target_pairs={{1,0},{2,1},{3,2},{5,4},{6,5},{7,6},{9,8},{10,9},{11,10},{13,12},{... | collective-permute-start | bytes 73736 | tf_op jit(solution)/shard_map/ppermute | solution.py:448
  10.3 13.9 %collective-permute-start.2 = (f32[3,72,128]{2,1,0:T(8,128)S(1)}, f32[3,72,128]{2,1,0:T(8,128)S(1)}, u32[]{:S(2)}, u32[]{:S(2)}) collective-permute-start(f32[3,72,128]{2,1,0:T(8,128)S(1)} %get-tuple-element.28), channel_id=1, source_target_pairs={{0,4},{4,8},{8,12},{12,16},{16,20},{20,24},{24,28},{1,5},{5,9},{9,... | collective-permute-start | bytes 331784 | tf_op jit(solution)/shard_map/ppermute | solution.py:448
  13.7 10.5 %collective-permute-start.3 = (f32[3,72,128]{2,1,0:T(8,128)S(1)}, f32[3,72,128]{2,1,0:T(8,128)S(1)}, u32[]{:S(2)}, u32[]{:S(2)}) collective-permute-start(f32[3,72,128]{2,1,0:T(8,128)S(1)} %get-tuple-element.29), channel_id=1, source_target_pairs={{4,0},{8,4},{12,8},{16,12},{20,16},{24,20},{28,24},{5,1},{9,5},{13... | collective-permute-start | bytes 331784 | tf_op jit(solution)/shard_map/ppermute | solution.py:448
  30.4 22.1 %all-to-all-start = ((f32[8,2,8,8,128]{4,3,2,1,0:T(8,128)}), f32[8,2,8,8,128]{4,3,2,1,0:T(8,128)S(1)}, u32[]{:S(2)}, u32[]{:S(2)}) async-start(f32[8,2,8,8,128]{4,3,2,1,0:T(8,128)} %get-tuple-element.37), calls=%async_computation | async-start | bytes 1048576 | tf_op jit(solution)/shard_map/all_to_all | solution.py:510
  38.1 4.0 %collective-permute-start.4 = (f32[2,2,16,128]{3,2,1,0:T(8,128)S(1)}, f32[2,2,16,128]{3,2,1,0:T(8,128)S(1)}, u32[]{:S(2)}, u32[]{:S(2)}) collective-permute-start(f32[2,2,16,128]{3,2,1,0:T(8,128)S(1)} %get-tuple-element.43), channel_id=1, source_target_pairs={{0,1},{1,2},{2,3},{3,0},{4,5},{5,6},{6,7},{7,4},{8,9},{9,10},{10,1... | collective-permute-start | bytes 98312 | tf_op jit(solution)/shard_map/ppermute | solution.py:522
  39.9 4.1 %collective-permute-start.5 = (f32[2,2,16,128]{3,2,1,0:T(8,128)S(1)}, f32[2,2,16,128]{3,2,1,0:T(8,128)S(1)}, u32[]{:S(2)}, u32[]{:S(2)}) collective-permute-start(f32[2,2,16,128]{3,2,1,0:T(8,128)S(1)} %get-tuple-element.44), channel_id=1, source_target_pairs={{0,2},{1,3},{2,0},{3,1},{4,6},{5,7},{6,4},{7,5},{8,10},{9,11},{10,... | collective-permute-start | bytes 98312 | tf_op jit(solution)/shard_map/ppermute | solution.py:522
  40.7 3.3 %collective-permute-start.6 = (f32[2,2,16,128]{3,2,1,0:T(8,128)S(1)}, f32[2,2,16,128]{3,2,1,0:T(8,128)S(1)}, u32[]{:S(2)}, u32[]{:S(2)}) collective-permute-start(f32[2,2,16,128]{3,2,1,0:T(8,128)S(1)} %get-tuple-element.45), channel_id=1, source_target_pairs={{0,3},{1,0},{2,1},{3,2},{4,7},{5,4},{6,5},{7,6},{8,11},{9,8},{10,9... | collective-permute-start | bytes 98312 | tf_op jit(solution)/shard_map/ppermute | solution.py:522

commit v5 on v4

--- a/solution.py
+++ b/solution.py
@@ -49,10 +49,22 @@
     return jnp.where(mask, jnp.dot(inner, right, preferred_element_type=F32), 0.0)
 
 
-def turn_kernel(field_ref, turned_ref, first_ref, last_ref):
+def turn_kernel(field_hbm, turned_ref, first_ref, last_ref, field_ref, arrived):
     layers, length, width = field_ref.shape
     half = length // 2
+    copies = []
+    for i in range(length // SUB):
+        part = (slice(None), pl.ds(i * SUB, SUB))
+        copies.append(
+            pltpu.make_async_copy(field_hbm.at[part], field_ref.at[part], arrived.at[i])
+        )
+    order = [i for k in range(half // SUB) for i in (k, k + half // SUB)]
+    for i in order:
+        copies[i].start()
     for k in range(half):
+        if k % SUB == 0:
+            copies[k // SUB].wait()
+            copies[(k + half) // SUB].wait()
         turned = jnp.concatenate([field_ref[:, k, :], field_ref[:, k + half, :]], axis=0).T
         turned_ref[k, REACH : REACH + width] = turned
         for j in range(REACH):
@@ -60,8 +72,7 @@
             last_ref[j, k : k + 1] = turned[width - REACH + j : width - REACH + j + 1]
 
 
-def weights_kernel(in_ref, out_ref, after_ref, win_ref, wout_ref):
-    del after_ref
+def spread_weights(in_ref, out_ref, win_ref, wout_ref):
     units, feats = in_ref.shape
     channels = out_ref.shape[0]
     bands = channels // 2
@@ -78,17 +89,20 @@
     wout_ref[...] = spread(out_ref[...], left, right, mask).astype(BF16)
 
 
-def sides_kernel(rows_in, turned_ref, before_ref, after_ref, wide_ref, first_ref, last_ref):
+def sides_kernel(width, count_y, turned_ref, before_ref, after_ref, wide_ref, first_ref, last_ref):
     half, rows, _ = turned_ref.shape
-    width = rows_in
     layers = LANES // 2
     part = rows // 2
     front = iota((part, LANES), 1) < layers
+    at_y = lax.axis_index("by")
+    keep_low = jnp.where(at_y == 0, 0.0, 1.0)
+    keep_high = jnp.where(at_y == count_y - 1, 0.0, 1.0)
     for k in range(half):
         wide_ref[k, REACH : REACH + width] = turned_ref[k, REACH : REACH + width]
         for j in range(REACH):
-            wide_ref[k, j : j + 1] = before_ref[j, k : k + 1]
-            wide_ref[k, REACH + width + j : REACH + width + j + 1] = after_ref[j, k : k + 1]
+            at = REACH + width + j
+            wide_ref[k, j : j + 1] = before_ref[j, k : k + 1] * keep_low
+            wide_ref[k, at : at + 1] = after_ref[j, k : k + 1] * keep_high
         wide_ref[k, 2 * REACH + width :] = jnp.zeros((rows - 2 * REACH - width, LANES), F32)
     for j in range(REACH):
         top, low = wide_ref[j, :part], wide_ref[j, part:]
@@ -200,6 +214,8 @@
     counts,
     steps,
     wide_ref,
+    in_ref,
+    out_ref,
     win_ref,
     wout_ref,
     once_out_ref,
@@ -218,7 +234,7 @@
     stencil = Stencil(run, counts)
     many_x, many_y = spans
     inner = half - 2 * REACH
-
+    spread_weights(in_ref, out_ref, win_ref, wout_ref)
     for k in range(inner + 4):
         stencil.once(wide_ref, k + 1, once_ref, k)
     for k in range(inner + 2):
@@ -281,25 +297,25 @@
     ridge_in_ref,
     cx_ref,
     tx_ref,
-    image_x_ref,
     cy_ref,
     ty_ref,
-    raw_ref,
-    once_ref,
-    twice_ref,
-    ridge_ref,
+    *refs,
 ):
+    outs, (image_ref, raw_ref, once_ref, twice_ref, ridge_ref) = refs[: counts[0]], refs[counts[0] :]
     half, rows, _ = wide_ref.shape
     run = cx_ref.shape[0]
     layers = LANES // 2
     stencil = Stencil(run, counts)
     part = rows // 2
     front = iota((part, LANES), 1) < layers
+    at_x = lax.axis_index("bx")
+    keep_low = jnp.where(at_x == 0, 0.0, 1.0)
+    keep_high = jnp.where(at_x == counts[0] - 1, 0.0, 1.0)
     for j in range(REACH):
-        halo, own = before_ref[j], wide_ref[half - REACH + j]
+        halo, own = before_ref[j] * keep_low, wide_ref[half - REACH + j]
         raw_ref[0, j, :part] = jnp.where(front, halo, roll(own[:part], layers))
         raw_ref[0, j, part:] = jnp.where(front, roll(halo, layers), roll(own[part:], layers))
-        halo, own = after_ref[j], wide_ref[j]
+        halo, own = after_ref[j] * keep_high, wide_ref[j]
         raw_ref[1, 2 + j, :part] = jnp.where(front, roll(own[:part], layers), roll(halo, layers))
         raw_ref[1, 2 + j, part:] = jnp.where(front, roll(own[part:], layers), halo)
     for j in range(2):
@@ -361,11 +377,16 @@
             for j in range(many_y):
                 near, far = d * many_y + j, (d + layers // SUB) * many_y + j
                 q = images[1][near]
-                image_x_ref[d, 0, y0 + j] = images[0][near] + q * images[0][far]
-                image_x_ref[d, 1, y0 + j] = q * images[1][far]
+                at = pl.ds(d * SUB, SUB)
+                image_ref[0, y0 + j, at] = images[0][near] + q * images[0][far]
+                image_ref[1, y0 + j, at] = q * images[1][far]
 
     for step in range(run // many_y):
         block(step)
+    share = layers // counts[0]
+    for s, out_ref in enumerate(outs):
+        start = pl.multiple_of(lax.rem(at_x + s, counts[0]) * share, share)
+        out_ref[...] = image_ref[:, :, pl.ds(start, share), :]
 
 
 def columns_kernel(share, peers, cy_ref, ty_ref, cy_ends_ref, ty_ends_ref, *refs):
@@ -418,17 +439,22 @@
     out_ref[1] = clear
 
 
-def fold_x_kernel(pieces_ref, out_ref):
-    peers, _, run, share, _ = pieces_ref.shape
+def fold_x_kernel(*refs):
+    pieces, out_ref = refs[:-1], refs[-1]
+    _, run, share, _ = pieces[0].shape
     lane = iota((share, LANES), 1)
+    me = lax.axis_index("bx")
     kinds = [[], []]
     for y in range(run):
-        colour, clear = pieces_ref[0, 0, y], pieces_ref[0, 1, y]
-        for k in range(1, peers):
-            colour = colour + clear * pieces_ref[k, 0, y]
-            clear = clear * pieces_ref[k, 1, y]
-        kinds[0].append(colour)
-        kinds[1].append(clear)
+        behind = colour, clear = jnp.zeros((share, LANES), F32), jnp.ones((share, LANES), F32)
+        for s in reversed(range(len(pieces))):
+            start = me == s
+            behind = jnp.where(start, colour, behind[0]), jnp.where(start, clear, behind[1])
+            colour, clear = jnp.where(start, 0.0, colour), jnp.where(start, 1.0, clear)
+            colour = colour + clear * pieces[s][0, y]
+            clear = clear * pieces[s][1, y]
+        kinds[0].append(colour + clear * behind[0])
+        kinds[1].append(clear * behind[1])
     for kind, values in enumerate(kinds):
         for s in (1, 2, 4):
             for i in range(run):
@@ -443,9 +469,17 @@
 
 def exchange(last, first, axis):
     peers = lax.axis_size(axis)
-    up = [(i, i + 1) for i in range(peers - 1)]
+    up = [(i, (i + 1) % peers) for i in range(peers)]
     down = [(j, i) for i, j in up]
     return lax.ppermute(last, axis, up), lax.ppermute(first, axis, down)
+
+
+def shifted(pieces, axis):
+    peers = lax.axis_size(axis)
+    return [pieces[0]] + [
+        lax.ppermute(pieces[s], axis, [(i, (i + s) % peers) for i in range(peers)])
+        for s in range(1, peers)
+    ]
 
 
 def body(scalar_field, transfer_in, transfer_out):
@@ -463,24 +497,32 @@
     ]
 
     edge = sds(REACH, half, LANES)
-    turned, first, last = call(turn_kernel, "turn", [sds(half, rows, LANES), edge, edge], 1)(
-        scalar_field
-    )
-    win, wout = call(weights_kernel, "weights", weights, 3)(transfer_in, transfer_out, first)
+    turned, first, last = pl.pallas_call(
+        turn_kernel,
+        out_shape=[sds(half, rows, LANES), edge, edge],
+        in_specs=[pl.BlockSpec(memory_space=pltpu.HBM)],
+        out_specs=[VMEM] * 3,
+        scratch_shapes=[
+            pltpu.VMEM(scalar_field.shape, F32),
+            pltpu.SemaphoreType.DMA((local_x // SUB,)),
+        ],
+        compiler_params=PARAMS,
+        name="turn",
+    )(scalar_field)
     before, after = exchange(last, first, "by")
     edge = sds(REACH, rows // 2, LANES)
     wide, first, last = call(
-        functools.partial(sides_kernel, local_y), "sides", [sds(half, rows, LANES), edge, edge], 3
+        functools.partial(sides_kernel, local_y, count_y), "sides", [sds(half, rows, LANES), edge, edge], 3
     )(turned, before, after)
     before, after = exchange(last, first, "bx")
     inner = half - 2 * REACH
     counts = (count_x, count_y)
     plane = lambda *lead: sds(*lead, CHUNKS, LANES)
     many_x, many_y = inner, 2
-    once, twice, ridge, colour_x, clear_x, colour_y, clear_y = call(
+    win, wout, once, twice, ridge, colour_x, clear_x, colour_y, clear_y = call(
         functools.partial(middle_kernel, (many_x, many_y), counts, steps),
         "middle",
-        [plane(2, 4, run + 4), plane(2, 2, run + 2), plane(2, 2, run + 2)]
+        weights + [plane(2, 4, run + 4), plane(2, 2, run + 2), plane(2, 2, run + 2)]
         + [sds(run, LANES, LANES)] * 2
         + [sds(inner, LANES, LANES)] * 2,
         3,
@@ -489,26 +531,24 @@
             pltpu.VMEM((inner + 2, run + 2, CHUNKS, LANES), F32),
             pltpu.VMEM((inner + 2, run + 2, CHUNKS, LANES), F32),
         ],
-    )(wide, win, wout)
-    image_x, colour_ends, clear_ends = call(
+    )(wide, transfer_in, transfer_out)
+    share = layers // count_x
+    piece = sds(2, run, share, LANES)
+    colour_ends, clear_ends, *pieces = call(
         functools.partial(ends_kernel, many_y, counts, steps),
         "ends",
-        [sds(layers // SUB, 2, run, SUB, LANES)] + [sds(2 * REACH, LANES, LANES)] * 2,
+        [sds(2 * REACH, LANES, LANES)] * 2 + [piece] * count_x,
         10,
         [
+            pltpu.VMEM((2, run, layers, LANES), F32),
             pltpu.VMEM((2, 5, rows, LANES), F32),
             pltpu.VMEM((2, 7, run + 4, CHUNKS, LANES), F32),
             pltpu.VMEM((2, 5, run + 2, CHUNKS, LANES), F32),
             pltpu.VMEM((2, 5, run + 2, CHUNKS, LANES), F32),
         ],
     )(wide, before, after, win, wout, once, twice, ridge, colour_x, clear_x)
-
-    share_x = layers // count_x
-    if share_x != SUB:
-        image_x = jnp.transpose(image_x, (1, 2, 0, 3, 4)).reshape(2, run, count_x, share_x, LANES)
-        image_x = jnp.transpose(image_x, (2, 0, 1, 3, 4))
-    pieces = lax.all_to_all(image_x, "bx", split_axis=0, concat_axis=0, tiled=True)
-    view_x = call(fold_x_kernel, "fold_x", sds(2, bands, share_x, local_y), 1)(pieces)
+    pieces = shifted(pieces, "bx")
+    view_x = call(fold_x_kernel, "fold_x", sds(2, bands, share, local_y), count_x)(*pieces)
 
     share = layers // count_y
     piece = sds(2, 2, share, LANES)
@@ -516,10 +556,7 @@
     pieces = call(
         functools.partial(columns_kernel, share, count_y), "columns", [piece] * count_y, 4, scratch
     )(colour_y, clear_y, colour_ends, clear_ends)
-    pieces = list(pieces)
-    for s in range(1, count_y):
-        pairs = [(i, (i + s) % count_y) for i in range(count_y)]
-        pieces[s] = lax.ppermute(pieces[s], "by", pairs)
+    pieces = shifted(pieces, "by")
     view_y = call(fold_y_kernel, "fold_y", piece, count_y)(*pieces)
     view_y = view_y.reshape(2, 2, share, half, bands)
     view_y = jnp.transpose(view_y, (0, 4, 2, 1, 3)).reshape(2, bands, share, local_x)

time: 53.9 us -> 46 us (0.85)
  waiting for transfers between devices: 13.5 us -> 4.14 us
  starting transfers between devices: 19.3 us -> 21.6 us
  Pallas kernels: 17.7 us -> 17.1 us
    ppermute x3 -> x10, starting transfers between devices: 3.97 us -> 13.7 us  [shifted(): lax.ppermute(pieces[s], axis, [(i, (i + s) % peers) for i in range(peers)])]
    all_to_all x1 -> x0, waiting for transfers between devices: 7.61 us -> none  [body(): lax.all_to_all(image_x, 'bx', split_axis=0, concat_axis=0, tiled=True)]
    all_to_all x1 -> x0, starting transfers between devices: 6.95 us -> none  [body(): lax.all_to_all(image_x, 'bx', split_axis=0, concat_axis=0, tiled=True)]
    ppermute x4, waiting for transfers between devices: 3.92 us -> 1.53 us  [exchange(): return (lax.ppermute(last, axis, up), lax.ppermute(first, axis, down))]
    ppermute x3 -> x10, waiting for transfers between devices: 1.95 us -> 2.61 us  [shifted(): lax.ppermute(pieces[s], axis, [(i, (i + s) % peers) for i in range(peers)])]
    pallas_call x1, Pallas kernels: 6.24 us -> 5.61 us  [body(): call(functools.partial(ends_kernel, many_y, counts, steps), 'ends', [sds(...]
    pallas_call x4 -> x3, Pallas kernels: 2.14 us -> 1.97 us  [the longest x1 0.92 us: body(): call(fold_x_kernel, 'fold_x', sds(2, bands, share, local_y), count_x)]
  transfers between devices with their start and end apart: 8 -> 14, of which waited for: 3 -> 5; matrix products, arithmetic and copies ran while one was open for 2% -> 2% of each run, Pallas kernels for 18% -> 21%
where the time goes in v5:
time: 46 us; the launch traced here: 45.8 us
  starting transfers between devices  21.6 us (47%)
  Pallas kernels  17.1 us (37%)
  waiting for transfers between devices  4.14 us (9%)
  local copies, waits for them, and re-layouts  2.23 us (5%)
  between operations  0.72 us (2%)
    ppermute x10, starting transfers between devices, shifted(): lax.ppermute(pieces[s], axis, [(i, (i + s) % peers) for i in range(peers)])  13.7 us
    pallas_call x1, Pallas kernels, body(): call(functools.partial(middle_kernel, (many_x, many_y), counts, steps), '...  8.81 us
    ppermute x4, starting transfers between devices, exchange(): return (lax.ppermute(last, axis, up), lax.ppermute(first, axis, down))  7.88 us
    pallas_call x1, Pallas kernels, body(): call(functools.partial(ends_kernel, many_y, counts, steps), 'ends', [sds(...  5.61 us
    ppermute x10, waiting for transfers between devices, shifted(): lax.ppermute(pieces[s], axis, [(i, (i + s) % peers) for i in range(peers)])  2.61 us
    unnamed x8, local copies, waits for them, and re-layouts  2.11 us
    ppermute x4, waiting for transfers between devices, exchange(): return (lax.ppermute(last, axis, up), lax.ppermute(first, axis, down))  1.53 us
  transfers between devices with their start and end apart: 14, of which 5 were waited for; matrix products, arithmetic and copies ran while one was open for 2% of the time, Pallas kernels for 21%

profile of v5, /device:TPU:0, one launch (start us, length us, event | category | flops | bytes accessed | tf_op | source)
XLA Modules:
  0.0 45.8 jit_solution(16594261391623698969)
XLA Ops:
  0.6 0.0 copy-start
  0.6 1.2 %copy-done = f32[64,32,128]{2,1,0:T(8,128)S(1)} copy-done((f32[64,32,128]{2,1,0:T(8,128)S(1)}, f32[64,32,128]{2,1,0:T(8,128)}, u32[]{:S(2)}) %copy-start) | copy-done | bytes 1048600
  1.9 0.0 copy-start.2
  1.9 0.0 copy-start.1
  1.9 0.9 %turn.1 = (f32[16,144,128]{2,1,0:T(8,128)S(1)}, f32[3,16,128]{2,1,0:T(8,128)S(1)}, f32[3,16,128]{2,1,0:T(8,128)S(1)}) custom-call(f32[64,32,128]{2,1,0:T(8,128)S(1)} %copy-done), custom_call_target="tpu_custom_call" | custom-call | tf_op jit(solution)/shard_map/turn/pallas_call | solution.py:500
  2.8 0.5 %collective-permute-start = (f32[3,16,128]{2,1,0:T(8,128)S(1)}, f32[3,16,128]{2,1,0:T(8,128)S(1)}, u32[]{:S(2)}, u32[]{:S(2)}) collective-permute-start(f32[3,16,128]{2,1,0:T(8,128)S(1)} %get-tuple-element.32), channel_id=1, source_target_pairs={{0,1},{1,2},{2,3},{3,0},{4,5},{5,6},{6,7},{7,4},{8,9},{9,10},{10,1... | collective-permute-start | bytes 73736 | tf_op jit(solution)/shard_map/ppermute | solution.py:474
  3.3 2.0 %collective-permute-start.1 = (f32[3,16,128]{2,1,0:T(8,128)S(1)}, f32[3,16,128]{2,1,0:T(8,128)S(1)}, u32[]{:S(2)}, u32[]{:S(2)}) collective-permute-start(f32[3,16,128]{2,1,0:T(8,128)S(1)} %get-tuple-element.33), channel_id=1, source_target_pairs={{1,0},{2,1},{3,2},{0,3},{5,4},{6,5},{7,6},{4,7},{9,8},{10,9},{11,1... | collective-permute-start | bytes 73736 | tf_op jit(solution)/shard_map/ppermute | solution.py:474
  5.3 1.4 %collective-permute-done.before_ref = f32[3,16,128]{2,1,0:T(8,128)S(1)} collective-permute-done((f32[3,16,128]{2,1,0:T(8,128)S(1)}, f32[3,16,128]{2,1,0:T(8,128)S(1)}, u32[]{:S(2)}, u32[]{:S(2)}) %collective-permute-start) | collective-permute-done | bytes 24608 | tf_op jit(solution)/shard_map/ppermute | solution.py:474
  6.7 0.1 collective-permute-done.1.after_ref
  6.8 0.2 sides.1
  7.0 2.3 %collective-permute-start.2 = (f32[3,72,128]{2,1,0:T(8,128)S(1)}, f32[3,72,128]{2,1,0:T(8,128)S(1)}, u32[]{:S(2)}, u32[]{:S(2)}) collective-permute-start(f32[3,72,128]{2,1,0:T(8,128)S(1)} %get-tuple-element.35), channel_id=1, source_target_pairs={{0,4},{4,8},{8,12},{12,16},{16,20},{20,24},{24,28},{28,0},{1,5},{5... | collective-permute-start | bytes 331784 | tf_op jit(solution)/shard_map/ppermute | solution.py:474
  9.2 3.1 %collective-permute-start.3 = (f32[3,72,128]{2,1,0:T(8,128)S(1)}, f32[3,72,128]{2,1,0:T(8,128)S(1)}, u32[]{:S(2)}, u32[]{:S(2)}) collective-permute-start(f32[3,72,128]{2,1,0:T(8,128)S(1)} %get-tuple-element.36), channel_id=1, source_target_pairs={{4,0},{8,4},{12,8},{16,12},{20,16},{24,20},{28,24},{0,28},{5,1},{9... | collective-permute-start | bytes 331784 | tf_op jit(solution)/shard_map/ppermute | solution.py:474
  12.3 0.0 copy-done.2
  12.3 0.1 copy.7.in_ref
  12.4 0.0 copy-done.1
  12.4 8.8 %middle.1 = (bf16[128,256]{1,0:T(8,128)(2,1)S(1)}, bf16[256,256]{1,0:T(8,128)(2,1)S(1)}, f32[2,4,12,16,128]{4,3,2,1,0:T(8,128)S(1)}, f32[2,2,10,16,128]{4,3,2,1,...) custom-call(f32[16,144,128]{2,1,0:T(8,128)S(1)} %get-tuple-element.3, ...), custom_call_target="tpu_custom_call" | custom-call | tf_op jit(solution)/shard_map/middle/pallas_call | solution.py:522
  21.2 0.0 collective-permute-done.2.before_ref
  21.3 0.0 collective-permute-done.3.after_ref
  21.3 5.6 %ends.1 = (f32[6,128,128]{2,1,0:T(8,128)S(1)}, f32[6,128,128]{2,1,0:T(8,128)S(1)}, f32[2,8,8,128]{3,2,1,0:T(8,128)S(1)}, f32[2,8,8,128]{3,2,1,0:T(8,128)S(1)}, f...) custom-call(f32[16,144,128]{2,1,0:T(8,128)S(1)} %get-tuple-element.3, ...), custom_call_target="tpu_custom_call" | custom-call | tf_op jit(solution)/shard_map/ends/pallas_call | solution.py:537
  26.9 0.1 collective-permute-start.4
  27.0 0.5 %collective-permute-start.5 = (f32[2,8,8,128]{3,2,1,0:T(8,128)S(1)}, f32[2,8,8,128]{3,2,1,0:T(8,128)S(1)}, u32[]{:S(2)}, u32[]{:S(2)}) collective-permute-start(f32[2,8,8,128]{3,2,1,0:T(8,128)S(1)} %get-tuple-element.46), channel_id=1, source_target_pairs={{0,8},{4,12},{8,16},{12,20},{16,24},{20,28},{24,0},{28,4},{1,9},{5... | collective-permute-start | bytes 196616 | tf_op jit(solution)/shard_map/ppermute | solution.py:480
  27.4 0.7 %columns.1 = (f32[2,2,16,128]{3,2,1,0:T(8,128)S(1)}, f32[2,2,16,128]{3,2,1,0:T(8,128)S(1)}, f32[2,2,16,128]{3,2,1,0:T(8,128)S(1)}, f32[2,2,16,128]{3,2,1,0:T(8,128)S(1)}) custom-call(f32[10,128,128]{2,1,0:T(8,128)S(1)} %get-tuple-element.52.cy_ref, f32[10,128,128]{2,1,0:T(8,128)S(1)} %get-tuple-element.53.ty_ref, ...), custom_call_target="tpu_custom_call" | custom-call | tf_op jit(solution)/shard_map/columns/pallas_call | solution.py:556
  28.1 1.0 %collective-permute-start.11 = (f32[2,2,16,128]{3,2,1,0:T(8,128)S(1)}, f32[2,2,16,128]{3,2,1,0:T(8,128)S(1)}, u32[]{:S(2)}, u32[]{:S(2)}) collective-permute-start(f32[2,2,16,128]{3,2,1,0:T(8,128)S(1)} %get-tuple-element.57), channel_id=1, source_target_pairs={{0,1},{1,2},{2,3},{3,0},{4,5},{5,6},{6,7},{7,4},{8,9},{9,10},{10,1... | collective-permute-start | bytes 98312 | tf_op jit(solution)/shard_map/ppermute | solution.py:480
  29.1 0.7 %collective-permute-start.12 = (f32[2,2,16,128]{3,2,1,0:T(8,128)S(1)}, f32[2,2,16,128]{3,2,1,0:T(8,128)S(1)}, u32[]{:S(2)}, u32[]{:S(2)}) collective-permute-start(f32[2,2,16,128]{3,2,1,0:T(8,128)S(1)} %get-tuple-element.58), channel_id=1, source_target_pairs={{0,2},{1,3},{2,0},{3,1},{4,6},{5,7},{6,4},{7,5},{8,10},{9,11},{10,... | collective-permute-start | bytes 98312 | tf_op jit(solution)/shard_map/ppermute | solution.py:480
  29.8 1.4 %collective-permute-start.13 = (f32[2,2,16,128]{3,2,1,0:T(8,128)S(1)}, f32[2,2,16,128]{3,2,1,0:T(8,128)S(1)}, u32[]{:S(2)}, u32[]{:S(2)}) collective-permute-start(f32[2,2,16,128]{3,2,1,0:T(8,128)S(1)} %get-tuple-element.59), channel_id=1, source_target_pairs={{0,3},{1,0},{2,1},{3,2},{4,7},{5,4},{6,5},{7,6},{8,11},{9,8},{10,9... | collective-permute-start | bytes 98312 | tf_op jit(solution)/shard_map/ppermute | solution.py:480
  31.2 0.4 collective-permute-done.11.refs_1_
  31.5 3.5 %collective-permute-start.6 = (f32[2,8,8,128]{3,2,1,0:T(8,128)S(1)}, f32[2,8,8,128]{3,2,1,0:T(8,128)S(1)}, u32[]{:S(2)}, u32[]{:S(2)}) collective-permute-start(f32[2,8,8,128]{3,2,1,0:T(8,128)S(1)} %get-tuple-element.47), channel_id=1, source_target_pairs={{0,12},{4,16},{8,20},{12,24},{16,28},{20,0},{24,4},{28,8},{1,13},{... | collective-permute-start | bytes 196616 | tf_op jit(solution)/shard_map/ppermute | solution.py:480
  35.0 0.0 collective-permute-done.12.refs_2_
  35.0 1.3 %collective-permute-start.7 = (f32[2,8,8,128]{3,2,1,0:T(8,128)S(1)}, f32[2,8,8,128]{3,2,1,0:T(8,128)S(1)}, u32[]{:S(2)}, u32[]{:S(2)}) collective-permute-start(f32[2,8,8,128]{3,2,1,0:T(8,128)S(1)} %get-tuple-element.48), channel_id=1, source_target_pairs={{0,16},{4,20},{8,24},{12,28},{16,0},{20,4},{24,8},{28,12},{1,17},{... | collective-permute-start | bytes 196616 | tf_op jit(solution)/shard_map/ppermute | solution.py:480
  36.3 0.0 collective-permute-done.13.refs_3_
  36.3 1.6 %collective-permute-start.8 = (f32[2,8,8,128]{3,2,1,0:T(8,128)S(1)}, f32[2,8,8,128]{3,2,1,0:T(8,128)S(1)}, u32[]{:S(2)}, u32[]{:S(2)}) collective-permute-start(f32[2,8,8,128]{3,2,1,0:T(8,128)S(1)} %get-tuple-element.49), channel_id=1, source_target_pairs={{0,20},{4,24},{8,28},{12,0},{16,4},{20,8},{24,12},{28,16},{1,21},{... | collective-permute-start | bytes 196616 | tf_op jit(solution)/shard_map/ppermute | solution.py:480
  37.9 0.0 collective-permute-done.4.refs_1_
  37.9 2.6 %collective-permute-start.9 = (f32[2,8,8,128]{3,2,1,0:T(8,128)S(1)}, f32[2,8,8,128]{3,2,1,0:T(8,128)S(1)}, u32[]{:S(2)}, u32[]{:S(2)}) collective-permute-start(f32[2,8,8,128]{3,2,1,0:T(8,128)S(1)} %get-tuple-element.50), channel_id=1, source_target_pairs={{0,24},{4,28},{8,0},{12,4},{16,8},{20,12},{24,16},{28,20},{1,25},{... | collective-permute-start | bytes 196616 | tf_op jit(solution)/shard_map/ppermute | solution.py:480
  40.6 0.0 collective-permute-done.5.refs_2_
  40.6 1.1 %collective-permute-start.10 = (f32[2,8,8,128]{3,2,1,0:T(8,128)S(1)}, f32[2,8,8,128]{3,2,1,0:T(8,128)S(1)}, u32[]{:S(2)}, u32[]{:S(2)}) collective-permute-start(f32[2,8,8,128]{3,2,1,0:T(8,128)S(1)} %get-tuple-element.51), channel_id=1, source_target_pairs={{0,28},{4,0},{8,4},{12,8},{16,12},{20,16},{24,20},{28,24},{1,29},{... | collective-permute-start | bytes 196616 | tf_op jit(solution)/shard_map/ppermute | solution.py:480
  41.7 0.1 copy.8
  41.8 0.8 %copy.9 = f32[2,8,16,32]{3,2,1,0:T(8,128)} copy(f32[2,8,16,32]{2,1,3,0:T(8,128)S(1)} %bitcast.5) | data formatting | bytes 65536
  42.6 0.0 collective-permute-done.6.refs_3_
  42.6 0.0 collective-permute-done.7.refs_4_
  42.6 0.0 collective-permute-done.8.refs_5_
  42.6 0.7 %collective-permute-done.9.refs_6_ = f32[2,8,8,128]{3,2,1,0:T(8,128)S(1)} collective-permute-done((f32[2,8,8,128]{3,2,1,0:T(8,128)S(1)}, f32[2,8,8,128]{3,2,1,0:T(8,128)S(1)}, u32[]{:S(2)}, u32[]{:S(2)}) %collective-permute-start.9) | collective-permute-done | bytes 65568 | tf_op jit(solution)/shard_map/ppermute | solution.py:480
  43.3 1.5 %collective-permute-done.10.refs_7_ = f32[2,8,8,128]{3,2,1,0:T(8,128)S(1)} collective-permute-done((f32[2,8,8,128]{3,2,1,0:T(8,128)S(1)}, f32[2,8,8,128]{3,2,1,0:T(8,128)S(1)}, u32[]{:S(2)}, u32[]{:S(2)}) %collective-permute-start.10) | collective-permute-done | bytes 65568 | tf_op jit(solution)/shard_map/ppermute | solution.py:480
  44.8 0.9 %fold_x.1 = f32[2,8,8,128]{3,2,1,0:T(8,128)} custom-call(f32[2,8,8,128]{3,2,1,0:T(8,128)S(1)} %get-tuple-element.44.refs_0_, f32[2,8,8,128]{3,2,1,0:T(8,128)S(1)} %collective-permute-done.4.refs_1_, f32[2,8,8,128]{3,2,1,0:T(8,128)S(1)} %collective-permute-done.5.refs_2_, f32[2,8,8,128]{3,2,1,0:T(8,128)S(1)} %collective-permute-done.6.refs_3_, ...), custom_call_target="tpu_custom_call" | custom-call | tf_op jit(solution)/shard_map/fold_x/pallas_call | solution.py:551
  (1 shorter events, 0.0 us)
Async XLA Ops:
  0.6 1.2 %copy-start = (f32[64,32,128]{2,1,0:T(8,128)S(1)}, f32[64,32,128]{2,1,0:T(8,128)}, u32[]{:S(2)}) copy-start(f32[64,32,128]{2,1,0:T(8,128)} %field_hbm.1) | copy-start | bytes 3145732
  1.9 10.5 %copy-start.2 = (bf16[16,8]{0,1:T(8,128)(2,1)S(1)}, bf16[16,8]{0,1:T(8,128)(2,1)}, u32[]{:S(2)}) copy-start(bf16[16,8]{0,1:T(8,128)(2,1)} %param.4) | copy-start | bytes 772
  1.9 10.6 %copy-start.1 = (bf16[16,16]{1,0:T(8,128)(2,1)S(1)}, bf16[16,16]{1,0:T(8,128)(2,1)}, u32[]{:S(2)}) copy-start(bf16[16,16]{1,0:T(8,128)(2,1)} %out_ref.1) | copy-start | bytes 1540
  2.8 4.0 %collective-permute-start = (f32[3,16,128]{2,1,0:T(8,128)S(1)}, f32[3,16,128]{2,1,0:T(8,128)S(1)}, u32[]{:S(2)}, u32[]{:S(2)}) collective-permute-start(f32[3,16,128]{2,1,0:T(8,128)S(1)} %get-tuple-element.32), channel_id=1, source_target_pairs={{0,1},{1,2},{2,3},{3,0},{4,5},{5,6},{6,7},{7,4},{8,9},{9,10},{10,1... | collective-permute-start | bytes 73736 | tf_op jit(solution)/shard_map/ppermute | solution.py:474
  3.3 3.5 %collective-permute-start.1 = (f32[3,16,128]{2,1,0:T(8,128)S(1)}, f32[3,16,128]{2,1,0:T(8,128)S(1)}, u32[]{:S(2)}, u32[]{:S(2)}) collective-permute-start(f32[3,16,128]{2,1,0:T(8,128)S(1)} %get-tuple-element.33), channel_id=1, source_target_pairs={{1,0},{2,1},{3,2},{0,3},{5,4},{6,5},{7,6},{4,7},{9,8},{10,9},{11,1... | collective-permute-start | bytes 73736 | tf_op jit(solution)/shard_map/ppermute | solution.py:474
  7.0 14.3 %collective-permute-start.2 = (f32[3,72,128]{2,1,0:T(8,128)S(1)}, f32[3,72,128]{2,1,0:T(8,128)S(1)}, u32[]{:S(2)}, u32[]{:S(2)}) collective-permute-start(f32[3,72,128]{2,1,0:T(8,128)S(1)} %get-tuple-element.35), channel_id=1, source_target_pairs={{0,4},{4,8},{8,12},{12,16},{16,20},{20,24},{24,28},{28,0},{1,5},{5... | collective-permute-start | bytes 331784 | tf_op jit(solution)/shard_map/ppermute | solution.py:474
  9.2 12.0 %collective-permute-start.3 = (f32[3,72,128]{2,1,0:T(8,128)S(1)}, f32[3,72,128]{2,1,0:T(8,128)S(1)}, u32[]{:S(2)}, u32[]{:S(2)}) collective-permute-start(f32[3,72,128]{2,1,0:T(8,128)S(1)} %get-tuple-element.36), channel_id=1, source_target_pairs={{4,0},{8,4},{12,8},{16,12},{20,16},{24,20},{28,24},{0,28},{5,1},{9... | collective-permute-start | bytes 331784 | tf_op jit(solution)/shard_map/ppermute | solution.py:474
  26.9 11.1 %collective-permute-start.4 = (f32[2,8,8,128]{3,2,1,0:T(8,128)S(1)}, f32[2,8,8,128]{3,2,1,0:T(8,128)S(1)}, u32[]{:S(2)}, u32[]{:S(2)}) collective-permute-start(f32[2,8,8,128]{3,2,1,0:T(8,128)S(1)} %get-tuple-element.45), channel_id=1, source_target_pairs={{0,4},{4,8},{8,12},{12,16},{16,20},{20,24},{24,28},{28,0},{1,5},{5... | collective-permute-start | bytes 196616 | tf_op jit(solution)/shard_map/ppermute | solution.py:480
  27.0 13.6 %collective-permute-start.5 = (f32[2,8,8,128]{3,2,1,0:T(8,128)S(1)}, f32[2,8,8,128]{3,2,1,0:T(8,128)S(1)}, u32[]{:S(2)}, u32[]{:S(2)}) collective-permute-start(f32[2,8,8,128]{3,2,1,0:T(8,128)S(1)} %get-tuple-element.46), channel_id=1, source_target_pairs={{0,8},{4,12},{8,16},{12,20},{16,24},{20,28},{24,0},{28,4},{1,9},{5... | collective-permute-start | bytes 196616 | tf_op jit(solution)/shard_map/ppermute | solution.py:480
  28.1 3.4 %collective-permute-start.11 = (f32[2,2,16,128]{3,2,1,0:T(8,128)S(1)}, f32[2,2,16,128]{3,2,1,0:T(8,128)S(1)}, u32[]{:S(2)}, u32[]{:S(2)}) collective-permute-start(f32[2,2,16,128]{3,2,1,0:T(8,128)S(1)} %get-tuple-element.57), channel_id=1, source_target_pairs={{0,1},{1,2},{2,3},{3,0},{4,5},{5,6},{6,7},{7,4},{8,9},{9,10},{10,1... | collective-permute-start | bytes 98312 | tf_op jit(solution)/shard_map/ppermute | solution.py:480
  29.1 5.9 %collective-permute-start.12 = (f32[2,2,16,128]{3,2,1,0:T(8,128)S(1)}, f32[2,2,16,128]{3,2,1,0:T(8,128)S(1)}, u32[]{:S(2)}, u32[]{:S(2)}) collective-permute-start(f32[2,2,16,128]{3,2,1,0:T(8,128)S(1)} %get-tuple-element.58), channel_id=1, source_target_pairs={{0,2},{1,3},{2,0},{3,1},{4,6},{5,7},{6,4},{7,5},{8,10},{9,11},{10,... | collective-permute-start | bytes 98312 | tf_op jit(solution)/shard_map/ppermute | solution.py:480
  29.8 6.5 %collective-permute-start.13 = (f32[2,2,16,128]{3,2,1,0:T(8,128)S(1)}, f32[2,2,16,128]{3,2,1,0:T(8,128)S(1)}, u32[]{:S(2)}, u32[]{:S(2)}) collective-permute-start(f32[2,2,16,128]{3,2,1,0:T(8,128)S(1)} %get-tuple-element.59), channel_id=1, source_target_pairs={{0,3},{1,0},{2,1},{3,2},{4,7},{5,4},{6,5},{7,6},{8,11},{9,8},{10,9... | collective-permute-start | bytes 98312 | tf_op jit(solution)/shard_map/ppermute | solution.py:480
  31.5 11.1 %collective-permute-start.6 = (f32[2,8,8,128]{3,2,1,0:T(8,128)S(1)}, f32[2,8,8,128]{3,2,1,0:T(8,128)S(1)}, u32[]{:S(2)}, u32[]{:S(2)}) collective-permute-start(f32[2,8,8,128]{3,2,1,0:T(8,128)S(1)} %get-tuple-element.47), channel_id=1, source_target_pairs={{0,12},{4,16},{8,20},{12,24},{16,28},{20,0},{24,4},{28,8},{1,13},{... | collective-permute-start | bytes 196616 | tf_op jit(solution)/shard_map/ppermute | solution.py:480
  35.0 7.6 %collective-permute-start.7 = (f32[2,8,8,128]{3,2,1,0:T(8,128)S(1)}, f32[2,8,8,128]{3,2,1,0:T(8,128)S(1)}, u32[]{:S(2)}, u32[]{:S(2)}) collective-permute-start(f32[2,8,8,128]{3,2,1,0:T(8,128)S(1)} %get-tuple-element.48), channel_id=1, source_target_pairs={{0,16},{4,20},{8,24},{12,28},{16,0},{20,4},{24,8},{28,12},{1,17},{... | collective-permute-start | bytes 196616 | tf_op jit(solution)/shard_map/ppermute | solution.py:480
  36.3 6.3 %collective-permute-start.8 = (f32[2,8,8,128]{3,2,1,0:T(8,128)S(1)}, f32[2,8,8,128]{3,2,1,0:T(8,128)S(1)}, u32[]{:S(2)}, u32[]{:S(2)}) collective-permute-start(f32[2,8,8,128]{3,2,1,0:T(8,128)S(1)} %get-tuple-element.49), channel_id=1, source_target_pairs={{0,20},{4,24},{8,28},{12,0},{16,4},{20,8},{24,12},{28,16},{1,21},{... | collective-permute-start | bytes 196616 | tf_op jit(solution)/shard_map/ppermute | solution.py:480
  37.9 5.3 %collective-permute-start.9 = (f32[2,8,8,128]{3,2,1,0:T(8,128)S(1)}, f32[2,8,8,128]{3,2,1,0:T(8,128)S(1)}, u32[]{:S(2)}, u32[]{:S(2)}) collective-permute-start(f32[2,8,8,128]{3,2,1,0:T(8,128)S(1)} %get-tuple-element.50), channel_id=1, source_target_pairs={{0,24},{4,28},{8,0},{12,4},{16,8},{20,12},{24,16},{28,20},{1,25},{... | collective-permute-start | bytes 196616 | tf_op jit(solution)/shard_map/ppermute | solution.py:480
  40.6 4.3 %collective-permute-start.10 = (f32[2,8,8,128]{3,2,1,0:T(8,128)S(1)}, f32[2,8,8,128]{3,2,1,0:T(8,128)S(1)}, u32[]{:S(2)}, u32[]{:S(2)}) collective-permute-start(f32[2,8,8,128]{3,2,1,0:T(8,128)S(1)} %get-tuple-element.51), channel_id=1, source_target_pairs={{0,28},{4,0},{8,4},{12,8},{16,12},{20,16},{24,20},{28,24},{1,29},{... | collective-permute-start | bytes 196616 | tf_op jit(solution)/shard_map/ppermute | solution.py:480

commit v6 on v5

--- a/solution.py
+++ b/solution.py
@@ -297,11 +297,14 @@
     ridge_in_ref,
     cx_ref,
     tx_ref,
-    cy_ref,
-    ty_ref,
+    cy_middle_ref,
+    ty_middle_ref,
+    kept_ref,
+    sent_ref,
     *refs,
 ):
-    outs, (image_ref, raw_ref, once_ref, twice_ref, ridge_ref) = refs[: counts[0]], refs[counts[0] :]
+    outs, refs = refs[: counts[0]], refs[counts[0] :]
+    image_ref, raw_ref, once_ref, twice_ref, ridge_ref, cy_ref, ty_ref, rows_ref, columns_ref = refs
     half, rows, _ = wide_ref.shape
     run = cx_ref.shape[0]
     layers = LANES // 2
@@ -388,55 +391,56 @@
         start = pl.multiple_of(lax.rem(at_x + s, counts[0]) * share, share)
         out_ref[...] = image_ref[:, :, pl.ds(start, share), :]
 
-
-def columns_kernel(share, peers, cy_ref, ty_ref, cy_ends_ref, ty_ends_ref, *refs):
-    outs, (rows_ref, turned_ref) = refs[:peers], refs[peers:]
-    inner = ty_ref.shape[0]
-    half = inner + 2 * REACH
-    layers = LANES // 2
+    inner = half - 2 * REACH
     for k in range(half):
-        if k < REACH:
-            colours, clears = cy_ends_ref[k].T, ty_ends_ref[k].T
-        elif k < REACH + inner:
-            colours, clears = cy_ref[k - REACH].T, ty_ref[k - REACH].T
+        if REACH <= k < REACH + inner:
+            image = column_image(cy_middle_ref[k - REACH], ty_middle_ref[k - REACH])
         else:
-            colours, clears = cy_ends_ref[k - inner].T, ty_ends_ref[k - inner].T
-        colour, clear = colours[:SUB], clears[:SUB]
-        for c in range(1, CHUNKS):
-            at = slice(c * SUB, (c + 1) * SUB)
-            colour = colour + clear * colours[at]
-            clear = clear * clears[at]
-        rows_ref[0, k * SUB : (k + 1) * SUB] = colour
-        rows_ref[1, k * SUB : (k + 1) * SUB] = clear
-    me = lax.axis_index("by")
+            i = k if k < REACH else k - inner
+            image = column_image(cy_ref[i], ty_ref[i])
+        for kind in range(2):
+            rows_ref[kind, k * SUB : (k + 1) * SUB] = image[kind]
+    share = layers // counts[1]
+    mine = lax.axis_index("by") & 1
     for kind in range(2):
-        turned_ref[kind] = rows_ref[kind].T
-        for s in range(peers):
-            start = pl.multiple_of(lax.rem(me + s, peers) * share, share)
-            for part in range(2):
-                outs[s][kind, part] = turned_ref[kind, pl.ds(part * layers + start, share)]
-
-
-def fold_y_kernel(*refs):
-    pieces, out_ref = refs[:-1], refs[-1]
-    peers = len(pieces)
-    me = lax.axis_index("by")
-
-    def piece(source):
-        shift = lax.rem(me - source + peers, peers)
-        value = pieces[0][...]
-        for s in range(1, peers):
-            value = jnp.where(shift == s, pieces[s][...], value)
-        return value
-
-    value = piece(0)
-    colour, clear = value[0], value[1]
-    for source in range(1, peers):
-        value = piece(source)
-        colour = colour + clear * value[0]
-        clear = clear * value[1]
-    out_ref[0] = colour
-    out_ref[1] = clear
+        columns_ref[kind] = rows_ref[kind].T
+        for r in range(counts[1] // 2):
+            for out_ref, bit in ((kept_ref, mine), (sent_ref, 1 - mine)):
+                for part in range(2):
+                    start = pl.multiple_of((2 * r + bit) * share + part * layers, share)
+                    out_ref[r, kind, part] = columns_ref[kind, pl.ds(start, share)]
+
+
+def column_image(colours, clears):
+    colours, clears = colours.T, clears.T
+    colour, clear = colours[:SUB], clears[:SUB]
+    for c in range(1, CHUNKS):
+        at = slice(c * SUB, (c + 1) * SUB)
+        colour = colour + clear * colours[at]
+        clear = clear * clears[at]
+    return colour, clear
+
+
+def merge_kernel(level, peers, kept_ref, received_ref, *refs):
+    me = lax.axis_index("by") >> (level - 1)
+    later = (me & 1) == 1
+    kept, received = kept_ref[...], received_ref[...]
+    front = jnp.where(later, received, kept)
+    back = jnp.where(later, kept, received)
+    many = kept.shape[0]
+    colour = front[:, 0] + front[:, 1] * back[:, 0]
+    clear = front[:, 1] * back[:, 1]
+    if many == 1:
+        refs[0][0] = colour[0]
+        refs[0][1] = clear[0]
+        return
+    out_kept_ref, out_sent_ref = refs
+    bit = ((me >> 1) & 1) == 1
+    for r in range(many // 2):
+        for kind, value in enumerate((colour, clear)):
+            even, odd = value[2 * r], value[2 * r + 1]
+            out_kept_ref[r, kind] = jnp.where(bit, odd, even)
+            out_sent_ref[r, kind] = jnp.where(bit, even, odd)
 
 
 def fold_x_kernel(*refs):
@@ -506,7 +510,7 @@
             pltpu.VMEM(scalar_field.shape, F32),
             pltpu.SemaphoreType.DMA((local_x // SUB,)),
         ],
-        compiler_params=PARAMS,
+        compiler_params=pltpu.CompilerParams(vmem_limit_bytes=52 * 1024 * 1024),
         name="turn",
     )(scalar_field)
     before, after = exchange(last, first, "by")
@@ -533,33 +537,42 @@
         ],
     )(wide, transfer_in, transfer_out)
     share = layers // count_x
+    share_y = layers // count_y
     piece = sds(2, run, share, LANES)
-    colour_ends, clear_ends, *pieces = call(
+    parts = sds(count_y // 2, 2, 2, share_y, LANES)
+    kept, sent, *pieces = call(
         functools.partial(ends_kernel, many_y, counts, steps),
         "ends",
-        [sds(2 * REACH, LANES, LANES)] * 2 + [piece] * count_x,
-        10,
+        [parts] * 2 + [piece] * count_x,
+        12,
         [
             pltpu.VMEM((2, run, layers, LANES), F32),
             pltpu.VMEM((2, 5, rows, LANES), F32),
             pltpu.VMEM((2, 7, run + 4, CHUNKS, LANES), F32),
             pltpu.VMEM((2, 5, run + 2, CHUNKS, LANES), F32),
             pltpu.VMEM((2, 5, run + 2, CHUNKS, LANES), F32),
+            pltpu.VMEM((2 * REACH, LANES, LANES), F32),
+            pltpu.VMEM((2 * REACH, LANES, LANES), F32),
+            pltpu.VMEM((2, LANES, LANES), F32),
+            pltpu.VMEM((2, LANES, LANES), F32),
         ],
-    )(wide, before, after, win, wout, once, twice, ridge, colour_x, clear_x)
+    )(wide, before, after, win, wout, once, twice, ridge, colour_x, clear_x, colour_y, clear_y)
+
+    level, many = 1, count_y // 2
+    while many:
+        pairs = [(i, i ^ level) for i in range(count_y)]
+        received = lax.ppermute(sent, "by", pairs)
+        merge = functools.partial(merge_kernel, level.bit_length(), count_y)
+        if many > 1:
+            half_parts = sds(many // 2, 2, 2, share_y, LANES)
+            kept, sent = call(merge, "merge", [half_parts] * 2, 2)(kept, received)
+        else:
+            view_y = call(merge, "merge", sds(2, 2, share_y, LANES), 2)(kept, received)
+        level, many = 2 * level, many // 2
     pieces = shifted(pieces, "bx")
     view_x = call(fold_x_kernel, "fold_x", sds(2, bands, share, local_y), count_x)(*pieces)
-
-    share = layers // count_y
-    piece = sds(2, 2, share, LANES)
-    scratch = [pltpu.VMEM((2, LANES, LANES), F32), pltpu.VMEM((2, LANES, LANES), F32)]
-    pieces = call(
-        functools.partial(columns_kernel, share, count_y), "columns", [piece] * count_y, 4, scratch
-    )(colour_y, clear_y, colour_ends, clear_ends)
-    pieces = shifted(pieces, "by")
-    view_y = call(fold_y_kernel, "fold_y", piece, count_y)(*pieces)
-    view_y = view_y.reshape(2, 2, share, half, bands)
-    view_y = jnp.transpose(view_y, (0, 4, 2, 1, 3)).reshape(2, bands, share, local_x)
+    view_y = view_y.reshape(2, 2, share_y, half, bands)
+    view_y = jnp.transpose(view_y, (0, 4, 2, 1, 3)).reshape(2, bands, share_y, local_x)
     return (view_x, view_y)
 
 

time: 46 us -> 48.6 us (1.057)
  waiting for transfers between devices: 4.14 us -> 7.13 us
  starting transfers between devices: 21.6 us -> 18.8 us
  local copies, waits for them, and re-layouts: 2.23 us -> 3.5 us
  Pallas kernels: 17.1 us -> 18.3 us
    ppermute x10 -> x7, starting transfers between devices: 13.7 us -> 9.09 us  [shifted(): lax.ppermute(pieces[s], axis, [(i, (i + s) % peers) for i in range(peers)])]
    ppermute x10 -> x7, waiting for transfers between devices: 2.61 us -> 5.08 us  [shifted(): lax.ppermute(pieces[s], axis, [(i, (i + s) % peers) for i in range(peers)])]
    ppermute x0 -> x2, starting transfers between devices: none -> 1.81 us  [body(): received = lax.ppermute(sent, 'by', pairs)]
    unnamed x8 -> x10, local copies, waits for them, and re-layouts: 2.11 us -> 3.38 us
    pallas_call x1, Pallas kernels: 0.88 us -> 1.92 us  [body(): pl.pallas_call(turn_kernel, out_shape=[sds(half, rows, LANES), edge, edge...]
    ppermute x0 -> x2, waiting for transfers between devices: none -> 0.52 us  [body(): received = lax.ppermute(sent, 'by', pairs)]
  transfers between devices with their start and end apart: 14 -> 13, of which waited for: 5 -> 6; matrix products, arithmetic and copies ran while one was open for 2% -> 0% of each run, Pallas kernels for 21% -> 20%
where the time goes in v6:
time: 48.6 us; the launch traced here: 48.4 us
  starting transfers between devices  18.8 us (39%)
  Pallas kernels  18.3 us (38%)
  waiting for transfers between devices  7.13 us (15%)
  local copies, waits for them, and re-layouts  3.5 us (7%)
  between operations  0.71 us (1%)
    ppermute x7, starting transfers between devices, shifted(): lax.ppermute(pieces[s], axis, [(i, (i + s) % peers) for i in range(peers)])  9.09 us
    pallas_call x1, Pallas kernels, body(): call(functools.partial(middle_kernel, (many_x, many_y), counts, steps), '...  8.78 us
    ppermute x4, starting transfers between devices, exchange(): return (lax.ppermute(last, axis, up), lax.ppermute(first, axis, down))  7.89 us
    pallas_call x1, Pallas kernels, body(): call(functools.partial(ends_kernel, many_y, counts, steps), 'ends', [part...  6.48 us
    ppermute x7, waiting for transfers between devices, shifted(): lax.ppermute(pieces[s], axis, [(i, (i + s) % peers) for i in range(peers)])  5.08 us
    unnamed x10, local copies, waits for them, and re-layouts  3.38 us
    pallas_call x1, Pallas kernels, body(): pl.pallas_call(turn_kernel, out_shape=[sds(half, rows, LANES), edge, edge...  1.92 us
    ppermute x2, starting transfers between devices, body(): received = lax.ppermute(sent, 'by', pairs)  1.81 us
  transfers between devices with their start and end apart: 13, of which 6 were waited for; matrix products, arithmetic and copies ran while one was open for 0% of the time, Pallas kernels for 20%

profile of v6, /device:TPU:0, one launch (start us, length us, event | category | flops | bytes accessed | tf_op | source)
XLA Modules:
  0.0 48.4 jit_solution(889053105376263744)
XLA Ops:
  0.6 0.0 copy-start.1
  0.6 1.2 %copy-done.1 = f32[64,32,128]{2,1,0:T(8,128)S(1)} copy-done((f32[64,32,128]{2,1,0:T(8,128)S(1)}, f32[64,32,128]{2,1,0:T(8,128)}, u32[]{:S(2)}) %copy-start.1) | copy-done | bytes 1048600
  1.9 0.0 copy-start.3
  1.9 0.0 copy-start.2
  1.9 1.9 %turn.1 = (f32[16,144,128]{2,1,0:T(8,128)}, f32[3,16,128]{2,1,0:T(8,128)S(1)}, f32[3,16,128]{2,1,0:T(8,128)S(1)}) custom-call(f32[64,32,128]{2,1,0:T(8,128)S(1)} %copy-done.1), custom_call_target="tpu_custom_call" | custom-call | tf_op jit(solution)/shard_map/turn/pallas_call | solution.py:504
  3.8 0.5 %collective-permute-start = (f32[3,16,128]{2,1,0:T(8,128)S(1)}, f32[3,16,128]{2,1,0:T(8,128)S(1)}, u32[]{:S(2)}, u32[]{:S(2)}) collective-permute-start(f32[3,16,128]{2,1,0:T(8,128)S(1)} %get-tuple-element.30), channel_id=1, source_target_pairs={{0,1},{1,2},{2,3},{3,0},{4,5},{5,6},{6,7},{7,4},{8,9},{9,10},{10,1... | collective-permute-start | bytes 73736 | tf_op jit(solution)/shard_map/ppermute | solution.py:478
  4.3 2.0 %collective-permute-start.1 = (f32[3,16,128]{2,1,0:T(8,128)S(1)}, f32[3,16,128]{2,1,0:T(8,128)S(1)}, u32[]{:S(2)}, u32[]{:S(2)}) collective-permute-start(f32[3,16,128]{2,1,0:T(8,128)S(1)} %get-tuple-element.31), channel_id=1, source_target_pairs={{1,0},{2,1},{3,2},{0,3},{5,4},{6,5},{7,6},{4,7},{9,8},{10,9},{11,1... | collective-permute-start | bytes 73736 | tf_op jit(solution)/shard_map/ppermute | solution.py:478
  6.3 1.4 %collective-permute-done.before_ref = f32[3,16,128]{2,1,0:T(8,128)S(1)} collective-permute-done((f32[3,16,128]{2,1,0:T(8,128)S(1)}, f32[3,16,128]{2,1,0:T(8,128)S(1)}, u32[]{:S(2)}, u32[]{:S(2)}) %collective-permute-start) | collective-permute-done | bytes 24608 | tf_op jit(solution)/shard_map/ppermute | solution.py:478
  7.8 0.1 collective-permute-done.1.after_ref
  7.8 0.0 copy-start
  7.8 1.3 %copy-done = f32[16,144,128]{2,1,0:T(8,128)S(1)} copy-done((f32[16,144,128]{2,1,0:T(8,128)S(1)}, f32[16,144,128]{2,1,0:T(8,128)}, u32[]{:S(2)}) %copy-start) | copy-done | bytes 1179672
  9.1 0.2 sides.1
  9.3 2.3 %collective-permute-start.2 = (f32[3,72,128]{2,1,0:T(8,128)S(1)}, f32[3,72,128]{2,1,0:T(8,128)S(1)}, u32[]{:S(2)}, u32[]{:S(2)}) collective-permute-start(f32[3,72,128]{2,1,0:T(8,128)S(1)} %get-tuple-element.33), channel_id=1, source_target_pairs={{0,4},{4,8},{8,12},{12,16},{16,20},{20,24},{24,28},{28,0},{1,5},{5... | collective-permute-start | bytes 331784 | tf_op jit(solution)/shard_map/ppermute | solution.py:478
  11.5 3.1 %collective-permute-start.3 = (f32[3,72,128]{2,1,0:T(8,128)S(1)}, f32[3,72,128]{2,1,0:T(8,128)S(1)}, u32[]{:S(2)}, u32[]{:S(2)}) collective-permute-start(f32[3,72,128]{2,1,0:T(8,128)S(1)} %get-tuple-element.34), channel_id=1, source_target_pairs={{4,0},{8,4},{12,8},{16,12},{20,16},{24,20},{28,24},{0,28},{5,1},{9... | collective-permute-start | bytes 331784 | tf_op jit(solution)/shard_map/ppermute | solution.py:478
  14.6 0.0 copy-done.3
  14.6 0.1 copy.7.in_ref
  14.7 0.0 copy-done.2
  14.7 8.8 %middle.1 = (bf16[128,256]{1,0:T(8,128)(2,1)S(1)}, bf16[256,256]{1,0:T(8,128)(2,1)S(1)}, f32[2,4,12,16,128]{4,3,2,1,0:T(8,128)S(1)}, f32[2,2,10,16,128]{4,3,2,1,...) custom-call(f32[16,144,128]{2,1,0:T(8,128)S(1)} %get-tuple-element.3, ...), custom_call_target="tpu_custom_call" | custom-call | tf_op jit(solution)/shard_map/middle/pallas_call | solution.py:526
  23.5 0.0 collective-permute-done.2.before_ref
  23.5 0.0 collective-permute-done.3.after_ref
  23.5 6.5 %ends.1 = (f32[2,2,2,16,128]{4,3,2,1,0:T(8,128)S(1)}, f32[2,2,2,16,128]{4,3,2,1,0:T(8,128)S(1)}, f32[2,8,8,128]{3,2,1,0:T(8,128)S(1)}, f32[2,8,8,128]{3,2,1,0:T(...) custom-call(f32[16,144,128]{2,1,0:T(8,128)S(1)} %get-tuple-element.3, ...), custom_call_target="tpu_custom_call" | custom-call | tf_op jit(solution)/shard_map/ends/pallas_call | solution.py:543
  30.0 0.1 collective-permute-start.4
  30.1 0.5 collective-permute-start.5
  30.6 1.0 %collective-permute-start.11 = (f32[2,2,2,16,128]{4,3,2,1,0:T(8,128)S(1)}, f32[2,2,2,16,128]{4,3,2,1,0:T(8,128)S(1)}, u32[]{:S(2)}, u32[]{:S(2)}) collective-permute-start(f32[2,2,2,16,128]{4,3,2,1,0:T(8,128)S(1)} %get-tuple-element.53), channel_id=1, source_target_pairs={{0,1},{1,0},{2,3},{3,2},{4,5},{5,4},{6,7},{7,6},{8,9},{9,8},{10,11... | collective-permute-start | bytes 196616 | tf_op jit(solution)/shard_map/ppermute | solution.py:564
  31.6 3.0 %collective-permute-start.6 = (f32[2,8,8,128]{3,2,1,0:T(8,128)S(1)}, f32[2,8,8,128]{3,2,1,0:T(8,128)S(1)}, u32[]{:S(2)}, u32[]{:S(2)}) collective-permute-start(f32[2,8,8,128]{3,2,1,0:T(8,128)S(1)} %get-tuple-element.47), channel_id=1, source_target_pairs={{0,12},{4,16},{8,20},{12,24},{16,28},{20,0},{24,4},{28,8},{1,13},{... | collective-permute-start | bytes 196616 | tf_op jit(solution)/shard_map/ppermute | solution.py:484
  34.5 1.9 %collective-permute-start.7 = (f32[2,8,8,128]{3,2,1,0:T(8,128)S(1)}, f32[2,8,8,128]{3,2,1,0:T(8,128)S(1)}, u32[]{:S(2)}, u32[]{:S(2)}) collective-permute-start(f32[2,8,8,128]{3,2,1,0:T(8,128)S(1)} %get-tuple-element.48), channel_id=1, source_target_pairs={{0,16},{4,20},{8,24},{12,28},{16,0},{20,4},{24,8},{28,12},{1,17},{... | collective-permute-start | bytes 196616 | tf_op jit(solution)/shard_map/ppermute | solution.py:484
  36.4 1.1 %collective-permute-done.4.refs_1_ = f32[2,8,8,128]{3,2,1,0:T(8,128)S(1)} collective-permute-done((f32[2,8,8,128]{3,2,1,0:T(8,128)S(1)}, f32[2,8,8,128]{3,2,1,0:T(8,128)S(1)}, u32[]{:S(2)}, u32[]{:S(2)}) %collective-permute-start.4) | collective-permute-done | bytes 65568 | tf_op jit(solution)/shard_map/ppermute | solution.py:484
  37.5 0.0 collective-permute-start.8
  37.5 0.0 collective-permute-done.5.refs_2_
  37.5 1.6 %collective-permute-start.9 = (f32[2,8,8,128]{3,2,1,0:T(8,128)S(1)}, f32[2,8,8,128]{3,2,1,0:T(8,128)S(1)}, u32[]{:S(2)}, u32[]{:S(2)}) collective-permute-start(f32[2,8,8,128]{3,2,1,0:T(8,128)S(1)} %get-tuple-element.50), channel_id=1, source_target_pairs={{0,24},{4,28},{8,0},{12,4},{16,8},{20,12},{24,16},{28,20},{1,25},{... | collective-permute-start | bytes 196616 | tf_op jit(solution)/shard_map/ppermute | solution.py:484
  39.1 0.0 collective-permute-done.11.received_ref
  39.1 2.0 %collective-permute-start.10 = (f32[2,8,8,128]{3,2,1,0:T(8,128)S(1)}, f32[2,8,8,128]{3,2,1,0:T(8,128)S(1)}, u32[]{:S(2)}, u32[]{:S(2)}) collective-permute-start(f32[2,8,8,128]{3,2,1,0:T(8,128)S(1)} %get-tuple-element.51), channel_id=1, source_target_pairs={{0,28},{4,0},{8,4},{12,8},{16,12},{20,16},{24,20},{28,24},{1,29},{... | collective-permute-start | bytes 196616 | tf_op jit(solution)/shard_map/ppermute | solution.py:484
  41.2 2.4 %collective-permute-done.6.refs_3_ = f32[2,8,8,128]{3,2,1,0:T(8,128)S(1)} collective-permute-done((f32[2,8,8,128]{3,2,1,0:T(8,128)S(1)}, f32[2,8,8,128]{3,2,1,0:T(8,128)S(1)}, u32[]{:S(2)}, u32[]{:S(2)}) %collective-permute-start.6) | collective-permute-done | bytes 65568 | tf_op jit(solution)/shard_map/ppermute | solution.py:484
  43.6 0.8 %collective-permute-start.12 = (f32[1,2,2,16,128]{4,3,2,1,0:T(8,128)S(1)}, f32[1,2,2,16,128]{4,3,2,1,0:T(8,128)S(1)}, u32[]{:S(2)}, u32[]{:S(2)}) collective-permute-start(f32[1,2,2,16,128]{4,3,2,1,0:T(8,128)S(1)} %get-tuple-element.55), channel_id=1, source_target_pairs={{0,2},{1,3},{2,0},{3,1},{4,6},{5,7},{6,4},{7,5},{8,10},{9,11},{10,... | collective-permute-start | bytes 98312 | tf_op jit(solution)/shard_map/ppermute | solution.py:564
  44.4 0.0 collective-permute-done.7.refs_4_
  44.4 1.7 %collective-permute-done.8.refs_5_ = f32[2,8,8,128]{3,2,1,0:T(8,128)S(1)} collective-permute-done((f32[2,8,8,128]{3,2,1,0:T(8,128)S(1)}, f32[2,8,8,128]{3,2,1,0:T(8,128)S(1)}, u32[]{:S(2)}, u32[]{:S(2)}) %collective-permute-start.8) | collective-permute-done | bytes 65568 | tf_op jit(solution)/shard_map/ppermute | solution.py:484
  46.0 0.0 collective-permute-done.9.refs_6_
  46.0 0.0 collective-permute-done.10.refs_7_
  46.0 0.9 %fold_x.1 = f32[2,8,8,128]{3,2,1,0:T(8,128)} custom-call(f32[2,8,8,128]{3,2,1,0:T(8,128)S(1)} %get-tuple-element.44.refs_0_, f32[2,8,8,128]{3,2,1,0:T(8,128)S(1)} %collective-permute-done.4.refs_1_, f32[2,8,8,128]{3,2,1,0:T(8,128)S(1)} %collective-permute-done.5.refs_2_, f32[2,8,8,128]{3,2,1,0:T(8,128)S(1)} %collective-permute-done.6.refs_3_, ...), custom_call_target="tpu_custom_call" | custom-call | tf_op jit(solution)/shard_map/fold_x/pallas_call | solution.py:573
  47.0 0.5 %collective-permute-done.12.received_ref = f32[1,2,2,16,128]{4,3,2,1,0:T(8,128)S(1)} collective-permute-done((f32[1,2,2,16,128]{4,3,2,1,0:T(8,128)S(1)}, f32[1,2,2,16,128]{4,3,2,1,0:T(8,128)S(1)}, u32[]{:S(2)}, u32[]{:S(2)}) %collective-permute-start.12) | collective-permute-done | bytes 32800 | tf_op jit(solution)/shard_map/ppermute | solution.py:564
  47.5 0.1 copy.8
  47.6 0.8 %copy.9 = f32[2,8,16,32]{3,2,1,0:T(8,128)} copy(f32[2,8,16,32]{2,1,3,0:T(8,128)S(1)} %bitcast.5) | data formatting | bytes 65536
  (2 shorter events, 0.0 us)
Async XLA Ops:
  0.6 1.2 %copy-start.1 = (f32[64,32,128]{2,1,0:T(8,128)S(1)}, f32[64,32,128]{2,1,0:T(8,128)}, u32[]{:S(2)}) copy-start(f32[64,32,128]{2,1,0:T(8,128)} %field_hbm.1) | copy-start | bytes 3145732
  1.9 12.8 %copy-start.3 = (bf16[16,8]{0,1:T(8,128)(2,1)S(1)}, bf16[16,8]{0,1:T(8,128)(2,1)}, u32[]{:S(2)}) copy-start(bf16[16,8]{0,1:T(8,128)(2,1)} %param.4) | copy-start | bytes 772
  1.9 12.9 %copy-start.2 = (bf16[16,16]{1,0:T(8,128)(2,1)S(1)}, bf16[16,16]{1,0:T(8,128)(2,1)}, u32[]{:S(2)}) copy-start(bf16[16,16]{1,0:T(8,128)(2,1)} %out_ref.1) | copy-start | bytes 1540
  3.8 4.0 %collective-permute-start = (f32[3,16,128]{2,1,0:T(8,128)S(1)}, f32[3,16,128]{2,1,0:T(8,128)S(1)}, u32[]{:S(2)}, u32[]{:S(2)}) collective-permute-start(f32[3,16,128]{2,1,0:T(8,128)S(1)} %get-tuple-element.30), channel_id=1, source_target_pairs={{0,1},{1,2},{2,3},{3,0},{4,5},{5,6},{6,7},{7,4},{8,9},{9,10},{10,1... | collective-permute-start | bytes 73736 | tf_op jit(solution)/shard_map/ppermute | solution.py:478
  4.3 3.5 %collective-permute-start.1 = (f32[3,16,128]{2,1,0:T(8,128)S(1)}, f32[3,16,128]{2,1,0:T(8,128)S(1)}, u32[]{:S(2)}, u32[]{:S(2)}) collective-permute-start(f32[3,16,128]{2,1,0:T(8,128)S(1)} %get-tuple-element.31), channel_id=1, source_target_pairs={{1,0},{2,1},{3,2},{0,3},{5,4},{6,5},{7,6},{4,7},{9,8},{10,9},{11,1... | collective-permute-start | bytes 73736 | tf_op jit(solution)/shard_map/ppermute | solution.py:478
  7.8 1.3 %copy-start = (f32[16,144,128]{2,1,0:T(8,128)S(1)}, f32[16,144,128]{2,1,0:T(8,128)}, u32[]{:S(2)}) copy-start(f32[16,144,128]{2,1,0:T(8,128)} %get-tuple-element.29.turned_ref) | copy-start | bytes 3538948
  9.3 14.2 %collective-permute-start.2 = (f32[3,72,128]{2,1,0:T(8,128)S(1)}, f32[3,72,128]{2,1,0:T(8,128)S(1)}, u32[]{:S(2)}, u32[]{:S(2)}) collective-permute-start(f32[3,72,128]{2,1,0:T(8,128)S(1)} %get-tuple-element.33), channel_id=1, source_target_pairs={{0,4},{4,8},{8,12},{12,16},{16,20},{20,24},{24,28},{28,0},{1,5},{5... | collective-permute-start | bytes 331784 | tf_op jit(solution)/shard_map/ppermute | solution.py:478
  11.5 12.0 %collective-permute-start.3 = (f32[3,72,128]{2,1,0:T(8,128)S(1)}, f32[3,72,128]{2,1,0:T(8,128)S(1)}, u32[]{:S(2)}, u32[]{:S(2)}) collective-permute-start(f32[3,72,128]{2,1,0:T(8,128)S(1)} %get-tuple-element.34), channel_id=1, source_target_pairs={{4,0},{8,4},{12,8},{16,12},{20,16},{24,20},{28,24},{0,28},{5,1},{9... | collective-permute-start | bytes 331784 | tf_op jit(solution)/shard_map/ppermute | solution.py:478
  30.0 7.5 %collective-permute-start.4 = (f32[2,8,8,128]{3,2,1,0:T(8,128)S(1)}, f32[2,8,8,128]{3,2,1,0:T(8,128)S(1)}, u32[]{:S(2)}, u32[]{:S(2)}) collective-permute-start(f32[2,8,8,128]{3,2,1,0:T(8,128)S(1)} %get-tuple-element.45), channel_id=1, source_target_pairs={{0,4},{4,8},{8,12},{12,16},{16,20},{20,24},{24,28},{28,0},{1,5},{5... | collective-permute-start | bytes 196616 | tf_op jit(solution)/shard_map/ppermute | solution.py:484
  30.1 7.4 %collective-permute-start.5 = (f32[2,8,8,128]{3,2,1,0:T(8,128)S(1)}, f32[2,8,8,128]{3,2,1,0:T(8,128)S(1)}, u32[]{:S(2)}, u32[]{:S(2)}) collective-permute-start(f32[2,8,8,128]{3,2,1,0:T(8,128)S(1)} %get-tuple-element.46), channel_id=1, source_target_pairs={{0,8},{4,12},{8,16},{12,20},{16,24},{20,28},{24,0},{28,4},{1,9},{5... | collective-permute-start | bytes 196616 | tf_op jit(solution)/shard_map/ppermute | solution.py:484
  30.6 8.6 %collective-permute-start.11 = (f32[2,2,2,16,128]{4,3,2,1,0:T(8,128)S(1)}, f32[2,2,2,16,128]{4,3,2,1,0:T(8,128)S(1)}, u32[]{:S(2)}, u32[]{:S(2)}) collective-permute-start(f32[2,2,2,16,128]{4,3,2,1,0:T(8,128)S(1)} %get-tuple-element.53), channel_id=1, source_target_pairs={{0,1},{1,0},{2,3},{3,2},{4,5},{5,4},{6,7},{7,6},{8,9},{9,8},{10,11... | collective-permute-start | bytes 196616 | tf_op jit(solution)/shard_map/ppermute | solution.py:564
  31.6 12.0 %collective-permute-start.6 = (f32[2,8,8,128]{3,2,1,0:T(8,128)S(1)}, f32[2,8,8,128]{3,2,1,0:T(8,128)S(1)}, u32[]{:S(2)}, u32[]{:S(2)}) collective-permute-start(f32[2,8,8,128]{3,2,1,0:T(8,128)S(1)} %get-tuple-element.47), channel_id=1, source_target_pairs={{0,12},{4,16},{8,20},{12,24},{16,28},{20,0},{24,4},{28,8},{1,13},{... | collective-permute-start | bytes 196616 | tf_op jit(solution)/shard_map/ppermute | solution.py:484
  34.5 9.9 %collective-permute-start.7 = (f32[2,8,8,128]{3,2,1,0:T(8,128)S(1)}, f32[2,8,8,128]{3,2,1,0:T(8,128)S(1)}, u32[]{:S(2)}, u32[]{:S(2)}) collective-permute-start(f32[2,8,8,128]{3,2,1,0:T(8,128)S(1)} %get-tuple-element.48), channel_id=1, source_target_pairs={{0,16},{4,20},{8,24},{12,28},{16,0},{20,4},{24,8},{28,12},{1,17},{... | collective-permute-start | bytes 196616 | tf_op jit(solution)/shard_map/ppermute | solution.py:484
  37.5 8.5 %collective-permute-start.8 = (f32[2,8,8,128]{3,2,1,0:T(8,128)S(1)}, f32[2,8,8,128]{3,2,1,0:T(8,128)S(1)}, u32[]{:S(2)}, u32[]{:S(2)}) collective-permute-start(f32[2,8,8,128]{3,2,1,0:T(8,128)S(1)} %get-tuple-element.49), channel_id=1, source_target_pairs={{0,20},{4,24},{8,28},{12,0},{16,4},{20,8},{24,12},{28,16},{1,21},{... | collective-permute-start | bytes 196616 | tf_op jit(solution)/shard_map/ppermute | solution.py:484
  37.5 8.5 %collective-permute-start.9 = (f32[2,8,8,128]{3,2,1,0:T(8,128)S(1)}, f32[2,8,8,128]{3,2,1,0:T(8,128)S(1)}, u32[]{:S(2)}, u32[]{:S(2)}) collective-permute-start(f32[2,8,8,128]{3,2,1,0:T(8,128)S(1)} %get-tuple-element.50), channel_id=1, source_target_pairs={{0,24},{4,28},{8,0},{12,4},{16,8},{20,12},{24,16},{28,20},{1,25},{... | collective-permute-start | bytes 196616 | tf_op jit(solution)/shard_map/ppermute | solution.py:484
  39.1 6.9 %collective-permute-start.10 = (f32[2,8,8,128]{3,2,1,0:T(8,128)S(1)}, f32[2,8,8,128]{3,2,1,0:T(8,128)S(1)}, u32[]{:S(2)}, u32[]{:S(2)}) collective-permute-start(f32[2,8,8,128]{3,2,1,0:T(8,128)S(1)} %get-tuple-element.51), channel_id=1, source_target_pairs={{0,28},{4,0},{8,4},{12,8},{16,12},{20,16},{24,20},{28,24},{1,29},{... | collective-permute-start | bytes 196616 | tf_op jit(solution)/shard_map/ppermute | solution.py:484
  43.6 3.9 %collective-permute-start.12 = (f32[1,2,2,16,128]{4,3,2,1,0:T(8,128)S(1)}, f32[1,2,2,16,128]{4,3,2,1,0:T(8,128)S(1)}, u32[]{:S(2)}, u32[]{:S(2)}) collective-permute-start(f32[1,2,2,16,128]{4,3,2,1,0:T(8,128)S(1)} %get-tuple-element.55), channel_id=1, source_target_pairs={{0,2},{1,3},{2,0},{3,1},{4,6},{5,7},{6,4},{7,5},{8,10},{9,11},{10,... | collective-permute-start | bytes 98312 | tf_op jit(solution)/shard_map/ppermute | solution.py:564

commit v7 on v6

--- a/solution.py
+++ b/solution.py
@@ -15,7 +15,7 @@
 CHUNKS = 16
 REACH = 3
 VMEM = pl.BlockSpec(memory_space=pltpu.VMEM)
-PARAMS = pltpu.CompilerParams(vmem_limit_bytes=48 * 1024 * 1024)
+PARAMS = pltpu.CompilerParams(vmem_limit_bytes=36 * 1024 * 1024)
 
 
 def call(kernel, name, outs, count, scratch=()):
@@ -49,22 +49,10 @@
     return jnp.where(mask, jnp.dot(inner, right, preferred_element_type=F32), 0.0)
 
 
-def turn_kernel(field_hbm, turned_ref, first_ref, last_ref, field_ref, arrived):
+def turn_kernel(field_ref, turned_ref, first_ref, last_ref):
     layers, length, width = field_ref.shape
     half = length // 2
-    copies = []
-    for i in range(length // SUB):
-        part = (slice(None), pl.ds(i * SUB, SUB))
-        copies.append(
-            pltpu.make_async_copy(field_hbm.at[part], field_ref.at[part], arrived.at[i])
-        )
-    order = [i for k in range(half // SUB) for i in (k, k + half // SUB)]
-    for i in order:
-        copies[i].start()
     for k in range(half):
-        if k % SUB == 0:
-            copies[k // SUB].wait()
-            copies[(k + half) // SUB].wait()
         turned = jnp.concatenate([field_ref[:, k, :], field_ref[:, k + half, :]], axis=0).T
         turned_ref[k, REACH : REACH + width] = turned
         for j in range(REACH):
@@ -283,8 +271,57 @@
         block(step)
 
 
-def ends_kernel(
-    many_y,
+def parts_of(image_ref, kept_ref, sent_ref, mine):
+    many, share = kept_ref.shape[0], kept_ref.shape[3]
+    for r in range(many):
+        for out_ref, bit in ((kept_ref, mine), (sent_ref, 1 - mine)):
+            start = pl.multiple_of((2 * r + bit) * share, share)
+            out_ref[r] = image_ref[:, :, pl.ds(start, share), :]
+
+
+def march_ends(stencil, steps, first, weights, fields, middle, rays, image_ref):
+    twice_ref, ridge_ref = fields
+    cx_ref, tx_ref = middle
+    cy_ref, ty_ref = rays
+    layers = stencil.layers
+    many_y = image_ref.shape[1]
+    ratio = steps[0] / steps[1]
+    planes = [(0, 1), (0, 2), (0, 3), (1, 1), (1, 2), (1, 3)]
+    tiles = [
+        stencil.features(twice_ref.at[side], ridge_ref.at[side], k, first + j)
+        for j in range(many_y)
+        for side, k in planes
+    ]
+    emission, clear = network(tiles, *weights, steps[1])
+    images = [[], []]
+    for g in range(LANES // SUB):
+        at = pl.ds(g * SUB, SUB)
+        rays_y = [(cy_ref[i, at], ty_ref[i, at]) for i in range(len(planes))]
+        for j in range(many_y):
+            ray_x = jnp.zeros((SUB, LANES), F32), jnp.ones((SUB, LANES), F32)
+            for i in range(len(planes)):
+                if i == REACH:
+                    colour, light = ray_x
+                    colour = colour + light * cx_ref[first + j, at]
+                    ray_x = colour, light * tx_ref[first + j, at]
+                start = (j * len(planes) + i) * LANES + g * SUB
+                e, q = emission[start : start + SUB], clear[start : start + SUB]
+                rays_y[i] = step_ray(rays_y[i], q, e)
+                ray_x = step_ray(ray_x, clear_of_x(q, ratio), e)
+            images[0].append(ray_x[0])
+            images[1].append(ray_x[1])
+        for i in range(len(planes)):
+            cy_ref[i, at], ty_ref[i, at] = rays_y[i]
+    for d in range(layers // SUB):
+        for j in range(many_y):
+            near, far = d * many_y + j, (d + layers // SUB) * many_y + j
+            q = images[1][near]
+            at = pl.ds(d * SUB, SUB)
+            image_ref[0, j, at] = images[0][near] + q * images[0][far]
+            image_ref[1, j, at] = q * images[1][far]
+
+
+def ends_first_kernel(
     counts,
     steps,
     wide_ref,
@@ -297,14 +334,16 @@
     ridge_in_ref,
     cx_ref,
     tx_ref,
-    cy_middle_ref,
-    ty_middle_ref,
+    twice_ref,
+    ridge_ref,
+    cy_ref,
+    ty_ref,
     kept_ref,
     sent_ref,
-    *refs,
+    image_ref,
+    raw_ref,
+    once_ref,
 ):
-    outs, refs = refs[: counts[0]], refs[counts[0] :]
-    image_ref, raw_ref, once_ref, twice_ref, ridge_ref, cy_ref, ty_ref, rows_ref, columns_ref = refs
     half, rows, _ = wide_ref.shape
     run = cx_ref.shape[0]
     layers = LANES // 2
@@ -342,56 +381,63 @@
             kept = edge if k == 2 * side else None
             at = k + 2 * side
             stencil.twice(once_ref.at[side], at + 1, twice_ref.at[side], ridge_ref.at[side], at, kept)
-
-    ratio = steps[0] / steps[1]
-    planes = [(0, 1), (0, 2), (0, 3), (1, 1), (1, 2), (1, 3)]
-    for k in range(len(planes)):
+    for k in range(2 * REACH):
         ty_ref[k] = jnp.ones((LANES, LANES), F32)
         cy_ref[k] = jnp.zeros((LANES, LANES), F32)
-
-    def block(step):
-        y0 = step * many_y
-        tiles = [
-            stencil.features(twice_ref.at[side], ridge_ref.at[side], k, y0 + j)
-            for j in range(many_y)
-            for side, k in planes
-        ]
-        emission, clear = network(tiles, win_ref, wout_ref, steps[1])
-        images = [[], []]
-        for g in range(LANES // SUB):
-            at = pl.ds(g * SUB, SUB)
-            rays_y = [(cy_ref[i, at], ty_ref[i, at]) for i in range(len(planes))]
-            for j in range(many_y):
-                ray_x = jnp.zeros((SUB, LANES), F32), jnp.ones((SUB, LANES), F32)
-                for i in range(len(planes)):
-                    if i == REACH:
-                        colour, light = ray_x
-                        colour = colour + light * cx_ref[y0 + j, at]
-                        ray_x = colour, light * tx_ref[y0 + j, at]
-                    start = (j * len(planes) + i) * LANES + g * SUB
-                    e, q = emission[start : start + SUB], clear[start : start + SUB]
-                    rays_y[i] = step_ray(rays_y[i], q, e)
-                    ray_x = step_ray(ray_x, clear_of_x(q, ratio), e)
-                images[0].append(ray_x[0])
-                images[1].append(ray_x[1])
-            for i in range(len(planes)):
-                cy_ref[i, at], ty_ref[i, at] = rays_y[i]
-        for d in range(layers // SUB):
-            for j in range(many_y):
-                near, far = d * many_y + j, (d + layers // SUB) * many_y + j
-                q = images[1][near]
-                at = pl.ds(d * SUB, SUB)
-                image_ref[0, y0 + j, at] = images[0][near] + q * images[0][far]
-                image_ref[1, y0 + j, at] = q * images[1][far]
-
-    for step in range(run // many_y):
-        block(step)
-    share = layers // counts[0]
-    for s, out_ref in enumerate(outs):
-        start = pl.multiple_of(lax.rem(at_x + s, counts[0]) * share, share)
-        out_ref[...] = image_ref[:, :, pl.ds(start, share), :]
-
-    inner = half - 2 * REACH
+    march_ends(
+        stencil,
+        steps,
+        0,
+        (win_ref, wout_ref),
+        (twice_ref, ridge_ref),
+        (cx_ref, tx_ref),
+        (cy_ref, ty_ref),
+        image_ref,
+    )
+    parts_of(image_ref, kept_ref, sent_ref, at_x & 1)
+
+
+def ends_last_kernel(
+    counts,
+    steps,
+    win_ref,
+    wout_ref,
+    twice_ref,
+    ridge_ref,
+    cx_ref,
+    tx_ref,
+    cy_in_ref,
+    ty_in_ref,
+    cy_middle_ref,
+    ty_middle_ref,
+    kept_ref,
+    sent_ref,
+    kept_y_ref,
+    sent_y_ref,
+    image_ref,
+    cy_ref,
+    ty_ref,
+    rows_ref,
+    columns_ref,
+):
+    run = cx_ref.shape[0]
+    stencil = Stencil(run, counts)
+    layers = stencil.layers
+    cy_ref[...] = cy_in_ref[...]
+    ty_ref[...] = ty_in_ref[...]
+    march_ends(
+        stencil,
+        steps,
+        run - image_ref.shape[1],
+        (win_ref, wout_ref),
+        (twice_ref, ridge_ref),
+        (cx_ref, tx_ref),
+        (cy_ref, ty_ref),
+        image_ref,
+    )
+    parts_of(image_ref, kept_ref, sent_ref, lax.axis_index("bx") & 1)
+    inner = cy_middle_ref.shape[0]
+    half = inner + 2 * REACH
     for k in range(half):
         if REACH <= k < REACH + inner:
             image = column_image(cy_middle_ref[k - REACH], ty_middle_ref[k - REACH])
@@ -400,15 +446,11 @@
             image = column_image(cy_ref[i], ty_ref[i])
         for kind in range(2):
             rows_ref[kind, k * SUB : (k + 1) * SUB] = image[kind]
-    share = layers // counts[1]
-    mine = lax.axis_index("by") & 1
     for kind in range(2):
-        columns_ref[kind] = rows_ref[kind].T
-        for r in range(counts[1] // 2):
-            for out_ref, bit in ((kept_ref, mine), (sent_ref, 1 - mine)):
-                for part in range(2):
-                    start = pl.multiple_of((2 * r + bit) * share + part * layers, share)
-                    out_ref[r, kind, part] = columns_ref[kind, pl.ds(start, share)]
+        turned = rows_ref[kind].T
+        for part in range(2):
+            columns_ref[kind, part] = turned[part * layers : (part + 1) * layers]
+    parts_of(columns_ref, kept_y_ref, sent_y_ref, lax.axis_index("by") & 1)
 
 
 def column_image(colours, clears):
@@ -421,7 +463,7 @@
     return colour, clear
 
 
-def merge_kernel(level, peers, kept_ref, received_ref, *refs):
+def merge_kernel(level, kept_ref, received_ref, *refs):
     me = lax.axis_index("by") >> (level - 1)
     later = (me & 1) == 1
     kept, received = kept_ref[...], received_ref[...]
@@ -443,11 +485,27 @@
             out_sent_ref[r, kind] = jnp.where(bit, even, odd)
 
 
+def merge_x_kernel(*refs):
+    ins, outs = refs[:4], refs[4:]
+    many, _, some, _, _ = ins[0].shape
+    at = lax.axis_index("bx")
+    later = (at & 1) == 1
+    for i in range(2):
+        kept_ref, received_ref = ins[2 * i], ins[2 * i + 1]
+        for t in range(many):
+            r = lax.rem((at >> 1) + t, many)
+            kept, received = kept_ref[r], received_ref[r]
+            front = jnp.where(later, received, kept)
+            back = jnp.where(later, kept, received)
+            outs[t][0, i * some : (i + 1) * some] = front[0] + front[1] * back[0]
+            outs[t][1, i * some : (i + 1) * some] = front[1] * back[1]
+
+
 def fold_x_kernel(*refs):
     pieces, out_ref = refs[:-1], refs[-1]
     _, run, share, _ = pieces[0].shape
     lane = iota((share, LANES), 1)
-    me = lax.axis_index("bx")
+    me = lax.axis_index("bx") >> 1
     kinds = [[], []]
     for y in range(run):
         behind = colour, clear = jnp.zeros((share, LANES), F32), jnp.ones((share, LANES), F32)
@@ -478,12 +536,8 @@
     return lax.ppermute(last, axis, up), lax.ppermute(first, axis, down)
 
 
-def shifted(pieces, axis):
-    peers = lax.axis_size(axis)
-    return [pieces[0]] + [
-        lax.ppermute(pieces[s], axis, [(i, (i + s) % peers) for i in range(peers)])
-        for s in range(1, peers)
-    ]
+def swap(value, axis, bit):
+    return lax.ppermute(value, axis, [(i, i ^ bit) for i in range(lax.axis_size(axis))])
 
 
 def body(scalar_field, transfer_in, transfer_out):
@@ -501,18 +555,9 @@
     ]
 
     edge = sds(REACH, half, LANES)
-    turned, first, last = pl.pallas_call(
-        turn_kernel,
-        out_shape=[sds(half, rows, LANES), edge, edge],
-        in_specs=[pl.BlockSpec(memory_space=pltpu.HBM)],
-        out_specs=[VMEM] * 3,
-        scratch_shapes=[
-            pltpu.VMEM(scalar_field.shape, F32),
-            pltpu.SemaphoreType.DMA((local_x // SUB,)),
-        ],
-        compiler_params=pltpu.CompilerParams(vmem_limit_bytes=52 * 1024 * 1024),
-        name="turn",
-    )(scalar_field)
+    turned, first, last = call(turn_kernel, "turn", [sds(half, rows, LANES), edge, edge], 1)(
+        scalar_field
+    )
     before, after = exchange(last, first, "by")
     edge = sds(REACH, rows // 2, LANES)
     wide, first, last = call(
@@ -538,39 +583,55 @@
     )(wide, transfer_in, transfer_out)
     share = layers // count_x
     share_y = layers // count_y
-    piece = sds(2, run, share, LANES)
-    parts = sds(count_y // 2, 2, 2, share_y, LANES)
-    kept, sent, *pieces = call(
-        functools.partial(ends_kernel, many_y, counts, steps),
-        "ends",
-        [parts] * 2 + [piece] * count_x,
-        12,
+    parts = sds(count_x // 2, 2, run // 2, share, LANES)
+    parts_y = sds(count_y // 2, 2, 2, share_y, LANES)
+    image = pltpu.VMEM((2, run // 2, layers, LANES), F32)
+    ray = pltpu.VMEM((2 * REACH, LANES, LANES), F32)
+    field = plane(2, 5, run + 2)
+    twice, ridge, colour_ends, clear_ends, kept, sent = call(
+        functools.partial(ends_first_kernel, counts, steps),
+        "ends_first",
+        [field] * 2 + [sds(2 * REACH, LANES, LANES)] * 2 + [parts] * 2,
+        10,
         [
-            pltpu.VMEM((2, run, layers, LANES), F32),
+            image,
             pltpu.VMEM((2, 5, rows, LANES), F32),
             pltpu.VMEM((2, 7, run + 4, CHUNKS, LANES), F32),
-            pltpu.VMEM((2, 5, run + 2, CHUNKS, LANES), F32),
-            pltpu.VMEM((2, 5, run + 2, CHUNKS, LANES), F32),
-            pltpu.VMEM((2 * REACH, LANES, LANES), F32),
-            pltpu.VMEM((2 * REACH, LANES, LANES), F32),
+        ],
+    )(wide, before, after, win, wout, once, twice, ridge, colour_x, clear_x)
+    halves = [kept, swap(sent, "bx", 1)]
+    kept, sent, kept_y, sent_y = call(
+        functools.partial(ends_last_kernel, counts, steps),
+        "ends_last",
+        [parts] * 2 + [parts_y] * 2,
+        10,
+        [
+            image,
+            ray,
+            ray,
             pltpu.VMEM((2, LANES, LANES), F32),
-            pltpu.VMEM((2, LANES, LANES), F32),
+            pltpu.VMEM((2, 2, layers, LANES), F32),
         ],
-    )(wide, before, after, win, wout, once, twice, ridge, colour_x, clear_x, colour_y, clear_y)
+    )(win, wout, twice, ridge, colour_x, clear_x, colour_ends, clear_ends, colour_y, clear_y)
+    halves += [kept, swap(sent, "bx", 1)]
 
     level, many = 1, count_y // 2
     while many:
-        pairs = [(i, i ^ level) for i in range(count_y)]
-        received = lax.ppermute(sent, "by", pairs)
-        merge = functools.partial(merge_kernel, level.bit_length(), count_y)
+        received = swap(sent_y, "by", level)
+        merge = functools.partial(merge_kernel, level.bit_length())
         if many > 1:
             half_parts = sds(many // 2, 2, 2, share_y, LANES)
-            kept, sent = call(merge, "merge", [half_parts] * 2, 2)(kept, received)
+            kept_y, sent_y = call(merge, "merge", [half_parts] * 2, 2)(kept_y, received)
         else:
-            view_y = call(merge, "merge", sds(2, 2, share_y, LANES), 2)(kept, received)
+            view_y = call(merge, "merge", sds(2, 2, share_y, LANES), 2)(kept_y, received)
         level, many = 2 * level, many // 2
-    pieces = shifted(pieces, "bx")
-    view_x = call(fold_x_kernel, "fold_x", sds(2, bands, share, local_y), count_x)(*pieces)
+    many = count_x // 2
+    piece = sds(2, run, share, LANES)
+    pieces = list(call(merge_x_kernel, "merge_x", [piece] * many, 4)(*halves))
+    for t in range(1, many):
+        pairs = [(i, (i + 2 * t) % count_x) for i in range(count_x)]
+        pieces[t] = lax.ppermute(pieces[t], "bx", pairs)
+    view_x = call(fold_x_kernel, "fold_x", sds(2, bands, share, local_y), many)(*pieces)
     view_y = view_y.reshape(2, 2, share_y, half, bands)
     view_y = jnp.transpose(view_y, (0, 4, 2, 1, 3)).reshape(2, bands, share_y, local_x)
     return (view_x, view_y)

time: 48.6 us -> 45 us (0.926)
  starting transfers between devices: 18.8 us -> 16 us
  local copies, waits for them, and re-layouts: 3.5 us -> 2.23 us
  waiting for transfers between devices: 7.13 us -> 8.23 us
  Pallas kernels: 18.3 us -> 17.6 us
    ppermute x9 -> x7, starting transfers between devices: 10.9 us -> 8.09 us  [the longest x3 4.58 us: body(): pieces[t] = lax.ppermute(pieces[t], 'bx', pairs)]
    unnamed x10 -> x8, local copies, waits for them, and re-layouts: 3.38 us -> 2.11 us
    ppermute x9 -> x7, waiting for transfers between devices: 5.6 us -> 6.7 us  [the longest x4 6.69 us: swap(): lax.ppermute(value, axis, [(i, i ^ bit) for i in range(lax.axis_size(axis...]
    pallas_call x5 -> x7, Pallas kernels: 9.35 us -> 8.64 us  [the longest x1 4.23 us: body(): call(functools.partial(ends_first_kernel, counts, steps), 'ends_first', [...]
  transfers between devices with their start and end apart: 13 -> 11, of which waited for: 6 -> 5; matrix products, arithmetic and copies ran while one was open for 0% -> 2% of each run, Pallas kernels for 20% -> 26%
where the time goes in v7:
time: 45 us; the launch traced here: 44.8 us
  Pallas kernels  17.6 us (39%)
  starting transfers between devices  16 us (36%)
  waiting for transfers between devices  8.23 us (18%)
  local copies, waits for them, and re-layouts  2.23 us (5%)
  between operations  0.71 us (2%)
    pallas_call x1, Pallas kernels, body(): call(functools.partial(middle_kernel, (many_x, many_y), counts, steps), '...  8.84 us
    ppermute x4, starting transfers between devices, exchange(): return (lax.ppermute(last, axis, up), lax.ppermute(first, axis, down))  7.88 us
    ppermute x4, waiting for transfers between devices, swap(): lax.ppermute(value, axis, [(i, i ^ bit) for i in range(lax.axis_size(axis...  6.69 us
    ppermute x3, starting transfers between devices, body(): pieces[t] = lax.ppermute(pieces[t], 'bx', pairs)  4.58 us
    pallas_call x1, Pallas kernels, body(): call(functools.partial(ends_first_kernel, counts, steps), 'ends_first', [...  4.23 us
    ppermute x4, starting transfers between devices, swap(): lax.ppermute(value, axis, [(i, i ^ bit) for i in range(lax.axis_size(axis...  3.51 us
    pallas_call x1, Pallas kernels, body(): call(functools.partial(ends_last_kernel, counts, steps), 'ends_last', [pa...  2.8 us
    unnamed x8, local copies, waits for them, and re-layouts  2.11 us
  transfers between devices with their start and end apart: 11, of which 5 were waited for; matrix products, arithmetic and copies ran while one was open for 2% of the time, Pallas kernels for 26%

profile of v7, /device:TPU:0, one launch (start us, length us, event | category | flops | bytes accessed | tf_op | source)
XLA Modules:
  0.0 44.8 jit_solution(4722034179180419596)
XLA Ops:
  0.6 0.0 copy-start
  0.6 1.2 %copy-done = f32[64,32,128]{2,1,0:T(8,128)S(1)} copy-done((f32[64,32,128]{2,1,0:T(8,128)S(1)}, f32[64,32,128]{2,1,0:T(8,128)}, u32[]{:S(2)}) %copy-start) | copy-done | bytes 1048600
  1.9 0.0 copy-start.2
  1.9 0.0 copy-start.1
  1.9 0.6 %turn.1 = (f32[16,144,128]{2,1,0:T(8,128)S(1)}, f32[3,16,128]{2,1,0:T(8,128)S(1)}, f32[3,16,128]{2,1,0:T(8,128)S(1)}) custom-call(f32[64,32,128]{2,1,0:T(8,128)S(1)} %copy-done), custom_call_target="tpu_custom_call" | custom-call | tf_op jit(solution)/shard_map/turn/pallas_call | solution.py:558
  2.5 0.5 %collective-permute-start = (f32[3,16,128]{2,1,0:T(8,128)S(1)}, f32[3,16,128]{2,1,0:T(8,128)S(1)}, u32[]{:S(2)}, u32[]{:S(2)}) collective-permute-start(f32[3,16,128]{2,1,0:T(8,128)S(1)} %get-tuple-element.34), channel_id=1, source_target_pairs={{0,1},{1,2},{2,3},{3,0},{4,5},{5,6},{6,7},{7,4},{8,9},{9,10},{10,1... | collective-permute-start | bytes 73736 | tf_op jit(solution)/shard_map/ppermute | solution.py:536
  3.0 2.0 %collective-permute-start.1 = (f32[3,16,128]{2,1,0:T(8,128)S(1)}, f32[3,16,128]{2,1,0:T(8,128)S(1)}, u32[]{:S(2)}, u32[]{:S(2)}) collective-permute-start(f32[3,16,128]{2,1,0:T(8,128)S(1)} %get-tuple-element.35), channel_id=1, source_target_pairs={{1,0},{2,1},{3,2},{0,3},{5,4},{6,5},{7,6},{4,7},{9,8},{10,9},{11,1... | collective-permute-start | bytes 73736 | tf_op jit(solution)/shard_map/ppermute | solution.py:536
  5.0 1.4 %collective-permute-done.before_ref = f32[3,16,128]{2,1,0:T(8,128)S(1)} collective-permute-done((f32[3,16,128]{2,1,0:T(8,128)S(1)}, f32[3,16,128]{2,1,0:T(8,128)S(1)}, u32[]{:S(2)}, u32[]{:S(2)}) %collective-permute-start) | collective-permute-done | bytes 24608 | tf_op jit(solution)/shard_map/ppermute | solution.py:536
  6.5 0.1 collective-permute-done.1.after_ref
  6.6 0.2 sides.1
  6.7 2.3 %collective-permute-start.2 = (f32[3,72,128]{2,1,0:T(8,128)S(1)}, f32[3,72,128]{2,1,0:T(8,128)S(1)}, u32[]{:S(2)}, u32[]{:S(2)}) collective-permute-start(f32[3,72,128]{2,1,0:T(8,128)S(1)} %get-tuple-element.37), channel_id=1, source_target_pairs={{0,4},{4,8},{8,12},{12,16},{16,20},{20,24},{24,28},{28,0},{1,5},{5... | collective-permute-start | bytes 331784 | tf_op jit(solution)/shard_map/ppermute | solution.py:536
  9.0 3.1 %collective-permute-start.3 = (f32[3,72,128]{2,1,0:T(8,128)S(1)}, f32[3,72,128]{2,1,0:T(8,128)S(1)}, u32[]{:S(2)}, u32[]{:S(2)}) collective-permute-start(f32[3,72,128]{2,1,0:T(8,128)S(1)} %get-tuple-element.38), channel_id=1, source_target_pairs={{4,0},{8,4},{12,8},{16,12},{20,16},{24,20},{28,24},{0,28},{5,1},{9... | collective-permute-start | bytes 331784 | tf_op jit(solution)/shard_map/ppermute | solution.py:536
  12.1 0.0 copy-done.2
  12.1 0.1 copy.7.in_ref
  12.2 0.0 copy-done.1
  12.2 8.8 %middle.1 = (bf16[128,256]{1,0:T(8,128)(2,1)S(1)}, bf16[256,256]{1,0:T(8,128)(2,1)S(1)}, f32[2,4,12,16,128]{4,3,2,1,0:T(8,128)S(1)}, f32[2,2,10,16,128]{4,3,2,1,...) custom-call(f32[16,144,128]{2,1,0:T(8,128)S(1)} %get-tuple-element.3, ...), custom_call_target="tpu_custom_call" | custom-call | tf_op jit(solution)/shard_map/middle/pallas_call | solution.py:571
  21.0 0.0 collective-permute-done.2.before_ref
  21.0 0.0 collective-permute-done.3.after_ref
  21.0 4.2 %ends_first.1 = (f32[2,5,10,16,128]{4,3,2,1,0:T(8,128)S(1)}, f32[2,5,10,16,128]{4,3,2,1,0:T(8,128)S(1)}, f32[6,128,128]{2,1,0:T(8,128)S(1)}, f32[6,128,128]{2,1,...) custom-call(f32[16,144,128]{2,1,0:T(8,128)S(1)} %get-tuple-element.36.wide_ref, ...), custom_call_target="tpu_custom_call" | custom-call | tf_op jit(solution)/shard_map/ends_first/pallas_call | solution.py:591
  25.3 0.1 collective-permute-start.4
  25.4 2.8 %ends_last.1 = (f32[4,2,4,8,128]{4,3,2,1,0:T(8,128)S(1)}, f32[4,2,4,8,128]{4,3,2,1,0:T(8,128)S(1)}, f32[2,2,2,16,128]{4,3,2,1,0:T(8,128)S(1)}, f32[2,2,2,16,128]{4,3,2,1,0:T(8,128)S(1)}) custom-call(bf16[128,256]{1,0:T(8,128)(2,1)S(1)} %get-tuple-element.39.win_ref, bf16[256,256]{1,0:T(8,128)(2,1)S(1)} %get-tuple-element.40.wout_ref, ...), custom_call_target="tpu_custom_call" | custom-call | tf_op jit(solution)/shard_map/ends_last/pallas_call | solution.py:603
  28.2 2.1 %collective-permute-start.5 = (f32[4,2,4,8,128]{4,3,2,1,0:T(8,128)S(1)}, f32[4,2,4,8,128]{4,3,2,1,0:T(8,128)S(1)}, u32[]{:S(2)}, u32[]{:S(2)}) collective-permute-start(f32[4,2,4,8,128]{4,3,2,1,0:T(8,128)S(1)} %get-tuple-element.55), channel_id=1, source_target_pairs={{0,4},{4,0},{8,12},{12,8},{16,20},{20,16},{24,28},{28,24},{1,5},{5... | collective-permute-start | bytes 393224 | tf_op jit(solution)/shard_map/ppermute | solution.py:540
  30.2 0.8 %collective-permute-start.9 = (f32[2,2,2,16,128]{4,3,2,1,0:T(8,128)S(1)}, f32[2,2,2,16,128]{4,3,2,1,0:T(8,128)S(1)}, u32[]{:S(2)}, u32[]{:S(2)}) collective-permute-start(f32[2,2,2,16,128]{4,3,2,1,0:T(8,128)S(1)} %get-tuple-element.61), channel_id=1, source_target_pairs={{0,1},{1,0},{2,3},{3,2},{4,5},{5,4},{6,7},{7,6},{8,9},{9,8},{10,11... | collective-permute-start | bytes 196616 | tf_op jit(solution)/shard_map/ppermute | solution.py:540
  31.0 0.4 collective-permute-done.4.refs_1_
  31.4 2.9 %collective-permute-done.5.refs_3_ = f32[4,2,4,8,128]{4,3,2,1,0:T(8,128)S(1)} collective-permute-done((f32[4,2,4,8,128]{4,3,2,1,0:T(8,128)S(1)}, f32[4,2,4,8,128]{4,3,2,1,0:T(8,128)S(1)}, u32[]{:S(2)}, u32[]{:S(2)}) %collective-permute-start.5) | collective-permute-done | bytes 131104 | tf_op jit(solution)/shard_map/ppermute | solution.py:540
  34.4 0.6 %collective-permute-start.6 = (f32[2,8,8,128]{3,2,1,0:T(8,128)S(1)}, f32[2,8,8,128]{3,2,1,0:T(8,128)S(1)}, u32[]{:S(2)}, u32[]{:S(2)}) collective-permute-start(f32[2,8,8,128]{3,2,1,0:T(8,128)S(1)} %get-tuple-element.57), channel_id=1, source_target_pairs={{0,8},{4,12},{8,16},{12,20},{16,24},{20,28},{24,0},{28,4},{1,9},{5... | collective-permute-start | bytes 196616 | tf_op jit(solution)/shard_map/ppermute | solution.py:633
  35.0 2.6 %collective-permute-start.7 = (f32[2,8,8,128]{3,2,1,0:T(8,128)S(1)}, f32[2,8,8,128]{3,2,1,0:T(8,128)S(1)}, u32[]{:S(2)}, u32[]{:S(2)}) collective-permute-start(f32[2,8,8,128]{3,2,1,0:T(8,128)S(1)} %get-tuple-element.58), channel_id=1, source_target_pairs={{0,16},{4,20},{8,24},{12,28},{16,0},{20,4},{24,8},{28,12},{1,17},{... | collective-permute-start | bytes 196616 | tf_op jit(solution)/shard_map/ppermute | solution.py:633
  37.6 1.3 %collective-permute-start.8 = (f32[2,8,8,128]{3,2,1,0:T(8,128)S(1)}, f32[2,8,8,128]{3,2,1,0:T(8,128)S(1)}, u32[]{:S(2)}, u32[]{:S(2)}) collective-permute-start(f32[2,8,8,128]{3,2,1,0:T(8,128)S(1)} %get-tuple-element.59), channel_id=1, source_target_pairs={{0,24},{4,28},{8,0},{12,4},{16,8},{20,12},{24,16},{28,20},{1,25},{... | collective-permute-start | bytes 196616 | tf_op jit(solution)/shard_map/ppermute | solution.py:633
  38.9 0.0 collective-permute-done.9.received_ref
  39.0 0.6 %collective-permute-start.10 = (f32[1,2,2,16,128]{4,3,2,1,0:T(8,128)S(1)}, f32[1,2,2,16,128]{4,3,2,1,0:T(8,128)S(1)}, u32[]{:S(2)}, u32[]{:S(2)}) collective-permute-start(f32[1,2,2,16,128]{4,3,2,1,0:T(8,128)S(1)} %get-tuple-element.63), channel_id=1, source_target_pairs={{0,2},{1,3},{2,0},{3,1},{4,6},{5,7},{6,4},{7,5},{8,10},{9,11},{10,... | collective-permute-start | bytes 98312 | tf_op jit(solution)/shard_map/ppermute | solution.py:540
  39.5 3.4 %collective-permute-done.10.received_ref = f32[1,2,2,16,128]{4,3,2,1,0:T(8,128)S(1)} collective-permute-done((f32[1,2,2,16,128]{4,3,2,1,0:T(8,128)S(1)}, f32[1,2,2,16,128]{4,3,2,1,0:T(8,128)S(1)}, u32[]{:S(2)}, u32[]{:S(2)}) %collective-permute-start.10) | collective-permute-done | bytes 32800 | tf_op jit(solution)/shard_map/ppermute | solution.py:540
  43.0 0.1 copy.8
  43.1 0.8 %copy.9 = f32[2,8,16,32]{3,2,1,0:T(8,128)} copy(f32[2,8,16,32]{2,1,3,0:T(8,128)S(1)} %bitcast.5) | data formatting | bytes 65536
  43.9 0.0 collective-permute-done.6.refs_1_
  43.9 0.0 collective-permute-done.7.refs_2_
  43.9 0.0 collective-permute-done.8.refs_3_
  43.9 0.9 %fold_x.1 = f32[2,8,8,128]{3,2,1,0:T(8,128)} custom-call(f32[2,8,8,128]{3,2,1,0:T(8,128)S(1)} %get-tuple-element.56.refs_0_, f32[2,8,8,128]{3,2,1,0:T(8,128)S(1)} %collective-permute-done.6.refs_1_, f32[2,8,8,128]{3,2,1,0:T(8,128)S(1)} %collective-permute-done.7.refs_2_, f32[2,8,8,128]{3,2,1,0:T(8,128)S(1)} %collective-permute-done.8.refs_3_), custom_call_target="tpu_custom_call" | custom-call | tf_op jit(solution)/shard_map/fold_x/pallas_call | solution.py:634
  (3 shorter events, 0.1 us)
Async XLA Ops:
  0.6 1.2 %copy-start = (f32[64,32,128]{2,1,0:T(8,128)S(1)}, f32[64,32,128]{2,1,0:T(8,128)}, u32[]{:S(2)}) copy-start(f32[64,32,128]{2,1,0:T(8,128)} %field_ref.1) | copy-start | bytes 3145732
  1.9 10.2 %copy-start.2 = (bf16[16,8]{0,1:T(8,128)(2,1)S(1)}, bf16[16,8]{0,1:T(8,128)(2,1)}, u32[]{:S(2)}) copy-start(bf16[16,8]{0,1:T(8,128)(2,1)} %param.4) | copy-start | bytes 772
  1.9 10.3 %copy-start.1 = (bf16[16,16]{1,0:T(8,128)(2,1)S(1)}, bf16[16,16]{1,0:T(8,128)(2,1)}, u32[]{:S(2)}) copy-start(bf16[16,16]{1,0:T(8,128)(2,1)} %out_ref.1) | copy-start | bytes 1540
  2.5 4.0 %collective-permute-start = (f32[3,16,128]{2,1,0:T(8,128)S(1)}, f32[3,16,128]{2,1,0:T(8,128)S(1)}, u32[]{:S(2)}, u32[]{:S(2)}) collective-permute-start(f32[3,16,128]{2,1,0:T(8,128)S(1)} %get-tuple-element.34), channel_id=1, source_target_pairs={{0,1},{1,2},{2,3},{3,0},{4,5},{5,6},{6,7},{7,4},{8,9},{9,10},{10,1... | collective-permute-start | bytes 73736 | tf_op jit(solution)/shard_map/ppermute | solution.py:536
  3.0 3.5 %collective-permute-start.1 = (f32[3,16,128]{2,1,0:T(8,128)S(1)}, f32[3,16,128]{2,1,0:T(8,128)S(1)}, u32[]{:S(2)}, u32[]{:S(2)}) collective-permute-start(f32[3,16,128]{2,1,0:T(8,128)S(1)} %get-tuple-element.35), channel_id=1, source_target_pairs={{1,0},{2,1},{3,2},{0,3},{5,4},{6,5},{7,6},{4,7},{9,8},{10,9},{11,1... | collective-permute-start | bytes 73736 | tf_op jit(solution)/shard_map/ppermute | solution.py:536
  6.7 14.3 %collective-permute-start.2 = (f32[3,72,128]{2,1,0:T(8,128)S(1)}, f32[3,72,128]{2,1,0:T(8,128)S(1)}, u32[]{:S(2)}, u32[]{:S(2)}) collective-permute-start(f32[3,72,128]{2,1,0:T(8,128)S(1)} %get-tuple-element.37), channel_id=1, source_target_pairs={{0,4},{4,8},{8,12},{12,16},{16,20},{20,24},{24,28},{28,0},{1,5},{5... | collective-permute-start | bytes 331784 | tf_op jit(solution)/shard_map/ppermute | solution.py:536
  9.0 12.1 %collective-permute-start.3 = (f32[3,72,128]{2,1,0:T(8,128)S(1)}, f32[3,72,128]{2,1,0:T(8,128)S(1)}, u32[]{:S(2)}, u32[]{:S(2)}) collective-permute-start(f32[3,72,128]{2,1,0:T(8,128)S(1)} %get-tuple-element.38), channel_id=1, source_target_pairs={{4,0},{8,4},{12,8},{16,12},{20,16},{24,20},{28,24},{0,28},{5,1},{9... | collective-permute-start | bytes 331784 | tf_op jit(solution)/shard_map/ppermute | solution.py:536
  25.3 6.1 %collective-permute-start.4 = (f32[4,2,4,8,128]{4,3,2,1,0:T(8,128)S(1)}, f32[4,2,4,8,128]{4,3,2,1,0:T(8,128)S(1)}, u32[]{:S(2)}, u32[]{:S(2)}) collective-permute-start(f32[4,2,4,8,128]{4,3,2,1,0:T(8,128)S(1)} %get-tuple-element.47), channel_id=1, source_target_pairs={{0,4},{4,0},{8,12},{12,8},{16,20},{20,16},{24,28},{28,24},{1,5},{5... | collective-permute-start | bytes 393224 | tf_op jit(solution)/shard_map/ppermute | solution.py:540
  28.2 6.1 %collective-permute-start.5 = (f32[4,2,4,8,128]{4,3,2,1,0:T(8,128)S(1)}, f32[4,2,4,8,128]{4,3,2,1,0:T(8,128)S(1)}, u32[]{:S(2)}, u32[]{:S(2)}) collective-permute-start(f32[4,2,4,8,128]{4,3,2,1,0:T(8,128)S(1)} %get-tuple-element.55), channel_id=1, source_target_pairs={{0,4},{4,0},{8,12},{12,8},{16,20},{20,16},{24,28},{28,24},{1,5},{5... | collective-permute-start | bytes 393224 | tf_op jit(solution)/shard_map/ppermute | solution.py:540
  30.2 8.7 %collective-permute-start.9 = (f32[2,2,2,16,128]{4,3,2,1,0:T(8,128)S(1)}, f32[2,2,2,16,128]{4,3,2,1,0:T(8,128)S(1)}, u32[]{:S(2)}, u32[]{:S(2)}) collective-permute-start(f32[2,2,2,16,128]{4,3,2,1,0:T(8,128)S(1)} %get-tuple-element.61), channel_id=1, source_target_pairs={{0,1},{1,0},{2,3},{3,2},{4,5},{5,4},{6,7},{7,6},{8,9},{9,8},{10,11... | collective-permute-start | bytes 196616 | tf_op jit(solution)/shard_map/ppermute | solution.py:540
  34.4 9.5 %collective-permute-start.6 = (f32[2,8,8,128]{3,2,1,0:T(8,128)S(1)}, f32[2,8,8,128]{3,2,1,0:T(8,128)S(1)}, u32[]{:S(2)}, u32[]{:S(2)}) collective-permute-start(f32[2,8,8,128]{3,2,1,0:T(8,128)S(1)} %get-tuple-element.57), channel_id=1, source_target_pairs={{0,8},{4,12},{8,16},{12,20},{16,24},{20,28},{24,0},{28,4},{1,9},{5... | collective-permute-start | bytes 196616 | tf_op jit(solution)/shard_map/ppermute | solution.py:633
  35.0 8.9 %collective-permute-start.7 = (f32[2,8,8,128]{3,2,1,0:T(8,128)S(1)}, f32[2,8,8,128]{3,2,1,0:T(8,128)S(1)}, u32[]{:S(2)}, u32[]{:S(2)}) collective-permute-start(f32[2,8,8,128]{3,2,1,0:T(8,128)S(1)} %get-tuple-element.58), channel_id=1, source_target_pairs={{0,16},{4,20},{8,24},{12,28},{16,0},{20,4},{24,8},{28,12},{1,17},{... | collective-permute-start | bytes 196616 | tf_op jit(solution)/shard_map/ppermute | solution.py:633
  37.6 6.3 %collective-permute-start.8 = (f32[2,8,8,128]{3,2,1,0:T(8,128)S(1)}, f32[2,8,8,128]{3,2,1,0:T(8,128)S(1)}, u32[]{:S(2)}, u32[]{:S(2)}) collective-permute-start(f32[2,8,8,128]{3,2,1,0:T(8,128)S(1)} %get-tuple-element.59), channel_id=1, source_target_pairs={{0,24},{4,28},{8,0},{12,4},{16,8},{20,12},{24,16},{28,20},{1,25},{... | collective-permute-start | bytes 196616 | tf_op jit(solution)/shard_map/ppermute | solution.py:633
  39.0 4.0 %collective-permute-start.10 = (f32[1,2,2,16,128]{4,3,2,1,0:T(8,128)S(1)}, f32[1,2,2,16,128]{4,3,2,1,0:T(8,128)S(1)}, u32[]{:S(2)}, u32[]{:S(2)}) collective-permute-start(f32[1,2,2,16,128]{4,3,2,1,0:T(8,128)S(1)} %get-tuple-element.63), channel_id=1, source_target_pairs={{0,2},{1,3},{2,0},{3,1},{4,6},{5,7},{6,4},{7,5},{8,10},{9,11},{10,... | collective-permute-start | bytes 98312 | tf_op jit(solution)/shard_map/ppermute | solution.py:540

commit v8 on v7

--- a/solution.py
+++ b/solution.py
@@ -14,6 +14,7 @@
 LANES = 128
 CHUNKS = 16
 REACH = 3
+AHEAD = 2
 VMEM = pl.BlockSpec(memory_space=pltpu.VMEM)
 PARAMS = pltpu.CompilerParams(vmem_limit_bytes=36 * 1024 * 1024)
 
@@ -49,15 +50,32 @@
     return jnp.where(mask, jnp.dot(inner, right, preferred_element_type=F32), 0.0)
 
 
-def turn_kernel(field_ref, turned_ref, first_ref, last_ref):
+def is_even(axis):
+    return (lax.axis_index(axis) & 1) == 0
+
+
+def to_partners(axis, first, last):
+    even = is_even(axis)
+    return jnp.where(even, last, first), jnp.where(even, first, last)
+
+
+def from_partners(axis, peers, pair, other):
+    at, even = lax.axis_index(axis), is_even(axis)
+    before, after = jnp.where(even, other, pair), jnp.where(even, pair, other)
+    return jnp.where(at == 0, 0.0, before), jnp.where(at == peers - 1, 0.0, after)
+
+
+def turn_kernel(field_ref, pair_ref, other_ref, turned_ref):
     layers, length, width = field_ref.shape
     half = length // 2
     for k in range(half):
         turned = jnp.concatenate([field_ref[:, k, :], field_ref[:, k + half, :]], axis=0).T
         turned_ref[k, REACH : REACH + width] = turned
+        first, last = turned[:REACH], turned[width - REACH :]
+        pair, other = to_partners("by", first, last)
         for j in range(REACH):
-            first_ref[j, k : k + 1] = turned[j : j + 1]
-            last_ref[j, k : k + 1] = turned[width - REACH + j : width - REACH + j + 1]
+            pair_ref[j, k : k + 1] = pair[j : j + 1]
+            other_ref[j, k : k + 1] = other[j : j + 1]
 
 
 def spread_weights(in_ref, out_ref, win_ref, wout_ref):
@@ -77,27 +95,28 @@
     wout_ref[...] = spread(out_ref[...], left, right, mask).astype(BF16)
 
 
-def sides_kernel(width, count_y, turned_ref, before_ref, after_ref, wide_ref, first_ref, last_ref):
+def sides_kernel(
+    width, count_y, turned_ref, pair_in_ref, other_in_ref, wide_ref, pair_ref, other_ref
+):
     half, rows, _ = turned_ref.shape
     layers = LANES // 2
     part = rows // 2
     front = iota((part, LANES), 1) < layers
-    at_y = lax.axis_index("by")
-    keep_low = jnp.where(at_y == 0, 0.0, 1.0)
-    keep_high = jnp.where(at_y == count_y - 1, 0.0, 1.0)
+    befores, afters = from_partners("by", count_y, pair_in_ref[...], other_in_ref[...])
     for k in range(half):
         wide_ref[k, REACH : REACH + width] = turned_ref[k, REACH : REACH + width]
         for j in range(REACH):
             at = REACH + width + j
-            wide_ref[k, j : j + 1] = before_ref[j, k : k + 1] * keep_low
-            wide_ref[k, at : at + 1] = after_ref[j, k : k + 1] * keep_high
+            wide_ref[k, j : j + 1] = befores[j, k : k + 1]
+            wide_ref[k, at : at + 1] = afters[j, k : k + 1]
         wide_ref[k, 2 * REACH + width :] = jnp.zeros((rows - 2 * REACH - width, LANES), F32)
     for j in range(REACH):
         top, low = wide_ref[j, :part], wide_ref[j, part:]
-        first_ref[j] = jnp.where(front, top, pltpu.roll(low, layers, axis=1))
+        first = jnp.where(front, top, pltpu.roll(low, layers, axis=1))
         k = half - REACH + j
         top, low = wide_ref[k, :part], wide_ref[k, part:]
-        last_ref[j] = jnp.where(front, pltpu.roll(top, layers, axis=1), low)
+        last = jnp.where(front, pltpu.roll(top, layers, axis=1), low)
+        pair_ref[j], other_ref[j] = to_partners("bx", first, last)
 
 
 class Stencil:
@@ -145,16 +164,18 @@
             value = self.smooth(column[i], [column[i - 1], column[i + 1]] + sides)
             out[at, i - 1] = self.inside(value, y, edge)
 
-    def twice(self, once, k, out, ridge, at, edge=None):
+    def twice(self, once, k, out, ridge, slope, at, edge=None):
         column = [once[k, i] for i in range(self.run + 4)]
         for i in range(1, len(column) - 1):
             sides = [once[k - 1, i], once[k + 1, i]]
             value = self.smooth(column[i], [column[i - 1], column[i + 1]] + sides)
             value = self.inside(value, i - 2, edge)
             out[at, i - 1] = value
-            ridge[at, i - 1] = 2.0 * value + self.z_sum(value)
-
-    def features(self, twice, ridge, k, y):
+            below, above = roll(value, 1) * self.near, roll(value, -1) * self.far
+            ridge[at, i - 1] = 2.0 * value + (below + above)
+            slope[at, i - 1] = above - below
+
+    def features(self, twice, ridge, slope, k, y):
         p = lambda a, b: twice[k + a, y + 1 + b]
         r = lambda a, b: ridge[k + a, y + 1 + b]
         centre = p(0, 0)
@@ -162,8 +183,8 @@
         third = 1.0 / 3.0
         gx = (main + cross + (r(1, 0) - r(-1, 0))) * third
         gy = (main - cross + (r(0, 1) - r(0, -1))) * third
-        around = 2.0 * centre + ((p(1, 0) + p(-1, 0)) + (p(0, 1) + p(0, -1)))
-        gz = (roll(around, -1) * self.far - roll(around, 1) * self.near) * third
+        d = lambda a, b: slope[k + a, y + 1 + b]
+        gz = (2.0 * d(0, 0) + ((d(1, 0) + d(-1, 0)) + (d(0, 1) + d(0, -1)))) * third
         m = jnp.sqrt(1.0 + gx * gx + gy * gy + gz * gz)
         parts = [centre, gx, gy, gz, m, centre * m, centre * centre]
         packed = [part.astype(BF16) for part in parts] + [jnp.ones(self.shape, BF16)]
@@ -209,6 +230,7 @@
     once_out_ref,
     twice_out_ref,
     ridge_out_ref,
+    slope_out_ref,
     cx_ref,
     tx_ref,
     cy_ref,
@@ -216,26 +238,13 @@
     once_ref,
     twice_ref,
     ridge_ref,
+    slope_ref,
 ):
     half = wide_ref.shape[0]
     run = cx_ref.shape[0]
     stencil = Stencil(run, counts)
-    many_x, many_y = spans
     inner = half - 2 * REACH
     spread_weights(in_ref, out_ref, win_ref, wout_ref)
-    for k in range(inner + 4):
-        stencil.once(wide_ref, k + 1, once_ref, k)
-    for k in range(inner + 2):
-        stencil.twice(once_ref, k + 1, twice_ref, ridge_ref, k)
-    for k in range(4):
-        once_out_ref[0, k] = once_ref[k]
-        once_out_ref[1, k] = once_ref[inner + k]
-    for k in range(2):
-        twice_out_ref[0, k] = twice_ref[k]
-        twice_out_ref[1, k] = twice_ref[inner + k]
-        ridge_out_ref[0, k] = ridge_ref[k]
-        ridge_out_ref[1, k] = ridge_ref[inner + k]
-
     for k in range(run):
         tx_ref[k] = jnp.ones((LANES, LANES), F32)
         cx_ref[k] = jnp.zeros((LANES, LANES), F32)
@@ -243,12 +252,17 @@
         ty_ref[k] = jnp.ones((LANES, LANES), F32)
         cy_ref[k] = jnp.zeros((LANES, LANES), F32)
     ratio = steps[0] / steps[1]
-    down = run // many_y
-
-    def block(step):
-        x0, y0 = (step // down) * many_x, (step % down) * many_y
+
+    def prepare(first, last):
+        start = 0 if first == 0 else first + 2
+        for k in range(start, last + 2):
+            stencil.once(wide_ref, k + 1, once_ref, k)
+        for k in range(first, last):
+            stencil.twice(once_ref, k + 1, twice_ref, ridge_ref, slope_ref, k)
+
+    def block(x0, y0, many_x, many_y):
         tiles = [
-            stencil.features(twice_ref, ridge_ref, x0 + i + 1, y0 + j)
+            stencil.features(twice_ref, ridge_ref, slope_ref, x0 + i + 1, y0 + j)
             for j in range(many_y)
             for i in range(many_x)
         ]
@@ -267,8 +281,23 @@
             for i in range(many_x):
                 cy_ref[x0 + i, at], ty_ref[x0 + i, at] = rays_y[i]
 
-    for step in range(inner // many_x * down):
-        block(step)
+    many_x, many_y = spans
+    ready = 0
+    for x0 in range(0, inner, many_x):
+        ahead = min(inner + 2, x0 + many_x + 2 + AHEAD)
+        prepare(ready, ahead)
+        ready = ahead
+        for y0 in range(0, run, many_y):
+            block(x0, y0, many_x, many_y)
+    for k in range(4):
+        once_out_ref[0, k] = once_ref[k]
+        once_out_ref[1, k] = once_ref[inner + k]
+    for k in range(2):
+        for out_ref, ref in ((twice_out_ref, twice_ref), (ridge_out_ref, ridge_ref)):
+            out_ref[0, k] = ref[k]
+            out_ref[1, k] = ref[inner + k]
+        slope_out_ref[0, k] = slope_ref[k]
+        slope_out_ref[1, k] = slope_ref[inner + k]
 
 
 def parts_of(image_ref, kept_ref, sent_ref, mine):
@@ -280,7 +309,6 @@
 
 
 def march_ends(stencil, steps, first, weights, fields, middle, rays, image_ref):
-    twice_ref, ridge_ref = fields
     cx_ref, tx_ref = middle
     cy_ref, ty_ref = rays
     layers = stencil.layers
@@ -288,7 +316,7 @@
     ratio = steps[0] / steps[1]
     planes = [(0, 1), (0, 2), (0, 3), (1, 1), (1, 2), (1, 3)]
     tiles = [
-        stencil.features(twice_ref.at[side], ridge_ref.at[side], k, first + j)
+        stencil.features(*[ref.at[side] for ref in fields], k, first + j)
         for j in range(many_y)
         for side, k in planes
     ]
@@ -325,17 +353,19 @@
     counts,
     steps,
     wide_ref,
-    before_ref,
-    after_ref,
+    pair_ref,
+    other_ref,
     win_ref,
     wout_ref,
     once_in_ref,
     twice_in_ref,
     ridge_in_ref,
+    slope_in_ref,
     cx_ref,
     tx_ref,
     twice_ref,
     ridge_ref,
+    slope_ref,
     cy_ref,
     ty_ref,
     kept_ref,
@@ -351,13 +381,12 @@
     part = rows // 2
     front = iota((part, LANES), 1) < layers
     at_x = lax.axis_index("bx")
-    keep_low = jnp.where(at_x == 0, 0.0, 1.0)
-    keep_high = jnp.where(at_x == counts[0] - 1, 0.0, 1.0)
     for j in range(REACH):
-        halo, own = before_ref[j] * keep_low, wide_ref[half - REACH + j]
+        before, after = from_partners("bx", counts[0], pair_ref[j], other_ref[j])
+        halo, own = before, wide_ref[half - REACH + j]
         raw_ref[0, j, :part] = jnp.where(front, halo, roll(own[:part], layers))
         raw_ref[0, j, part:] = jnp.where(front, roll(halo, layers), roll(own[part:], layers))
-        halo, own = after_ref[j] * keep_high, wide_ref[j]
+        halo, own = after, wide_ref[j]
         raw_ref[1, 2 + j, :part] = jnp.where(front, roll(own[:part], layers), roll(halo, layers))
         raw_ref[1, 2 + j, part:] = jnp.where(front, roll(own[part:], layers), halo)
     for j in range(2):
@@ -371,6 +400,8 @@
         twice_ref[1, k] = twice_in_ref[1, k]
         ridge_ref[0, 3 + k] = ridge_in_ref[0, k]
         ridge_ref[1, k] = ridge_in_ref[1, k]
+        slope_ref[0, 3 + k] = slope_in_ref[0, k]
+        slope_ref[1, k] = slope_in_ref[1, k]
     for side, edge in enumerate((stencil.x_low, stencil.x_high)):
         outside = (0, 1) if side == 0 else (1, 2)
         for k in range(3):
@@ -380,7 +411,8 @@
         for k in range(3):
             kept = edge if k == 2 * side else None
             at = k + 2 * side
-            stencil.twice(once_ref.at[side], at + 1, twice_ref.at[side], ridge_ref.at[side], at, kept)
+            outs = [ref.at[side] for ref in (twice_ref, ridge_ref, slope_ref)]
+            stencil.twice(once_ref.at[side], at + 1, *outs, at, kept)
     for k in range(2 * REACH):
         ty_ref[k] = jnp.ones((LANES, LANES), F32)
         cy_ref[k] = jnp.zeros((LANES, LANES), F32)
@@ -389,7 +421,7 @@
         steps,
         0,
         (win_ref, wout_ref),
-        (twice_ref, ridge_ref),
+        (twice_ref, ridge_ref, slope_ref),
         (cx_ref, tx_ref),
         (cy_ref, ty_ref),
         image_ref,
@@ -404,6 +436,7 @@
     wout_ref,
     twice_ref,
     ridge_ref,
+    slope_ref,
     cx_ref,
     tx_ref,
     cy_in_ref,
@@ -430,7 +463,7 @@
         steps,
         run - image_ref.shape[1],
         (win_ref, wout_ref),
-        (twice_ref, ridge_ref),
+        (twice_ref, ridge_ref, slope_ref),
         (cx_ref, tx_ref),
         (cy_ref, ty_ref),
         image_ref,
@@ -485,36 +518,37 @@
             out_sent_ref[r, kind] = jnp.where(bit, even, odd)
 
 
-def merge_x_kernel(*refs):
-    ins, outs = refs[:4], refs[4:]
-    many, _, some, _, _ = ins[0].shape
+def merge_x_kernel(kept_ref, received_ref, *refs):
+    many, _, some, _, _ = kept_ref.shape
+    outs = refs[-many:]
     at = lax.axis_index("bx")
     later = (at & 1) == 1
-    for i in range(2):
-        kept_ref, received_ref = ins[2 * i], ins[2 * i + 1]
-        for t in range(many):
-            r = lax.rem((at >> 1) + t, many)
-            kept, received = kept_ref[r], received_ref[r]
-            front = jnp.where(later, received, kept)
-            back = jnp.where(later, kept, received)
-            outs[t][0, i * some : (i + 1) * some] = front[0] + front[1] * back[0]
-            outs[t][1, i * some : (i + 1) * some] = front[1] * back[1]
+    for t in range(many):
+        r = lax.rem((at >> 1) + t, many)
+        kept, received = kept_ref[r], received_ref[r]
+        front = jnp.where(later, received, kept)
+        back = jnp.where(later, kept, received)
+        outs[t][0] = front[0] + front[1] * back[0]
+        outs[t][1] = front[1] * back[1]
 
 
 def fold_x_kernel(*refs):
-    pieces, out_ref = refs[:-1], refs[-1]
-    _, run, share, _ = pieces[0].shape
+    out_ref = refs[-1]
+    many = (len(refs) - 1) // 2
+    _, some, share, _ = refs[0].shape
+    run = 2 * some
     lane = iota((share, LANES), 1)
     me = lax.axis_index("bx") >> 1
     kinds = [[], []]
     for y in range(run):
+        pieces = refs[(y // some) * many :][:many]
         behind = colour, clear = jnp.zeros((share, LANES), F32), jnp.ones((share, LANES), F32)
-        for s in reversed(range(len(pieces))):
+        for s in reversed(range(many)):
             start = me == s
             behind = jnp.where(start, colour, behind[0]), jnp.where(start, clear, behind[1])
             colour, clear = jnp.where(start, 0.0, colour), jnp.where(start, 1.0, clear)
-            colour = colour + clear * pieces[s][0, y]
-            clear = clear * pieces[s][1, y]
+            colour = colour + clear * pieces[s][0, y % some]
+            clear = clear * pieces[s][1, y % some]
         kinds[0].append(colour + clear * behind[0])
         kinds[1].append(clear * behind[1])
     for kind, values in enumerate(kinds):
@@ -529,11 +563,12 @@
             out_ref[kind, band] = value
 
 
-def exchange(last, first, axis):
+def exchange(pair, other, axis, around):
     peers = lax.axis_size(axis)
-    up = [(i, (i + 1) % peers) for i in range(peers)]
-    down = [(j, i) for i, j in up]
-    return lax.ppermute(last, axis, up), lax.ppermute(first, axis, down)
+    sides = [(i, (i + 1) % peers if i & 1 else (i - 1) % peers) for i in range(peers)]
+    if not around:
+        sides = [(i, i) if i in (0, peers - 1) else (i, j) for i, j in sides]
+    return swap(pair, axis, 1), lax.ppermute(other, axis, sides)
 
 
 def swap(value, axis, bit):
@@ -555,28 +590,29 @@
     ]
 
     edge = sds(REACH, half, LANES)
-    turned, first, last = call(turn_kernel, "turn", [sds(half, rows, LANES), edge, edge], 1)(
+    pair, other, turned = call(turn_kernel, "turn", [edge, edge, sds(half, rows, LANES)], 1)(
         scalar_field
     )
-    before, after = exchange(last, first, "by")
+    pair, other = exchange(pair, other, "by", True)
     edge = sds(REACH, rows // 2, LANES)
-    wide, first, last = call(
+    wide, pair, other = call(
         functools.partial(sides_kernel, local_y, count_y), "sides", [sds(half, rows, LANES), edge, edge], 3
-    )(turned, before, after)
-    before, after = exchange(last, first, "bx")
+    )(turned, pair, other)
+    pair, other = exchange(pair, other, "bx", False)
     inner = half - 2 * REACH
     counts = (count_x, count_y)
     plane = lambda *lead: sds(*lead, CHUNKS, LANES)
     many_x, many_y = inner, 2
-    win, wout, once, twice, ridge, colour_x, clear_x, colour_y, clear_y = call(
+    win, wout, once, twice, ridge, slope, colour_x, clear_x, colour_y, clear_y = call(
         functools.partial(middle_kernel, (many_x, many_y), counts, steps),
         "middle",
-        weights + [plane(2, 4, run + 4), plane(2, 2, run + 2), plane(2, 2, run + 2)]
+        weights + [plane(2, 4, run + 4)] + [plane(2, 2, run + 2)] * 3
         + [sds(run, LANES, LANES)] * 2
         + [sds(inner, LANES, LANES)] * 2,
         3,
         [
             pltpu.VMEM((inner + 4, run + 4, CHUNKS, LANES), F32),
+            pltpu.VMEM((inner + 2, run + 2, CHUNKS, LANES), F32),
             pltpu.VMEM((inner + 2, run + 2, CHUNKS, LANES), F32),
             pltpu.VMEM((inner + 2, run + 2, CHUNKS, LANES), F32),
         ],
@@ -588,23 +624,23 @@
     image = pltpu.VMEM((2, run // 2, layers, LANES), F32)
     ray = pltpu.VMEM((2 * REACH, LANES, LANES), F32)
     field = plane(2, 5, run + 2)
-    twice, ridge, colour_ends, clear_ends, kept, sent = call(
+    twice, ridge, slope, colour_ends, clear_ends, kept, sent = call(
         functools.partial(ends_first_kernel, counts, steps),
         "ends_first",
-        [field] * 2 + [sds(2 * REACH, LANES, LANES)] * 2 + [parts] * 2,
-        10,
+        [field] * 3 + [sds(2 * REACH, LANES, LANES)] * 2 + [parts] * 2,
+        11,
         [
             image,
             pltpu.VMEM((2, 5, rows, LANES), F32),
             pltpu.VMEM((2, 7, run + 4, CHUNKS, LANES), F32),
         ],
-    )(wide, before, after, win, wout, once, twice, ridge, colour_x, clear_x)
-    halves = [kept, swap(sent, "bx", 1)]
+    )(wide, pair, other, win, wout, once, twice, ridge, slope, colour_x, clear_x)
+    halves = [(kept, swap(sent, "bx", 1))]
     kept, sent, kept_y, sent_y = call(
         functools.partial(ends_last_kernel, counts, steps),
         "ends_last",
         [parts] * 2 + [parts_y] * 2,
-        10,
+        11,
         [
             image,
             ray,
@@ -612,9 +648,21 @@
             pltpu.VMEM((2, LANES, LANES), F32),
             pltpu.VMEM((2, 2, layers, LANES), F32),
         ],
-    )(win, wout, twice, ridge, colour_x, clear_x, colour_ends, clear_ends, colour_y, clear_y)
-    halves += [kept, swap(sent, "bx", 1)]
-
+    )(
+        win, wout, twice, ridge, slope, colour_x, clear_x, colour_ends, clear_ends, colour_y, clear_y
+    )
+    halves += [(kept, swap(sent, "bx", 1))]
+
+    def send_round(*operands):
+        many = count_x // 2
+        piece = sds(2, run // 2, share, LANES)
+        pieces = list(call(merge_x_kernel, "merge_x", [piece] * many, len(operands))(*operands))
+        for t in range(1, many):
+            pairs = [(i, (i + 2 * t) % count_x) for i in range(count_x)]
+            pieces[t] = lax.ppermute(pieces[t], "bx", pairs)
+        return pieces
+
+    pieces = send_round(*halves[0])
     level, many = 1, count_y // 2
     while many:
         received = swap(sent_y, "by", level)
@@ -625,13 +673,8 @@
         else:
             view_y = call(merge, "merge", sds(2, 2, share_y, LANES), 2)(kept_y, received)
         level, many = 2 * level, many // 2
-    many = count_x // 2
-    piece = sds(2, run, share, LANES)
-    pieces = list(call(merge_x_kernel, "merge_x", [piece] * many, 4)(*halves))
-    for t in range(1, many):
-        pairs = [(i, (i + 2 * t) % count_x) for i in range(count_x)]
-        pieces[t] = lax.ppermute(pieces[t], "bx", pairs)
-    view_x = call(fold_x_kernel, "fold_x", sds(2, bands, share, local_y), many)(*pieces)
+    pieces += send_round(*halves[1], sent_y)
+    view_x = call(fold_x_kernel, "fold_x", sds(2, bands, share, local_y), count_x)(*pieces)
     view_y = view_y.reshape(2, 2, share_y, half, bands)
     view_y = jnp.transpose(view_y, (0, 4, 2, 1, 3)).reshape(2, bands, share_y, local_x)
     return (view_x, view_y)

time: 45 us -> 44.7 us (level)
  starting transfers between devices: 16 us -> 21.1 us
  waiting for transfers between devices: 8.23 us -> 4.23 us
  Pallas kernels: 17.6 us -> 16.3 us
    ppermute x4 -> x6, waiting for transfers between devices: 6.69 us -> 1.25 us  [swap(): lax.ppermute(value, axis, [(i, i ^ bit) for i in range(lax.axis_size(axis...]
    ppermute x4 -> x6, starting transfers between devices: 3.51 us -> 8.32 us  [swap(): lax.ppermute(value, axis, [(i, i ^ bit) for i in range(lax.axis_size(axis...]
    ppermute x7 -> x8, waiting for transfers between devices: 1.54 us -> 2.97 us  [the longest x2 1.52 us: exchange(): return (swap(pair, axis, 1), lax.ppermute(other, axis, sides))]
    pallas_call x1, Pallas kernels: 4.23 us -> 3.18 us  [body(): call(functools.partial(ends_first_kernel, counts, steps), 'ends_first', [...]
    ppermute x7 -> x8, starting transfers between devices: 12.5 us -> 12.8 us  [the longest x6 9.49 us: send_round(): pieces[t] = lax.ppermute(pieces[t], 'bx', pairs)]
    pallas_call x3 -> x4, Pallas kernels: 1.57 us -> 1.57 us  [the longest x1 0.89 us: body(): call(fold_x_kernel, 'fold_x', sds(2, bands, share, local_y), count_x)]
  transfers between devices with their start and end apart: 11 -> 14, of which waited for: 5 -> 4; matrix products, arithmetic and copies ran while one was open for 2% -> 2% of each run, Pallas kernels for 26% -> 26%
where the time goes in v8:
time: 44.7 us; the launch traced here: 44.6 us
  starting transfers between devices  21.1 us (47%)
  Pallas kernels  16.3 us (36%)
  waiting for transfers between devices  4.23 us (9%)
  local copies, waits for them, and re-layouts  2.23 us (5%)
  between operations  0.74 us (2%)
    ppermute x6, starting transfers between devices, send_round(): pieces[t] = lax.ppermute(pieces[t], 'bx', pairs)  9.49 us
    pallas_call x1, Pallas kernels, body(): call(functools.partial(middle_kernel, (many_x, many_y), counts, steps), '...  8.69 us
    ppermute x6, starting transfers between devices, swap(): lax.ppermute(value, axis, [(i, i ^ bit) for i in range(lax.axis_size(axis...  8.32 us
    ppermute x2, starting transfers between devices, exchange(): return (swap(pair, axis, 1), lax.ppermute(other, axis, sides))  3.3 us
    pallas_call x1, Pallas kernels, body(): call(functools.partial(ends_first_kernel, counts, steps), 'ends_first', [...  3.18 us
    pallas_call x1, Pallas kernels, body(): call(functools.partial(ends_last_kernel, counts, steps), 'ends_last', [pa...  2.64 us
    unnamed x8, local copies, waits for them, and re-layouts  2.11 us
    ppermute x2, waiting for transfers between devices, exchange(): return (swap(pair, axis, 1), lax.ppermute(other, axis, sides))  1.52 us
  transfers between devices with their start and end apart: 14, of which 4 were waited for; matrix products, arithmetic and copies ran while one was open for 2% of the time, Pallas kernels for 26%

profile of v8, /device:TPU:0, one launch (start us, length us, event | category | flops | bytes accessed | tf_op | source)
XLA Modules:
  0.0 44.6 jit_solution(10494579222418758857)
XLA Ops:
  0.6 0.0 copy-start
  0.6 1.2 %copy-done = f32[64,32,128]{2,1,0:T(8,128)S(1)} copy-done((f32[64,32,128]{2,1,0:T(8,128)S(1)}, f32[64,32,128]{2,1,0:T(8,128)}, u32[]{:S(2)}) %copy-start) | copy-done | bytes 1048600
  1.9 0.0 copy-start.2
  1.9 0.0 copy-start.1
  1.9 0.6 %turn.1 = (f32[3,16,128]{2,1,0:T(8,128)S(1)}, f32[3,16,128]{2,1,0:T(8,128)S(1)}, f32[16,144,128]{2,1,0:T(8,128)S(1)}) custom-call(f32[64,32,128]{2,1,0:T(8,128)S(1)} %copy-done), custom_call_target="tpu_custom_call" | custom-call | tf_op jit(solution)/shard_map/turn/pallas_call | solution.py:593
  2.5 0.5 %collective-permute-start = (f32[3,16,128]{2,1,0:T(8,128)S(1)}, f32[3,16,128]{2,1,0:T(8,128)S(1)}, u32[]{:S(2)}, u32[]{:S(2)}) collective-permute-start(f32[3,16,128]{2,1,0:T(8,128)S(1)} %get-tuple-element.40), channel_id=1, source_target_pairs={{0,1},{1,0},{2,3},{3,2},{4,5},{5,4},{6,7},{7,6},{8,9},{9,8},{10,11... | collective-permute-start | bytes 73736 | tf_op jit(solution)/shard_map/ppermute | solution.py:575
  3.0 2.6 %collective-permute-start.1 = (f32[3,16,128]{2,1,0:T(8,128)S(1)}, f32[3,16,128]{2,1,0:T(8,128)S(1)}, u32[]{:S(2)}, u32[]{:S(2)}) collective-permute-start(f32[3,16,128]{2,1,0:T(8,128)S(1)} %get-tuple-element.41), channel_id=1, source_target_pairs={{0,3},{1,2},{2,1},{3,0},{4,7},{5,6},{6,5},{7,4},{8,11},{9,10},{10,... | collective-permute-start | bytes 73736 | tf_op jit(solution)/shard_map/ppermute | solution.py:571
  5.7 0.0 collective-permute-done.pair_in_ref
  5.7 1.5 %collective-permute-done.1.other_in_ref = f32[3,16,128]{2,1,0:T(8,128)S(1)} collective-permute-done((f32[3,16,128]{2,1,0:T(8,128)S(1)}, f32[3,16,128]{2,1,0:T(8,128)S(1)}, u32[]{:S(2)}, u32[]{:S(2)}) %collective-permute-start.1) | collective-permute-done | bytes 24608 | tf_op jit(solution)/shard_map/ppermute | solution.py:571
  7.2 0.1 sides.1
  7.3 1.7 %collective-permute-start.2 = (f32[3,72,128]{2,1,0:T(8,128)S(1)}, f32[3,72,128]{2,1,0:T(8,128)S(1)}, u32[]{:S(2)}, u32[]{:S(2)}) collective-permute-start(f32[3,72,128]{2,1,0:T(8,128)S(1)} %get-tuple-element.43), channel_id=1, source_target_pairs={{0,4},{4,0},{8,12},{12,8},{16,20},{20,16},{24,28},{28,24},{1,5},{5... | collective-permute-start | bytes 331784 | tf_op jit(solution)/shard_map/ppermute | solution.py:575
  9.1 0.7 %collective-permute-start.3 = (f32[3,72,128]{2,1,0:T(8,128)S(1)}, f32[3,72,128]{2,1,0:T(8,128)S(1)}, u32[]{:S(2)}, u32[]{:S(2)}) collective-permute-start(f32[3,72,128]{2,1,0:T(8,128)S(1)} %get-tuple-element.44), channel_id=1, source_target_pairs={{0,0},{4,8},{8,4},{12,16},{16,12},{20,24},{24,20},{28,28},{1,1},{5... | collective-permute-start | bytes 331784 | tf_op jit(solution)/shard_map/ppermute | solution.py:571
  9.7 0.0 copy-done.2
  9.7 0.1 copy.7.in_ref
  9.8 0.0 copy-done.1
  9.8 8.7 %middle.1 = (bf16[128,256]{1,0:T(8,128)(2,1)S(1)}, bf16[256,256]{1,0:T(8,128)(2,1)S(1)}, f32[2,4,12,16,128]{4,3,2,1,0:T(8,128)S(1)}, f32[2,2,10,16,128]{4,3,2,1,...) custom-call(f32[16,144,128]{2,1,0:T(8,128)S(1)} %get-tuple-element.4, ...), custom_call_target="tpu_custom_call" | custom-call | tf_op jit(solution)/shard_map/middle/pallas_call | solution.py:606
  18.5 0.0 collective-permute-done.2.pair_ref
  18.5 0.0 collective-permute-done.3.other_ref
  18.5 3.2 %ends_first.1 = (f32[2,5,10,16,128]{4,3,2,1,0:T(8,128)S(1)}, f32[2,5,10,16,128]{4,3,2,1,0:T(8,128)S(1)}, f32[2,5,10,16,128]{4,3,2,1,0:T(8,128)S(1)}, f32[6,128,1...) custom-call(f32[16,144,128]{2,1,0:T(8,128)S(1)} %get-tuple-element.4, ...), custom_call_target="tpu_custom_call" | custom-call | tf_op jit(solution)/shard_map/ends_first/pallas_call | solution.py:627
  21.7 4.3 %collective-permute-start.4 = (f32[4,2,4,8,128]{4,3,2,1,0:T(8,128)S(1)}, f32[4,2,4,8,128]{4,3,2,1,0:T(8,128)S(1)}, u32[]{:S(2)}, u32[]{:S(2)}) collective-permute-start(f32[4,2,4,8,128]{4,3,2,1,0:T(8,128)S(1)} %get-tuple-element.54), channel_id=1, source_target_pairs={{0,4},{4,0},{8,12},{12,8},{16,20},{20,16},{24,28},{28,24},{1,5},{5... | collective-permute-start | bytes 393224 | tf_op jit(solution)/shard_map/ppermute | solution.py:575
  26.1 2.6 %ends_last.1 = (f32[4,2,4,8,128]{4,3,2,1,0:T(8,128)S(1)}, f32[4,2,4,8,128]{4,3,2,1,0:T(8,128)S(1)}, f32[2,2,2,16,128]{4,3,2,1,0:T(8,128)S(1)}, f32[2,2,2,16,128]{4,3,2,1,0:T(8,128)S(1)}) custom-call(bf16[128,256]{1,0:T(8,128)(2,1)S(1)} %get-tuple-element.45.win_ref, bf16[256,256]{1,0:T(8,128)(2,1)S(1)} %get-tuple-element.46.wout_ref, ...), custom_call_target="tpu_custom_call" | custom-call | tf_op jit(solution)/shard_map/ends_last/pallas_call | solution.py:639
  28.7 0.1 collective-permute-start.8
  28.8 0.1 collective-permute-start.9
  28.9 1.2 %collective-permute-done.9.received_ref = f32[2,2,2,16,128]{4,3,2,1,0:T(8,128)S(1)} collective-permute-done((f32[2,2,2,16,128]{4,3,2,1,0:T(8,128)S(1)}, f32[2,2,2,16,128]{4,3,2,1,0:T(8,128)S(1)}, u32[]{:S(2)}, u32[]{:S(2)}) %collective-permute-start.9) | collective-permute-done | bytes 65568 | tf_op jit(solution)/shard_map/ppermute | solution.py:575
  30.1 1.6 %collective-permute-start.13 = (f32[1,2,2,16,128]{4,3,2,1,0:T(8,128)S(1)}, f32[1,2,2,16,128]{4,3,2,1,0:T(8,128)S(1)}, u32[]{:S(2)}, u32[]{:S(2)}) collective-permute-start(f32[1,2,2,16,128]{4,3,2,1,0:T(8,128)S(1)} %get-tuple-element.70.refs_0_), channel_id=1, source_target_pairs={{0,2},{1,3},{2,0},{3,1},{4,6},{5,7},{6,4},{7,5},{8,10},{9,11},{10,... | collective-permute-start | bytes 98312 | tf_op jit(solution)/shard_map/ppermute | solution.py:575
  31.7 0.0 collective-permute-done.4.received_ref
  31.8 1.6 %collective-permute-start.5 = (f32[2,4,8,128]{3,2,1,0:T(8,128)S(1)}, f32[2,4,8,128]{3,2,1,0:T(8,128)S(1)}, u32[]{:S(2)}, u32[]{:S(2)}) collective-permute-start(f32[2,4,8,128]{3,2,1,0:T(8,128)S(1)} %get-tuple-element.56), channel_id=1, source_target_pairs={{0,8},{4,12},{8,16},{12,20},{16,24},{20,28},{24,0},{28,4},{1,9},{5... | collective-permute-start | bytes 98312 | tf_op jit(solution)/shard_map/ppermute | solution.py:662
  33.4 1.9 %collective-permute-start.6 = (f32[2,4,8,128]{3,2,1,0:T(8,128)S(1)}, f32[2,4,8,128]{3,2,1,0:T(8,128)S(1)}, u32[]{:S(2)}, u32[]{:S(2)}) collective-permute-start(f32[2,4,8,128]{3,2,1,0:T(8,128)S(1)} %get-tuple-element.57), channel_id=1, source_target_pairs={{0,16},{4,20},{8,24},{12,28},{16,0},{20,4},{24,8},{28,12},{1,17},{... | collective-permute-start | bytes 98312 | tf_op jit(solution)/shard_map/ppermute | solution.py:662
  35.3 2.0 %collective-permute-start.7 = (f32[2,4,8,128]{3,2,1,0:T(8,128)S(1)}, f32[2,4,8,128]{3,2,1,0:T(8,128)S(1)}, u32[]{:S(2)}, u32[]{:S(2)}) collective-permute-start(f32[2,4,8,128]{3,2,1,0:T(8,128)S(1)} %get-tuple-element.58), channel_id=1, source_target_pairs={{0,24},{4,28},{8,0},{12,4},{16,8},{20,12},{24,16},{28,20},{1,25},{... | collective-permute-start | bytes 98312 | tf_op jit(solution)/shard_map/ppermute | solution.py:662
  37.3 0.0 collective-permute-done.8.received_ref
  37.4 0.1 collective-permute-start.10
  37.4 0.0 collective-permute-done.13.received_ref
  37.4 1.0 %collective-permute-start.11 = (f32[2,4,8,128]{3,2,1,0:T(8,128)S(1)}, f32[2,4,8,128]{3,2,1,0:T(8,128)S(1)}, u32[]{:S(2)}, u32[]{:S(2)}) collective-permute-start(f32[2,4,8,128]{3,2,1,0:T(8,128)S(1)} %get-tuple-element.73), channel_id=1, source_target_pairs={{0,16},{4,20},{8,24},{12,28},{16,0},{20,4},{24,8},{28,12},{1,17},{... | collective-permute-start | bytes 98312 | tf_op jit(solution)/shard_map/ppermute | solution.py:662
  38.4 0.0 collective-permute-done.5.refs_1_
  38.4 2.9 %collective-permute-start.12 = (f32[2,4,8,128]{3,2,1,0:T(8,128)S(1)}, f32[2,4,8,128]{3,2,1,0:T(8,128)S(1)}, u32[]{:S(2)}, u32[]{:S(2)}) collective-permute-start(f32[2,4,8,128]{3,2,1,0:T(8,128)S(1)} %get-tuple-element.74), channel_id=1, source_target_pairs={{0,24},{4,28},{8,0},{12,4},{16,8},{20,12},{24,16},{28,20},{1,25},{... | collective-permute-start | bytes 98312 | tf_op jit(solution)/shard_map/ppermute | solution.py:662
  41.3 0.1 copy.8
  41.4 0.8 %copy.9 = f32[2,8,16,32]{3,2,1,0:T(8,128)} copy(f32[2,8,16,32]{2,1,3,0:T(8,128)S(1)} %bitcast.5) | data formatting | bytes 65536
  42.2 0.0 collective-permute-done.6.refs_2_
  42.2 0.0 collective-permute-done.7.refs_3_
  42.2 0.9 %collective-permute-done.10.refs_5_ = f32[2,4,8,128]{3,2,1,0:T(8,128)S(1)} collective-permute-done((f32[2,4,8,128]{3,2,1,0:T(8,128)S(1)}, f32[2,4,8,128]{3,2,1,0:T(8,128)S(1)}, u32[]{:S(2)}, u32[]{:S(2)}) %collective-permute-start.10) | collective-permute-done | bytes 32800 | tf_op jit(solution)/shard_map/ppermute | solution.py:662
  43.1 0.0 collective-permute-done.11.refs_6_
  43.1 0.6 %collective-permute-done.12.refs_7_ = f32[2,4,8,128]{3,2,1,0:T(8,128)S(1)} collective-permute-done((f32[2,4,8,128]{3,2,1,0:T(8,128)S(1)}, f32[2,4,8,128]{3,2,1,0:T(8,128)S(1)}, u32[]{:S(2)}, u32[]{:S(2)}) %collective-permute-start.12) | collective-permute-done | bytes 32800 | tf_op jit(solution)/shard_map/ppermute | solution.py:662
  43.7 0.9 %fold_x.1 = f32[2,8,8,128]{3,2,1,0:T(8,128)} custom-call(f32[2,4,8,128]{3,2,1,0:T(8,128)S(1)} %get-tuple-element.55.refs_0_, f32[2,4,8,128]{3,2,1,0:T(8,128)S(1)} %collective-permute-done.5.refs_1_, f32[2,4,8,128]{3,2,1,0:T(8,128)S(1)} %collective-permute-done.6.refs_2_, f32[2,4,8,128]{3,2,1,0:T(8,128)S(1)} %collective-permute-done.7.refs_3_, ...), custom_call_target="tpu_custom_call" | custom-call | tf_op jit(solution)/shard_map/fold_x/pallas_call | solution.py:677
  (4 shorter events, 0.1 us)
Async XLA Ops:
  0.6 1.2 %copy-start = (f32[64,32,128]{2,1,0:T(8,128)S(1)}, f32[64,32,128]{2,1,0:T(8,128)}, u32[]{:S(2)}) copy-start(f32[64,32,128]{2,1,0:T(8,128)} %field_ref.1) | copy-start | bytes 3145732
  1.9 7.9 %copy-start.2 = (bf16[16,8]{0,1:T(8,128)(2,1)S(1)}, bf16[16,8]{0,1:T(8,128)(2,1)}, u32[]{:S(2)}) copy-start(bf16[16,8]{0,1:T(8,128)(2,1)} %param.4) | copy-start | bytes 772
  1.9 8.0 %copy-start.1 = (bf16[16,16]{1,0:T(8,128)(2,1)S(1)}, bf16[16,16]{1,0:T(8,128)(2,1)}, u32[]{:S(2)}) copy-start(bf16[16,16]{1,0:T(8,128)(2,1)} %out_ref.1) | copy-start | bytes 1540
  2.5 3.2 %collective-permute-start = (f32[3,16,128]{2,1,0:T(8,128)S(1)}, f32[3,16,128]{2,1,0:T(8,128)S(1)}, u32[]{:S(2)}, u32[]{:S(2)}) collective-permute-start(f32[3,16,128]{2,1,0:T(8,128)S(1)} %get-tuple-element.40), channel_id=1, source_target_pairs={{0,1},{1,0},{2,3},{3,2},{4,5},{5,4},{6,7},{7,6},{8,9},{9,8},{10,11... | collective-permute-start | bytes 73736 | tf_op jit(solution)/shard_map/ppermute | solution.py:575
  3.0 4.2 %collective-permute-start.1 = (f32[3,16,128]{2,1,0:T(8,128)S(1)}, f32[3,16,128]{2,1,0:T(8,128)S(1)}, u32[]{:S(2)}, u32[]{:S(2)}) collective-permute-start(f32[3,16,128]{2,1,0:T(8,128)S(1)} %get-tuple-element.41), channel_id=1, source_target_pairs={{0,3},{1,2},{2,1},{3,0},{4,7},{5,6},{6,5},{7,4},{8,11},{9,10},{10,... | collective-permute-start | bytes 73736 | tf_op jit(solution)/shard_map/ppermute | solution.py:571
  7.3 11.2 %collective-permute-start.2 = (f32[3,72,128]{2,1,0:T(8,128)S(1)}, f32[3,72,128]{2,1,0:T(8,128)S(1)}, u32[]{:S(2)}, u32[]{:S(2)}) collective-permute-start(f32[3,72,128]{2,1,0:T(8,128)S(1)} %get-tuple-element.43), channel_id=1, source_target_pairs={{0,4},{4,0},{8,12},{12,8},{16,20},{20,16},{24,28},{28,24},{1,5},{5... | collective-permute-start | bytes 331784 | tf_op jit(solution)/shard_map/ppermute | solution.py:575
  9.1 9.5 %collective-permute-start.3 = (f32[3,72,128]{2,1,0:T(8,128)S(1)}, f32[3,72,128]{2,1,0:T(8,128)S(1)}, u32[]{:S(2)}, u32[]{:S(2)}) collective-permute-start(f32[3,72,128]{2,1,0:T(8,128)S(1)} %get-tuple-element.44), channel_id=1, source_target_pairs={{0,0},{4,8},{8,4},{12,16},{16,12},{20,24},{24,20},{28,28},{1,1},{5... | collective-permute-start | bytes 331784 | tf_op jit(solution)/shard_map/ppermute | solution.py:571
  21.7 10.0 %collective-permute-start.4 = (f32[4,2,4,8,128]{4,3,2,1,0:T(8,128)S(1)}, f32[4,2,4,8,128]{4,3,2,1,0:T(8,128)S(1)}, u32[]{:S(2)}, u32[]{:S(2)}) collective-permute-start(f32[4,2,4,8,128]{4,3,2,1,0:T(8,128)S(1)} %get-tuple-element.54), channel_id=1, source_target_pairs={{0,4},{4,0},{8,12},{12,8},{16,20},{20,16},{24,28},{28,24},{1,5},{5... | collective-permute-start | bytes 393224 | tf_op jit(solution)/shard_map/ppermute | solution.py:575
  28.7 8.6 %collective-permute-start.8 = (f32[4,2,4,8,128]{4,3,2,1,0:T(8,128)S(1)}, f32[4,2,4,8,128]{4,3,2,1,0:T(8,128)S(1)}, u32[]{:S(2)}, u32[]{:S(2)}) collective-permute-start(f32[4,2,4,8,128]{4,3,2,1,0:T(8,128)S(1)} %get-tuple-element.67), channel_id=1, source_target_pairs={{0,4},{4,0},{8,12},{12,8},{16,20},{20,16},{24,28},{28,24},{1,5},{5... | collective-permute-start | bytes 393224 | tf_op jit(solution)/shard_map/ppermute | solution.py:575
  28.8 1.3 %collective-permute-start.9 = (f32[2,2,2,16,128]{4,3,2,1,0:T(8,128)S(1)}, f32[2,2,2,16,128]{4,3,2,1,0:T(8,128)S(1)}, u32[]{:S(2)}, u32[]{:S(2)}) collective-permute-start(f32[2,2,2,16,128]{4,3,2,1,0:T(8,128)S(1)} %get-tuple-element.69), channel_id=1, source_target_pairs={{0,1},{1,0},{2,3},{3,2},{4,5},{5,4},{6,7},{7,6},{8,9},{9,8},{10,11... | collective-permute-start | bytes 196616 | tf_op jit(solution)/shard_map/ppermute | solution.py:575
  30.1 7.3 %collective-permute-start.13 = (f32[1,2,2,16,128]{4,3,2,1,0:T(8,128)S(1)}, f32[1,2,2,16,128]{4,3,2,1,0:T(8,128)S(1)}, u32[]{:S(2)}, u32[]{:S(2)}) collective-permute-start(f32[1,2,2,16,128]{4,3,2,1,0:T(8,128)S(1)} %get-tuple-element.70.refs_0_), channel_id=1, source_target_pairs={{0,2},{1,3},{2,0},{3,1},{4,6},{5,7},{6,4},{7,5},{8,10},{9,11},{10,... | collective-permute-start | bytes 98312 | tf_op jit(solution)/shard_map/ppermute | solution.py:575
  31.8 6.7 %collective-permute-start.5 = (f32[2,4,8,128]{3,2,1,0:T(8,128)S(1)}, f32[2,4,8,128]{3,2,1,0:T(8,128)S(1)}, u32[]{:S(2)}, u32[]{:S(2)}) collective-permute-start(f32[2,4,8,128]{3,2,1,0:T(8,128)S(1)} %get-tuple-element.56), channel_id=1, source_target_pairs={{0,8},{4,12},{8,16},{12,20},{16,24},{20,28},{24,0},{28,4},{1,9},{5... | collective-permute-start | bytes 98312 | tf_op jit(solution)/shard_map/ppermute | solution.py:662
  33.4 8.9 %collective-permute-start.6 = (f32[2,4,8,128]{3,2,1,0:T(8,128)S(1)}, f32[2,4,8,128]{3,2,1,0:T(8,128)S(1)}, u32[]{:S(2)}, u32[]{:S(2)}) collective-permute-start(f32[2,4,8,128]{3,2,1,0:T(8,128)S(1)} %get-tuple-element.57), channel_id=1, source_target_pairs={{0,16},{4,20},{8,24},{12,28},{16,0},{20,4},{24,8},{28,12},{1,17},{... | collective-permute-start | bytes 98312 | tf_op jit(solution)/shard_map/ppermute | solution.py:662
  35.3 6.9 %collective-permute-start.7 = (f32[2,4,8,128]{3,2,1,0:T(8,128)S(1)}, f32[2,4,8,128]{3,2,1,0:T(8,128)S(1)}, u32[]{:S(2)}, u32[]{:S(2)}) collective-permute-start(f32[2,4,8,128]{3,2,1,0:T(8,128)S(1)} %get-tuple-element.58), channel_id=1, source_target_pairs={{0,24},{4,28},{8,0},{12,4},{16,8},{20,12},{24,16},{28,20},{1,25},{... | collective-permute-start | bytes 98312 | tf_op jit(solution)/shard_map/ppermute | solution.py:662
  37.4 5.8 %collective-permute-start.10 = (f32[2,4,8,128]{3,2,1,0:T(8,128)S(1)}, f32[2,4,8,128]{3,2,1,0:T(8,128)S(1)}, u32[]{:S(2)}, u32[]{:S(2)}) collective-permute-start(f32[2,4,8,128]{3,2,1,0:T(8,128)S(1)} %get-tuple-element.72), channel_id=1, source_target_pairs={{0,8},{4,12},{8,16},{12,20},{16,24},{20,28},{24,0},{28,4},{1,9},{5... | collective-permute-start | bytes 98312 | tf_op jit(solution)/shard_map/ppermute | solution.py:662
  37.4 5.7 %collective-permute-start.11 = (f32[2,4,8,128]{3,2,1,0:T(8,128)S(1)}, f32[2,4,8,128]{3,2,1,0:T(8,128)S(1)}, u32[]{:S(2)}, u32[]{:S(2)}) collective-permute-start(f32[2,4,8,128]{3,2,1,0:T(8,128)S(1)} %get-tuple-element.73), channel_id=1, source_target_pairs={{0,16},{4,20},{8,24},{12,28},{16,0},{20,4},{24,8},{28,12},{1,17},{... | collective-permute-start | bytes 98312 | tf_op jit(solution)/shard_map/ppermute | solution.py:662
  38.4 5.3 %collective-permute-start.12 = (f32[2,4,8,128]{3,2,1,0:T(8,128)S(1)}, f32[2,4,8,128]{3,2,1,0:T(8,128)S(1)}, u32[]{:S(2)}, u32[]{:S(2)}) collective-permute-start(f32[2,4,8,128]{3,2,1,0:T(8,128)S(1)} %get-tuple-element.74), channel_id=1, source_target_pairs={{0,24},{4,28},{8,0},{12,4},{16,8},{20,12},{24,16},{28,20},{1,25},{... | collective-permute-start | bytes 98312 | tf_op jit(solution)/shard_map/ppermute | solution.py:662

commit v9 on v8

--- a/solution.py
+++ b/solution.py
@@ -50,32 +50,20 @@
     return jnp.where(mask, jnp.dot(inner, right, preferred_element_type=F32), 0.0)
 
 
-def is_even(axis):
-    return (lax.axis_index(axis) & 1) == 0
-
-
-def to_partners(axis, first, last):
-    even = is_even(axis)
-    return jnp.where(even, last, first), jnp.where(even, first, last)
-
-
-def from_partners(axis, peers, pair, other):
-    at, even = lax.axis_index(axis), is_even(axis)
-    before, after = jnp.where(even, other, pair), jnp.where(even, pair, other)
+def inside_grid(axis, peers, before, after):
+    at = lax.axis_index(axis)
     return jnp.where(at == 0, 0.0, before), jnp.where(at == peers - 1, 0.0, after)
 
 
-def turn_kernel(field_ref, pair_ref, other_ref, turned_ref):
+def turn_kernel(field_ref, turned_ref, first_ref, last_ref):
     layers, length, width = field_ref.shape
     half = length // 2
     for k in range(half):
         turned = jnp.concatenate([field_ref[:, k, :], field_ref[:, k + half, :]], axis=0).T
         turned_ref[k, REACH : REACH + width] = turned
-        first, last = turned[:REACH], turned[width - REACH :]
-        pair, other = to_partners("by", first, last)
         for j in range(REACH):
-            pair_ref[j, k : k + 1] = pair[j : j + 1]
-            other_ref[j, k : k + 1] = other[j : j + 1]
+            first_ref[j, k : k + 1] = turned[j : j + 1]
+            last_ref[j, k : k + 1] = turned[width - REACH + j : width - REACH + j + 1]
 
 
 def spread_weights(in_ref, out_ref, win_ref, wout_ref):
@@ -96,13 +84,13 @@
 
 
 def sides_kernel(
-    width, count_y, turned_ref, pair_in_ref, other_in_ref, wide_ref, pair_ref, other_ref
+    width, count_y, turned_ref, before_ref, after_ref, wide_ref, first_ref, last_ref
 ):
     half, rows, _ = turned_ref.shape
     layers = LANES // 2
     part = rows // 2
     front = iota((part, LANES), 1) < layers
-    befores, afters = from_partners("by", count_y, pair_in_ref[...], other_in_ref[...])
+    befores, afters = inside_grid("by", count_y, before_ref[...], after_ref[...])
     for k in range(half):
         wide_ref[k, REACH : REACH + width] = turned_ref[k, REACH : REACH + width]
         for j in range(REACH):
@@ -112,11 +100,10 @@
         wide_ref[k, 2 * REACH + width :] = jnp.zeros((rows - 2 * REACH - width, LANES), F32)
     for j in range(REACH):
         top, low = wide_ref[j, :part], wide_ref[j, part:]
-        first = jnp.where(front, top, pltpu.roll(low, layers, axis=1))
+        first_ref[j] = jnp.where(front, top, pltpu.roll(low, layers, axis=1))
         k = half - REACH + j
         top, low = wide_ref[k, :part], wide_ref[k, part:]
-        last = jnp.where(front, pltpu.roll(top, layers, axis=1), low)
-        pair_ref[j], other_ref[j] = to_partners("bx", first, last)
+        last_ref[j] = jnp.where(front, pltpu.roll(top, layers, axis=1), low)
 
 
 class Stencil:
@@ -185,7 +172,8 @@
         gy = (main - cross + (r(0, 1) - r(0, -1))) * third
         d = lambda a, b: slope[k + a, y + 1 + b]
         gz = (2.0 * d(0, 0) + ((d(1, 0) + d(-1, 0)) + (d(0, 1) + d(0, -1)))) * third
-        m = jnp.sqrt(1.0 + gx * gx + gy * gy + gz * gz)
+        square = 1.0 + gx * gx + gy * gy + gz * gz
+        m = square * lax.rsqrt(square)
         parts = [centre, gx, gy, gz, m, centre * m, centre * centre]
         packed = [part.astype(BF16) for part in parts] + [jnp.ones(self.shape, BF16)]
         return jnp.concatenate(packed, axis=0).T
@@ -353,8 +341,8 @@
     counts,
     steps,
     wide_ref,
-    pair_ref,
-    other_ref,
+    before_ref,
+    after_ref,
     win_ref,
     wout_ref,
     once_in_ref,
@@ -382,7 +370,7 @@
     front = iota((part, LANES), 1) < layers
     at_x = lax.axis_index("bx")
     for j in range(REACH):
-        before, after = from_partners("bx", counts[0], pair_ref[j], other_ref[j])
+        before, after = inside_grid("bx", counts[0], before_ref[j], after_ref[j])
         halo, own = before, wide_ref[half - REACH + j]
         raw_ref[0, j, :part] = jnp.where(front, halo, roll(own[:part], layers))
         raw_ref[0, j, part:] = jnp.where(front, roll(halo, layers), roll(own[part:], layers))
@@ -518,37 +506,36 @@
             out_sent_ref[r, kind] = jnp.where(bit, even, odd)
 
 
-def merge_x_kernel(kept_ref, received_ref, *refs):
-    many, _, some, _, _ = kept_ref.shape
-    outs = refs[-many:]
+def merge_x_kernel(*refs):
+    many, _, some, _, _ = refs[0].shape
+    ins, outs = refs[:4], refs[-many:]
     at = lax.axis_index("bx")
     later = (at & 1) == 1
-    for t in range(many):
-        r = lax.rem((at >> 1) + t, many)
-        kept, received = kept_ref[r], received_ref[r]
-        front = jnp.where(later, received, kept)
-        back = jnp.where(later, kept, received)
-        outs[t][0] = front[0] + front[1] * back[0]
-        outs[t][1] = front[1] * back[1]
+    for i in range(2):
+        kept_ref, received_ref = ins[2 * i], ins[2 * i + 1]
+        for t in range(many):
+            r = lax.rem((at >> 1) + t, many)
+            kept, received = kept_ref[r], received_ref[r]
+            front = jnp.where(later, received, kept)
+            back = jnp.where(later, kept, received)
+            outs[t][0, i * some : (i + 1) * some] = front[0] + front[1] * back[0]
+            outs[t][1, i * some : (i + 1) * some] = front[1] * back[1]
 
 
 def fold_x_kernel(*refs):
-    out_ref = refs[-1]
-    many = (len(refs) - 1) // 2
-    _, some, share, _ = refs[0].shape
-    run = 2 * some
+    pieces, out_ref = refs[:-1], refs[-1]
+    _, run, share, _ = pieces[0].shape
     lane = iota((share, LANES), 1)
     me = lax.axis_index("bx") >> 1
     kinds = [[], []]
     for y in range(run):
-        pieces = refs[(y // some) * many :][:many]
         behind = colour, clear = jnp.zeros((share, LANES), F32), jnp.ones((share, LANES), F32)
-        for s in reversed(range(many)):
+        for s in reversed(range(len(pieces))):
             start = me == s
             behind = jnp.where(start, colour, behind[0]), jnp.where(start, clear, behind[1])
             colour, clear = jnp.where(start, 0.0, colour), jnp.where(start, 1.0, clear)
-            colour = colour + clear * pieces[s][0, y % some]
-            clear = clear * pieces[s][1, y % some]
+            colour = colour + clear * pieces[s][0, y]
+            clear = clear * pieces[s][1, y]
         kinds[0].append(colour + clear * behind[0])
         kinds[1].append(clear * behind[1])
     for kind, values in enumerate(kinds):
@@ -563,12 +550,11 @@
             out_ref[kind, band] = value
 
 
-def exchange(pair, other, axis, around):
+def exchange(last, first, axis):
     peers = lax.axis_size(axis)
-    sides = [(i, (i + 1) % peers if i & 1 else (i - 1) % peers) for i in range(peers)]
-    if not around:
-        sides = [(i, i) if i in (0, peers - 1) else (i, j) for i, j in sides]
-    return swap(pair, axis, 1), lax.ppermute(other, axis, sides)
+    up = [(i, (i + 1) % peers) for i in range(peers)]
+    down = [(j, i) for i, j in up]
+    return lax.ppermute(last, axis, up), lax.ppermute(first, axis, down)
 
 
 def swap(value, axis, bit):
@@ -590,15 +576,15 @@
     ]
 
     edge = sds(REACH, half, LANES)
-    pair, other, turned = call(turn_kernel, "turn", [edge, edge, sds(half, rows, LANES)], 1)(
+    turned, first, last = call(turn_kernel, "turn", [sds(half, rows, LANES), edge, edge], 1)(
         scalar_field
     )
-    pair, other = exchange(pair, other, "by", True)
+    before, after = exchange(last, first, "by")
     edge = sds(REACH, rows // 2, LANES)
-    wide, pair, other = call(
+    wide, first, last = call(
         functools.partial(sides_kernel, local_y, count_y), "sides", [sds(half, rows, LANES), edge, edge], 3
-    )(turned, pair, other)
-    pair, other = exchange(pair, other, "bx", False)
+    )(turned, before, after)
+    before, after = exchange(last, first, "bx")
     inner = half - 2 * REACH
     counts = (count_x, count_y)
     plane = lambda *lead: sds(*lead, CHUNKS, LANES)
@@ -634,7 +620,7 @@
             pltpu.VMEM((2, 5, rows, LANES), F32),
             pltpu.VMEM((2, 7, run + 4, CHUNKS, LANES), F32),
         ],
-    )(wide, pair, other, win, wout, once, twice, ridge, slope, colour_x, clear_x)
+    )(wide, before, after, win, wout, once, twice, ridge, slope, colour_x, clear_x)
     halves = [(kept, swap(sent, "bx", 1))]
     kept, sent, kept_y, sent_y = call(
         functools.partial(ends_last_kernel, counts, steps),
@@ -653,16 +639,6 @@
     )
     halves += [(kept, swap(sent, "bx", 1))]
 
-    def send_round(*operands):
-        many = count_x // 2
-        piece = sds(2, run // 2, share, LANES)
-        pieces = list(call(merge_x_kernel, "merge_x", [piece] * many, len(operands))(*operands))
-        for t in range(1, many):
-            pairs = [(i, (i + 2 * t) % count_x) for i in range(count_x)]
-            pieces[t] = lax.ppermute(pieces[t], "bx", pairs)
-        return pieces
-
-    pieces = send_round(*halves[0])
     level, many = 1, count_y // 2
     while many:
         received = swap(sent_y, "by", level)
@@ -673,8 +649,14 @@
         else:
             view_y = call(merge, "merge", sds(2, 2, share_y, LANES), 2)(kept_y, received)
         level, many = 2 * level, many // 2
-    pieces += send_round(*halves[1], sent_y)
-    view_x = call(fold_x_kernel, "fold_x", sds(2, bands, share, local_y), count_x)(*pieces)
+    many = count_x // 2
+    piece = sds(2, run, share, LANES)
+    operands = [*halves[0], *halves[1], sent_y]
+    pieces = list(call(merge_x_kernel, "merge_x", [piece] * many, len(operands))(*operands))
+    for t in range(1, many):
+        pairs = [(i, (i + 2 * t) % count_x) for i in range(count_x)]
+        pieces[t] = lax.ppermute(pieces[t], "bx", pairs)
+    view_x = call(fold_x_kernel, "fold_x", sds(2, bands, share, local_y), many)(*pieces)
     view_y = view_y.reshape(2, 2, share_y, half, bands)
     view_y = jnp.transpose(view_y, (0, 4, 2, 1, 3)).reshape(2, bands, share_y, local_x)
     return (view_x, view_y)

time: 44.7 us -> 43.3 us (0.969)
  starting transfers between devices: 21.1 us -> 15.9 us
  waiting for transfers between devices: 4.23 us -> 8.24 us
    ppermute x6 -> x4, waiting for transfers between devices: 1.25 us -> 6.7 us  [swap(): lax.ppermute(value, axis, [(i, i ^ bit) for i in range(lax.axis_size(axis...]
    ppermute x6 -> x4, starting transfers between devices: 8.32 us -> 3.49 us  [swap(): lax.ppermute(value, axis, [(i, i ^ bit) for i in range(lax.axis_size(axis...]
    ppermute x8 -> x7, waiting for transfers between devices: 2.97 us -> 1.54 us  [the longest x4 1.53 us: exchange(): return (lax.ppermute(last, axis, up), lax.ppermute(first, axis, down))]
    ppermute x8 -> x7, starting transfers between devices: 12.8 us -> 12.4 us  [the longest x4 7.89 us: exchange(): return (lax.ppermute(last, axis, up), lax.ppermute(first, axis, down))]
    pallas_call x4 -> x3, Pallas kernels: 1.57 us -> 1.57 us  [the longest x1 0.9 us: body(): call(fold_x_kernel, 'fold_x', sds(2, bands, share, local_y), many)(*pieces)]
  transfers between devices with their start and end apart: 14 -> 11, of which waited for: 4 -> 5; matrix products, arithmetic and copies ran while one was open for 2% -> 2% of each run, Pallas kernels for 26% -> 26%
where the time goes in v9:
time: 43.3 us; the launch traced here: 43.2 us
  Pallas kernels  16.1 us (37%)
  starting transfers between devices  15.9 us (37%)
  waiting for transfers between devices  8.24 us (19%)
  local copies, waits for them, and re-layouts  2.23 us (5%)
  between operations  0.72 us (2%)
    pallas_call x1, Pallas kernels, body(): call(functools.partial(middle_kernel, (many_x, many_y), counts, steps), '...  8.58 us
    ppermute x4, starting transfers between devices, exchange(): return (lax.ppermute(last, axis, up), lax.ppermute(first, axis, down))  7.89 us
    ppermute x4, waiting for transfers between devices, swap(): lax.ppermute(value, axis, [(i, i ^ bit) for i in range(lax.axis_size(axis...  6.7 us
    ppermute x3, starting transfers between devices, body(): pieces[t] = lax.ppermute(pieces[t], 'bx', pairs)  4.48 us
    ppermute x4, starting transfers between devices, swap(): lax.ppermute(value, axis, [(i, i ^ bit) for i in range(lax.axis_size(axis...  3.49 us
    pallas_call x1, Pallas kernels, body(): call(functools.partial(ends_first_kernel, counts, steps), 'ends_first', [...  3.13 us
    pallas_call x1, Pallas kernels, body(): call(functools.partial(ends_last_kernel, counts, steps), 'ends_last', [pa...  2.64 us
    unnamed x8, local copies, waits for them, and re-layouts  2.11 us
  transfers between devices with their start and end apart: 11, of which 5 were waited for; matrix products, arithmetic and copies ran while one was open for 2% of the time, Pallas kernels for 26%

profile of v9, /device:TPU:0, one launch (start us, length us, event | category | flops | bytes accessed | tf_op | source)
XLA Modules:
  0.0 43.2 jit_solution(17448518519913814098)
XLA Ops:
  0.6 0.0 copy-start
  0.6 1.2 %copy-done = f32[64,32,128]{2,1,0:T(8,128)S(1)} copy-done((f32[64,32,128]{2,1,0:T(8,128)S(1)}, f32[64,32,128]{2,1,0:T(8,128)}, u32[]{:S(2)}) %copy-start) | copy-done | bytes 1048600
  1.9 0.0 copy-start.2
  1.9 0.0 copy-start.1
  1.9 0.6 %turn.1 = (f32[16,144,128]{2,1,0:T(8,128)S(1)}, f32[3,16,128]{2,1,0:T(8,128)S(1)}, f32[3,16,128]{2,1,0:T(8,128)S(1)}) custom-call(f32[64,32,128]{2,1,0:T(8,128)S(1)} %copy-done), custom_call_target="tpu_custom_call" | custom-call | tf_op jit(solution)/shard_map/turn/pallas_call | solution.py:579
  2.5 0.5 %collective-permute-start = (f32[3,16,128]{2,1,0:T(8,128)S(1)}, f32[3,16,128]{2,1,0:T(8,128)S(1)}, u32[]{:S(2)}, u32[]{:S(2)}) collective-permute-start(f32[3,16,128]{2,1,0:T(8,128)S(1)} %get-tuple-element.36), channel_id=1, source_target_pairs={{0,1},{1,2},{2,3},{3,0},{4,5},{5,6},{6,7},{7,4},{8,9},{9,10},{10,1... | collective-permute-start | bytes 73736 | tf_op jit(solution)/shard_map/ppermute | solution.py:557
  3.0 2.0 %collective-permute-start.1 = (f32[3,16,128]{2,1,0:T(8,128)S(1)}, f32[3,16,128]{2,1,0:T(8,128)S(1)}, u32[]{:S(2)}, u32[]{:S(2)}) collective-permute-start(f32[3,16,128]{2,1,0:T(8,128)S(1)} %get-tuple-element.37), channel_id=1, source_target_pairs={{1,0},{2,1},{3,2},{0,3},{5,4},{6,5},{7,6},{4,7},{9,8},{10,9},{11,1... | collective-permute-start | bytes 73736 | tf_op jit(solution)/shard_map/ppermute | solution.py:557
  5.0 1.4 %collective-permute-done.before_ref = f32[3,16,128]{2,1,0:T(8,128)S(1)} collective-permute-done((f32[3,16,128]{2,1,0:T(8,128)S(1)}, f32[3,16,128]{2,1,0:T(8,128)S(1)}, u32[]{:S(2)}, u32[]{:S(2)}) %collective-permute-start) | collective-permute-done | bytes 24608 | tf_op jit(solution)/shard_map/ppermute | solution.py:557
  6.5 0.1 collective-permute-done.1.after_ref
  6.6 0.2 sides.1
  6.7 2.3 %collective-permute-start.2 = (f32[3,72,128]{2,1,0:T(8,128)S(1)}, f32[3,72,128]{2,1,0:T(8,128)S(1)}, u32[]{:S(2)}, u32[]{:S(2)}) collective-permute-start(f32[3,72,128]{2,1,0:T(8,128)S(1)} %get-tuple-element.39), channel_id=1, source_target_pairs={{0,4},{4,8},{8,12},{12,16},{16,20},{20,24},{24,28},{28,0},{1,5},{5... | collective-permute-start | bytes 331784 | tf_op jit(solution)/shard_map/ppermute | solution.py:557
  9.0 3.1 %collective-permute-start.3 = (f32[3,72,128]{2,1,0:T(8,128)S(1)}, f32[3,72,128]{2,1,0:T(8,128)S(1)}, u32[]{:S(2)}, u32[]{:S(2)}) collective-permute-start(f32[3,72,128]{2,1,0:T(8,128)S(1)} %get-tuple-element.40), channel_id=1, source_target_pairs={{4,0},{8,4},{12,8},{16,12},{20,16},{24,20},{28,24},{0,28},{5,1},{9... | collective-permute-start | bytes 331784 | tf_op jit(solution)/shard_map/ppermute | solution.py:557
  12.1 0.0 copy-done.2
  12.1 0.1 copy.7.in_ref
  12.2 0.0 copy-done.1
  12.2 8.6 %middle.1 = (bf16[128,256]{1,0:T(8,128)(2,1)S(1)}, bf16[256,256]{1,0:T(8,128)(2,1)S(1)}, f32[2,4,12,16,128]{4,3,2,1,0:T(8,128)S(1)}, f32[2,2,10,16,128]{4,3,2,1,...) custom-call(f32[16,144,128]{2,1,0:T(8,128)S(1)} %get-tuple-element.3, ...), custom_call_target="tpu_custom_call" | custom-call | tf_op jit(solution)/shard_map/middle/pallas_call | solution.py:592
  20.8 0.0 collective-permute-done.2.before_ref
  20.8 0.0 collective-permute-done.3.after_ref
  20.8 3.1 %ends_first.1 = (f32[2,5,10,16,128]{4,3,2,1,0:T(8,128)S(1)}, f32[2,5,10,16,128]{4,3,2,1,0:T(8,128)S(1)}, f32[2,5,10,16,128]{4,3,2,1,0:T(8,128)S(1)}, f32[6,128,1...) custom-call(f32[16,144,128]{2,1,0:T(8,128)S(1)} %get-tuple-element.3, ...), custom_call_target="tpu_custom_call" | custom-call | tf_op jit(solution)/shard_map/ends_first/pallas_call | solution.py:613
  23.9 0.1 collective-permute-start.4
  24.0 2.6 %ends_last.1 = (f32[4,2,4,8,128]{4,3,2,1,0:T(8,128)S(1)}, f32[4,2,4,8,128]{4,3,2,1,0:T(8,128)S(1)}, f32[2,2,2,16,128]{4,3,2,1,0:T(8,128)S(1)}, f32[2,2,2,16,128]{4,3,2,1,0:T(8,128)S(1)}) custom-call(bf16[128,256]{1,0:T(8,128)(2,1)S(1)} %get-tuple-element.41.win_ref, bf16[256,256]{1,0:T(8,128)(2,1)S(1)} %get-tuple-element.42.wout_ref, ...), custom_call_target="tpu_custom_call" | custom-call | tf_op jit(solution)/shard_map/ends_last/pallas_call | solution.py:625
  26.6 2.1 %collective-permute-start.5 = (f32[4,2,4,8,128]{4,3,2,1,0:T(8,128)S(1)}, f32[4,2,4,8,128]{4,3,2,1,0:T(8,128)S(1)}, u32[]{:S(2)}, u32[]{:S(2)}) collective-permute-start(f32[4,2,4,8,128]{4,3,2,1,0:T(8,128)S(1)} %get-tuple-element.59), channel_id=1, source_target_pairs={{0,4},{4,0},{8,12},{12,8},{16,20},{20,16},{24,28},{28,24},{1,5},{5... | collective-permute-start | bytes 393224 | tf_op jit(solution)/shard_map/ppermute | solution.py:561
  28.7 0.8 %collective-permute-start.6 = (f32[2,2,2,16,128]{4,3,2,1,0:T(8,128)S(1)}, f32[2,2,2,16,128]{4,3,2,1,0:T(8,128)S(1)}, u32[]{:S(2)}, u32[]{:S(2)}) collective-permute-start(f32[2,2,2,16,128]{4,3,2,1,0:T(8,128)S(1)} %get-tuple-element.61), channel_id=1, source_target_pairs={{0,1},{1,0},{2,3},{3,2},{4,5},{5,4},{6,7},{7,6},{8,9},{9,8},{10,11... | collective-permute-start | bytes 196616 | tf_op jit(solution)/shard_map/ppermute | solution.py:561
  29.5 0.9 %collective-permute-done.6.received_ref = f32[2,2,2,16,128]{4,3,2,1,0:T(8,128)S(1)} collective-permute-done((f32[2,2,2,16,128]{4,3,2,1,0:T(8,128)S(1)}, f32[2,2,2,16,128]{4,3,2,1,0:T(8,128)S(1)}, u32[]{:S(2)}, u32[]{:S(2)}) %collective-permute-start.6) | collective-permute-done | bytes 65568 | tf_op jit(solution)/shard_map/ppermute | solution.py:561
  30.4 0.0 collective-permute-done.4.refs_1_
  30.4 2.4 %collective-permute-done.5.refs_3_ = f32[4,2,4,8,128]{4,3,2,1,0:T(8,128)S(1)} collective-permute-done((f32[4,2,4,8,128]{4,3,2,1,0:T(8,128)S(1)}, f32[4,2,4,8,128]{4,3,2,1,0:T(8,128)S(1)}, u32[]{:S(2)}, u32[]{:S(2)}) %collective-permute-start.5) | collective-permute-done | bytes 131104 | tf_op jit(solution)/shard_map/ppermute | solution.py:561
  32.9 0.5 %collective-permute-start.7 = (f32[2,8,8,128]{3,2,1,0:T(8,128)S(1)}, f32[2,8,8,128]{3,2,1,0:T(8,128)S(1)}, u32[]{:S(2)}, u32[]{:S(2)}) collective-permute-start(f32[2,8,8,128]{3,2,1,0:T(8,128)S(1)} %get-tuple-element.64), channel_id=1, source_target_pairs={{0,8},{4,12},{8,16},{12,20},{16,24},{20,28},{24,0},{28,4},{1,9},{5... | collective-permute-start | bytes 196616 | tf_op jit(solution)/shard_map/ppermute | solution.py:658
  33.5 2.6 %collective-permute-start.8 = (f32[2,8,8,128]{3,2,1,0:T(8,128)S(1)}, f32[2,8,8,128]{3,2,1,0:T(8,128)S(1)}, u32[]{:S(2)}, u32[]{:S(2)}) collective-permute-start(f32[2,8,8,128]{3,2,1,0:T(8,128)S(1)} %get-tuple-element.65), channel_id=1, source_target_pairs={{0,16},{4,20},{8,24},{12,28},{16,0},{20,4},{24,8},{28,12},{1,17},{... | collective-permute-start | bytes 196616 | tf_op jit(solution)/shard_map/ppermute | solution.py:658
  36.0 1.3 %collective-permute-start.9 = (f32[2,8,8,128]{3,2,1,0:T(8,128)S(1)}, f32[2,8,8,128]{3,2,1,0:T(8,128)S(1)}, u32[]{:S(2)}, u32[]{:S(2)}) collective-permute-start(f32[2,8,8,128]{3,2,1,0:T(8,128)S(1)} %get-tuple-element.66), channel_id=1, source_target_pairs={{0,24},{4,28},{8,0},{12,4},{16,8},{20,12},{24,16},{28,20},{1,25},{... | collective-permute-start | bytes 196616 | tf_op jit(solution)/shard_map/ppermute | solution.py:658
  37.4 0.6 %collective-permute-start.10 = (f32[1,2,2,16,128]{4,3,2,1,0:T(8,128)S(1)}, f32[1,2,2,16,128]{4,3,2,1,0:T(8,128)S(1)}, u32[]{:S(2)}, u32[]{:S(2)}) collective-permute-start(f32[1,2,2,16,128]{4,3,2,1,0:T(8,128)S(1)} %get-tuple-element.62.refs_4_), channel_id=1, source_target_pairs={{0,2},{1,3},{2,0},{3,1},{4,6},{5,7},{6,4},{7,5},{8,10},{9,11},{10,... | collective-permute-start | bytes 98312 | tf_op jit(solution)/shard_map/ppermute | solution.py:561
  38.0 3.4 %collective-permute-done.10.received_ref = f32[1,2,2,16,128]{4,3,2,1,0:T(8,128)S(1)} collective-permute-done((f32[1,2,2,16,128]{4,3,2,1,0:T(8,128)S(1)}, f32[1,2,2,16,128]{4,3,2,1,0:T(8,128)S(1)}, u32[]{:S(2)}, u32[]{:S(2)}) %collective-permute-start.10) | collective-permute-done | bytes 32800 | tf_op jit(solution)/shard_map/ppermute | solution.py:561
  41.3 0.1 copy.8
  41.5 0.8 %copy.9 = f32[2,8,16,32]{3,2,1,0:T(8,128)} copy(f32[2,8,16,32]{2,1,3,0:T(8,128)S(1)} %bitcast.5) | data formatting | bytes 65536
  42.3 0.0 collective-permute-done.7.refs_1_
  42.3 0.0 collective-permute-done.8.refs_2_
  42.3 0.0 collective-permute-done.9.refs_3_
  42.3 0.9 %fold_x.1 = f32[2,8,8,128]{3,2,1,0:T(8,128)} custom-call(f32[2,8,8,128]{3,2,1,0:T(8,128)S(1)} %get-tuple-element.63.refs_0_, f32[2,8,8,128]{3,2,1,0:T(8,128)S(1)} %collective-permute-done.7.refs_1_, f32[2,8,8,128]{3,2,1,0:T(8,128)S(1)} %collective-permute-done.8.refs_2_, f32[2,8,8,128]{3,2,1,0:T(8,128)S(1)} %collective-permute-done.9.refs_3_), custom_call_target="tpu_custom_call" | custom-call | tf_op jit(solution)/shard_map/fold_x/pallas_call | solution.py:659
  (3 shorter events, 0.1 us)
Async XLA Ops:
  0.6 1.2 %copy-start = (f32[64,32,128]{2,1,0:T(8,128)S(1)}, f32[64,32,128]{2,1,0:T(8,128)}, u32[]{:S(2)}) copy-start(f32[64,32,128]{2,1,0:T(8,128)} %field_ref.1) | copy-start | bytes 3145732
  1.9 10.2 %copy-start.2 = (bf16[16,8]{0,1:T(8,128)(2,1)S(1)}, bf16[16,8]{0,1:T(8,128)(2,1)}, u32[]{:S(2)}) copy-start(bf16[16,8]{0,1:T(8,128)(2,1)} %param.4) | copy-start | bytes 772
  1.9 10.3 %copy-start.1 = (bf16[16,16]{1,0:T(8,128)(2,1)S(1)}, bf16[16,16]{1,0:T(8,128)(2,1)}, u32[]{:S(2)}) copy-start(bf16[16,16]{1,0:T(8,128)(2,1)} %out_ref.1) | copy-start | bytes 1540
  2.5 4.0 %collective-permute-start = (f32[3,16,128]{2,1,0:T(8,128)S(1)}, f32[3,16,128]{2,1,0:T(8,128)S(1)}, u32[]{:S(2)}, u32[]{:S(2)}) collective-permute-start(f32[3,16,128]{2,1,0:T(8,128)S(1)} %get-tuple-element.36), channel_id=1, source_target_pairs={{0,1},{1,2},{2,3},{3,0},{4,5},{5,6},{6,7},{7,4},{8,9},{9,10},{10,1... | collective-permute-start | bytes 73736 | tf_op jit(solution)/shard_map/ppermute | solution.py:557
  3.0 3.5 %collective-permute-start.1 = (f32[3,16,128]{2,1,0:T(8,128)S(1)}, f32[3,16,128]{2,1,0:T(8,128)S(1)}, u32[]{:S(2)}, u32[]{:S(2)}) collective-permute-start(f32[3,16,128]{2,1,0:T(8,128)S(1)} %get-tuple-element.37), channel_id=1, source_target_pairs={{1,0},{2,1},{3,2},{0,3},{5,4},{6,5},{7,6},{4,7},{9,8},{10,9},{11,1... | collective-permute-start | bytes 73736 | tf_op jit(solution)/shard_map/ppermute | solution.py:557
  6.7 14.0 %collective-permute-start.2 = (f32[3,72,128]{2,1,0:T(8,128)S(1)}, f32[3,72,128]{2,1,0:T(8,128)S(1)}, u32[]{:S(2)}, u32[]{:S(2)}) collective-permute-start(f32[3,72,128]{2,1,0:T(8,128)S(1)} %get-tuple-element.39), channel_id=1, source_target_pairs={{0,4},{4,8},{8,12},{12,16},{16,20},{20,24},{24,28},{28,0},{1,5},{5... | collective-permute-start | bytes 331784 | tf_op jit(solution)/shard_map/ppermute | solution.py:557
  9.0 11.8 %collective-permute-start.3 = (f32[3,72,128]{2,1,0:T(8,128)S(1)}, f32[3,72,128]{2,1,0:T(8,128)S(1)}, u32[]{:S(2)}, u32[]{:S(2)}) collective-permute-start(f32[3,72,128]{2,1,0:T(8,128)S(1)} %get-tuple-element.40), channel_id=1, source_target_pairs={{4,0},{8,4},{12,8},{16,12},{20,16},{24,20},{28,24},{0,28},{5,1},{9... | collective-permute-start | bytes 331784 | tf_op jit(solution)/shard_map/ppermute | solution.py:557
  23.9 6.5 %collective-permute-start.4 = (f32[4,2,4,8,128]{4,3,2,1,0:T(8,128)S(1)}, f32[4,2,4,8,128]{4,3,2,1,0:T(8,128)S(1)}, u32[]{:S(2)}, u32[]{:S(2)}) collective-permute-start(f32[4,2,4,8,128]{4,3,2,1,0:T(8,128)S(1)} %get-tuple-element.50), channel_id=1, source_target_pairs={{0,4},{4,0},{8,12},{12,8},{16,20},{20,16},{24,28},{28,24},{1,5},{5... | collective-permute-start | bytes 393224 | tf_op jit(solution)/shard_map/ppermute | solution.py:561
  26.6 6.2 %collective-permute-start.5 = (f32[4,2,4,8,128]{4,3,2,1,0:T(8,128)S(1)}, f32[4,2,4,8,128]{4,3,2,1,0:T(8,128)S(1)}, u32[]{:S(2)}, u32[]{:S(2)}) collective-permute-start(f32[4,2,4,8,128]{4,3,2,1,0:T(8,128)S(1)} %get-tuple-element.59), channel_id=1, source_target_pairs={{0,4},{4,0},{8,12},{12,8},{16,20},{20,16},{24,28},{28,24},{1,5},{5... | collective-permute-start | bytes 393224 | tf_op jit(solution)/shard_map/ppermute | solution.py:561
  28.7 1.7 %collective-permute-start.6 = (f32[2,2,2,16,128]{4,3,2,1,0:T(8,128)S(1)}, f32[2,2,2,16,128]{4,3,2,1,0:T(8,128)S(1)}, u32[]{:S(2)}, u32[]{:S(2)}) collective-permute-start(f32[2,2,2,16,128]{4,3,2,1,0:T(8,128)S(1)} %get-tuple-element.61), channel_id=1, source_target_pairs={{0,1},{1,0},{2,3},{3,2},{4,5},{5,4},{6,7},{7,6},{8,9},{9,8},{10,11... | collective-permute-start | bytes 196616 | tf_op jit(solution)/shard_map/ppermute | solution.py:561
  32.9 9.4 %collective-permute-start.7 = (f32[2,8,8,128]{3,2,1,0:T(8,128)S(1)}, f32[2,8,8,128]{3,2,1,0:T(8,128)S(1)}, u32[]{:S(2)}, u32[]{:S(2)}) collective-permute-start(f32[2,8,8,128]{3,2,1,0:T(8,128)S(1)} %get-tuple-element.64), channel_id=1, source_target_pairs={{0,8},{4,12},{8,16},{12,20},{16,24},{20,28},{24,0},{28,4},{1,9},{5... | collective-permute-start | bytes 196616 | tf_op jit(solution)/shard_map/ppermute | solution.py:658
  33.5 8.8 %collective-permute-start.8 = (f32[2,8,8,128]{3,2,1,0:T(8,128)S(1)}, f32[2,8,8,128]{3,2,1,0:T(8,128)S(1)}, u32[]{:S(2)}, u32[]{:S(2)}) collective-permute-start(f32[2,8,8,128]{3,2,1,0:T(8,128)S(1)} %get-tuple-element.65), channel_id=1, source_target_pairs={{0,16},{4,20},{8,24},{12,28},{16,0},{20,4},{24,8},{28,12},{1,17},{... | collective-permute-start | bytes 196616 | tf_op jit(solution)/shard_map/ppermute | solution.py:658
  36.0 6.2 %collective-permute-start.9 = (f32[2,8,8,128]{3,2,1,0:T(8,128)S(1)}, f32[2,8,8,128]{3,2,1,0:T(8,128)S(1)}, u32[]{:S(2)}, u32[]{:S(2)}) collective-permute-start(f32[2,8,8,128]{3,2,1,0:T(8,128)S(1)} %get-tuple-element.66), channel_id=1, source_target_pairs={{0,24},{4,28},{8,0},{12,4},{16,8},{20,12},{24,16},{28,20},{1,25},{... | collective-permute-start | bytes 196616 | tf_op jit(solution)/shard_map/ppermute | solution.py:658
  37.4 3.9 %collective-permute-start.10 = (f32[1,2,2,16,128]{4,3,2,1,0:T(8,128)S(1)}, f32[1,2,2,16,128]{4,3,2,1,0:T(8,128)S(1)}, u32[]{:S(2)}, u32[]{:S(2)}) collective-permute-start(f32[1,2,2,16,128]{4,3,2,1,0:T(8,128)S(1)} %get-tuple-element.62.refs_4_), channel_id=1, source_target_pairs={{0,2},{1,3},{2,0},{3,1},{4,6},{5,7},{6,4},{7,5},{8,10},{9,11},{10,... | collective-permute-start | bytes 98312 | tf_op jit(solution)/shard_map/ppermute | solution.py:561

commit v10 on v9

--- a/solution.py
+++ b/solution.py
@@ -507,19 +507,21 @@
 
 
 def merge_x_kernel(*refs):
-    many, _, some, _, _ = refs[0].shape
+    many = refs[0].shape[0]
     ins, outs = refs[:4], refs[-many:]
     at = lax.axis_index("bx")
     later = (at & 1) == 1
-    for i in range(2):
-        kept_ref, received_ref = ins[2 * i], ins[2 * i + 1]
+    first = 0
+    for kept_ref, received_ref in (ins[:2], ins[2:]):
+        last = first + kept_ref.shape[2]
         for t in range(many):
             r = lax.rem((at >> 1) + t, many)
             kept, received = kept_ref[r], received_ref[r]
             front = jnp.where(later, received, kept)
             back = jnp.where(later, kept, received)
-            outs[t][0, i * some : (i + 1) * some] = front[0] + front[1] * back[0]
-            outs[t][1, i * some : (i + 1) * some] = front[1] * back[1]
+            outs[t][0, first:last] = front[0] + front[1] * back[0]
+            outs[t][1, first:last] = front[1] * back[1]
+        first = last
 
 
 def fold_x_kernel(*refs):
@@ -605,18 +607,19 @@
     )(wide, transfer_in, transfer_out)
     share = layers // count_x
     share_y = layers // count_y
-    parts = sds(count_x // 2, 2, run // 2, share, LANES)
+    ahead = run - run // 4
+    parts = lambda many: [sds(count_x // 2, 2, many, share, LANES)] * 2
     parts_y = sds(count_y // 2, 2, 2, share_y, LANES)
-    image = pltpu.VMEM((2, run // 2, layers, LANES), F32)
+    image = lambda many: pltpu.VMEM((2, many, layers, LANES), F32)
     ray = pltpu.VMEM((2 * REACH, LANES, LANES), F32)
     field = plane(2, 5, run + 2)
     twice, ridge, slope, colour_ends, clear_ends, kept, sent = call(
         functools.partial(ends_first_kernel, counts, steps),
         "ends_first",
-        [field] * 3 + [sds(2 * REACH, LANES, LANES)] * 2 + [parts] * 2,
+        [field] * 3 + [sds(2 * REACH, LANES, LANES)] * 2 + parts(ahead),
         11,
         [
-            image,
+            image(ahead),
             pltpu.VMEM((2, 5, rows, LANES), F32),
             pltpu.VMEM((2, 7, run + 4, CHUNKS, LANES), F32),
         ],
@@ -625,10 +628,10 @@
     kept, sent, kept_y, sent_y = call(
         functools.partial(ends_last_kernel, counts, steps),
         "ends_last",
-        [parts] * 2 + [parts_y] * 2,
+        parts(run - ahead) + [parts_y] * 2,
         11,
         [
-            image,
+            image(run - ahead),
             ray,
             ray,
             pltpu.VMEM((2, LANES, LANES), F32),
@@ -651,7 +654,7 @@
         level, many = 2 * level, many // 2
     many = count_x // 2
     piece = sds(2, run, share, LANES)
-    operands = [*halves[0], *halves[1], sent_y]
+    operands = [*halves[0], *halves[1], received]
     pieces = list(call(merge_x_kernel, "merge_x", [piece] * many, len(operands))(*operands))
     for t in range(1, many):
         pairs = [(i, (i + 2 * t) % count_x) for i in range(count_x)]

time: 43.3 us -> 43.8 us (1.012)
    ppermute x3, waiting for transfers between devices: 0.01 us -> 3.64 us  [body(): pieces[t] = lax.ppermute(pieces[t], 'bx', pairs)]
    ppermute x4, waiting for transfers between devices: 6.7 us -> 3.4 us  [swap(): lax.ppermute(value, axis, [(i, i ^ bit) for i in range(lax.axis_size(axis...]
    pallas_call x1, Pallas kernels: 2.64 us -> 1.41 us  [body(): call(functools.partial(ends_last_kernel, counts, steps), 'ends_last', par...]
    pallas_call x1, Pallas kernels: 3.13 us -> 4.33 us  [body(): call(functools.partial(ends_first_kernel, counts, steps), 'ends_first', [...]
    ppermute x4, starting transfers between devices: 3.49 us -> 4.11 us  [swap(): lax.ppermute(value, axis, [(i, i ^ bit) for i in range(lax.axis_size(axis...]
  transfers between devices with their start and end apart: 11 -> 11, of which waited for: 5 -> 5; matrix products, arithmetic and copies ran while one was open for 2% -> 2% of each run, Pallas kernels for 26% -> 23%
where the time goes in v10:
time: 43.8 us; the launch traced here: 43.7 us
  Pallas kernels  16.1 us (37%)
  starting transfers between devices  16.1 us (37%)
  waiting for transfers between devices  8.58 us (20%)
  local copies, waits for them, and re-layouts  2.23 us (5%)
  between operations  0.71 us (2%)
    pallas_call x1, Pallas kernels, body(): call(functools.partial(middle_kernel, (many_x, many_y), counts, steps), '...  8.58 us
    ppermute x4, starting transfers between devices, exchange(): return (lax.ppermute(last, axis, up), lax.ppermute(first, axis, down))  7.89 us
    pallas_call x1, Pallas kernels, body(): call(functools.partial(ends_first_kernel, counts, steps), 'ends_first', [...  4.33 us
    ppermute x4, starting transfers between devices, swap(): lax.ppermute(value, axis, [(i, i ^ bit) for i in range(lax.axis_size(axis...  4.11 us
    ppermute x3, starting transfers between devices, body(): pieces[t] = lax.ppermute(pieces[t], 'bx', pairs)  4.09 us
    ppermute x3, waiting for transfers between devices, body(): pieces[t] = lax.ppermute(pieces[t], 'bx', pairs)  3.64 us
    ppermute x4, waiting for transfers between devices, swap(): lax.ppermute(value, axis, [(i, i ^ bit) for i in range(lax.axis_size(axis...  3.4 us
    unnamed x8, local copies, waits for them, and re-layouts  2.11 us
  transfers between devices with their start and end apart: 11, of which 5 were waited for; matrix products, arithmetic and copies ran while one was open for 2% of the time, Pallas kernels for 23%

profile of v10, /device:TPU:0, one launch (start us, length us, event | category | flops | bytes accessed | tf_op | source)
XLA Modules:
  0.0 43.7 jit_solution(1266863490071046121)
XLA Ops:
  0.6 0.0 copy-start
  0.6 1.2 %copy-done = f32[64,32,128]{2,1,0:T(8,128)S(1)} copy-done((f32[64,32,128]{2,1,0:T(8,128)S(1)}, f32[64,32,128]{2,1,0:T(8,128)}, u32[]{:S(2)}) %copy-start) | copy-done | bytes 1048600
  1.9 0.0 copy-start.2
  1.9 0.0 copy-start.1
  1.9 0.6 %turn.1 = (f32[16,144,128]{2,1,0:T(8,128)S(1)}, f32[3,16,128]{2,1,0:T(8,128)S(1)}, f32[3,16,128]{2,1,0:T(8,128)S(1)}) custom-call(f32[64,32,128]{2,1,0:T(8,128)S(1)} %copy-done), custom_call_target="tpu_custom_call" | custom-call | tf_op jit(solution)/shard_map/turn/pallas_call | solution.py:581
  2.5 0.5 %collective-permute-start = (f32[3,16,128]{2,1,0:T(8,128)S(1)}, f32[3,16,128]{2,1,0:T(8,128)S(1)}, u32[]{:S(2)}, u32[]{:S(2)}) collective-permute-start(f32[3,16,128]{2,1,0:T(8,128)S(1)} %get-tuple-element.36), channel_id=1, source_target_pairs={{0,1},{1,2},{2,3},{3,0},{4,5},{5,6},{6,7},{7,4},{8,9},{9,10},{10,1... | collective-permute-start | bytes 73736 | tf_op jit(solution)/shard_map/ppermute | solution.py:559
  3.0 2.0 %collective-permute-start.1 = (f32[3,16,128]{2,1,0:T(8,128)S(1)}, f32[3,16,128]{2,1,0:T(8,128)S(1)}, u32[]{:S(2)}, u32[]{:S(2)}) collective-permute-start(f32[3,16,128]{2,1,0:T(8,128)S(1)} %get-tuple-element.37), channel_id=1, source_target_pairs={{1,0},{2,1},{3,2},{0,3},{5,4},{6,5},{7,6},{4,7},{9,8},{10,9},{11,1... | collective-permute-start | bytes 73736 | tf_op jit(solution)/shard_map/ppermute | solution.py:559
  5.0 1.4 %collective-permute-done.before_ref = f32[3,16,128]{2,1,0:T(8,128)S(1)} collective-permute-done((f32[3,16,128]{2,1,0:T(8,128)S(1)}, f32[3,16,128]{2,1,0:T(8,128)S(1)}, u32[]{:S(2)}, u32[]{:S(2)}) %collective-permute-start) | collective-permute-done | bytes 24608 | tf_op jit(solution)/shard_map/ppermute | solution.py:559
  6.5 0.1 collective-permute-done.1.after_ref
  6.6 0.2 sides.1
  6.7 2.3 %collective-permute-start.2 = (f32[3,72,128]{2,1,0:T(8,128)S(1)}, f32[3,72,128]{2,1,0:T(8,128)S(1)}, u32[]{:S(2)}, u32[]{:S(2)}) collective-permute-start(f32[3,72,128]{2,1,0:T(8,128)S(1)} %get-tuple-element.39), channel_id=1, source_target_pairs={{0,4},{4,8},{8,12},{12,16},{16,20},{20,24},{24,28},{28,0},{1,5},{5... | collective-permute-start | bytes 331784 | tf_op jit(solution)/shard_map/ppermute | solution.py:559
  9.0 3.1 %collective-permute-start.3 = (f32[3,72,128]{2,1,0:T(8,128)S(1)}, f32[3,72,128]{2,1,0:T(8,128)S(1)}, u32[]{:S(2)}, u32[]{:S(2)}) collective-permute-start(f32[3,72,128]{2,1,0:T(8,128)S(1)} %get-tuple-element.40), channel_id=1, source_target_pairs={{4,0},{8,4},{12,8},{16,12},{20,16},{24,20},{28,24},{0,28},{5,1},{9... | collective-permute-start | bytes 331784 | tf_op jit(solution)/shard_map/ppermute | solution.py:559
  12.1 0.0 copy-done.2
  12.1 0.1 copy.7.in_ref
  12.2 0.0 copy-done.1
  12.2 8.6 %middle.1 = (bf16[128,256]{1,0:T(8,128)(2,1)S(1)}, bf16[256,256]{1,0:T(8,128)(2,1)S(1)}, f32[2,4,12,16,128]{4,3,2,1,0:T(8,128)S(1)}, f32[2,2,10,16,128]{4,3,2,1,...) custom-call(f32[16,144,128]{2,1,0:T(8,128)S(1)} %get-tuple-element.3, ...), custom_call_target="tpu_custom_call" | custom-call | tf_op jit(solution)/shard_map/middle/pallas_call | solution.py:594
  20.8 0.0 collective-permute-done.2.before_ref
  20.8 0.0 collective-permute-done.3.after_ref
  20.8 4.3 %ends_first.1 = (f32[2,5,10,16,128]{4,3,2,1,0:T(8,128)S(1)}, f32[2,5,10,16,128]{4,3,2,1,0:T(8,128)S(1)}, f32[2,5,10,16,128]{4,3,2,1,0:T(8,128)S(1)}, f32[6,128,1...) custom-call(f32[16,144,128]{2,1,0:T(8,128)S(1)} %get-tuple-element.3, ...), custom_call_target="tpu_custom_call" | custom-call | tf_op jit(solution)/shard_map/ends_first/pallas_call | solution.py:616
  25.1 0.1 collective-permute-start.4
  25.2 1.4 %ends_last.1 = (f32[4,2,2,8,128]{4,3,2,1,0:T(8,128)S(1)}, f32[4,2,2,8,128]{4,3,2,1,0:T(8,128)S(1)}, f32[2,2,2,16,128]{4,3,2,1,0:T(8,128)S(1)}, f32[2,2,2,16,128]{4,3,2,1,0:T(8,128)S(1)}) custom-call(bf16[128,256]{1,0:T(8,128)(2,1)S(1)} %get-tuple-element.41.win_ref, bf16[256,256]{1,0:T(8,128)(2,1)S(1)} %get-tuple-element.42.wout_ref, ...), custom_call_target="tpu_custom_call" | custom-call | tf_op jit(solution)/shard_map/ends_last/pallas_call | solution.py:628
  26.6 1.4 %collective-permute-start.6 = (f32[2,2,2,16,128]{4,3,2,1,0:T(8,128)S(1)}, f32[2,2,2,16,128]{4,3,2,1,0:T(8,128)S(1)}, u32[]{:S(2)}, u32[]{:S(2)}) collective-permute-start(f32[2,2,2,16,128]{4,3,2,1,0:T(8,128)S(1)} %get-tuple-element.61), channel_id=1, source_target_pairs={{0,1},{1,0},{2,3},{3,2},{4,5},{5,4},{6,7},{7,6},{8,9},{9,8},{10,11... | collective-permute-start | bytes 196616 | tf_op jit(solution)/shard_map/ppermute | solution.py:563
  28.0 1.7 %collective-permute-start.5 = (f32[4,2,2,8,128]{4,3,2,1,0:T(8,128)S(1)}, f32[4,2,2,8,128]{4,3,2,1,0:T(8,128)S(1)}, u32[]{:S(2)}, u32[]{:S(2)}) collective-permute-start(f32[4,2,2,8,128]{4,3,2,1,0:T(8,128)S(1)} %get-tuple-element.59), channel_id=1, source_target_pairs={{0,4},{4,0},{8,12},{12,8},{16,20},{20,16},{24,28},{28,24},{1,5},{5... | collective-permute-start | bytes 196616 | tf_op jit(solution)/shard_map/ppermute | solution.py:563
  29.7 0.0 collective-permute-done.6.received_ref
  29.8 0.9 %collective-permute-start.7 = (f32[1,2,2,16,128]{4,3,2,1,0:T(8,128)S(1)}, f32[1,2,2,16,128]{4,3,2,1,0:T(8,128)S(1)}, u32[]{:S(2)}, u32[]{:S(2)}) collective-permute-start(f32[1,2,2,16,128]{4,3,2,1,0:T(8,128)S(1)} %get-tuple-element.62), channel_id=1, source_target_pairs={{0,2},{1,3},{2,0},{3,1},{4,6},{5,7},{6,4},{7,5},{8,10},{9,11},{10,... | collective-permute-start | bytes 98312 | tf_op jit(solution)/shard_map/ppermute | solution.py:563
  30.7 3.4 %collective-permute-done.5.refs_3_ = f32[4,2,2,8,128]{4,3,2,1,0:T(8,128)S(1)} collective-permute-done((f32[4,2,2,8,128]{4,3,2,1,0:T(8,128)S(1)}, f32[4,2,2,8,128]{4,3,2,1,0:T(8,128)S(1)}, u32[]{:S(2)}, u32[]{:S(2)}) %collective-permute-start.5) | collective-permute-done | bytes 65568 | tf_op jit(solution)/shard_map/ppermute | solution.py:563
  34.1 0.0 collective-permute-done.7.refs_4_.received_ref
  34.1 0.0 collective-permute-done.4.refs_1_
  34.1 0.2 collective-permute-start.8
  34.3 2.6 %collective-permute-start.9 = (f32[2,8,8,128]{3,2,1,0:T(8,128)S(1)}, f32[2,8,8,128]{3,2,1,0:T(8,128)S(1)}, u32[]{:S(2)}, u32[]{:S(2)}) collective-permute-start(f32[2,8,8,128]{3,2,1,0:T(8,128)S(1)} %get-tuple-element.65), channel_id=1, source_target_pairs={{0,16},{4,20},{8,24},{12,28},{16,0},{20,4},{24,8},{28,12},{1,17},{... | collective-permute-start | bytes 196616 | tf_op jit(solution)/shard_map/ppermute | solution.py:661
  36.8 1.3 %collective-permute-start.10 = (f32[2,8,8,128]{3,2,1,0:T(8,128)S(1)}, f32[2,8,8,128]{3,2,1,0:T(8,128)S(1)}, u32[]{:S(2)}, u32[]{:S(2)}) collective-permute-start(f32[2,8,8,128]{3,2,1,0:T(8,128)S(1)} %get-tuple-element.66), channel_id=1, source_target_pairs={{0,24},{4,28},{8,0},{12,4},{16,8},{20,12},{24,16},{28,20},{1,25},{... | collective-permute-start | bytes 196616 | tf_op jit(solution)/shard_map/ppermute | solution.py:661
  38.2 0.1 copy.8
  38.3 0.8 %copy.9 = f32[2,8,16,32]{3,2,1,0:T(8,128)} copy(f32[2,8,16,32]{2,1,3,0:T(8,128)S(1)} %bitcast.5) | data formatting | bytes 65536
  39.1 1.8 %collective-permute-done.8.refs_1_ = f32[2,8,8,128]{3,2,1,0:T(8,128)S(1)} collective-permute-done((f32[2,8,8,128]{3,2,1,0:T(8,128)S(1)}, f32[2,8,8,128]{3,2,1,0:T(8,128)S(1)}, u32[]{:S(2)}, u32[]{:S(2)}) %collective-permute-start.8) | collective-permute-done | bytes 65568 | tf_op jit(solution)/shard_map/ppermute | solution.py:661
  40.9 1.8 %collective-permute-done.9.refs_2_ = f32[2,8,8,128]{3,2,1,0:T(8,128)S(1)} collective-permute-done((f32[2,8,8,128]{3,2,1,0:T(8,128)S(1)}, f32[2,8,8,128]{3,2,1,0:T(8,128)S(1)}, u32[]{:S(2)}, u32[]{:S(2)}) %collective-permute-start.9) | collective-permute-done | bytes 65568 | tf_op jit(solution)/shard_map/ppermute | solution.py:661
  42.8 0.0 collective-permute-done.10.refs_3_
  42.8 0.9 %fold_x.1 = f32[2,8,8,128]{3,2,1,0:T(8,128)} custom-call(f32[2,8,8,128]{3,2,1,0:T(8,128)S(1)} %get-tuple-element.63.refs_0_, f32[2,8,8,128]{3,2,1,0:T(8,128)S(1)} %collective-permute-done.8.refs_1_, f32[2,8,8,128]{3,2,1,0:T(8,128)S(1)} %collective-permute-done.9.refs_2_, f32[2,8,8,128]{3,2,1,0:T(8,128)S(1)} %collective-permute-done.10.refs_3_), custom_call_target="tpu_custom_call" | custom-call | tf_op jit(solution)/shard_map/fold_x/pallas_call | solution.py:662
  (3 shorter events, 0.1 us)
Async XLA Ops:
  0.6 1.2 %copy-start = (f32[64,32,128]{2,1,0:T(8,128)S(1)}, f32[64,32,128]{2,1,0:T(8,128)}, u32[]{:S(2)}) copy-start(f32[64,32,128]{2,1,0:T(8,128)} %field_ref.1) | copy-start | bytes 3145732
  1.9 10.2 %copy-start.2 = (bf16[16,8]{0,1:T(8,128)(2,1)S(1)}, bf16[16,8]{0,1:T(8,128)(2,1)}, u32[]{:S(2)}) copy-start(bf16[16,8]{0,1:T(8,128)(2,1)} %param.4) | copy-start | bytes 772
  1.9 10.3 %copy-start.1 = (bf16[16,16]{1,0:T(8,128)(2,1)S(1)}, bf16[16,16]{1,0:T(8,128)(2,1)}, u32[]{:S(2)}) copy-start(bf16[16,16]{1,0:T(8,128)(2,1)} %out_ref.1) | copy-start | bytes 1540
  2.5 4.0 %collective-permute-start = (f32[3,16,128]{2,1,0:T(8,128)S(1)}, f32[3,16,128]{2,1,0:T(8,128)S(1)}, u32[]{:S(2)}, u32[]{:S(2)}) collective-permute-start(f32[3,16,128]{2,1,0:T(8,128)S(1)} %get-tuple-element.36), channel_id=1, source_target_pairs={{0,1},{1,2},{2,3},{3,0},{4,5},{5,6},{6,7},{7,4},{8,9},{9,10},{10,1... | collective-permute-start | bytes 73736 | tf_op jit(solution)/shard_map/ppermute | solution.py:559
  3.0 3.5 %collective-permute-start.1 = (f32[3,16,128]{2,1,0:T(8,128)S(1)}, f32[3,16,128]{2,1,0:T(8,128)S(1)}, u32[]{:S(2)}, u32[]{:S(2)}) collective-permute-start(f32[3,16,128]{2,1,0:T(8,128)S(1)} %get-tuple-element.37), channel_id=1, source_target_pairs={{1,0},{2,1},{3,2},{0,3},{5,4},{6,5},{7,6},{4,7},{9,8},{10,9},{11,1... | collective-permute-start | bytes 73736 | tf_op jit(solution)/shard_map/ppermute | solution.py:559
  6.7 14.0 %collective-permute-start.2 = (f32[3,72,128]{2,1,0:T(8,128)S(1)}, f32[3,72,128]{2,1,0:T(8,128)S(1)}, u32[]{:S(2)}, u32[]{:S(2)}) collective-permute-start(f32[3,72,128]{2,1,0:T(8,128)S(1)} %get-tuple-element.39), channel_id=1, source_target_pairs={{0,4},{4,8},{8,12},{12,16},{16,20},{20,24},{24,28},{28,0},{1,5},{5... | collective-permute-start | bytes 331784 | tf_op jit(solution)/shard_map/ppermute | solution.py:559
  9.0 11.8 %collective-permute-start.3 = (f32[3,72,128]{2,1,0:T(8,128)S(1)}, f32[3,72,128]{2,1,0:T(8,128)S(1)}, u32[]{:S(2)}, u32[]{:S(2)}) collective-permute-start(f32[3,72,128]{2,1,0:T(8,128)S(1)} %get-tuple-element.40), channel_id=1, source_target_pairs={{4,0},{8,4},{12,8},{16,12},{20,16},{24,20},{28,24},{0,28},{5,1},{9... | collective-permute-start | bytes 331784 | tf_op jit(solution)/shard_map/ppermute | solution.py:559
  25.1 9.0 %collective-permute-start.4 = (f32[4,2,6,8,128]{4,3,2,1,0:T(8,128)S(1)}, f32[4,2,6,8,128]{4,3,2,1,0:T(8,128)S(1)}, u32[]{:S(2)}, u32[]{:S(2)}) collective-permute-start(f32[4,2,6,8,128]{4,3,2,1,0:T(8,128)S(1)} %get-tuple-element.50), channel_id=1, source_target_pairs={{0,4},{4,0},{8,12},{12,8},{16,20},{20,16},{24,28},{28,24},{1,5},{5... | collective-permute-start | bytes 589832 | tf_op jit(solution)/shard_map/ppermute | solution.py:563
  26.6 3.1 %collective-permute-start.6 = (f32[2,2,2,16,128]{4,3,2,1,0:T(8,128)S(1)}, f32[2,2,2,16,128]{4,3,2,1,0:T(8,128)S(1)}, u32[]{:S(2)}, u32[]{:S(2)}) collective-permute-start(f32[2,2,2,16,128]{4,3,2,1,0:T(8,128)S(1)} %get-tuple-element.61), channel_id=1, source_target_pairs={{0,1},{1,0},{2,3},{3,2},{4,5},{5,4},{6,7},{7,6},{8,9},{9,8},{10,11... | collective-permute-start | bytes 196616 | tf_op jit(solution)/shard_map/ppermute | solution.py:563
  28.0 6.1 %collective-permute-start.5 = (f32[4,2,2,8,128]{4,3,2,1,0:T(8,128)S(1)}, f32[4,2,2,8,128]{4,3,2,1,0:T(8,128)S(1)}, u32[]{:S(2)}, u32[]{:S(2)}) collective-permute-start(f32[4,2,2,8,128]{4,3,2,1,0:T(8,128)S(1)} %get-tuple-element.59), channel_id=1, source_target_pairs={{0,4},{4,0},{8,12},{12,8},{16,20},{20,16},{24,28},{28,24},{1,5},{5... | collective-permute-start | bytes 196616 | tf_op jit(solution)/shard_map/ppermute | solution.py:563
  29.8 4.3 %collective-permute-start.7 = (f32[1,2,2,16,128]{4,3,2,1,0:T(8,128)S(1)}, f32[1,2,2,16,128]{4,3,2,1,0:T(8,128)S(1)}, u32[]{:S(2)}, u32[]{:S(2)}) collective-permute-start(f32[1,2,2,16,128]{4,3,2,1,0:T(8,128)S(1)} %get-tuple-element.62), channel_id=1, source_target_pairs={{0,2},{1,3},{2,0},{3,1},{4,6},{5,7},{6,4},{7,5},{8,10},{9,11},{10,... | collective-permute-start | bytes 98312 | tf_op jit(solution)/shard_map/ppermute | solution.py:563
  34.1 6.8 %collective-permute-start.8 = (f32[2,8,8,128]{3,2,1,0:T(8,128)S(1)}, f32[2,8,8,128]{3,2,1,0:T(8,128)S(1)}, u32[]{:S(2)}, u32[]{:S(2)}) collective-permute-start(f32[2,8,8,128]{3,2,1,0:T(8,128)S(1)} %get-tuple-element.64), channel_id=1, source_target_pairs={{0,8},{4,12},{8,16},{12,20},{16,24},{20,28},{24,0},{28,4},{1,9},{5... | collective-permute-start | bytes 196616 | tf_op jit(solution)/shard_map/ppermute | solution.py:661
  34.3 8.5 %collective-permute-start.9 = (f32[2,8,8,128]{3,2,1,0:T(8,128)S(1)}, f32[2,8,8,128]{3,2,1,0:T(8,128)S(1)}, u32[]{:S(2)}, u32[]{:S(2)}) collective-permute-start(f32[2,8,8,128]{3,2,1,0:T(8,128)S(1)} %get-tuple-element.65), channel_id=1, source_target_pairs={{0,16},{4,20},{8,24},{12,28},{16,0},{20,4},{24,8},{28,12},{1,17},{... | collective-permute-start | bytes 196616 | tf_op jit(solution)/shard_map/ppermute | solution.py:661
  36.8 5.9 %collective-permute-start.10 = (f32[2,8,8,128]{3,2,1,0:T(8,128)S(1)}, f32[2,8,8,128]{3,2,1,0:T(8,128)S(1)}, u32[]{:S(2)}, u32[]{:S(2)}) collective-permute-start(f32[2,8,8,128]{3,2,1,0:T(8,128)S(1)} %get-tuple-element.66), channel_id=1, source_target_pairs={{0,24},{4,28},{8,0},{12,4},{16,8},{20,12},{24,16},{28,20},{1,25},{... | collective-permute-start | bytes 196616 | tf_op jit(solution)/shard_map/ppermute | solution.py:661

commit v11 on v10

--- a/solution.py
+++ b/solution.py
@@ -14,7 +14,6 @@
 LANES = 128
 CHUNKS = 16
 REACH = 3
-AHEAD = 2
 VMEM = pl.BlockSpec(memory_space=pltpu.VMEM)
 PARAMS = pltpu.CompilerParams(vmem_limit_bytes=36 * 1024 * 1024)
 
@@ -207,7 +206,6 @@
 
 
 def middle_kernel(
-    spans,
     counts,
     steps,
     wide_ref,
@@ -223,30 +221,21 @@
     tx_ref,
     cy_ref,
     ty_ref,
-    once_ref,
-    twice_ref,
-    ridge_ref,
-    slope_ref,
+    *refs,
 ):
+    later_refs, (once_ref, twice_ref, ridge_ref, slope_ref) = refs[:3], refs[3:]
     half = wide_ref.shape[0]
-    run = cx_ref.shape[0]
+    run, ahead = once_ref.shape[1] - 4, cx_ref.shape[0]
     stencil = Stencil(run, counts)
     inner = half - 2 * REACH
     spread_weights(in_ref, out_ref, win_ref, wout_ref)
-    for k in range(run):
+    for k in range(ahead):
         tx_ref[k] = jnp.ones((LANES, LANES), F32)
         cx_ref[k] = jnp.zeros((LANES, LANES), F32)
     for k in range(inner):
         ty_ref[k] = jnp.ones((LANES, LANES), F32)
         cy_ref[k] = jnp.zeros((LANES, LANES), F32)
     ratio = steps[0] / steps[1]
-
-    def prepare(first, last):
-        start = 0 if first == 0 else first + 2
-        for k in range(start, last + 2):
-            stencil.once(wide_ref, k + 1, once_ref, k)
-        for k in range(first, last):
-            stencil.twice(once_ref, k + 1, twice_ref, ridge_ref, slope_ref, k)
 
     def block(x0, y0, many_x, many_y):
         tiles = [
@@ -269,23 +258,23 @@
             for i in range(many_x):
                 cy_ref[x0 + i, at], ty_ref[x0 + i, at] = rays_y[i]
 
-    many_x, many_y = spans
-    ready = 0
-    for x0 in range(0, inner, many_x):
-        ahead = min(inner + 2, x0 + many_x + 2 + AHEAD)
-        prepare(ready, ahead)
-        ready = ahead
-        for y0 in range(0, run, many_y):
-            block(x0, y0, many_x, many_y)
+    many_y = 2 if ahead % 2 == 0 else 1
+    for k in range(inner + 4):
+        stencil.once(wide_ref, k + 1, once_ref, k)
+    for k in range(inner + 2):
+        stencil.twice(once_ref, k + 1, twice_ref, ridge_ref, slope_ref, k)
+    for y0 in range(0, ahead, many_y):
+        block(0, y0, inner, many_y)
     for k in range(4):
         once_out_ref[0, k] = once_ref[k]
         once_out_ref[1, k] = once_ref[inner + k]
-    for k in range(2):
-        for out_ref, ref in ((twice_out_ref, twice_ref), (ridge_out_ref, ridge_ref)):
+    fields = (twice_ref, ridge_ref, slope_ref)
+    outs = (twice_out_ref, ridge_out_ref, slope_out_ref)
+    for out_ref, later_ref, ref in zip(outs, later_refs, fields):
+        for k in range(2):
             out_ref[0, k] = ref[k]
             out_ref[1, k] = ref[inner + k]
-        slope_out_ref[0, k] = slope_ref[k]
-        slope_out_ref[1, k] = slope_ref[inner + k]
+        later_ref[...] = ref[:, ahead:]
 
 
 def parts_of(image_ref, kept_ref, sent_ref, mine):
@@ -296,38 +285,30 @@
             out_ref[r] = image_ref[:, :, pl.ds(start, share), :]
 
 
-def march_ends(stencil, steps, first, weights, fields, middle, rays, image_ref):
-    cx_ref, tx_ref = middle
-    cy_ref, ty_ref = rays
+def march_planes(stencil, steps, tiles, many_y, weights, rays, middle, image_ref):
     layers = stencil.layers
-    many_y = image_ref.shape[1]
     ratio = steps[0] / steps[1]
-    planes = [(0, 1), (0, 2), (0, 3), (1, 1), (1, 2), (1, 3)]
-    tiles = [
-        stencil.features(*[ref.at[side] for ref in fields], k, first + j)
-        for j in range(many_y)
-        for side, k in planes
-    ]
+    many_x = len(rays)
     emission, clear = network(tiles, *weights, steps[1])
     images = [[], []]
     for g in range(LANES // SUB):
         at = pl.ds(g * SUB, SUB)
-        rays_y = [(cy_ref[i, at], ty_ref[i, at]) for i in range(len(planes))]
+        rays_y = [(cy_ref[at], ty_ref[at]) for cy_ref, ty_ref in rays]
         for j in range(many_y):
             ray_x = jnp.zeros((SUB, LANES), F32), jnp.ones((SUB, LANES), F32)
-            for i in range(len(planes)):
-                if i == REACH:
+            for i in range(many_x):
+                if i == REACH and middle is not None:
                     colour, light = ray_x
-                    colour = colour + light * cx_ref[first + j, at]
-                    ray_x = colour, light * tx_ref[first + j, at]
-                start = (j * len(planes) + i) * LANES + g * SUB
+                    colour = colour + light * middle[0][j, at]
+                    ray_x = colour, light * middle[1][j, at]
+                start = (j * many_x + i) * LANES + g * SUB
                 e, q = emission[start : start + SUB], clear[start : start + SUB]
                 rays_y[i] = step_ray(rays_y[i], q, e)
                 ray_x = step_ray(ray_x, clear_of_x(q, ratio), e)
             images[0].append(ray_x[0])
             images[1].append(ray_x[1])
-        for i in range(len(planes)):
-            cy_ref[i, at], ty_ref[i, at] = rays_y[i]
+        for (cy_ref, ty_ref), ray in zip(rays, rays_y):
+            cy_ref[at], ty_ref[at] = ray
     for d in range(layers // SUB):
         for j in range(many_y):
             near, far = d * many_y + j, (d + layers // SUB) * many_y + j
@@ -363,7 +344,7 @@
     once_ref,
 ):
     half, rows, _ = wide_ref.shape
-    run = cx_ref.shape[0]
+    run = once_ref.shape[2] - 4
     layers = LANES // 2
     stencil = Stencil(run, counts)
     part = rows // 2
@@ -404,67 +385,51 @@
     for k in range(2 * REACH):
         ty_ref[k] = jnp.ones((LANES, LANES), F32)
         cy_ref[k] = jnp.zeros((LANES, LANES), F32)
-    march_ends(
-        stencil,
-        steps,
-        0,
-        (win_ref, wout_ref),
-        (twice_ref, ridge_ref, slope_ref),
-        (cx_ref, tx_ref),
-        (cy_ref, ty_ref),
-        image_ref,
+    fields = (twice_ref, ridge_ref, slope_ref)
+    ahead = image_ref.shape[1]
+    tiles = [
+        stencil.features(*[ref.at[side] for ref in fields], k, y)
+        for y in range(ahead)
+        for side in range(2)
+        for k in range(1, REACH + 1)
+    ]
+    rays = [(cy_ref.at[k], ty_ref.at[k]) for k in range(2 * REACH)]
+    march_planes(
+        stencil, steps, tiles, ahead, (win_ref, wout_ref), rays, (cx_ref, tx_ref), image_ref
     )
     parts_of(image_ref, kept_ref, sent_ref, at_x & 1)
 
 
-def ends_last_kernel(
-    counts,
-    steps,
-    win_ref,
-    wout_ref,
-    twice_ref,
-    ridge_ref,
-    slope_ref,
-    cx_ref,
-    tx_ref,
-    cy_in_ref,
-    ty_in_ref,
-    cy_middle_ref,
-    ty_middle_ref,
-    kept_ref,
-    sent_ref,
-    kept_y_ref,
-    sent_y_ref,
-    image_ref,
-    cy_ref,
-    ty_ref,
-    rows_ref,
-    columns_ref,
-):
-    run = cx_ref.shape[0]
+def last_kernel(counts, steps, *refs):
+    win_ref, wout_ref, *refs = refs
+    ends, middle, refs = refs[:3], refs[3:6], refs[6:]
+    cy_ends_ref, ty_ends_ref, cy_middle_ref, ty_middle_ref = refs[:4]
+    kept_ref, sent_ref, kept_y_ref, sent_y_ref = refs[4:8]
+    image_ref, cy_ref, ty_ref, rows_ref, columns_ref = refs[8:]
+    run = ends[0].shape[2] - 2
     stencil = Stencil(run, counts)
     layers = stencil.layers
-    cy_ref[...] = cy_in_ref[...]
-    ty_ref[...] = ty_in_ref[...]
-    march_ends(
-        stencil,
-        steps,
-        run - image_ref.shape[1],
-        (win_ref, wout_ref),
-        (twice_ref, ridge_ref, slope_ref),
-        (cx_ref, tx_ref),
-        (cy_ref, ty_ref),
-        image_ref,
-    )
-    parts_of(image_ref, kept_ref, sent_ref, lax.axis_index("bx") & 1)
     inner = cy_middle_ref.shape[0]
     half = inner + 2 * REACH
+    many_y = image_ref.shape[1]
+    for old, new in ((cy_ends_ref, cy_ref), (ty_ends_ref, ty_ref)):
+        new[:REACH], new[half - REACH :] = old[:REACH], old[REACH:]
+    for old, new in ((cy_middle_ref, cy_ref), (ty_middle_ref, ty_ref)):
+        new[REACH : half - REACH] = old[...]
+    tiles = []
+    for j in range(many_y):
+        for k in range(half):
+            if REACH <= k < half - REACH:
+                tiles.append(stencil.features(*middle, k - REACH + 1, j))
+            else:
+                side, k = (0, k + 1) if k < REACH else (1, k - half + REACH + 1)
+                fields = [ref.at[side] for ref in ends]
+                tiles.append(stencil.features(*fields, k, run - many_y + j))
+    rays = [(cy_ref.at[k], ty_ref.at[k]) for k in range(half)]
+    march_planes(stencil, steps, tiles, many_y, (win_ref, wout_ref), rays, None, image_ref)
+    parts_of(image_ref, kept_ref, sent_ref, lax.axis_index("bx") & 1)
     for k in range(half):
-        if REACH <= k < REACH + inner:
-            image = column_image(cy_middle_ref[k - REACH], ty_middle_ref[k - REACH])
-        else:
-            i = k if k < REACH else k - inner
-            image = column_image(cy_ref[i], ty_ref[i])
+        image = column_image(cy_ref[k], ty_ref[k])
         for kind in range(2):
             rows_ref[kind, k * SUB : (k + 1) * SUB] = image[kind]
     for kind in range(2):
@@ -590,13 +555,17 @@
     inner = half - 2 * REACH
     counts = (count_x, count_y)
     plane = lambda *lead: sds(*lead, CHUNKS, LANES)
-    many_x, many_y = inner, 2
-    win, wout, once, twice, ridge, slope, colour_x, clear_x, colour_y, clear_y = call(
-        functools.partial(middle_kernel, (many_x, many_y), counts, steps),
+    ahead = run - run // 4
+    later = run - ahead
+    win, wout, once, twice, ridge, slope, colour_x, clear_x, colour_y, clear_y, *fields = call(
+        functools.partial(middle_kernel, counts, steps),
         "middle",
-        weights + [plane(2, 4, run + 4)] + [plane(2, 2, run + 2)] * 3
-        + [sds(run, LANES, LANES)] * 2
-        + [sds(inner, LANES, LANES)] * 2,
+        weights
+        + [plane(2, 4, run + 4)]
+        + [plane(2, 2, run + 2)] * 3
+        + [sds(ahead, LANES, LANES)] * 2
+        + [sds(inner, LANES, LANES)] * 2
+        + [plane(inner + 2, later + 2)] * 3,
         3,
         [
             pltpu.VMEM((inner + 4, run + 4, CHUNKS, LANES), F32),
@@ -607,11 +576,9 @@
     )(wide, transfer_in, transfer_out)
     share = layers // count_x
     share_y = layers // count_y
-    ahead = run - run // 4
     parts = lambda many: [sds(count_x // 2, 2, many, share, LANES)] * 2
     parts_y = sds(count_y // 2, 2, 2, share_y, LANES)
     image = lambda many: pltpu.VMEM((2, many, layers, LANES), F32)
-    ray = pltpu.VMEM((2 * REACH, LANES, LANES), F32)
     field = plane(2, 5, run + 2)
     twice, ridge, slope, colour_ends, clear_ends, kept, sent = call(
         functools.partial(ends_first_kernel, counts, steps),
@@ -625,21 +592,20 @@
         ],
     )(wide, before, after, win, wout, once, twice, ridge, slope, colour_x, clear_x)
     halves = [(kept, swap(sent, "bx", 1))]
+    ray = pltpu.VMEM((half, LANES, LANES), F32)
     kept, sent, kept_y, sent_y = call(
-        functools.partial(ends_last_kernel, counts, steps),
-        "ends_last",
-        parts(run - ahead) + [parts_y] * 2,
-        11,
+        functools.partial(last_kernel, counts, steps),
+        "last",
+        parts(later) + [parts_y] * 2,
+        12,
         [
-            image(run - ahead),
+            image(later),
             ray,
             ray,
             pltpu.VMEM((2, LANES, LANES), F32),
             pltpu.VMEM((2, 2, layers, LANES), F32),
         ],
-    )(
-        win, wout, twice, ridge, slope, colour_x, clear_x, colour_ends, clear_ends, colour_y, clear_y
-    )
+    )(win, wout, twice, ridge, slope, *fields, colour_ends, clear_ends, colour_y, clear_y)
     halves += [(kept, swap(sent, "bx", 1))]
 
     level, many = 1, count_y // 2

time: 43.8 us -> 42.3 us (0.966)
  waiting for transfers between devices: 8.58 us -> 7.32 us
    ppermute x3, waiting for transfers between devices: 3.64 us -> 2.7 us  [body(): pieces[t] = lax.ppermute(pieces[t], 'bx', pairs)]
  transfers between devices with their start and end apart: 11 -> 11, of which waited for: 5 -> 6; matrix products, arithmetic and copies ran while one was open for 2% -> 2% of each run, Pallas kernels for 23% -> 24%
where the time goes in v11:
time: 42.3 us; the launch traced here: 42.2 us
  Pallas kernels  16.1 us (38%)
  starting transfers between devices  15.9 us (38%)
  waiting for transfers between devices  7.32 us (17%)
  local copies, waits for them, and re-layouts  2.23 us (5%)
  between operations  0.72 us (2%)
    ppermute x4, starting transfers between devices, exchange(): return (lax.ppermute(last, axis, up), lax.ppermute(first, axis, down))  7.89 us
    pallas_call x1, Pallas kernels, body(): call(functools.partial(middle_kernel, counts, steps), 'middle', weights +...  6.96 us
    pallas_call x1, Pallas kernels, body(): call(functools.partial(ends_first_kernel, counts, steps), 'ends_first', [...  4.15 us
    ppermute x4, starting transfers between devices, swap(): lax.ppermute(value, axis, [(i, i ^ bit) for i in range(lax.axis_size(axis...  4.11 us
    ppermute x3, starting transfers between devices, body(): pieces[t] = lax.ppermute(pieces[t], 'bx', pairs)  3.87 us
    pallas_call x1, Pallas kernels, body(): call(functools.partial(last_kernel, counts, steps), 'last', parts(later)...  3.19 us
    ppermute x4, waiting for transfers between devices, swap(): lax.ppermute(value, axis, [(i, i ^ bit) for i in range(lax.axis_size(axis...  3.09 us
    ppermute x3, waiting for transfers between devices, body(): pieces[t] = lax.ppermute(pieces[t], 'bx', pairs)  2.7 us
  transfers between devices with their start and end apart: 11, of which 6 were waited for; matrix products, arithmetic and copies ran while one was open for 2% of the time, Pallas kernels for 24%

profile of v11, /device:TPU:0, one launch (start us, length us, event | category | flops | bytes accessed | tf_op | source)
XLA Modules:
  0.0 42.2 jit_solution(8702580392250072561)
XLA Ops:
  0.6 0.0 copy-start
  0.6 1.2 %copy-done = f32[64,32,128]{2,1,0:T(8,128)S(1)} copy-done((f32[64,32,128]{2,1,0:T(8,128)S(1)}, f32[64,32,128]{2,1,0:T(8,128)}, u32[]{:S(2)}) %copy-start) | copy-done | bytes 1048600
  1.9 0.0 copy-start.2
  1.9 0.0 copy-start.1
  1.9 0.6 %turn.1 = (f32[16,144,128]{2,1,0:T(8,128)S(1)}, f32[3,16,128]{2,1,0:T(8,128)S(1)}, f32[3,16,128]{2,1,0:T(8,128)S(1)}) custom-call(f32[64,32,128]{2,1,0:T(8,128)S(1)} %copy-done), custom_call_target="tpu_custom_call" | custom-call | tf_op jit(solution)/shard_map/turn/pallas_call | solution.py:546
  2.5 0.5 %collective-permute-start = (f32[3,16,128]{2,1,0:T(8,128)S(1)}, f32[3,16,128]{2,1,0:T(8,128)S(1)}, u32[]{:S(2)}, u32[]{:S(2)}) collective-permute-start(f32[3,16,128]{2,1,0:T(8,128)S(1)} %get-tuple-element.39), channel_id=1, source_target_pairs={{0,1},{1,2},{2,3},{3,0},{4,5},{5,6},{6,7},{7,4},{8,9},{9,10},{10,1... | collective-permute-start | bytes 73736 | tf_op jit(solution)/shard_map/ppermute | solution.py:524
  3.0 2.0 %collective-permute-start.1 = (f32[3,16,128]{2,1,0:T(8,128)S(1)}, f32[3,16,128]{2,1,0:T(8,128)S(1)}, u32[]{:S(2)}, u32[]{:S(2)}) collective-permute-start(f32[3,16,128]{2,1,0:T(8,128)S(1)} %get-tuple-element.40), channel_id=1, source_target_pairs={{1,0},{2,1},{3,2},{0,3},{5,4},{6,5},{7,6},{4,7},{9,8},{10,9},{11,1... | collective-permute-start | bytes 73736 | tf_op jit(solution)/shard_map/ppermute | solution.py:524
  5.0 1.4 %collective-permute-done.before_ref = f32[3,16,128]{2,1,0:T(8,128)S(1)} collective-permute-done((f32[3,16,128]{2,1,0:T(8,128)S(1)}, f32[3,16,128]{2,1,0:T(8,128)S(1)}, u32[]{:S(2)}, u32[]{:S(2)}) %collective-permute-start) | collective-permute-done | bytes 24608 | tf_op jit(solution)/shard_map/ppermute | solution.py:524
  6.5 0.1 collective-permute-done.1.after_ref
  6.6 0.2 sides.1
  6.7 2.3 %collective-permute-start.2 = (f32[3,72,128]{2,1,0:T(8,128)S(1)}, f32[3,72,128]{2,1,0:T(8,128)S(1)}, u32[]{:S(2)}, u32[]{:S(2)}) collective-permute-start(f32[3,72,128]{2,1,0:T(8,128)S(1)} %get-tuple-element.42), channel_id=1, source_target_pairs={{0,4},{4,8},{8,12},{12,16},{16,20},{20,24},{24,28},{28,0},{1,5},{5... | collective-permute-start | bytes 331784 | tf_op jit(solution)/shard_map/ppermute | solution.py:524
  9.0 3.1 %collective-permute-start.3 = (f32[3,72,128]{2,1,0:T(8,128)S(1)}, f32[3,72,128]{2,1,0:T(8,128)S(1)}, u32[]{:S(2)}, u32[]{:S(2)}) collective-permute-start(f32[3,72,128]{2,1,0:T(8,128)S(1)} %get-tuple-element.43), channel_id=1, source_target_pairs={{4,0},{8,4},{12,8},{16,12},{20,16},{24,20},{28,24},{0,28},{5,1},{9... | collective-permute-start | bytes 331784 | tf_op jit(solution)/shard_map/ppermute | solution.py:524
  12.1 0.0 copy-done.2
  12.1 0.1 copy.7.in_ref
  12.2 0.0 copy-done.1
  12.2 7.0 %middle.1 = (bf16[128,256]{1,0:T(8,128)(2,1)S(1)}, bf16[256,256]{1,0:T(8,128)(2,1)S(1)}, f32[2,4,12,16,128]{4,3,2,1,0:T(8,128)S(1)}, f32[2,2,10,16,128]{4,3,2,1,...) custom-call(f32[16,144,128]{2,1,0:T(8,128)S(1)} %get-tuple-element.4, ...), custom_call_target="tpu_custom_call" | custom-call | tf_op jit(solution)/shard_map/middle/pallas_call | solution.py:560
  19.1 0.0 collective-permute-done.2.before_ref
  19.1 0.0 collective-permute-done.3.after_ref
  19.2 4.1 %ends_first.1 = (f32[2,5,10,16,128]{4,3,2,1,0:T(8,128)S(1)}, f32[2,5,10,16,128]{4,3,2,1,0:T(8,128)S(1)}, f32[2,5,10,16,128]{4,3,2,1,0:T(8,128)S(1)}, f32[6,128,1...) custom-call(f32[16,144,128]{2,1,0:T(8,128)S(1)} %get-tuple-element.4, ...), custom_call_target="tpu_custom_call" | custom-call | tf_op jit(solution)/shard_map/ends_first/pallas_call | solution.py:583
  23.3 0.1 collective-permute-start.4
  23.4 3.2 %last.1 = (f32[4,2,2,8,128]{4,3,2,1,0:T(8,128)S(1)}, f32[4,2,2,8,128]{4,3,2,1,0:T(8,128)S(1)}, f32[2,2,2,16,128]{4,3,2,1,0:T(8,128)S(1)}, f32[2,2,2,16,128]{4,3,2,1,0:T(8,128)S(1)}) custom-call(bf16[128,256]{1,0:T(8,128)(2,1)S(1)} %get-tuple-element.44.win_ref.refs_0_, bf16[256,256]{1,0:T(8,128)(2,1)S(1)} %get-tuple-element.45.wout_ref.refs_1_, ...), custom_call_target="tpu_custom_call" | custom-call | tf_op jit(solution)/shard_map/last/pallas_call | solution.py:596
  26.6 1.4 %collective-permute-start.6 = (f32[2,2,2,16,128]{4,3,2,1,0:T(8,128)S(1)}, f32[2,2,2,16,128]{4,3,2,1,0:T(8,128)S(1)}, u32[]{:S(2)}, u32[]{:S(2)}) collective-permute-start(f32[2,2,2,16,128]{4,3,2,1,0:T(8,128)S(1)} %get-tuple-element.67), channel_id=1, source_target_pairs={{0,1},{1,0},{2,3},{3,2},{4,5},{5,4},{6,7},{7,6},{8,9},{9,8},{10,11... | collective-permute-start | bytes 196616 | tf_op jit(solution)/shard_map/ppermute | solution.py:528
  28.0 1.7 %collective-permute-start.5 = (f32[4,2,2,8,128]{4,3,2,1,0:T(8,128)S(1)}, f32[4,2,2,8,128]{4,3,2,1,0:T(8,128)S(1)}, u32[]{:S(2)}, u32[]{:S(2)}) collective-permute-start(f32[4,2,2,8,128]{4,3,2,1,0:T(8,128)S(1)} %get-tuple-element.65), channel_id=1, source_target_pairs={{0,4},{4,0},{8,12},{12,8},{16,20},{20,16},{24,28},{28,24},{1,5},{5... | collective-permute-start | bytes 196616 | tf_op jit(solution)/shard_map/ppermute | solution.py:528
  29.7 0.0 collective-permute-done.6.received_ref
  29.8 0.9 %collective-permute-start.7 = (f32[1,2,2,16,128]{4,3,2,1,0:T(8,128)S(1)}, f32[1,2,2,16,128]{4,3,2,1,0:T(8,128)S(1)}, u32[]{:S(2)}, u32[]{:S(2)}) collective-permute-start(f32[1,2,2,16,128]{4,3,2,1,0:T(8,128)S(1)} %get-tuple-element.68), channel_id=1, source_target_pairs={{0,2},{1,3},{2,0},{3,1},{4,6},{5,7},{6,4},{7,5},{8,10},{9,11},{10,... | collective-permute-start | bytes 98312 | tf_op jit(solution)/shard_map/ppermute | solution.py:528
  30.7 1.9 %collective-permute-done.5.refs_3_ = f32[4,2,2,8,128]{4,3,2,1,0:T(8,128)S(1)} collective-permute-done((f32[4,2,2,8,128]{4,3,2,1,0:T(8,128)S(1)}, f32[4,2,2,8,128]{4,3,2,1,0:T(8,128)S(1)}, u32[]{:S(2)}, u32[]{:S(2)}) %collective-permute-start.5) | collective-permute-done | bytes 65568 | tf_op jit(solution)/shard_map/ppermute | solution.py:528
  32.6 1.2 %collective-permute-done.7.refs_4_.received_ref = f32[1,2,2,16,128]{4,3,2,1,0:T(8,128)S(1)} collective-permute-done((f32[1,2,2,16,128]{4,3,2,1,0:T(8,128)S(1)}, f32[1,2,2,16,128]{4,3,2,1,0:T(8,128)S(1)}, u32[]{:S(2)}, u32[]{:S(2)}) %collective-permute-start.7) | collective-permute-done | bytes 32800 | tf_op jit(solution)/shard_map/ppermute | solution.py:528
  33.7 0.0 collective-permute-done.4.refs_1_
  33.8 0.1 collective-permute-start.8
  33.8 2.2 %collective-permute-start.9 = (f32[2,8,8,128]{3,2,1,0:T(8,128)S(1)}, f32[2,8,8,128]{3,2,1,0:T(8,128)S(1)}, u32[]{:S(2)}, u32[]{:S(2)}) collective-permute-start(f32[2,8,8,128]{3,2,1,0:T(8,128)S(1)} %get-tuple-element.71), channel_id=1, source_target_pairs={{0,16},{4,20},{8,24},{12,28},{16,0},{20,4},{24,8},{28,12},{1,17},{... | collective-permute-start | bytes 196616 | tf_op jit(solution)/shard_map/ppermute | solution.py:627
  36.0 1.6 %collective-permute-start.10 = (f32[2,8,8,128]{3,2,1,0:T(8,128)S(1)}, f32[2,8,8,128]{3,2,1,0:T(8,128)S(1)}, u32[]{:S(2)}, u32[]{:S(2)}) collective-permute-start(f32[2,8,8,128]{3,2,1,0:T(8,128)S(1)} %get-tuple-element.72), channel_id=1, source_target_pairs={{0,24},{4,28},{8,0},{12,4},{16,8},{20,12},{24,16},{28,20},{1,25},{... | collective-permute-start | bytes 196616 | tf_op jit(solution)/shard_map/ppermute | solution.py:627
  37.7 0.1 copy.8
  37.8 0.8 %copy.9 = f32[2,8,16,32]{3,2,1,0:T(8,128)} copy(f32[2,8,16,32]{2,1,3,0:T(8,128)S(1)} %bitcast.5) | data formatting | bytes 65536
  38.6 1.5 %collective-permute-done.8.refs_1_ = f32[2,8,8,128]{3,2,1,0:T(8,128)S(1)} collective-permute-done((f32[2,8,8,128]{3,2,1,0:T(8,128)S(1)}, f32[2,8,8,128]{3,2,1,0:T(8,128)S(1)}, u32[]{:S(2)}, u32[]{:S(2)}) %collective-permute-start.8) | collective-permute-done | bytes 65568 | tf_op jit(solution)/shard_map/ppermute | solution.py:627
  40.1 1.2 %collective-permute-done.9.refs_2_ = f32[2,8,8,128]{3,2,1,0:T(8,128)S(1)} collective-permute-done((f32[2,8,8,128]{3,2,1,0:T(8,128)S(1)}, f32[2,8,8,128]{3,2,1,0:T(8,128)S(1)}, u32[]{:S(2)}, u32[]{:S(2)}) %collective-permute-start.9) | collective-permute-done | bytes 65568 | tf_op jit(solution)/shard_map/ppermute | solution.py:627
  41.3 0.0 collective-permute-done.10.refs_3_
  41.3 0.9 %fold_x.1 = f32[2,8,8,128]{3,2,1,0:T(8,128)} custom-call(f32[2,8,8,128]{3,2,1,0:T(8,128)S(1)} %get-tuple-element.69.refs_0_, f32[2,8,8,128]{3,2,1,0:T(8,128)S(1)} %collective-permute-done.8.refs_1_, f32[2,8,8,128]{3,2,1,0:T(8,128)S(1)} %collective-permute-done.9.refs_2_, f32[2,8,8,128]{3,2,1,0:T(8,128)S(1)} %collective-permute-done.10.refs_3_), custom_call_target="tpu_custom_call" | custom-call | tf_op jit(solution)/shard_map/fold_x/pallas_call | solution.py:628
  (3 shorter events, 0.1 us)
Async XLA Ops:
  0.6 1.2 %copy-start = (f32[64,32,128]{2,1,0:T(8,128)S(1)}, f32[64,32,128]{2,1,0:T(8,128)}, u32[]{:S(2)}) copy-start(f32[64,32,128]{2,1,0:T(8,128)} %field_ref.1) | copy-start | bytes 3145732
  1.9 10.2 %copy-start.2 = (bf16[16,8]{0,1:T(8,128)(2,1)S(1)}, bf16[16,8]{0,1:T(8,128)(2,1)}, u32[]{:S(2)}) copy-start(bf16[16,8]{0,1:T(8,128)(2,1)} %param.4) | copy-start | bytes 772
  1.9 10.3 %copy-start.1 = (bf16[16,16]{1,0:T(8,128)(2,1)S(1)}, bf16[16,16]{1,0:T(8,128)(2,1)}, u32[]{:S(2)}) copy-start(bf16[16,16]{1,0:T(8,128)(2,1)} %out_ref.1) | copy-start | bytes 1540
  2.5 4.0 %collective-permute-start = (f32[3,16,128]{2,1,0:T(8,128)S(1)}, f32[3,16,128]{2,1,0:T(8,128)S(1)}, u32[]{:S(2)}, u32[]{:S(2)}) collective-permute-start(f32[3,16,128]{2,1,0:T(8,128)S(1)} %get-tuple-element.39), channel_id=1, source_target_pairs={{0,1},{1,2},{2,3},{3,0},{4,5},{5,6},{6,7},{7,4},{8,9},{9,10},{10,1... | collective-permute-start | bytes 73736 | tf_op jit(solution)/shard_map/ppermute | solution.py:524
  3.0 3.5 %collective-permute-start.1 = (f32[3,16,128]{2,1,0:T(8,128)S(1)}, f32[3,16,128]{2,1,0:T(8,128)S(1)}, u32[]{:S(2)}, u32[]{:S(2)}) collective-permute-start(f32[3,16,128]{2,1,0:T(8,128)S(1)} %get-tuple-element.40), channel_id=1, source_target_pairs={{1,0},{2,1},{3,2},{0,3},{5,4},{6,5},{7,6},{4,7},{9,8},{10,9},{11,1... | collective-permute-start | bytes 73736 | tf_op jit(solution)/shard_map/ppermute | solution.py:524
  6.7 12.4 %collective-permute-start.2 = (f32[3,72,128]{2,1,0:T(8,128)S(1)}, f32[3,72,128]{2,1,0:T(8,128)S(1)}, u32[]{:S(2)}, u32[]{:S(2)}) collective-permute-start(f32[3,72,128]{2,1,0:T(8,128)S(1)} %get-tuple-element.42), channel_id=1, source_target_pairs={{0,4},{4,8},{8,12},{12,16},{16,20},{20,24},{24,28},{28,0},{1,5},{5... | collective-permute-start | bytes 331784 | tf_op jit(solution)/shard_map/ppermute | solution.py:524
  9.0 10.2 %collective-permute-start.3 = (f32[3,72,128]{2,1,0:T(8,128)S(1)}, f32[3,72,128]{2,1,0:T(8,128)S(1)}, u32[]{:S(2)}, u32[]{:S(2)}) collective-permute-start(f32[3,72,128]{2,1,0:T(8,128)S(1)} %get-tuple-element.43), channel_id=1, source_target_pairs={{4,0},{8,4},{12,8},{16,12},{20,16},{24,20},{28,24},{0,28},{5,1},{9... | collective-permute-start | bytes 331784 | tf_op jit(solution)/shard_map/ppermute | solution.py:524
  23.3 10.4 %collective-permute-start.4 = (f32[4,2,6,8,128]{4,3,2,1,0:T(8,128)S(1)}, f32[4,2,6,8,128]{4,3,2,1,0:T(8,128)S(1)}, u32[]{:S(2)}, u32[]{:S(2)}) collective-permute-start(f32[4,2,6,8,128]{4,3,2,1,0:T(8,128)S(1)} %get-tuple-element.53), channel_id=1, source_target_pairs={{0,4},{4,0},{8,12},{12,8},{16,20},{20,16},{24,28},{28,24},{1,5},{5... | collective-permute-start | bytes 589832 | tf_op jit(solution)/shard_map/ppermute | solution.py:528
  26.6 3.1 %collective-permute-start.6 = (f32[2,2,2,16,128]{4,3,2,1,0:T(8,128)S(1)}, f32[2,2,2,16,128]{4,3,2,1,0:T(8,128)S(1)}, u32[]{:S(2)}, u32[]{:S(2)}) collective-permute-start(f32[2,2,2,16,128]{4,3,2,1,0:T(8,128)S(1)} %get-tuple-element.67), channel_id=1, source_target_pairs={{0,1},{1,0},{2,3},{3,2},{4,5},{5,4},{6,7},{7,6},{8,9},{9,8},{10,11... | collective-permute-start | bytes 196616 | tf_op jit(solution)/shard_map/ppermute | solution.py:528
  28.0 4.6 %collective-permute-start.5 = (f32[4,2,2,8,128]{4,3,2,1,0:T(8,128)S(1)}, f32[4,2,2,8,128]{4,3,2,1,0:T(8,128)S(1)}, u32[]{:S(2)}, u32[]{:S(2)}) collective-permute-start(f32[4,2,2,8,128]{4,3,2,1,0:T(8,128)S(1)} %get-tuple-element.65), channel_id=1, source_target_pairs={{0,4},{4,0},{8,12},{12,8},{16,20},{20,16},{24,28},{28,24},{1,5},{5... | collective-permute-start | bytes 196616 | tf_op jit(solution)/shard_map/ppermute | solution.py:528
  29.8 4.0 %collective-permute-start.7 = (f32[1,2,2,16,128]{4,3,2,1,0:T(8,128)S(1)}, f32[1,2,2,16,128]{4,3,2,1,0:T(8,128)S(1)}, u32[]{:S(2)}, u32[]{:S(2)}) collective-permute-start(f32[1,2,2,16,128]{4,3,2,1,0:T(8,128)S(1)} %get-tuple-element.68), channel_id=1, source_target_pairs={{0,2},{1,3},{2,0},{3,1},{4,6},{5,7},{6,4},{7,5},{8,10},{9,11},{10,... | collective-permute-start | bytes 98312 | tf_op jit(solution)/shard_map/ppermute | solution.py:528
  33.8 6.3 %collective-permute-start.8 = (f32[2,8,8,128]{3,2,1,0:T(8,128)S(1)}, f32[2,8,8,128]{3,2,1,0:T(8,128)S(1)}, u32[]{:S(2)}, u32[]{:S(2)}) collective-permute-start(f32[2,8,8,128]{3,2,1,0:T(8,128)S(1)} %get-tuple-element.70), channel_id=1, source_target_pairs={{0,8},{4,12},{8,16},{12,20},{16,24},{20,28},{24,0},{28,4},{1,9},{5... | collective-permute-start | bytes 196616 | tf_op jit(solution)/shard_map/ppermute | solution.py:627
  33.8 7.5 %collective-permute-start.9 = (f32[2,8,8,128]{3,2,1,0:T(8,128)S(1)}, f32[2,8,8,128]{3,2,1,0:T(8,128)S(1)}, u32[]{:S(2)}, u32[]{:S(2)}) collective-permute-start(f32[2,8,8,128]{3,2,1,0:T(8,128)S(1)} %get-tuple-element.71), channel_id=1, source_target_pairs={{0,16},{4,20},{8,24},{12,28},{16,0},{20,4},{24,8},{28,12},{1,17},{... | collective-permute-start | bytes 196616 | tf_op jit(solution)/shard_map/ppermute | solution.py:627
  36.0 5.3 %collective-permute-start.10 = (f32[2,8,8,128]{3,2,1,0:T(8,128)S(1)}, f32[2,8,8,128]{3,2,1,0:T(8,128)S(1)}, u32[]{:S(2)}, u32[]{:S(2)}) collective-permute-start(f32[2,8,8,128]{3,2,1,0:T(8,128)S(1)} %get-tuple-element.72), channel_id=1, source_target_pairs={{0,24},{4,28},{8,0},{12,4},{16,8},{20,12},{24,16},{28,20},{1,25},{... | collective-permute-start | bytes 196616 | tf_op jit(solution)/shard_map/ppermute | solution.py:627

commit v12 on v11

--- a/solution.py
+++ b/solution.py
@@ -449,62 +449,39 @@
     return colour, clear
 
 
-def merge_kernel(level, kept_ref, received_ref, *refs):
-    me = lax.axis_index("by") >> (level - 1)
-    later = (me & 1) == 1
-    kept, received = kept_ref[...], received_ref[...]
+def combine(later, kept, received):
     front = jnp.where(later, received, kept)
     back = jnp.where(later, kept, received)
-    many = kept.shape[0]
     colour = front[:, 0] + front[:, 1] * back[:, 0]
-    clear = front[:, 1] * back[:, 1]
-    if many == 1:
-        refs[0][0] = colour[0]
-        refs[0][1] = clear[0]
+    return colour, front[:, 1] * back[:, 1]
+
+
+def merge_kernel(axis, level, kept_ref, received_ref, *refs):
+    me = lax.axis_index(axis) >> (level - 1)
+    images = combine((me & 1) == 1, kept_ref[...], received_ref[...])
+    if kept_ref.shape[0] == 1:
+        for kind, value in enumerate(images):
+            refs[0][kind] = value[0]
         return
-    out_kept_ref, out_sent_ref = refs
+    out_kept_ref, out_sent_ref = refs[-2:]
     bit = ((me >> 1) & 1) == 1
-    for r in range(many // 2):
-        for kind, value in enumerate((colour, clear)):
+    for r in range(kept_ref.shape[0] // 2):
+        for kind, value in enumerate(images):
             even, odd = value[2 * r], value[2 * r + 1]
             out_kept_ref[r, kind] = jnp.where(bit, odd, even)
             out_sent_ref[r, kind] = jnp.where(bit, even, odd)
 
 
-def merge_x_kernel(*refs):
-    many = refs[0].shape[0]
-    ins, outs = refs[:4], refs[-many:]
-    at = lax.axis_index("bx")
-    later = (at & 1) == 1
-    first = 0
-    for kept_ref, received_ref in (ins[:2], ins[2:]):
-        last = first + kept_ref.shape[2]
-        for t in range(many):
-            r = lax.rem((at >> 1) + t, many)
-            kept, received = kept_ref[r], received_ref[r]
-            front = jnp.where(later, received, kept)
-            back = jnp.where(later, kept, received)
-            outs[t][0, first:last] = front[0] + front[1] * back[0]
-            outs[t][1, first:last] = front[1] * back[1]
-        first = last
-
-
-def fold_x_kernel(*refs):
-    pieces, out_ref = refs[:-1], refs[-1]
-    _, run, share, _ = pieces[0].shape
+def fold_x_kernel(level, *refs):
+    out_ref = refs[-1]
+    later = ((lax.axis_index("bx") >> (level - 1)) & 1) == 1
+    kinds = [[], []]
+    for kept_ref, received_ref in (refs[:2], refs[2:4]):
+        images = combine(later, kept_ref[...], received_ref[...])
+        for values, image in zip(kinds, images):
+            values += [image[0, y] for y in range(image.shape[1])]
+    run, share = len(kinds[0]), kinds[0][0].shape[0]
     lane = iota((share, LANES), 1)
-    me = lax.axis_index("bx") >> 1
-    kinds = [[], []]
-    for y in range(run):
-        behind = colour, clear = jnp.zeros((share, LANES), F32), jnp.ones((share, LANES), F32)
-        for s in reversed(range(len(pieces))):
-            start = me == s
-            behind = jnp.where(start, colour, behind[0]), jnp.where(start, clear, behind[1])
-            colour, clear = jnp.where(start, 0.0, colour), jnp.where(start, 1.0, clear)
-            colour = colour + clear * pieces[s][0, y]
-            clear = clear * pieces[s][1, y]
-        kinds[0].append(colour + clear * behind[0])
-        kinds[1].append(clear * behind[1])
     for kind, values in enumerate(kinds):
         for s in (1, 2, 4):
             for i in range(run):
@@ -608,24 +585,28 @@
     )(win, wout, twice, ridge, slope, *fields, colour_ends, clear_ends, colour_y, clear_y)
     halves += [(kept, swap(sent, "bx", 1))]
 
-    level, many = 1, count_y // 2
-    while many:
-        received = swap(sent_y, "by", level)
-        merge = functools.partial(merge_kernel, level.bit_length())
-        if many > 1:
-            half_parts = sds(many // 2, 2, 2, share_y, LANES)
-            kept_y, sent_y = call(merge, "merge", [half_parts] * 2, 2)(kept_y, received)
-        else:
-            view_y = call(merge, "merge", sds(2, 2, share_y, LANES), 2)(kept_y, received)
-        level, many = 2 * level, many // 2
-    many = count_x // 2
-    piece = sds(2, run, share, LANES)
-    operands = [*halves[0], *halves[1], received]
-    pieces = list(call(merge_x_kernel, "merge_x", [piece] * many, len(operands))(*operands))
-    for t in range(1, many):
-        pairs = [(i, (i + 2 * t) % count_x) for i in range(count_x)]
-        pieces[t] = lax.ppermute(pieces[t], "bx", pairs)
-    view_x = call(fold_x_kernel, "fold_x", sds(2, bands, share, local_y), many)(*pieces)
+    def merge(axis, level, kept, received, *order):
+        kernel = functools.partial(merge_kernel, axis, level)
+        many, *rest = kept.shape
+        outs = [sds(many // 2, *rest)] * 2 if many > 1 else sds(*rest)
+        operands = (kept, received, *order)
+        return call(kernel, "merge", outs, len(operands))(*operands)
+
+    order = (sent_y,)
+    level = 1
+    while kept_y.shape[0] > 1:
+        kept_y, sent_y = merge("by", level, kept_y, swap(sent_y, "by", 1 << (level - 1)))
+        level += 1
+    view_y = merge("by", level, kept_y, swap(sent_y, "by", 1 << (level - 1)))
+    level = 1
+    while halves[0][0].shape[0] > 1:
+        for i, part in enumerate(halves):
+            kept, sent = merge("bx", level, *part, *order)
+            halves[i] = (kept, swap(sent, "bx", 1 << level))
+        level, order = level + 1, ()
+    view_x = call(
+        functools.partial(fold_x_kernel, level), "fold_x", sds(2, bands, share, local_y), 4
+    )(*halves[0], *halves[1])
     view_y = view_y.reshape(2, 2, share_y, half, bands)
     view_y = jnp.transpose(view_y, (0, 4, 2, 1, 3)).reshape(2, bands, share_y, local_x)
     return (view_x, view_y)

time: 42.3 us -> 45.1 us (1.066)
  waiting for transfers between devices: 7.32 us -> 10.6 us
  starting transfers between devices: 15.9 us -> 15.3 us
    ppermute x4 -> x8, waiting for transfers between devices: 3.09 us -> 9.06 us  [swap(): lax.ppermute(value, axis, [(i, i ^ bit) for i in range(lax.axis_size(axis...]
    ppermute x3 -> x0, starting transfers between devices: 3.87 us -> none  [body(): pieces[t] = lax.ppermute(pieces[t], 'bx', pairs)]
    ppermute x4 -> x8, starting transfers between devices: 4.11 us -> 7.41 us  [swap(): lax.ppermute(value, axis, [(i, i ^ bit) for i in range(lax.axis_size(axis...]
    ppermute x3 -> x0, waiting for transfers between devices: 2.7 us -> none  [body(): pieces[t] = lax.ppermute(pieces[t], 'bx', pairs)]
    pallas_call x4 -> x7, Pallas kernels: 0.95 us -> 1 us  [the longest x1 0.88 us: body(): call(functools.partial(fold_x_kernel, level), 'fold_x', sds(2, bands, sha...]
  transfers between devices with their start and end apart: 11 -> 12, of which waited for: 6 -> 6; matrix products, arithmetic and copies ran while one was open for 2% -> 2% of each run, Pallas kernels for 24% -> 23%
where the time goes in v12:
time: 45.1 us; the launch traced here: 45 us
  Pallas kernels  16.1 us (36%)
  starting transfers between devices  15.3 us (34%)
  waiting for transfers between devices  10.6 us (24%)
  local copies, waits for them, and re-layouts  2.23 us (5%)
  between operations  0.73 us (2%)
    ppermute x8, waiting for transfers between devices, swap(): lax.ppermute(value, axis, [(i, i ^ bit) for i in range(lax.axis_size(axis...  9.06 us
    ppermute x4, starting transfers between devices, exchange(): return (lax.ppermute(last, axis, up), lax.ppermute(first, axis, down))  7.89 us
    ppermute x8, starting transfers between devices, swap(): lax.ppermute(value, axis, [(i, i ^ bit) for i in range(lax.axis_size(axis...  7.41 us
    pallas_call x1, Pallas kernels, body(): call(functools.partial(middle_kernel, counts, steps), 'middle', weights +...  6.96 us
    pallas_call x1, Pallas kernels, body(): call(functools.partial(ends_first_kernel, counts, steps), 'ends_first', [...  4.15 us
    pallas_call x1, Pallas kernels, body(): call(functools.partial(last_kernel, counts, steps), 'last', parts(later)...  3.19 us
    unnamed x8, local copies, waits for them, and re-layouts  2.11 us
    ppermute x4, waiting for transfers between devices, exchange(): return (lax.ppermute(last, axis, up), lax.ppermute(first, axis, down))  1.53 us
  transfers between devices with their start and end apart: 12, of which 6 were waited for; matrix products, arithmetic and copies ran while one was open for 2% of the time, Pallas kernels for 23%

profile of v12, /device:TPU:0, one launch (start us, length us, event | category | flops | bytes accessed | tf_op | source)
XLA Modules:
  0.0 45.0 jit_solution(16214093053816265323)
XLA Ops:
  0.6 0.0 copy-start
  0.6 1.2 %copy-done = f32[64,32,128]{2,1,0:T(8,128)S(1)} copy-done((f32[64,32,128]{2,1,0:T(8,128)S(1)}, f32[64,32,128]{2,1,0:T(8,128)}, u32[]{:S(2)}) %copy-start) | copy-done | bytes 1048600
  1.9 0.0 copy-start.2
  1.9 0.0 copy-start.1
  1.9 0.6 %turn.1 = (f32[16,144,128]{2,1,0:T(8,128)S(1)}, f32[3,16,128]{2,1,0:T(8,128)S(1)}, f32[3,16,128]{2,1,0:T(8,128)S(1)}) custom-call(f32[64,32,128]{2,1,0:T(8,128)S(1)} %copy-done), custom_call_target="tpu_custom_call" | custom-call | tf_op jit(solution)/shard_map/turn/pallas_call | solution.py:523
  2.5 0.5 %collective-permute-start = (f32[3,16,128]{2,1,0:T(8,128)S(1)}, f32[3,16,128]{2,1,0:T(8,128)S(1)}, u32[]{:S(2)}, u32[]{:S(2)}) collective-permute-start(f32[3,16,128]{2,1,0:T(8,128)S(1)} %get-tuple-element.43), channel_id=1, source_target_pairs={{0,1},{1,2},{2,3},{3,0},{4,5},{5,6},{6,7},{7,4},{8,9},{9,10},{10,1... | collective-permute-start | bytes 73736 | tf_op jit(solution)/shard_map/ppermute | solution.py:501
  3.0 2.0 %collective-permute-start.1 = (f32[3,16,128]{2,1,0:T(8,128)S(1)}, f32[3,16,128]{2,1,0:T(8,128)S(1)}, u32[]{:S(2)}, u32[]{:S(2)}) collective-permute-start(f32[3,16,128]{2,1,0:T(8,128)S(1)} %get-tuple-element.44), channel_id=1, source_target_pairs={{1,0},{2,1},{3,2},{0,3},{5,4},{6,5},{7,6},{4,7},{9,8},{10,9},{11,1... | collective-permute-start | bytes 73736 | tf_op jit(solution)/shard_map/ppermute | solution.py:501
  5.0 1.4 %collective-permute-done.before_ref = f32[3,16,128]{2,1,0:T(8,128)S(1)} collective-permute-done((f32[3,16,128]{2,1,0:T(8,128)S(1)}, f32[3,16,128]{2,1,0:T(8,128)S(1)}, u32[]{:S(2)}, u32[]{:S(2)}) %collective-permute-start) | collective-permute-done | bytes 24608 | tf_op jit(solution)/shard_map/ppermute | solution.py:501
  6.5 0.1 collective-permute-done.1.after_ref
  6.6 0.2 sides.1
  6.7 2.3 %collective-permute-start.2 = (f32[3,72,128]{2,1,0:T(8,128)S(1)}, f32[3,72,128]{2,1,0:T(8,128)S(1)}, u32[]{:S(2)}, u32[]{:S(2)}) collective-permute-start(f32[3,72,128]{2,1,0:T(8,128)S(1)} %get-tuple-element.46), channel_id=1, source_target_pairs={{0,4},{4,8},{8,12},{12,16},{16,20},{20,24},{24,28},{28,0},{1,5},{5... | collective-permute-start | bytes 331784 | tf_op jit(solution)/shard_map/ppermute | solution.py:501
  9.0 3.1 %collective-permute-start.3 = (f32[3,72,128]{2,1,0:T(8,128)S(1)}, f32[3,72,128]{2,1,0:T(8,128)S(1)}, u32[]{:S(2)}, u32[]{:S(2)}) collective-permute-start(f32[3,72,128]{2,1,0:T(8,128)S(1)} %get-tuple-element.47), channel_id=1, source_target_pairs={{4,0},{8,4},{12,8},{16,12},{20,16},{24,20},{28,24},{0,28},{5,1},{9... | collective-permute-start | bytes 331784 | tf_op jit(solution)/shard_map/ppermute | solution.py:501
  12.1 0.0 copy-done.2
  12.1 0.1 copy.7.in_ref
  12.2 0.0 copy-done.1
  12.2 7.0 %middle.1 = (bf16[128,256]{1,0:T(8,128)(2,1)S(1)}, bf16[256,256]{1,0:T(8,128)(2,1)S(1)}, f32[2,4,12,16,128]{4,3,2,1,0:T(8,128)S(1)}, f32[2,2,10,16,128]{4,3,2,1,...) custom-call(f32[16,144,128]{2,1,0:T(8,128)S(1)} %get-tuple-element.4, ...), custom_call_target="tpu_custom_call" | custom-call | tf_op jit(solution)/shard_map/middle/pallas_call | solution.py:537
  19.1 0.0 collective-permute-done.2.before_ref
  19.1 0.0 collective-permute-done.3.after_ref
  19.2 4.1 %ends_first.1 = (f32[2,5,10,16,128]{4,3,2,1,0:T(8,128)S(1)}, f32[2,5,10,16,128]{4,3,2,1,0:T(8,128)S(1)}, f32[2,5,10,16,128]{4,3,2,1,0:T(8,128)S(1)}, f32[6,128,1...) custom-call(f32[16,144,128]{2,1,0:T(8,128)S(1)} %get-tuple-element.4, ...), custom_call_target="tpu_custom_call" | custom-call | tf_op jit(solution)/shard_map/ends_first/pallas_call | solution.py:560
  23.3 0.1 collective-permute-start.4
  23.4 3.2 %last.1 = (f32[4,2,2,8,128]{4,3,2,1,0:T(8,128)S(1)}, f32[4,2,2,8,128]{4,3,2,1,0:T(8,128)S(1)}, f32[2,2,2,16,128]{4,3,2,1,0:T(8,128)S(1)}, f32[2,2,2,16,128]{4,3,2,1,0:T(8,128)S(1)}) custom-call(bf16[128,256]{1,0:T(8,128)(2,1)S(1)} %get-tuple-element.48.win_ref.refs_0_, bf16[256,256]{1,0:T(8,128)(2,1)S(1)} %get-tuple-element.49.wout_ref.refs_1_, ...), custom_call_target="tpu_custom_call" | custom-call | tf_op jit(solution)/shard_map/last/pallas_call | solution.py:573
  26.6 4.3 %collective-permute-done.4.received_ref = f32[4,2,6,8,128]{4,3,2,1,0:T(8,128)S(1)} collective-permute-done((f32[4,2,6,8,128]{4,3,2,1,0:T(8,128)S(1)}, f32[4,2,6,8,128]{4,3,2,1,0:T(8,128)S(1)}, u32[]{:S(2)}, u32[]{:S(2)}) %collective-permute-start.4) | collective-permute-done | bytes 196640 | tf_op jit(solution)/shard_map/ppermute | solution.py:505
  30.9 0.2 collective-permute-start.5
  31.1 0.6 %collective-permute-start.7 = (f32[4,2,2,8,128]{4,3,2,1,0:T(8,128)S(1)}, f32[4,2,2,8,128]{4,3,2,1,0:T(8,128)S(1)}, u32[]{:S(2)}, u32[]{:S(2)}) collective-permute-start(f32[4,2,2,8,128]{4,3,2,1,0:T(8,128)S(1)} %get-tuple-element.74), channel_id=1, source_target_pairs={{0,4},{4,0},{8,12},{12,8},{16,20},{20,16},{24,28},{28,24},{1,5},{5... | collective-permute-start | bytes 196616 | tf_op jit(solution)/shard_map/ppermute | solution.py:505
  31.7 0.0 collective-permute-start.10
  31.7 3.7 %collective-permute-done.7.received_ref = f32[4,2,2,8,128]{4,3,2,1,0:T(8,128)S(1)} collective-permute-done((f32[4,2,2,8,128]{4,3,2,1,0:T(8,128)S(1)}, f32[4,2,2,8,128]{4,3,2,1,0:T(8,128)S(1)}, u32[]{:S(2)}, u32[]{:S(2)}) %collective-permute-start.7) | collective-permute-done | bytes 65568 | tf_op jit(solution)/shard_map/ppermute | solution.py:505
  35.4 2.0 %collective-permute-start.8 = (f32[2,2,2,8,128]{4,3,2,1,0:T(8,128)S(1)}, f32[2,2,2,8,128]{4,3,2,1,0:T(8,128)S(1)}, u32[]{:S(2)}, u32[]{:S(2)}) collective-permute-start(f32[2,2,2,8,128]{4,3,2,1,0:T(8,128)S(1)} %get-tuple-element.76), channel_id=1, source_target_pairs={{0,8},{4,12},{8,0},{12,4},{16,24},{20,28},{24,16},{28,20},{1,9},{5... | collective-permute-start | bytes 98312 | tf_op jit(solution)/shard_map/ppermute | solution.py:505
  37.3 0.0 collective-permute-done.5.received_ref
  37.4 1.2 %collective-permute-start.6 = (f32[1,2,6,8,128]{4,3,2,1,0:T(8,128)S(1)}, f32[1,2,6,8,128]{4,3,2,1,0:T(8,128)S(1)}, u32[]{:S(2)}, u32[]{:S(2)}) collective-permute-start(f32[1,2,6,8,128]{4,3,2,1,0:T(8,128)S(1)} %get-tuple-element.72), channel_id=1, source_target_pairs={{0,16},{4,20},{8,24},{12,28},{16,0},{20,4},{24,8},{28,12},{1,17},{... | collective-permute-start | bytes 147464 | tf_op jit(solution)/shard_map/ppermute | solution.py:505
  38.6 0.0 collective-permute-done.10.received_ref
  38.6 0.7 %collective-permute-start.11 = (f32[1,2,2,16,128]{4,3,2,1,0:T(8,128)S(1)}, f32[1,2,2,16,128]{4,3,2,1,0:T(8,128)S(1)}, u32[]{:S(2)}, u32[]{:S(2)}) collective-permute-start(f32[1,2,2,16,128]{4,3,2,1,0:T(8,128)S(1)} %get-tuple-element.81), channel_id=1, source_target_pairs={{0,2},{1,3},{2,0},{3,1},{4,6},{5,7},{6,4},{7,5},{8,10},{9,11},{10,... | collective-permute-start | bytes 98312 | tf_op jit(solution)/shard_map/ppermute | solution.py:505
  39.3 0.0 collective-permute-done.8.received_ref
  39.4 2.7 %collective-permute-start.9 = (f32[1,2,2,8,128]{4,3,2,1,0:T(8,128)S(1)}, f32[1,2,2,8,128]{4,3,2,1,0:T(8,128)S(1)}, u32[]{:S(2)}, u32[]{:S(2)}) collective-permute-start(f32[1,2,2,8,128]{4,3,2,1,0:T(8,128)S(1)} %get-tuple-element.78), channel_id=1, source_target_pairs={{0,16},{4,20},{8,24},{12,28},{16,0},{20,4},{24,8},{28,12},{1,17},{... | collective-permute-start | bytes 49160 | tf_op jit(solution)/shard_map/ppermute | solution.py:505
  42.0 0.6 %collective-permute-done.11.received_ref = f32[1,2,2,16,128]{4,3,2,1,0:T(8,128)S(1)} collective-permute-done((f32[1,2,2,16,128]{4,3,2,1,0:T(8,128)S(1)}, f32[1,2,2,16,128]{4,3,2,1,0:T(8,128)S(1)}, u32[]{:S(2)}, u32[]{:S(2)}) %collective-permute-start.11) | collective-permute-done | bytes 32800 | tf_op jit(solution)/shard_map/ppermute | solution.py:505
  42.6 0.1 copy.8
  42.7 0.8 %copy.9 = f32[2,8,16,32]{3,2,1,0:T(8,128)} copy(f32[2,8,16,32]{2,1,3,0:T(8,128)S(1)} %bitcast.5) | data formatting | bytes 65536
  43.5 0.5 %collective-permute-done.9.refs_3_ = f32[1,2,2,8,128]{4,3,2,1,0:T(8,128)S(1)} collective-permute-done((f32[1,2,2,8,128]{4,3,2,1,0:T(8,128)S(1)}, f32[1,2,2,8,128]{4,3,2,1,0:T(8,128)S(1)}, u32[]{:S(2)}, u32[]{:S(2)}) %collective-permute-start.9) | collective-permute-done | bytes 16416 | tf_op jit(solution)/shard_map/ppermute | solution.py:505
  44.1 0.0 collective-permute-done.6.refs_1_
  44.1 0.9 %fold_x.1 = f32[2,8,8,128]{3,2,1,0:T(8,128)} custom-call(f32[1,2,6,8,128]{4,3,2,1,0:T(8,128)S(1)} %get-tuple-element.71.refs_0_, f32[1,2,6,8,128]{4,3,2,1,0:T(8,128)S(1)} %collective-permute-done.6.refs_1_, f32[1,2,2,8,128]{4,3,2,1,0:T(8,128)S(1)} %get-tuple-element.77.refs_2_, f32[1,2,2,8,128]{4,3,2,1,0:T(8,128)S(1)} %collective-permute-done.9.refs_3_), custom_call_target="tpu_custom_call" | custom-call | tf_op jit(solution)/shard_map/fold_x/pallas_call | solution.py:607
  (6 shorter events, 0.1 us)
Async XLA Ops:
  0.6 1.2 %copy-start = (f32[64,32,128]{2,1,0:T(8,128)S(1)}, f32[64,32,128]{2,1,0:T(8,128)}, u32[]{:S(2)}) copy-start(f32[64,32,128]{2,1,0:T(8,128)} %field_ref.1) | copy-start | bytes 3145732
  1.9 10.2 %copy-start.2 = (bf16[16,8]{0,1:T(8,128)(2,1)S(1)}, bf16[16,8]{0,1:T(8,128)(2,1)}, u32[]{:S(2)}) copy-start(bf16[16,8]{0,1:T(8,128)(2,1)} %param.4) | copy-start | bytes 772
  1.9 10.3 %copy-start.1 = (bf16[16,16]{1,0:T(8,128)(2,1)S(1)}, bf16[16,16]{1,0:T(8,128)(2,1)}, u32[]{:S(2)}) copy-start(bf16[16,16]{1,0:T(8,128)(2,1)} %out_ref.1) | copy-start | bytes 1540
  2.5 4.0 %collective-permute-start = (f32[3,16,128]{2,1,0:T(8,128)S(1)}, f32[3,16,128]{2,1,0:T(8,128)S(1)}, u32[]{:S(2)}, u32[]{:S(2)}) collective-permute-start(f32[3,16,128]{2,1,0:T(8,128)S(1)} %get-tuple-element.43), channel_id=1, source_target_pairs={{0,1},{1,2},{2,3},{3,0},{4,5},{5,6},{6,7},{7,4},{8,9},{9,10},{10,1... | collective-permute-start | bytes 73736 | tf_op jit(solution)/shard_map/ppermute | solution.py:501
  3.0 3.5 %collective-permute-start.1 = (f32[3,16,128]{2,1,0:T(8,128)S(1)}, f32[3,16,128]{2,1,0:T(8,128)S(1)}, u32[]{:S(2)}, u32[]{:S(2)}) collective-permute-start(f32[3,16,128]{2,1,0:T(8,128)S(1)} %get-tuple-element.44), channel_id=1, source_target_pairs={{1,0},{2,1},{3,2},{0,3},{5,4},{6,5},{7,6},{4,7},{9,8},{10,9},{11,1... | collective-permute-start | bytes 73736 | tf_op jit(solution)/shard_map/ppermute | solution.py:501
  6.7 12.4 %collective-permute-start.2 = (f32[3,72,128]{2,1,0:T(8,128)S(1)}, f32[3,72,128]{2,1,0:T(8,128)S(1)}, u32[]{:S(2)}, u32[]{:S(2)}) collective-permute-start(f32[3,72,128]{2,1,0:T(8,128)S(1)} %get-tuple-element.46), channel_id=1, source_target_pairs={{0,4},{4,8},{8,12},{12,16},{16,20},{20,24},{24,28},{28,0},{1,5},{5... | collective-permute-start | bytes 331784 | tf_op jit(solution)/shard_map/ppermute | solution.py:501
  9.0 10.2 %collective-permute-start.3 = (f32[3,72,128]{2,1,0:T(8,128)S(1)}, f32[3,72,128]{2,1,0:T(8,128)S(1)}, u32[]{:S(2)}, u32[]{:S(2)}) collective-permute-start(f32[3,72,128]{2,1,0:T(8,128)S(1)} %get-tuple-element.47), channel_id=1, source_target_pairs={{4,0},{8,4},{12,8},{16,12},{20,16},{24,20},{28,24},{0,28},{5,1},{9... | collective-permute-start | bytes 331784 | tf_op jit(solution)/shard_map/ppermute | solution.py:501
  23.3 7.5 %collective-permute-start.4 = (f32[4,2,6,8,128]{4,3,2,1,0:T(8,128)S(1)}, f32[4,2,6,8,128]{4,3,2,1,0:T(8,128)S(1)}, u32[]{:S(2)}, u32[]{:S(2)}) collective-permute-start(f32[4,2,6,8,128]{4,3,2,1,0:T(8,128)S(1)} %get-tuple-element.57), channel_id=1, source_target_pairs={{0,4},{4,0},{8,12},{12,8},{16,20},{20,16},{24,28},{28,24},{1,5},{5... | collective-permute-start | bytes 589832 | tf_op jit(solution)/shard_map/ppermute | solution.py:505
  30.9 6.4 %collective-permute-start.5 = (f32[2,2,6,8,128]{4,3,2,1,0:T(8,128)S(1)}, f32[2,2,6,8,128]{4,3,2,1,0:T(8,128)S(1)}, u32[]{:S(2)}, u32[]{:S(2)}) collective-permute-start(f32[2,2,6,8,128]{4,3,2,1,0:T(8,128)S(1)} %get-tuple-element.70), channel_id=1, source_target_pairs={{0,8},{4,12},{8,0},{12,4},{16,24},{20,28},{24,16},{28,20},{1,9},{5... | collective-permute-start | bytes 294920 | tf_op jit(solution)/shard_map/ppermute | solution.py:505
  31.1 4.3 %collective-permute-start.7 = (f32[4,2,2,8,128]{4,3,2,1,0:T(8,128)S(1)}, f32[4,2,2,8,128]{4,3,2,1,0:T(8,128)S(1)}, u32[]{:S(2)}, u32[]{:S(2)}) collective-permute-start(f32[4,2,2,8,128]{4,3,2,1,0:T(8,128)S(1)} %get-tuple-element.74), channel_id=1, source_target_pairs={{0,4},{4,0},{8,12},{12,8},{16,20},{20,16},{24,28},{28,24},{1,5},{5... | collective-permute-start | bytes 196616 | tf_op jit(solution)/shard_map/ppermute | solution.py:505
  31.7 6.9 %collective-permute-start.10 = (f32[2,2,2,16,128]{4,3,2,1,0:T(8,128)S(1)}, f32[2,2,2,16,128]{4,3,2,1,0:T(8,128)S(1)}, u32[]{:S(2)}, u32[]{:S(2)}) collective-permute-start(f32[2,2,2,16,128]{4,3,2,1,0:T(8,128)S(1)} %get-tuple-element.68.refs_0_), channel_id=1, source_target_pairs={{0,1},{1,0},{2,3},{3,2},{4,5},{5,4},{6,7},{7,6},{8,9},{9,8},{10,11... | collective-permute-start | bytes 196616 | tf_op jit(solution)/shard_map/ppermute | solution.py:505
  35.4 4.0 %collective-permute-start.8 = (f32[2,2,2,8,128]{4,3,2,1,0:T(8,128)S(1)}, f32[2,2,2,8,128]{4,3,2,1,0:T(8,128)S(1)}, u32[]{:S(2)}, u32[]{:S(2)}) collective-permute-start(f32[2,2,2,8,128]{4,3,2,1,0:T(8,128)S(1)} %get-tuple-element.76), channel_id=1, source_target_pairs={{0,8},{4,12},{8,0},{12,4},{16,24},{20,28},{24,16},{28,20},{1,9},{5... | collective-permute-start | bytes 98312 | tf_op jit(solution)/shard_map/ppermute | solution.py:505
  37.4 6.7 %collective-permute-start.6 = (f32[1,2,6,8,128]{4,3,2,1,0:T(8,128)S(1)}, f32[1,2,6,8,128]{4,3,2,1,0:T(8,128)S(1)}, u32[]{:S(2)}, u32[]{:S(2)}) collective-permute-start(f32[1,2,6,8,128]{4,3,2,1,0:T(8,128)S(1)} %get-tuple-element.72), channel_id=1, source_target_pairs={{0,16},{4,20},{8,24},{12,28},{16,0},{20,4},{24,8},{28,12},{1,17},{... | collective-permute-start | bytes 147464 | tf_op jit(solution)/shard_map/ppermute | solution.py:505
  38.6 4.0 %collective-permute-start.11 = (f32[1,2,2,16,128]{4,3,2,1,0:T(8,128)S(1)}, f32[1,2,2,16,128]{4,3,2,1,0:T(8,128)S(1)}, u32[]{:S(2)}, u32[]{:S(2)}) collective-permute-start(f32[1,2,2,16,128]{4,3,2,1,0:T(8,128)S(1)} %get-tuple-element.81), channel_id=1, source_target_pairs={{0,2},{1,3},{2,0},{3,1},{4,6},{5,7},{6,4},{7,5},{8,10},{9,11},{10,... | collective-permute-start | bytes 98312 | tf_op jit(solution)/shard_map/ppermute | solution.py:505
  39.4 4.7 %collective-permute-start.9 = (f32[1,2,2,8,128]{4,3,2,1,0:T(8,128)S(1)}, f32[1,2,2,8,128]{4,3,2,1,0:T(8,128)S(1)}, u32[]{:S(2)}, u32[]{:S(2)}) collective-permute-start(f32[1,2,2,8,128]{4,3,2,1,0:T(8,128)S(1)} %get-tuple-element.78), channel_id=1, source_target_pairs={{0,16},{4,20},{8,24},{12,28},{16,0},{20,4},{24,8},{28,12},{1,17},{... | collective-permute-start | bytes 49160 | tf_op jit(solution)/shard_map/ppermute | solution.py:505

commit v13 on v11

--- a/solution.py
+++ b/solution.py
@@ -83,8 +83,9 @@
 
 
 def sides_kernel(
-    width, count_y, turned_ref, before_ref, after_ref, wide_ref, first_ref, last_ref
+    width, count_y, turned_ref, before_ref, after_ref, early_ref, wide_ref, first_ref, last_ref
 ):
+    del early_ref
     half, rows, _ = turned_ref.shape
     layers = LANES // 2
     part = rows // 2
@@ -142,17 +143,21 @@
     def raw(self, ref, k, y):
         return ref[k, pl.ds(y + REACH, CHUNKS, stride=self.run), :]
 
-    def once(self, raw, k, out, at, edge=None):
-        column = [self.raw(raw, k, y) for y in range(-3, self.run + 3)]
-        for i in range(1, len(column) - 1):
-            y = i - 3
+    def once(self, raw, k, out, at, edge=None, offsets=None):
+        offsets = range(-2, self.run + 2) if offsets is None else offsets
+        held = {y + d: None for y in offsets for d in (-1, 0, 1)}
+        held = {y: self.raw(raw, k, y) for y in held}
+        for y in offsets:
+            i = y + 3
             sides = [self.raw(raw, k - 1, y), self.raw(raw, k + 1, y)]
-            value = self.smooth(column[i], [column[i - 1], column[i + 1]] + sides)
+            value = self.smooth(held[y], [held[y - 1], held[y + 1]] + sides)
             out[at, i - 1] = self.inside(value, y, edge)
 
-    def twice(self, once, k, out, ridge, slope, at, edge=None):
-        column = [once[k, i] for i in range(self.run + 4)]
-        for i in range(1, len(column) - 1):
+    def twice(self, once, k, out, ridge, slope, at, edge=None, offsets=None):
+        offsets = range(-1, self.run + 1) if offsets is None else offsets
+        held = {y + 2 + d: None for y in offsets for d in (-1, 0, 1)}
+        column = {i: once[k, i] for i in held}
+        for i in (y + 2 for y in offsets):
             sides = [once[k - 1, i], once[k + 1, i]]
             value = self.smooth(column[i], [column[i - 1], column[i + 1]] + sides)
             value = self.inside(value, i - 2, edge)
@@ -205,12 +210,29 @@
     return colour + (light - later) * emission, later
 
 
+def early_kernel(
+    counts, turned_ref, order_ref, once_ref, twice_ref, ridge_ref, slope_ref
+):
+    order_ref[...] = jnp.zeros_like(order_ref)
+    run = once_ref.shape[1] - 4
+    stencil = Stencil(run, counts)
+    for k in range(once_ref.shape[0]):
+        stencil.once(turned_ref, k + 1, once_ref, k, offsets=range(1, run - 1))
+    for k in range(twice_ref.shape[0]):
+        outs = (twice_ref, ridge_ref, slope_ref)
+        stencil.twice(once_ref, k + 1, *outs, k, offsets=range(2, run - 2))
+
+
 def middle_kernel(
     counts,
     steps,
     wide_ref,
     in_ref,
     out_ref,
+    once_in_ref,
+    twice_in_ref,
+    ridge_in_ref,
+    slope_in_ref,
     win_ref,
     wout_ref,
     once_out_ref,
@@ -259,16 +281,21 @@
                 cy_ref[x0 + i, at], ty_ref[x0 + i, at] = rays_y[i]
 
     many_y = 2 if ahead % 2 == 0 else 1
+    once_ref[:, 3 : run + 1] = once_in_ref[:, 3 : run + 1]
+    fields = (twice_ref, ridge_ref, slope_ref)
+    for ref, in_ref in zip(fields, (twice_in_ref, ridge_in_ref, slope_in_ref)):
+        ref[:, 3 : run - 1] = in_ref[:, 3 : run - 1]
+    ends = [-2, -1, 0, run - 1, run, run + 1]
     for k in range(inner + 4):
-        stencil.once(wide_ref, k + 1, once_ref, k)
+        stencil.once(wide_ref, k + 1, once_ref, k, offsets=ends)
+    ends = [-1, 0, 1, run - 2, run - 1, run]
     for k in range(inner + 2):
-        stencil.twice(once_ref, k + 1, twice_ref, ridge_ref, slope_ref, k)
+        stencil.twice(once_ref, k + 1, *fields, k, offsets=ends)
     for y0 in range(0, ahead, many_y):
         block(0, y0, inner, many_y)
     for k in range(4):
         once_out_ref[0, k] = once_ref[k]
         once_out_ref[1, k] = once_ref[inner + k]
-    fields = (twice_ref, ridge_ref, slope_ref)
     outs = (twice_out_ref, ridge_out_ref, slope_out_ref)
     for out_ref, later_ref, ref in zip(outs, later_refs, fields):
         for k in range(2):
@@ -547,10 +574,19 @@
         scalar_field
     )
     before, after = exchange(last, first, "by")
+    inner = half - 2 * REACH
+    counts = (count_x, count_y)
+    plane = lambda *lead: sds(*lead, CHUNKS, LANES)
+    order, *early = call(
+        functools.partial(early_kernel, counts),
+        "early",
+        [sds(SUB, LANES), plane(inner + 4, run + 4)] + [plane(inner + 2, run + 2)] * 3,
+        1,
+    )(turned)
     edge = sds(REACH, rows // 2, LANES)
     wide, first, last = call(
-        functools.partial(sides_kernel, local_y, count_y), "sides", [sds(half, rows, LANES), edge, edge], 3
-    )(turned, before, after)
+        functools.partial(sides_kernel, local_y, count_y), "sides", [sds(half, rows, LANES), edge, edge], 4
+    )(turned, before, after, order)
     before, after = exchange(last, first, "bx")
     inner = half - 2 * REACH
     counts = (count_x, count_y)
@@ -566,14 +602,14 @@
         + [sds(ahead, LANES, LANES)] * 2
         + [sds(inner, LANES, LANES)] * 2
         + [plane(inner + 2, later + 2)] * 3,
-        3,
+        7,
         [
             pltpu.VMEM((inner + 4, run + 4, CHUNKS, LANES), F32),
             pltpu.VMEM((inner + 2, run + 2, CHUNKS, LANES), F32),
             pltpu.VMEM((inner + 2, run + 2, CHUNKS, LANES), F32),
             pltpu.VMEM((inner + 2, run + 2, CHUNKS, LANES), F32),
         ],
-    )(wide, transfer_in, transfer_out)
+    )(wide, transfer_in, transfer_out, *early)
     share = layers // count_x
     share_y = layers // count_y
     parts = lambda many: [sds(count_x // 2, 2, many, share, LANES)] * 2

time: 42.3 us -> 47.6 us (1.13)
  Pallas kernels: 16.1 us -> 20.3 us
  local copies, waits for them, and re-layouts: 2.23 us -> 5.64 us
  waiting for transfers between devices: 7.32 us -> 4.92 us
    pallas_call x0 -> x1, Pallas kernels: none -> 3.69 us  [body(): call(functools.partial(early_kernel, counts), 'early', [sds(SUB, LANES),...]
    unnamed x8 -> x16, local copies, waits for them, and re-layouts: 2.11 us -> 5.51 us
    ppermute x4, waiting for transfers between devices: 1.53 us -> 0.01 us  [exchange(): return (lax.ppermute(last, axis, up), lax.ppermute(first, axis, down))]
    pallas_call x1, Pallas kernels: 6.96 us -> 5.85 us  [body(): call(functools.partial(middle_kernel, counts, steps), 'middle', weights +...]
    pallas_call x1, Pallas kernels: 4.15 us -> 5.1 us  [body(): call(functools.partial(ends_first_kernel, counts, steps), 'ends_first', [...]
    pallas_call x1, Pallas kernels: 0.16 us -> 1.04 us  [body(): call(functools.partial(sides_kernel, local_y, count_y), 'sides', [sds(hal...]
    ppermute x4, waiting for transfers between devices: 3.09 us -> 2.21 us  [swap(): lax.ppermute(value, axis, [(i, i ^ bit) for i in range(lax.axis_size(axis...]
  transfers between devices with their start and end apart: 11 -> 11, of which waited for: 6 -> 4; matrix products, arithmetic and copies ran while one was open for 2% -> 2% of each run, Pallas kernels for 24% -> 27%
where the time goes in v13:
time: 47.6 us; the launch traced here: 47.3 us
  Pallas kernels  20.3 us (43%)
  starting transfers between devices  15.7 us (33%)
  local copies, waits for them, and re-layouts  5.64 us (12%)
  waiting for transfers between devices  4.92 us (10%)
  between operations  0.74 us (2%)
    ppermute x4, starting transfers between devices, exchange(): return (lax.ppermute(last, axis, up), lax.ppermute(first, axis, down))  7.78 us
    pallas_call x1, Pallas kernels, body(): call(functools.partial(middle_kernel, counts, steps), 'middle', weights +...  5.85 us
    unnamed x16, local copies, waits for them, and re-layouts  5.51 us
    pallas_call x1, Pallas kernels, body(): call(functools.partial(ends_first_kernel, counts, steps), 'ends_first', [...  5.1 us
    ppermute x4, starting transfers between devices, swap(): lax.ppermute(value, axis, [(i, i ^ bit) for i in range(lax.axis_size(axis...  3.99 us
    ppermute x3, starting transfers between devices, body(): pieces[t] = lax.ppermute(pieces[t], 'bx', pairs)  3.95 us
    pallas_call x1, Pallas kernels, body(): call(functools.partial(early_kernel, counts), 'early', [sds(SUB, LANES),...  3.69 us
    pallas_call x1, Pallas kernels, body(): call(functools.partial(last_kernel, counts, steps), 'last', parts(later)...  3.03 us
  transfers between devices with their start and end apart: 11, of which 4 were waited for; matrix products, arithmetic and copies ran while one was open for 2% of the time, Pallas kernels for 27%

profile of v13, /device:TPU:0, one launch (start us, length us, event | category | flops | bytes accessed | tf_op | source)
XLA Modules:
  0.0 47.3 jit_solution(15680410277118033222)
XLA Ops:
  0.6 0.0 copy-start
  0.6 1.2 %copy-done = f32[64,32,128]{2,1,0:T(8,128)S(1)} copy-done((f32[64,32,128]{2,1,0:T(8,128)S(1)}, f32[64,32,128]{2,1,0:T(8,128)}, u32[]{:S(2)}) %copy-start) | copy-done | bytes 1048600
  1.9 0.6 %turn.1 = (f32[16,144,128]{2,1,0:T(8,128)S(1)}, f32[3,16,128]{2,1,0:T(8,128)S(1)}, f32[3,16,128]{2,1,0:T(8,128)S(1)}) custom-call(f32[64,32,128]{2,1,0:T(8,128)S(1)} %copy-done), custom_call_target="tpu_custom_call" | custom-call | tf_op jit(solution)/shard_map/turn/pallas_call | solution.py:573
  2.5 0.5 %collective-permute-start = (f32[3,16,128]{2,1,0:T(8,128)S(1)}, f32[3,16,128]{2,1,0:T(8,128)S(1)}, u32[]{:S(2)}, u32[]{:S(2)}) collective-permute-start(f32[3,16,128]{2,1,0:T(8,128)S(1)} %get-tuple-element.44), channel_id=1, source_target_pairs={{0,1},{1,2},{2,3},{3,0},{4,5},{5,6},{6,7},{7,4},{8,9},{9,10},{10,1... | collective-permute-start | bytes 73736 | tf_op jit(solution)/shard_map/ppermute | solution.py:551
  3.0 2.0 %collective-permute-start.1 = (f32[3,16,128]{2,1,0:T(8,128)S(1)}, f32[3,16,128]{2,1,0:T(8,128)S(1)}, u32[]{:S(2)}, u32[]{:S(2)}) collective-permute-start(f32[3,16,128]{2,1,0:T(8,128)S(1)} %get-tuple-element.45), channel_id=1, source_target_pairs={{1,0},{2,1},{3,2},{0,3},{5,4},{6,5},{7,6},{4,7},{9,8},{10,9},{11,1... | collective-permute-start | bytes 73736 | tf_op jit(solution)/shard_map/ppermute | solution.py:551
  5.0 0.0 copy-start.6
  5.0 0.0 copy-start.5
  5.0 3.7 %early.1 = (f32[8,128]{1,0:T(8,128)S(1)}, f32[14,12,16,128]{3,2,1,0:T(8,128)S(1)}, f32[12,10,16,128]{3,2,1,0:T(8,128)S(1)}, f32[12,10,16,128]{3,2,1,0:T(8,128)S(1)}, f32[12,10,16,128]{3,2,1,0:T(8,128)S(1)}) custom-call(f32[16,144,128]{2,1,0:T(8,128)S(1)} %get-tuple-element.43.turned_ref), custom_call_target="tpu_custom_call" | custom-call | tf_op jit(solution)/shard_map/early/pallas_call | solution.py:580
  8.7 0.0 copy-start.3
  8.7 1.0 %copy-done.3 = f32[12,10,16,128]{3,2,1,0:T(8,128)} copy-done((f32[12,10,16,128]{3,2,1,0:T(8,128)}, f32[12,10,16,128]{3,2,1,0:T(8,128)S(1)}, u32[]{:S(2)}) %copy-start.3) | copy-done | bytes 983064
  9.7 0.0 copy-start.1
  9.7 0.0 collective-permute-done.before_ref
  9.7 0.0 collective-permute-done.1.after_ref
  9.7 1.0 %sides.1 = (f32[16,144,128]{2,1,0:T(8,128)S(1)}, f32[3,72,128]{2,1,0:T(8,128)}, f32[3,72,128]{2,1,0:T(8,128)}) custom-call(f32[16,144,128]{2,1,0:T(8,128)S(1)} %get-tuple-element.43.turned_ref, f32[3,16,128]{2,1,0:T(8,128)S(1)} %collective-permute-done.before_ref, f32[3,16,128]{2,1,0:T(8,128)S(1)} %collective-permute-done.1.after_ref, ...), custom_call_target="tpu_custom_call" | custom-call | tf_op jit(solution)/shard_map/sides/pallas_call | solution.py:587
  10.7 0.0 copy-done.1
  10.8 2.2 %collective-permute-start.2 = (f32[3,72,128]{2,1,0:T(8,128)}, f32[3,72,128]{2,1,0:T(8,128)}, u32[]{:S(2)}, u32[]{:S(2)}) collective-permute-start(f32[3,72,128]{2,1,0:T(8,128)} %get-tuple-element.48), channel_id=1, source_target_pairs={{0,4},{4,8},{8,12},{12,16},{16,20},{20,24},{24,28},{28,0},{1,5},{5... | collective-permute-start | bytes 331784 | tf_op jit(solution)/shard_map/ppermute | solution.py:551
  13.0 3.0 %collective-permute-start.3 = (f32[3,72,128]{2,1,0:T(8,128)}, f32[3,72,128]{2,1,0:T(8,128)}, u32[]{:S(2)}, u32[]{:S(2)}) collective-permute-start(f32[3,72,128]{2,1,0:T(8,128)} %get-tuple-element.49), channel_id=1, source_target_pairs={{4,0},{8,4},{12,8},{16,12},{20,16},{24,20},{28,24},{0,28},{5,1},{9... | collective-permute-start | bytes 331784 | tf_op jit(solution)/shard_map/ppermute | solution.py:551
  16.0 0.0 copy-done.6
  16.0 0.1 copy.7.in_ref
  16.1 0.0 copy-done.5
  16.1 0.0 copy-start.2
  16.1 1.2 %copy-done.2 = f32[12,10,16,128]{3,2,1,0:T(8,128)S(1)} copy-done((f32[12,10,16,128]{3,2,1,0:T(8,128)S(1)}, f32[12,10,16,128]{3,2,1,0:T(8,128)}, u32[]{:S(2)}) %copy-start.2) | copy-done | bytes 983064
  17.3 0.0 copy-start.4
  17.3 1.2 %copy-done.4 = f32[12,10,16,128]{3,2,1,0:T(8,128)S(1)} copy-done((f32[12,10,16,128]{3,2,1,0:T(8,128)S(1)}, f32[12,10,16,128]{3,2,1,0:T(8,128)}, u32[]{:S(2)}) %copy-start.4) | copy-done | bytes 983064
  18.5 5.9 %middle.1 = (bf16[128,256]{1,0:T(8,128)(2,1)S(1)}, bf16[256,256]{1,0:T(8,128)(2,1)S(1)}, f32[2,4,12,16,128]{4,3,2,1,0:T(8,128)S(1)}, f32[2,2,10,16,128]{4,3,2,1,...) custom-call(f32[16,144,128]{2,1,0:T(8,128)S(1)} %get-tuple-element.4, ...), custom_call_target="tpu_custom_call" | custom-call | tf_op jit(solution)/shard_map/middle/pallas_call | solution.py:596
  24.4 0.0 collective-permute-done.2.before_ref
  24.4 0.0 collective-permute-done.3.after_ref
  24.4 5.1 %ends_first.1 = (f32[2,5,10,16,128]{4,3,2,1,0:T(8,128)S(1)}, f32[2,5,10,16,128]{4,3,2,1,0:T(8,128)S(1)}, f32[2,5,10,16,128]{4,3,2,1,0:T(8,128)S(1)}, f32[6,128,1...) custom-call(f32[16,144,128]{2,1,0:T(8,128)S(1)} %get-tuple-element.4, ...), custom_call_target="tpu_custom_call" | custom-call | tf_op jit(solution)/shard_map/ends_first/pallas_call | solution.py:619
  29.5 0.1 collective-permute-start.4
  29.6 3.0 %last.1 = (f32[4,2,2,8,128]{4,3,2,1,0:T(8,128)S(1)}, f32[4,2,2,8,128]{4,3,2,1,0:T(8,128)S(1)}, f32[2,2,2,16,128]{4,3,2,1,0:T(8,128)S(1)}, f32[2,2,2,16,128]{4,3,2,1,0:T(8,128)S(1)}) custom-call(bf16[128,256]{1,0:T(8,128)(2,1)S(1)} %get-tuple-element.54.win_ref.refs_0_, bf16[256,256]{1,0:T(8,128)(2,1)S(1)} %get-tuple-element.55.wout_ref.refs_1_, ...), custom_call_target="tpu_custom_call" | custom-call | tf_op jit(solution)/shard_map/last/pallas_call | solution.py:632
  32.6 0.1 collective-permute-start.6
  32.7 2.1 %collective-permute-start.5 = (f32[4,2,2,8,128]{4,3,2,1,0:T(8,128)S(1)}, f32[4,2,2,8,128]{4,3,2,1,0:T(8,128)S(1)}, u32[]{:S(2)}, u32[]{:S(2)}) collective-permute-start(f32[4,2,2,8,128]{4,3,2,1,0:T(8,128)S(1)} %get-tuple-element.75), channel_id=1, source_target_pairs={{0,4},{4,0},{8,12},{12,8},{16,20},{20,16},{24,28},{28,24},{1,5},{5... | collective-permute-start | bytes 196616 | tf_op jit(solution)/shard_map/ppermute | solution.py:555
  34.8 0.0 collective-permute-done.6.received_ref
  34.8 1.8 %collective-permute-start.7 = (f32[1,2,2,16,128]{4,3,2,1,0:T(8,128)S(1)}, f32[1,2,2,16,128]{4,3,2,1,0:T(8,128)S(1)}, u32[]{:S(2)}, u32[]{:S(2)}) collective-permute-start(f32[1,2,2,16,128]{4,3,2,1,0:T(8,128)S(1)} %get-tuple-element.78), channel_id=1, source_target_pairs={{0,2},{1,3},{2,0},{3,1},{4,6},{5,7},{6,4},{7,5},{8,10},{9,11},{10,... | collective-permute-start | bytes 98312 | tf_op jit(solution)/shard_map/ppermute | solution.py:555
  36.6 0.9 %collective-permute-done.5.refs_3_ = f32[4,2,2,8,128]{4,3,2,1,0:T(8,128)S(1)} collective-permute-done((f32[4,2,2,8,128]{4,3,2,1,0:T(8,128)S(1)}, f32[4,2,2,8,128]{4,3,2,1,0:T(8,128)S(1)}, u32[]{:S(2)}, u32[]{:S(2)}) %collective-permute-start.5) | collective-permute-done | bytes 65568 | tf_op jit(solution)/shard_map/ppermute | solution.py:555
  37.5 1.3 %collective-permute-done.7.refs_4_.received_ref = f32[1,2,2,16,128]{4,3,2,1,0:T(8,128)S(1)} collective-permute-done((f32[1,2,2,16,128]{4,3,2,1,0:T(8,128)S(1)}, f32[1,2,2,16,128]{4,3,2,1,0:T(8,128)S(1)}, u32[]{:S(2)}, u32[]{:S(2)}) %collective-permute-start.7) | collective-permute-done | bytes 32800 | tf_op jit(solution)/shard_map/ppermute | solution.py:555
  38.8 0.0 collective-permute-done.4.refs_1_
  38.8 0.1 collective-permute-start.8
  38.9 2.5 %collective-permute-start.9 = (f32[2,8,8,128]{3,2,1,0:T(8,128)S(1)}, f32[2,8,8,128]{3,2,1,0:T(8,128)S(1)}, u32[]{:S(2)}, u32[]{:S(2)}) collective-permute-start(f32[2,8,8,128]{3,2,1,0:T(8,128)S(1)} %get-tuple-element.81), channel_id=1, source_target_pairs={{0,16},{4,20},{8,24},{12,28},{16,0},{20,4},{24,8},{28,12},{1,17},{... | collective-permute-start | bytes 196616 | tf_op jit(solution)/shard_map/ppermute | solution.py:663
  41.4 1.4 %collective-permute-start.10 = (f32[2,8,8,128]{3,2,1,0:T(8,128)S(1)}, f32[2,8,8,128]{3,2,1,0:T(8,128)S(1)}, u32[]{:S(2)}, u32[]{:S(2)}) collective-permute-start(f32[2,8,8,128]{3,2,1,0:T(8,128)S(1)} %get-tuple-element.82), channel_id=1, source_target_pairs={{0,24},{4,28},{8,0},{12,4},{16,8},{20,12},{24,16},{28,20},{1,25},{... | collective-permute-start | bytes 196616 | tf_op jit(solution)/shard_map/ppermute | solution.py:663
  42.8 0.1 copy.8
  42.9 0.8 %copy.9 = f32[2,8,16,32]{3,2,1,0:T(8,128)} copy(f32[2,8,16,32]{2,1,3,0:T(8,128)S(1)} %bitcast.5) | data formatting | bytes 65536
  43.7 1.5 %collective-permute-done.8.refs_1_ = f32[2,8,8,128]{3,2,1,0:T(8,128)S(1)} collective-permute-done((f32[2,8,8,128]{3,2,1,0:T(8,128)S(1)}, f32[2,8,8,128]{3,2,1,0:T(8,128)S(1)}, u32[]{:S(2)}, u32[]{:S(2)}) %collective-permute-start.8) | collective-permute-done | bytes 65568 | tf_op jit(solution)/shard_map/ppermute | solution.py:663
  45.2 1.2 %collective-permute-done.9.refs_2_ = f32[2,8,8,128]{3,2,1,0:T(8,128)S(1)} collective-permute-done((f32[2,8,8,128]{3,2,1,0:T(8,128)S(1)}, f32[2,8,8,128]{3,2,1,0:T(8,128)S(1)}, u32[]{:S(2)}, u32[]{:S(2)}) %collective-permute-start.9) | collective-permute-done | bytes 65568 | tf_op jit(solution)/shard_map/ppermute | solution.py:663
  46.4 0.0 collective-permute-done.10.refs_3_
  46.4 0.9 %fold_x.1 = f32[2,8,8,128]{3,2,1,0:T(8,128)} custom-call(f32[2,8,8,128]{3,2,1,0:T(8,128)S(1)} %get-tuple-element.79.refs_0_, f32[2,8,8,128]{3,2,1,0:T(8,128)S(1)} %collective-permute-done.8.refs_1_, f32[2,8,8,128]{3,2,1,0:T(8,128)S(1)} %collective-permute-done.9.refs_2_, f32[2,8,8,128]{3,2,1,0:T(8,128)S(1)} %collective-permute-done.10.refs_3_), custom_call_target="tpu_custom_call" | custom-call | tf_op jit(solution)/shard_map/fold_x/pallas_call | solution.py:664
  (3 shorter events, 0.1 us)
Async XLA Ops:
  0.6 1.2 %copy-start = (f32[64,32,128]{2,1,0:T(8,128)S(1)}, f32[64,32,128]{2,1,0:T(8,128)}, u32[]{:S(2)}) copy-start(f32[64,32,128]{2,1,0:T(8,128)} %field_ref.1) | copy-start | bytes 3145732
  2.5 7.2 %collective-permute-start = (f32[3,16,128]{2,1,0:T(8,128)S(1)}, f32[3,16,128]{2,1,0:T(8,128)S(1)}, u32[]{:S(2)}, u32[]{:S(2)}) collective-permute-start(f32[3,16,128]{2,1,0:T(8,128)S(1)} %get-tuple-element.44), channel_id=1, source_target_pairs={{0,1},{1,2},{2,3},{3,0},{4,5},{5,6},{6,7},{7,4},{8,9},{9,10},{10,1... | collective-permute-start | bytes 73736 | tf_op jit(solution)/shard_map/ppermute | solution.py:551
  3.0 6.7 %collective-permute-start.1 = (f32[3,16,128]{2,1,0:T(8,128)S(1)}, f32[3,16,128]{2,1,0:T(8,128)S(1)}, u32[]{:S(2)}, u32[]{:S(2)}) collective-permute-start(f32[3,16,128]{2,1,0:T(8,128)S(1)} %get-tuple-element.45), channel_id=1, source_target_pairs={{1,0},{2,1},{3,2},{0,3},{5,4},{6,5},{7,6},{4,7},{9,8},{10,9},{11,1... | collective-permute-start | bytes 73736 | tf_op jit(solution)/shard_map/ppermute | solution.py:551
  5.0 11.0 %copy-start.6 = (bf16[16,8]{0,1:T(8,128)(2,1)S(1)}, bf16[16,8]{0,1:T(8,128)(2,1)}, u32[]{:S(2)}) copy-start(bf16[16,8]{0,1:T(8,128)(2,1)} %param.4) | copy-start | bytes 772
  5.0 11.1 %copy-start.5 = (bf16[16,16]{1,0:T(8,128)(2,1)S(1)}, bf16[16,16]{1,0:T(8,128)(2,1)}, u32[]{:S(2)}) copy-start(bf16[16,16]{1,0:T(8,128)(2,1)} %out_ref.1) | copy-start | bytes 1540
  8.7 1.0 %copy-start.3 = (f32[12,10,16,128]{3,2,1,0:T(8,128)}, f32[12,10,16,128]{3,2,1,0:T(8,128)S(1)}, u32[]{:S(2)}) copy-start(f32[12,10,16,128]{3,2,1,0:T(8,128)S(1)} %get-tuple-element.53.slope_in_ref) | copy-start | bytes 2949124
  9.7 1.1 %copy-start.1 = (f32[12,10,16,128]{3,2,1,0:T(8,128)}, f32[12,10,16,128]{3,2,1,0:T(8,128)S(1)}, u32[]{:S(2)}) copy-start(f32[12,10,16,128]{3,2,1,0:T(8,128)S(1)} %get-tuple-element.52.ridge_in_ref) | copy-start | bytes 2949124
  10.8 13.6 %collective-permute-start.2 = (f32[3,72,128]{2,1,0:T(8,128)}, f32[3,72,128]{2,1,0:T(8,128)}, u32[]{:S(2)}, u32[]{:S(2)}) collective-permute-start(f32[3,72,128]{2,1,0:T(8,128)} %get-tuple-element.48), channel_id=1, source_target_pairs={{0,4},{4,8},{8,12},{12,16},{16,20},{20,24},{24,28},{28,0},{1,5},{5... | collective-permute-start | bytes 331784 | tf_op jit(solution)/shard_map/ppermute | solution.py:551
  13.0 11.4 %collective-permute-start.3 = (f32[3,72,128]{2,1,0:T(8,128)}, f32[3,72,128]{2,1,0:T(8,128)}, u32[]{:S(2)}, u32[]{:S(2)}) collective-permute-start(f32[3,72,128]{2,1,0:T(8,128)} %get-tuple-element.49), channel_id=1, source_target_pairs={{4,0},{8,4},{12,8},{16,12},{20,16},{24,20},{28,24},{0,28},{5,1},{9... | collective-permute-start | bytes 331784 | tf_op jit(solution)/shard_map/ppermute | solution.py:551
  16.1 1.2 %copy-start.2 = (f32[12,10,16,128]{3,2,1,0:T(8,128)S(1)}, f32[12,10,16,128]{3,2,1,0:T(8,128)}, u32[]{:S(2)}) copy-start(f32[12,10,16,128]{3,2,1,0:T(8,128)} %copy-done.1) | copy-start | bytes 2949124
  17.3 1.2 %copy-start.4 = (f32[12,10,16,128]{3,2,1,0:T(8,128)S(1)}, f32[12,10,16,128]{3,2,1,0:T(8,128)}, u32[]{:S(2)}) copy-start(f32[12,10,16,128]{3,2,1,0:T(8,128)} %copy-done.3) | copy-start | bytes 2949124
  29.5 9.3 %collective-permute-start.4 = (f32[4,2,6,8,128]{4,3,2,1,0:T(8,128)S(1)}, f32[4,2,6,8,128]{4,3,2,1,0:T(8,128)S(1)}, u32[]{:S(2)}, u32[]{:S(2)}) collective-permute-start(f32[4,2,6,8,128]{4,3,2,1,0:T(8,128)S(1)} %get-tuple-element.63), channel_id=1, source_target_pairs={{0,4},{4,0},{8,12},{12,8},{16,20},{20,16},{24,28},{28,24},{1,5},{5... | collective-permute-start | bytes 589832 | tf_op jit(solution)/shard_map/ppermute | solution.py:555
  32.6 2.2 %collective-permute-start.6 = (f32[2,2,2,16,128]{4,3,2,1,0:T(8,128)S(1)}, f32[2,2,2,16,128]{4,3,2,1,0:T(8,128)S(1)}, u32[]{:S(2)}, u32[]{:S(2)}) collective-permute-start(f32[2,2,2,16,128]{4,3,2,1,0:T(8,128)S(1)} %get-tuple-element.77), channel_id=1, source_target_pairs={{0,1},{1,0},{2,3},{3,2},{4,5},{5,4},{6,7},{7,6},{8,9},{9,8},{10,11... | collective-permute-start | bytes 196616 | tf_op jit(solution)/shard_map/ppermute | solution.py:555
  32.7 4.8 %collective-permute-start.5 = (f32[4,2,2,8,128]{4,3,2,1,0:T(8,128)S(1)}, f32[4,2,2,8,128]{4,3,2,1,0:T(8,128)S(1)}, u32[]{:S(2)}, u32[]{:S(2)}) collective-permute-start(f32[4,2,2,8,128]{4,3,2,1,0:T(8,128)S(1)} %get-tuple-element.75), channel_id=1, source_target_pairs={{0,4},{4,0},{8,12},{12,8},{16,20},{20,16},{24,28},{28,24},{1,5},{5... | collective-permute-start | bytes 196616 | tf_op jit(solution)/shard_map/ppermute | solution.py:555
  34.8 4.0 %collective-permute-start.7 = (f32[1,2,2,16,128]{4,3,2,1,0:T(8,128)S(1)}, f32[1,2,2,16,128]{4,3,2,1,0:T(8,128)S(1)}, u32[]{:S(2)}, u32[]{:S(2)}) collective-permute-start(f32[1,2,2,16,128]{4,3,2,1,0:T(8,128)S(1)} %get-tuple-element.78), channel_id=1, source_target_pairs={{0,2},{1,3},{2,0},{3,1},{4,6},{5,7},{6,4},{7,5},{8,10},{9,11},{10,... | collective-permute-start | bytes 98312 | tf_op jit(solution)/shard_map/ppermute | solution.py:555
  38.8 6.4 %collective-permute-start.8 = (f32[2,8,8,128]{3,2,1,0:T(8,128)S(1)}, f32[2,8,8,128]{3,2,1,0:T(8,128)S(1)}, u32[]{:S(2)}, u32[]{:S(2)}) collective-permute-start(f32[2,8,8,128]{3,2,1,0:T(8,128)S(1)} %get-tuple-element.80), channel_id=1, source_target_pairs={{0,8},{4,12},{8,16},{12,20},{16,24},{20,28},{24,0},{28,4},{1,9},{5... | collective-permute-start | bytes 196616 | tf_op jit(solution)/shard_map/ppermute | solution.py:663
  38.9 7.5 %collective-permute-start.9 = (f32[2,8,8,128]{3,2,1,0:T(8,128)S(1)}, f32[2,8,8,128]{3,2,1,0:T(8,128)S(1)}, u32[]{:S(2)}, u32[]{:S(2)}) collective-permute-start(f32[2,8,8,128]{3,2,1,0:T(8,128)S(1)} %get-tuple-element.81), channel_id=1, source_target_pairs={{0,16},{4,20},{8,24},{12,28},{16,0},{20,4},{24,8},{28,12},{1,17},{... | collective-permute-start | bytes 196616 | tf_op jit(solution)/shard_map/ppermute | solution.py:663
  41.4 5.0 %collective-permute-start.10 = (f32[2,8,8,128]{3,2,1,0:T(8,128)S(1)}, f32[2,8,8,128]{3,2,1,0:T(8,128)S(1)}, u32[]{:S(2)}, u32[]{:S(2)}) collective-permute-start(f32[2,8,8,128]{3,2,1,0:T(8,128)S(1)} %get-tuple-element.82), channel_id=1, source_target_pairs={{0,24},{4,28},{8,0},{12,4},{16,8},{20,12},{24,16},{28,20},{1,25},{... | collective-permute-start | bytes 196616 | tf_op jit(solution)/shard_map/ppermute | solution.py:663

commit v14 on v13

--- a/solution.py
+++ b/solution.py
@@ -15,7 +15,7 @@
 CHUNKS = 16
 REACH = 3
 VMEM = pl.BlockSpec(memory_space=pltpu.VMEM)
-PARAMS = pltpu.CompilerParams(vmem_limit_bytes=36 * 1024 * 1024)
+PARAMS = pltpu.CompilerParams(vmem_limit_bytes=24 * 1024 * 1024)
 
 
 def call(kernel, name, outs, count, scratch=()):
@@ -211,16 +211,20 @@
 
 
 def early_kernel(
-    counts, turned_ref, order_ref, once_ref, twice_ref, ridge_ref, slope_ref
+    counts, turned_ref, order_ref, *refs
 ):
+    outs, (once_ref, twice_ref, ridge_ref, slope_ref) = refs[:4], refs[4:]
     order_ref[...] = jnp.zeros_like(order_ref)
     run = once_ref.shape[1] - 4
     stencil = Stencil(run, counts)
     for k in range(once_ref.shape[0]):
         stencil.once(turned_ref, k + 1, once_ref, k, offsets=range(1, run - 1))
     for k in range(twice_ref.shape[0]):
-        outs = (twice_ref, ridge_ref, slope_ref)
-        stencil.twice(once_ref, k + 1, *outs, k, offsets=range(2, run - 2))
+        fields = (twice_ref, ridge_ref, slope_ref)
+        stencil.twice(once_ref, k + 1, *fields, k, offsets=range(2, run - 2))
+    outs[0][...] = once_ref[:, 3 : run + 1]
+    for out_ref, ref in zip(outs[1:], (twice_ref, ridge_ref, slope_ref)):
+        out_ref[...] = ref[:, 3 : run - 1]
 
 
 def middle_kernel(
@@ -281,10 +285,10 @@
                 cy_ref[x0 + i, at], ty_ref[x0 + i, at] = rays_y[i]
 
     many_y = 2 if ahead % 2 == 0 else 1
-    once_ref[:, 3 : run + 1] = once_in_ref[:, 3 : run + 1]
+    once_ref[:, 3 : run + 1] = once_in_ref[...]
     fields = (twice_ref, ridge_ref, slope_ref)
     for ref, in_ref in zip(fields, (twice_in_ref, ridge_in_ref, slope_in_ref)):
-        ref[:, 3 : run - 1] = in_ref[:, 3 : run - 1]
+        ref[:, 3 : run - 1] = in_ref[...]
     ends = [-2, -1, 0, run - 1, run, run + 1]
     for k in range(inner + 4):
         stencil.once(wide_ref, k + 1, once_ref, k, offsets=ends)
@@ -580,8 +584,10 @@
     order, *early = call(
         functools.partial(early_kernel, counts),
         "early",
-        [sds(SUB, LANES), plane(inner + 4, run + 4)] + [plane(inner + 2, run + 2)] * 3,
+        [sds(SUB, LANES), plane(inner + 4, run - 2)] + [plane(inner + 2, run - 4)] * 3,
         1,
+        [pltpu.VMEM((inner + 4, run + 4, CHUNKS, LANES), F32)]
+        + [pltpu.VMEM((inner + 2, run + 2, CHUNKS, LANES), F32)] * 3,
     )(turned)
     edge = sds(REACH, rows // 2, LANES)
     wide, first, last = call(

time: 47.6 us -> 42.6 us (0.89)
  local copies, waits for them, and re-layouts: 5.64 us -> 2.23 us
  Pallas kernels: 20.3 us -> 18.5 us
    unnamed x16 -> x8, local copies, waits for them, and re-layouts: 5.51 us -> 2.11 us
    pallas_call x1, Pallas kernels: 5.1 us -> 4.15 us  [body(): call(functools.partial(ends_first_kernel, counts, steps), 'ends_first', [...]
    pallas_call x1, Pallas kernels: 1.04 us -> 0.16 us  [body(): call(functools.partial(sides_kernel, local_y, count_y), 'sides', [sds(hal...]
  transfers between devices with their start and end apart: 11 -> 11, of which waited for: 4 -> 4; matrix products, arithmetic and copies ran while one was open for 2% -> 2% of each run, Pallas kernels for 27% -> 30%
where the time goes in v14:
time: 42.6 us; the launch traced here: 42.4 us
  Pallas kernels  18.5 us (43%)
  starting transfers between devices  15.7 us (37%)
  waiting for transfers between devices  5.19 us (12%)
  local copies, waits for them, and re-layouts  2.23 us (5%)
  between operations  0.75 us (2%)
    ppermute x4, starting transfers between devices, exchange(): return (lax.ppermute(last, axis, up), lax.ppermute(first, axis, down))  8.07 us
    pallas_call x1, Pallas kernels, body(): call(functools.partial(middle_kernel, counts, steps), 'middle', weights +...  5.89 us
    pallas_call x1, Pallas kernels, body(): call(functools.partial(ends_first_kernel, counts, steps), 'ends_first', [...  4.15 us
    ppermute x3, starting transfers between devices, body(): pieces[t] = lax.ppermute(pieces[t], 'bx', pairs)  3.87 us
    ppermute x4, starting transfers between devices, swap(): lax.ppermute(value, axis, [(i, i ^ bit) for i in range(lax.axis_size(axis...  3.8 us
    pallas_call x1, Pallas kernels, body(): call(functools.partial(early_kernel, counts), 'early', [sds(SUB, LANES),...  3.66 us
    pallas_call x1, Pallas kernels, body(): call(functools.partial(last_kernel, counts, steps), 'last', parts(later)...  3.03 us
    ppermute x3, waiting for transfers between devices, body(): pieces[t] = lax.ppermute(pieces[t], 'bx', pairs)  2.78 us
  transfers between devices with their start and end apart: 11, of which 4 were waited for; matrix products, arithmetic and copies ran while one was open for 2% of the time, Pallas kernels for 30%

profile of v14, /device:TPU:0, one launch (start us, length us, event | category | flops | bytes accessed | tf_op | source)
XLA Modules:
  0.0 42.4 jit_solution(6255998949732845473)
XLA Ops:
  0.6 0.0 copy-start
  0.6 1.2 %copy-done = f32[64,32,128]{2,1,0:T(8,128)S(1)} copy-done((f32[64,32,128]{2,1,0:T(8,128)S(1)}, f32[64,32,128]{2,1,0:T(8,128)}, u32[]{:S(2)}) %copy-start) | copy-done | bytes 1048600
  1.9 0.6 %turn.1 = (f32[16,144,128]{2,1,0:T(8,128)S(1)}, f32[3,16,128]{2,1,0:T(8,128)S(1)}, f32[3,16,128]{2,1,0:T(8,128)S(1)}) custom-call(f32[64,32,128]{2,1,0:T(8,128)S(1)} %copy-done), custom_call_target="tpu_custom_call" | custom-call | tf_op jit(solution)/shard_map/turn/pallas_call | solution.py:577
  2.5 0.5 %collective-permute-start = (f32[3,16,128]{2,1,0:T(8,128)S(1)}, f32[3,16,128]{2,1,0:T(8,128)S(1)}, u32[]{:S(2)}, u32[]{:S(2)}) collective-permute-start(f32[3,16,128]{2,1,0:T(8,128)S(1)} %get-tuple-element.44), channel_id=1, source_target_pairs={{0,1},{1,2},{2,3},{3,0},{4,5},{5,6},{6,7},{7,4},{8,9},{9,10},{10,1... | collective-permute-start | bytes 73736 | tf_op jit(solution)/shard_map/ppermute | solution.py:555
  3.0 2.0 %collective-permute-start.1 = (f32[3,16,128]{2,1,0:T(8,128)S(1)}, f32[3,16,128]{2,1,0:T(8,128)S(1)}, u32[]{:S(2)}, u32[]{:S(2)}) collective-permute-start(f32[3,16,128]{2,1,0:T(8,128)S(1)} %get-tuple-element.45), channel_id=1, source_target_pairs={{1,0},{2,1},{3,2},{0,3},{5,4},{6,5},{7,6},{4,7},{9,8},{10,9},{11,1... | collective-permute-start | bytes 73736 | tf_op jit(solution)/shard_map/ppermute | solution.py:555
  5.0 0.0 copy-start.2
  5.0 0.0 copy-start.1
  5.0 3.7 %early.1 = (f32[8,128]{1,0:T(8,128)S(1)}, f32[14,6,16,128]{3,2,1,0:T(8,128)S(1)}, f32[12,4,16,128]{3,2,1,0:T(8,128)S(1)}, f32[12,4,16,128]{3,2,1,0:T(8,128)S(1)}, f32[12,4,16,128]{3,2,1,0:T(8,128)S(1)}) custom-call(f32[16,144,128]{2,1,0:T(8,128)S(1)} %get-tuple-element.43.turned_ref), custom_call_target="tpu_custom_call" | custom-call | tf_op jit(solution)/shard_map/early/pallas_call | solution.py:584
  8.7 0.0 collective-permute-done.before_ref
  8.7 0.0 collective-permute-done.1.after_ref
  8.7 0.2 sides.1
  8.9 2.3 %collective-permute-start.2 = (f32[3,72,128]{2,1,0:T(8,128)S(1)}, f32[3,72,128]{2,1,0:T(8,128)S(1)}, u32[]{:S(2)}, u32[]{:S(2)}) collective-permute-start(f32[3,72,128]{2,1,0:T(8,128)S(1)} %get-tuple-element.48), channel_id=1, source_target_pairs={{0,4},{4,8},{8,12},{12,16},{16,20},{20,24},{24,28},{28,0},{1,5},{5... | collective-permute-start | bytes 331784 | tf_op jit(solution)/shard_map/ppermute | solution.py:555
  11.1 3.3 %collective-permute-start.3 = (f32[3,72,128]{2,1,0:T(8,128)S(1)}, f32[3,72,128]{2,1,0:T(8,128)S(1)}, u32[]{:S(2)}, u32[]{:S(2)}) collective-permute-start(f32[3,72,128]{2,1,0:T(8,128)S(1)} %get-tuple-element.49), channel_id=1, source_target_pairs={{4,0},{8,4},{12,8},{16,12},{20,16},{24,20},{28,24},{0,28},{5,1},{9... | collective-permute-start | bytes 331784 | tf_op jit(solution)/shard_map/ppermute | solution.py:555
  14.4 0.0 copy-done.2
  14.4 0.1 copy.7.in_ref
  14.5 0.0 copy-done.1
  14.5 5.9 %middle.1 = (bf16[128,256]{1,0:T(8,128)(2,1)S(1)}, bf16[256,256]{1,0:T(8,128)(2,1)S(1)}, f32[2,4,12,16,128]{4,3,2,1,0:T(8,128)S(1)}, f32[2,2,10,16,128]{4,3,2,1,...) custom-call(f32[16,144,128]{2,1,0:T(8,128)S(1)} %get-tuple-element.4, ...), custom_call_target="tpu_custom_call" | custom-call | tf_op jit(solution)/shard_map/middle/pallas_call | solution.py:602
  20.4 0.0 collective-permute-done.2.before_ref
  20.4 0.0 collective-permute-done.3.after_ref
  20.4 4.1 %ends_first.1 = (f32[2,5,10,16,128]{4,3,2,1,0:T(8,128)S(1)}, f32[2,5,10,16,128]{4,3,2,1,0:T(8,128)S(1)}, f32[2,5,10,16,128]{4,3,2,1,0:T(8,128)S(1)}, f32[6,128,1...) custom-call(f32[16,144,128]{2,1,0:T(8,128)S(1)} %get-tuple-element.4, ...), custom_call_target="tpu_custom_call" | custom-call | tf_op jit(solution)/shard_map/ends_first/pallas_call | solution.py:625
  24.6 0.1 collective-permute-start.4
  24.7 3.0 %last.1 = (f32[4,2,2,8,128]{4,3,2,1,0:T(8,128)S(1)}, f32[4,2,2,8,128]{4,3,2,1,0:T(8,128)S(1)}, f32[2,2,2,16,128]{4,3,2,1,0:T(8,128)S(1)}, f32[2,2,2,16,128]{4,3,2,1,0:T(8,128)S(1)}) custom-call(bf16[128,256]{1,0:T(8,128)(2,1)S(1)} %get-tuple-element.54.win_ref.refs_0_, bf16[256,256]{1,0:T(8,128)(2,1)S(1)} %get-tuple-element.55.wout_ref.refs_1_, ...), custom_call_target="tpu_custom_call" | custom-call | tf_op jit(solution)/shard_map/last/pallas_call | solution.py:638
  27.7 0.1 collective-permute-start.6
  27.8 2.1 %collective-permute-start.5 = (f32[4,2,2,8,128]{4,3,2,1,0:T(8,128)S(1)}, f32[4,2,2,8,128]{4,3,2,1,0:T(8,128)S(1)}, u32[]{:S(2)}, u32[]{:S(2)}) collective-permute-start(f32[4,2,2,8,128]{4,3,2,1,0:T(8,128)S(1)} %get-tuple-element.75), channel_id=1, source_target_pairs={{0,4},{4,0},{8,12},{12,8},{16,20},{20,16},{24,28},{28,24},{1,5},{5... | collective-permute-start | bytes 196616 | tf_op jit(solution)/shard_map/ppermute | solution.py:559
  29.8 0.0 collective-permute-done.6.received_ref
  29.9 1.6 %collective-permute-start.7 = (f32[1,2,2,16,128]{4,3,2,1,0:T(8,128)S(1)}, f32[1,2,2,16,128]{4,3,2,1,0:T(8,128)S(1)}, u32[]{:S(2)}, u32[]{:S(2)}) collective-permute-start(f32[1,2,2,16,128]{4,3,2,1,0:T(8,128)S(1)} %get-tuple-element.78), channel_id=1, source_target_pairs={{0,2},{1,3},{2,0},{3,1},{4,6},{5,7},{6,4},{7,5},{8,10},{9,11},{10,... | collective-permute-start | bytes 98312 | tf_op jit(solution)/shard_map/ppermute | solution.py:559
  31.5 1.1 %collective-permute-done.5.refs_3_ = f32[4,2,2,8,128]{4,3,2,1,0:T(8,128)S(1)} collective-permute-done((f32[4,2,2,8,128]{4,3,2,1,0:T(8,128)S(1)}, f32[4,2,2,8,128]{4,3,2,1,0:T(8,128)S(1)}, u32[]{:S(2)}, u32[]{:S(2)}) %collective-permute-start.5) | collective-permute-done | bytes 65568 | tf_op jit(solution)/shard_map/ppermute | solution.py:559
  32.5 1.3 %collective-permute-done.7.refs_4_.received_ref = f32[1,2,2,16,128]{4,3,2,1,0:T(8,128)S(1)} collective-permute-done((f32[1,2,2,16,128]{4,3,2,1,0:T(8,128)S(1)}, f32[1,2,2,16,128]{4,3,2,1,0:T(8,128)S(1)}, u32[]{:S(2)}, u32[]{:S(2)}) %collective-permute-start.7) | collective-permute-done | bytes 32800 | tf_op jit(solution)/shard_map/ppermute | solution.py:559
  33.8 0.0 collective-permute-done.4.refs_1_
  33.9 0.1 collective-permute-start.8
  34.0 2.3 %collective-permute-start.9 = (f32[2,8,8,128]{3,2,1,0:T(8,128)S(1)}, f32[2,8,8,128]{3,2,1,0:T(8,128)S(1)}, u32[]{:S(2)}, u32[]{:S(2)}) collective-permute-start(f32[2,8,8,128]{3,2,1,0:T(8,128)S(1)} %get-tuple-element.81), channel_id=1, source_target_pairs={{0,16},{4,20},{8,24},{12,28},{16,0},{20,4},{24,8},{28,12},{1,17},{... | collective-permute-start | bytes 196616 | tf_op jit(solution)/shard_map/ppermute | solution.py:669
  36.3 1.5 %collective-permute-start.10 = (f32[2,8,8,128]{3,2,1,0:T(8,128)S(1)}, f32[2,8,8,128]{3,2,1,0:T(8,128)S(1)}, u32[]{:S(2)}, u32[]{:S(2)}) collective-permute-start(f32[2,8,8,128]{3,2,1,0:T(8,128)S(1)} %get-tuple-element.82), channel_id=1, source_target_pairs={{0,24},{4,28},{8,0},{12,4},{16,8},{20,12},{24,16},{28,20},{1,25},{... | collective-permute-start | bytes 196616 | tf_op jit(solution)/shard_map/ppermute | solution.py:669
  37.8 0.1 copy.8
  37.9 0.8 %copy.9 = f32[2,8,16,32]{3,2,1,0:T(8,128)} copy(f32[2,8,16,32]{2,1,3,0:T(8,128)S(1)} %bitcast.5) | data formatting | bytes 65536
  38.7 1.6 %collective-permute-done.8.refs_1_ = f32[2,8,8,128]{3,2,1,0:T(8,128)S(1)} collective-permute-done((f32[2,8,8,128]{3,2,1,0:T(8,128)S(1)}, f32[2,8,8,128]{3,2,1,0:T(8,128)S(1)}, u32[]{:S(2)}, u32[]{:S(2)}) %collective-permute-start.8) | collective-permute-done | bytes 65568 | tf_op jit(solution)/shard_map/ppermute | solution.py:669
  40.3 1.2 %collective-permute-done.9.refs_2_ = f32[2,8,8,128]{3,2,1,0:T(8,128)S(1)} collective-permute-done((f32[2,8,8,128]{3,2,1,0:T(8,128)S(1)}, f32[2,8,8,128]{3,2,1,0:T(8,128)S(1)}, u32[]{:S(2)}, u32[]{:S(2)}) %collective-permute-start.9) | collective-permute-done | bytes 65568 | tf_op jit(solution)/shard_map/ppermute | solution.py:669
  41.5 0.0 collective-permute-done.10.refs_3_
  41.5 0.9 %fold_x.1 = f32[2,8,8,128]{3,2,1,0:T(8,128)} custom-call(f32[2,8,8,128]{3,2,1,0:T(8,128)S(1)} %get-tuple-element.79.refs_0_, f32[2,8,8,128]{3,2,1,0:T(8,128)S(1)} %collective-permute-done.8.refs_1_, f32[2,8,8,128]{3,2,1,0:T(8,128)S(1)} %collective-permute-done.9.refs_2_, f32[2,8,8,128]{3,2,1,0:T(8,128)S(1)} %collective-permute-done.10.refs_3_), custom_call_target="tpu_custom_call" | custom-call | tf_op jit(solution)/shard_map/fold_x/pallas_call | solution.py:670
  (3 shorter events, 0.1 us)
Async XLA Ops:
  0.6 1.2 %copy-start = (f32[64,32,128]{2,1,0:T(8,128)S(1)}, f32[64,32,128]{2,1,0:T(8,128)}, u32[]{:S(2)}) copy-start(f32[64,32,128]{2,1,0:T(8,128)} %field_ref.1) | copy-start | bytes 3145732
  2.5 6.2 %collective-permute-start = (f32[3,16,128]{2,1,0:T(8,128)S(1)}, f32[3,16,128]{2,1,0:T(8,128)S(1)}, u32[]{:S(2)}, u32[]{:S(2)}) collective-permute-start(f32[3,16,128]{2,1,0:T(8,128)S(1)} %get-tuple-element.44), channel_id=1, source_target_pairs={{0,1},{1,2},{2,3},{3,0},{4,5},{5,6},{6,7},{7,4},{8,9},{9,10},{10,1... | collective-permute-start | bytes 73736 | tf_op jit(solution)/shard_map/ppermute | solution.py:555
  3.0 5.7 %collective-permute-start.1 = (f32[3,16,128]{2,1,0:T(8,128)S(1)}, f32[3,16,128]{2,1,0:T(8,128)S(1)}, u32[]{:S(2)}, u32[]{:S(2)}) collective-permute-start(f32[3,16,128]{2,1,0:T(8,128)S(1)} %get-tuple-element.45), channel_id=1, source_target_pairs={{1,0},{2,1},{3,2},{0,3},{5,4},{6,5},{7,6},{4,7},{9,8},{10,9},{11,1... | collective-permute-start | bytes 73736 | tf_op jit(solution)/shard_map/ppermute | solution.py:555
  5.0 9.4 %copy-start.2 = (bf16[16,8]{0,1:T(8,128)(2,1)S(1)}, bf16[16,8]{0,1:T(8,128)(2,1)}, u32[]{:S(2)}) copy-start(bf16[16,8]{0,1:T(8,128)(2,1)} %param.4) | copy-start | bytes 772
  5.0 9.5 %copy-start.1 = (bf16[16,16]{1,0:T(8,128)(2,1)S(1)}, bf16[16,16]{1,0:T(8,128)(2,1)}, u32[]{:S(2)}) copy-start(bf16[16,16]{1,0:T(8,128)(2,1)} %out_ref.1) | copy-start | bytes 1540
  8.9 11.5 %collective-permute-start.2 = (f32[3,72,128]{2,1,0:T(8,128)S(1)}, f32[3,72,128]{2,1,0:T(8,128)S(1)}, u32[]{:S(2)}, u32[]{:S(2)}) collective-permute-start(f32[3,72,128]{2,1,0:T(8,128)S(1)} %get-tuple-element.48), channel_id=1, source_target_pairs={{0,4},{4,8},{8,12},{12,16},{16,20},{20,24},{24,28},{28,0},{1,5},{5... | collective-permute-start | bytes 331784 | tf_op jit(solution)/shard_map/ppermute | solution.py:555
  11.1 9.3 %collective-permute-start.3 = (f32[3,72,128]{2,1,0:T(8,128)S(1)}, f32[3,72,128]{2,1,0:T(8,128)S(1)}, u32[]{:S(2)}, u32[]{:S(2)}) collective-permute-start(f32[3,72,128]{2,1,0:T(8,128)S(1)} %get-tuple-element.49), channel_id=1, source_target_pairs={{4,0},{8,4},{12,8},{16,12},{20,16},{24,20},{28,24},{0,28},{5,1},{9... | collective-permute-start | bytes 331784 | tf_op jit(solution)/shard_map/ppermute | solution.py:555
  24.6 9.3 %collective-permute-start.4 = (f32[4,2,6,8,128]{4,3,2,1,0:T(8,128)S(1)}, f32[4,2,6,8,128]{4,3,2,1,0:T(8,128)S(1)}, u32[]{:S(2)}, u32[]{:S(2)}) collective-permute-start(f32[4,2,6,8,128]{4,3,2,1,0:T(8,128)S(1)} %get-tuple-element.63), channel_id=1, source_target_pairs={{0,4},{4,0},{8,12},{12,8},{16,20},{20,16},{24,28},{28,24},{1,5},{5... | collective-permute-start | bytes 589832 | tf_op jit(solution)/shard_map/ppermute | solution.py:559
  27.7 2.2 %collective-permute-start.6 = (f32[2,2,2,16,128]{4,3,2,1,0:T(8,128)S(1)}, f32[2,2,2,16,128]{4,3,2,1,0:T(8,128)S(1)}, u32[]{:S(2)}, u32[]{:S(2)}) collective-permute-start(f32[2,2,2,16,128]{4,3,2,1,0:T(8,128)S(1)} %get-tuple-element.77), channel_id=1, source_target_pairs={{0,1},{1,0},{2,3},{3,2},{4,5},{5,4},{6,7},{7,6},{8,9},{9,8},{10,11... | collective-permute-start | bytes 196616 | tf_op jit(solution)/shard_map/ppermute | solution.py:559
  27.8 4.8 %collective-permute-start.5 = (f32[4,2,2,8,128]{4,3,2,1,0:T(8,128)S(1)}, f32[4,2,2,8,128]{4,3,2,1,0:T(8,128)S(1)}, u32[]{:S(2)}, u32[]{:S(2)}) collective-permute-start(f32[4,2,2,8,128]{4,3,2,1,0:T(8,128)S(1)} %get-tuple-element.75), channel_id=1, source_target_pairs={{0,4},{4,0},{8,12},{12,8},{16,20},{20,16},{24,28},{28,24},{1,5},{5... | collective-permute-start | bytes 196616 | tf_op jit(solution)/shard_map/ppermute | solution.py:559
  29.9 4.0 %collective-permute-start.7 = (f32[1,2,2,16,128]{4,3,2,1,0:T(8,128)S(1)}, f32[1,2,2,16,128]{4,3,2,1,0:T(8,128)S(1)}, u32[]{:S(2)}, u32[]{:S(2)}) collective-permute-start(f32[1,2,2,16,128]{4,3,2,1,0:T(8,128)S(1)} %get-tuple-element.78), channel_id=1, source_target_pairs={{0,2},{1,3},{2,0},{3,1},{4,6},{5,7},{6,4},{7,5},{8,10},{9,11},{10,... | collective-permute-start | bytes 98312 | tf_op jit(solution)/shard_map/ppermute | solution.py:559
  33.9 6.4 %collective-permute-start.8 = (f32[2,8,8,128]{3,2,1,0:T(8,128)S(1)}, f32[2,8,8,128]{3,2,1,0:T(8,128)S(1)}, u32[]{:S(2)}, u32[]{:S(2)}) collective-permute-start(f32[2,8,8,128]{3,2,1,0:T(8,128)S(1)} %get-tuple-element.80), channel_id=1, source_target_pairs={{0,8},{4,12},{8,16},{12,20},{16,24},{20,28},{24,0},{28,4},{1,9},{5... | collective-permute-start | bytes 196616 | tf_op jit(solution)/shard_map/ppermute | solution.py:669
  34.0 7.5 %collective-permute-start.9 = (f32[2,8,8,128]{3,2,1,0:T(8,128)S(1)}, f32[2,8,8,128]{3,2,1,0:T(8,128)S(1)}, u32[]{:S(2)}, u32[]{:S(2)}) collective-permute-start(f32[2,8,8,128]{3,2,1,0:T(8,128)S(1)} %get-tuple-element.81), channel_id=1, source_target_pairs={{0,16},{4,20},{8,24},{12,28},{16,0},{20,4},{24,8},{28,12},{1,17},{... | collective-permute-start | bytes 196616 | tf_op jit(solution)/shard_map/ppermute | solution.py:669
  36.3 5.2 %collective-permute-start.10 = (f32[2,8,8,128]{3,2,1,0:T(8,128)S(1)}, f32[2,8,8,128]{3,2,1,0:T(8,128)S(1)}, u32[]{:S(2)}, u32[]{:S(2)}) collective-permute-start(f32[2,8,8,128]{3,2,1,0:T(8,128)S(1)} %get-tuple-element.82), channel_id=1, source_target_pairs={{0,24},{4,28},{8,0},{12,4},{16,8},{20,12},{24,16},{28,20},{1,25},{... | collective-permute-start | bytes 196616 | tf_op jit(solution)/shard_map/ppermute | solution.py:669

commit v15 on v11

--- a/solution.py
+++ b/solution.py
@@ -620,7 +620,7 @@
         level, many = 2 * level, many // 2
     many = count_x // 2
     piece = sds(2, run, share, LANES)
-    operands = [*halves[0], *halves[1], received]
+    operands = [*halves[0], *halves[1], sent_y]
     pieces = list(call(merge_x_kernel, "merge_x", [piece] * many, len(operands))(*operands))
     for t in range(1, many):
         pairs = [(i, (i + 2 * t) % count_x) for i in range(count_x)]

time: 42.3 us -> 42.4 us (level)
    ppermute x4, waiting for transfers between devices: 3.09 us -> 5.86 us  [swap(): lax.ppermute(value, axis, [(i, i ^ bit) for i in range(lax.axis_size(axis...]
    ppermute x3, waiting for transfers between devices: 2.7 us -> 0.01 us  [body(): pieces[t] = lax.ppermute(pieces[t], 'bx', pairs)]
  transfers between devices with their start and end apart: 11 -> 11, of which waited for: 6 -> 4; matrix products, arithmetic and copies ran while one was open for 2% -> 2% of each run, Pallas kernels for 24% -> 24%
where the time goes in v15:
time: 42.4 us; the launch traced here: 42.3 us
  Pallas kernels  16.1 us (38%)
  starting transfers between devices  15.8 us (37%)
  waiting for transfers between devices  7.4 us (17%)
  local copies, waits for them, and re-layouts  2.23 us (5%)
  between operations  0.72 us (2%)
    ppermute x4, starting transfers between devices, exchange(): return (lax.ppermute(last, axis, up), lax.ppermute(first, axis, down))  7.89 us
    pallas_call x1, Pallas kernels, body(): call(functools.partial(middle_kernel, counts, steps), 'middle', weights +...  6.96 us
    ppermute x4, waiting for transfers between devices, swap(): lax.ppermute(value, axis, [(i, i ^ bit) for i in range(lax.axis_size(axis...  5.86 us
    pallas_call x1, Pallas kernels, body(): call(functools.partial(ends_first_kernel, counts, steps), 'ends_first', [...  4.15 us
    ppermute x4, starting transfers between devices, swap(): lax.ppermute(value, axis, [(i, i ^ bit) for i in range(lax.axis_size(axis...  4.07 us
    ppermute x3, starting transfers between devices, body(): pieces[t] = lax.ppermute(pieces[t], 'bx', pairs)  3.9 us
    pallas_call x1, Pallas kernels, body(): call(functools.partial(last_kernel, counts, steps), 'last', parts(later)...  3.19 us
    unnamed x8, local copies, waits for them, and re-layouts  2.11 us
  transfers between devices with their start and end apart: 11, of which 4 were waited for; matrix products, arithmetic and copies ran while one was open for 2% of the time, Pallas kernels for 24%

profile of v15, /device:TPU:0, one launch (start us, length us, event | category | flops | bytes accessed | tf_op | source)
XLA Modules:
  0.0 42.3 jit_solution(4752180839007429358)
XLA Ops:
  0.6 0.0 copy-start
  0.6 1.2 %copy-done = f32[64,32,128]{2,1,0:T(8,128)S(1)} copy-done((f32[64,32,128]{2,1,0:T(8,128)S(1)}, f32[64,32,128]{2,1,0:T(8,128)}, u32[]{:S(2)}) %copy-start) | copy-done | bytes 1048600
  1.9 0.0 copy-start.2
  1.9 0.0 copy-start.1
  1.9 0.6 %turn.1 = (f32[16,144,128]{2,1,0:T(8,128)S(1)}, f32[3,16,128]{2,1,0:T(8,128)S(1)}, f32[3,16,128]{2,1,0:T(8,128)S(1)}) custom-call(f32[64,32,128]{2,1,0:T(8,128)S(1)} %copy-done), custom_call_target="tpu_custom_call" | custom-call | tf_op jit(solution)/shard_map/turn/pallas_call | solution.py:546
  2.5 0.5 %collective-permute-start = (f32[3,16,128]{2,1,0:T(8,128)S(1)}, f32[3,16,128]{2,1,0:T(8,128)S(1)}, u32[]{:S(2)}, u32[]{:S(2)}) collective-permute-start(f32[3,16,128]{2,1,0:T(8,128)S(1)} %get-tuple-element.39), channel_id=1, source_target_pairs={{0,1},{1,2},{2,3},{3,0},{4,5},{5,6},{6,7},{7,4},{8,9},{9,10},{10,1... | collective-permute-start | bytes 73736 | tf_op jit(solution)/shard_map/ppermute | solution.py:524
  3.0 2.0 %collective-permute-start.1 = (f32[3,16,128]{2,1,0:T(8,128)S(1)}, f32[3,16,128]{2,1,0:T(8,128)S(1)}, u32[]{:S(2)}, u32[]{:S(2)}) collective-permute-start(f32[3,16,128]{2,1,0:T(8,128)S(1)} %get-tuple-element.40), channel_id=1, source_target_pairs={{1,0},{2,1},{3,2},{0,3},{5,4},{6,5},{7,6},{4,7},{9,8},{10,9},{11,1... | collective-permute-start | bytes 73736 | tf_op jit(solution)/shard_map/ppermute | solution.py:524
  5.0 1.4 %collective-permute-done.before_ref = f32[3,16,128]{2,1,0:T(8,128)S(1)} collective-permute-done((f32[3,16,128]{2,1,0:T(8,128)S(1)}, f32[3,16,128]{2,1,0:T(8,128)S(1)}, u32[]{:S(2)}, u32[]{:S(2)}) %collective-permute-start) | collective-permute-done | bytes 24608 | tf_op jit(solution)/shard_map/ppermute | solution.py:524
  6.5 0.1 collective-permute-done.1.after_ref
  6.6 0.2 sides.1
  6.7 2.3 %collective-permute-start.2 = (f32[3,72,128]{2,1,0:T(8,128)S(1)}, f32[3,72,128]{2,1,0:T(8,128)S(1)}, u32[]{:S(2)}, u32[]{:S(2)}) collective-permute-start(f32[3,72,128]{2,1,0:T(8,128)S(1)} %get-tuple-element.42), channel_id=1, source_target_pairs={{0,4},{4,8},{8,12},{12,16},{16,20},{20,24},{24,28},{28,0},{1,5},{5... | collective-permute-start | bytes 331784 | tf_op jit(solution)/shard_map/ppermute | solution.py:524
  9.0 3.1 %collective-permute-start.3 = (f32[3,72,128]{2,1,0:T(8,128)S(1)}, f32[3,72,128]{2,1,0:T(8,128)S(1)}, u32[]{:S(2)}, u32[]{:S(2)}) collective-permute-start(f32[3,72,128]{2,1,0:T(8,128)S(1)} %get-tuple-element.43), channel_id=1, source_target_pairs={{4,0},{8,4},{12,8},{16,12},{20,16},{24,20},{28,24},{0,28},{5,1},{9... | collective-permute-start | bytes 331784 | tf_op jit(solution)/shard_map/ppermute | solution.py:524
  12.1 0.0 copy-done.2
  12.1 0.1 copy.7.in_ref
  12.2 0.0 copy-done.1
  12.2 7.0 %middle.1 = (bf16[128,256]{1,0:T(8,128)(2,1)S(1)}, bf16[256,256]{1,0:T(8,128)(2,1)S(1)}, f32[2,4,12,16,128]{4,3,2,1,0:T(8,128)S(1)}, f32[2,2,10,16,128]{4,3,2,1,...) custom-call(f32[16,144,128]{2,1,0:T(8,128)S(1)} %get-tuple-element.4, ...), custom_call_target="tpu_custom_call" | custom-call | tf_op jit(solution)/shard_map/middle/pallas_call | solution.py:560
  19.1 0.0 collective-permute-done.2.before_ref
  19.1 0.0 collective-permute-done.3.after_ref
  19.2 4.1 %ends_first.1 = (f32[2,5,10,16,128]{4,3,2,1,0:T(8,128)S(1)}, f32[2,5,10,16,128]{4,3,2,1,0:T(8,128)S(1)}, f32[2,5,10,16,128]{4,3,2,1,0:T(8,128)S(1)}, f32[6,128,1...) custom-call(f32[16,144,128]{2,1,0:T(8,128)S(1)} %get-tuple-element.4, ...), custom_call_target="tpu_custom_call" | custom-call | tf_op jit(solution)/shard_map/ends_first/pallas_call | solution.py:583
  23.3 0.1 collective-permute-start.4
  23.4 3.2 %last.1 = (f32[4,2,2,8,128]{4,3,2,1,0:T(8,128)S(1)}, f32[4,2,2,8,128]{4,3,2,1,0:T(8,128)S(1)}, f32[2,2,2,16,128]{4,3,2,1,0:T(8,128)S(1)}, f32[2,2,2,16,128]{4,3,2,1,0:T(8,128)S(1)}) custom-call(bf16[128,256]{1,0:T(8,128)(2,1)S(1)} %get-tuple-element.44.win_ref.refs_0_, bf16[256,256]{1,0:T(8,128)(2,1)S(1)} %get-tuple-element.45.wout_ref.refs_1_, ...), custom_call_target="tpu_custom_call" | custom-call | tf_op jit(solution)/shard_map/last/pallas_call | solution.py:596
  26.6 1.4 %collective-permute-start.6 = (f32[2,2,2,16,128]{4,3,2,1,0:T(8,128)S(1)}, f32[2,2,2,16,128]{4,3,2,1,0:T(8,128)S(1)}, u32[]{:S(2)}, u32[]{:S(2)}) collective-permute-start(f32[2,2,2,16,128]{4,3,2,1,0:T(8,128)S(1)} %get-tuple-element.67), channel_id=1, source_target_pairs={{0,1},{1,0},{2,3},{3,2},{4,5},{5,4},{6,7},{7,6},{8,9},{9,8},{10,11... | collective-permute-start | bytes 196616 | tf_op jit(solution)/shard_map/ppermute | solution.py:528
  28.0 1.7 %collective-permute-start.5 = (f32[4,2,2,8,128]{4,3,2,1,0:T(8,128)S(1)}, f32[4,2,2,8,128]{4,3,2,1,0:T(8,128)S(1)}, u32[]{:S(2)}, u32[]{:S(2)}) collective-permute-start(f32[4,2,2,8,128]{4,3,2,1,0:T(8,128)S(1)} %get-tuple-element.65), channel_id=1, source_target_pairs={{0,4},{4,0},{8,12},{12,8},{16,20},{20,16},{24,28},{28,24},{1,5},{5... | collective-permute-start | bytes 196616 | tf_op jit(solution)/shard_map/ppermute | solution.py:528
  29.7 0.0 collective-permute-done.6.received_ref
  29.8 2.8 %collective-permute-done.5.refs_3_ = f32[4,2,2,8,128]{4,3,2,1,0:T(8,128)S(1)} collective-permute-done((f32[4,2,2,8,128]{4,3,2,1,0:T(8,128)S(1)}, f32[4,2,2,8,128]{4,3,2,1,0:T(8,128)S(1)}, u32[]{:S(2)}, u32[]{:S(2)}) %collective-permute-start.5) | collective-permute-done | bytes 65568 | tf_op jit(solution)/shard_map/ppermute | solution.py:528
  32.6 0.0 collective-permute-done.4.refs_1_
  32.6 0.1 collective-permute-start.7
  32.7 2.5 %collective-permute-start.8 = (f32[2,8,8,128]{3,2,1,0:T(8,128)S(1)}, f32[2,8,8,128]{3,2,1,0:T(8,128)S(1)}, u32[]{:S(2)}, u32[]{:S(2)}) collective-permute-start(f32[2,8,8,128]{3,2,1,0:T(8,128)S(1)} %get-tuple-element.71), channel_id=1, source_target_pairs={{0,16},{4,20},{8,24},{12,28},{16,0},{20,4},{24,8},{28,12},{1,17},{... | collective-permute-start | bytes 196616 | tf_op jit(solution)/shard_map/ppermute | solution.py:627
  35.2 1.3 %collective-permute-start.9 = (f32[2,8,8,128]{3,2,1,0:T(8,128)S(1)}, f32[2,8,8,128]{3,2,1,0:T(8,128)S(1)}, u32[]{:S(2)}, u32[]{:S(2)}) collective-permute-start(f32[2,8,8,128]{3,2,1,0:T(8,128)S(1)} %get-tuple-element.72), channel_id=1, source_target_pairs={{0,24},{4,28},{8,0},{12,4},{16,8},{20,12},{24,16},{28,20},{1,25},{... | collective-permute-start | bytes 196616 | tf_op jit(solution)/shard_map/ppermute | solution.py:627
  36.5 0.9 %collective-permute-start.10 = (f32[1,2,2,16,128]{4,3,2,1,0:T(8,128)S(1)}, f32[1,2,2,16,128]{4,3,2,1,0:T(8,128)S(1)}, u32[]{:S(2)}, u32[]{:S(2)}) collective-permute-start(f32[1,2,2,16,128]{4,3,2,1,0:T(8,128)S(1)} %get-tuple-element.68.refs_4_), channel_id=1, source_target_pairs={{0,2},{1,3},{2,0},{3,1},{4,6},{5,7},{6,4},{7,5},{8,10},{9,11},{10,... | collective-permute-start | bytes 98312 | tf_op jit(solution)/shard_map/ppermute | solution.py:528
  37.4 3.1 %collective-permute-done.10.received_ref = f32[1,2,2,16,128]{4,3,2,1,0:T(8,128)S(1)} collective-permute-done((f32[1,2,2,16,128]{4,3,2,1,0:T(8,128)S(1)}, f32[1,2,2,16,128]{4,3,2,1,0:T(8,128)S(1)}, u32[]{:S(2)}, u32[]{:S(2)}) %collective-permute-start.10) | collective-permute-done | bytes 32800 | tf_op jit(solution)/shard_map/ppermute | solution.py:528
  40.4 0.1 copy.8
  40.6 0.8 %copy.9 = f32[2,8,16,32]{3,2,1,0:T(8,128)} copy(f32[2,8,16,32]{2,1,3,0:T(8,128)S(1)} %bitcast.5) | data formatting | bytes 65536
  41.4 0.0 collective-permute-done.7.refs_1_
  41.4 0.0 collective-permute-done.8.refs_2_
  41.4 0.0 collective-permute-done.9.refs_3_
  41.4 0.9 %fold_x.1 = f32[2,8,8,128]{3,2,1,0:T(8,128)} custom-call(f32[2,8,8,128]{3,2,1,0:T(8,128)S(1)} %get-tuple-element.69.refs_0_, f32[2,8,8,128]{3,2,1,0:T(8,128)S(1)} %collective-permute-done.7.refs_1_, f32[2,8,8,128]{3,2,1,0:T(8,128)S(1)} %collective-permute-done.8.refs_2_, f32[2,8,8,128]{3,2,1,0:T(8,128)S(1)} %collective-permute-done.9.refs_3_), custom_call_target="tpu_custom_call" | custom-call | tf_op jit(solution)/shard_map/fold_x/pallas_call | solution.py:628
  (3 shorter events, 0.1 us)
Async XLA Ops:
  0.6 1.2 %copy-start = (f32[64,32,128]{2,1,0:T(8,128)S(1)}, f32[64,32,128]{2,1,0:T(8,128)}, u32[]{:S(2)}) copy-start(f32[64,32,128]{2,1,0:T(8,128)} %field_ref.1) | copy-start | bytes 3145732
  1.9 10.2 %copy-start.2 = (bf16[16,8]{0,1:T(8,128)(2,1)S(1)}, bf16[16,8]{0,1:T(8,128)(2,1)}, u32[]{:S(2)}) copy-start(bf16[16,8]{0,1:T(8,128)(2,1)} %param.4) | copy-start | bytes 772
  1.9 10.3 %copy-start.1 = (bf16[16,16]{1,0:T(8,128)(2,1)S(1)}, bf16[16,16]{1,0:T(8,128)(2,1)}, u32[]{:S(2)}) copy-start(bf16[16,16]{1,0:T(8,128)(2,1)} %out_ref.1) | copy-start | bytes 1540
  2.5 4.0 %collective-permute-start = (f32[3,16,128]{2,1,0:T(8,128)S(1)}, f32[3,16,128]{2,1,0:T(8,128)S(1)}, u32[]{:S(2)}, u32[]{:S(2)}) collective-permute-start(f32[3,16,128]{2,1,0:T(8,128)S(1)} %get-tuple-element.39), channel_id=1, source_target_pairs={{0,1},{1,2},{2,3},{3,0},{4,5},{5,6},{6,7},{7,4},{8,9},{9,10},{10,1... | collective-permute-start | bytes 73736 | tf_op jit(solution)/shard_map/ppermute | solution.py:524
  3.0 3.5 %collective-permute-start.1 = (f32[3,16,128]{2,1,0:T(8,128)S(1)}, f32[3,16,128]{2,1,0:T(8,128)S(1)}, u32[]{:S(2)}, u32[]{:S(2)}) collective-permute-start(f32[3,16,128]{2,1,0:T(8,128)S(1)} %get-tuple-element.40), channel_id=1, source_target_pairs={{1,0},{2,1},{3,2},{0,3},{5,4},{6,5},{7,6},{4,7},{9,8},{10,9},{11,1... | collective-permute-start | bytes 73736 | tf_op jit(solution)/shard_map/ppermute | solution.py:524
  6.7 12.4 %collective-permute-start.2 = (f32[3,72,128]{2,1,0:T(8,128)S(1)}, f32[3,72,128]{2,1,0:T(8,128)S(1)}, u32[]{:S(2)}, u32[]{:S(2)}) collective-permute-start(f32[3,72,128]{2,1,0:T(8,128)S(1)} %get-tuple-element.42), channel_id=1, source_target_pairs={{0,4},{4,8},{8,12},{12,16},{16,20},{20,24},{24,28},{28,0},{1,5},{5... | collective-permute-start | bytes 331784 | tf_op jit(solution)/shard_map/ppermute | solution.py:524
  9.0 10.2 %collective-permute-start.3 = (f32[3,72,128]{2,1,0:T(8,128)S(1)}, f32[3,72,128]{2,1,0:T(8,128)S(1)}, u32[]{:S(2)}, u32[]{:S(2)}) collective-permute-start(f32[3,72,128]{2,1,0:T(8,128)S(1)} %get-tuple-element.43), channel_id=1, source_target_pairs={{4,0},{8,4},{12,8},{16,12},{20,16},{24,20},{28,24},{0,28},{5,1},{9... | collective-permute-start | bytes 331784 | tf_op jit(solution)/shard_map/ppermute | solution.py:524
  23.3 9.2 %collective-permute-start.4 = (f32[4,2,6,8,128]{4,3,2,1,0:T(8,128)S(1)}, f32[4,2,6,8,128]{4,3,2,1,0:T(8,128)S(1)}, u32[]{:S(2)}, u32[]{:S(2)}) collective-permute-start(f32[4,2,6,8,128]{4,3,2,1,0:T(8,128)S(1)} %get-tuple-element.53), channel_id=1, source_target_pairs={{0,4},{4,0},{8,12},{12,8},{16,20},{20,16},{24,28},{28,24},{1,5},{5... | collective-permute-start | bytes 589832 | tf_op jit(solution)/shard_map/ppermute | solution.py:528
  26.6 3.1 %collective-permute-start.6 = (f32[2,2,2,16,128]{4,3,2,1,0:T(8,128)S(1)}, f32[2,2,2,16,128]{4,3,2,1,0:T(8,128)S(1)}, u32[]{:S(2)}, u32[]{:S(2)}) collective-permute-start(f32[2,2,2,16,128]{4,3,2,1,0:T(8,128)S(1)} %get-tuple-element.67), channel_id=1, source_target_pairs={{0,1},{1,0},{2,3},{3,2},{4,5},{5,4},{6,7},{7,6},{8,9},{9,8},{10,11... | collective-permute-start | bytes 196616 | tf_op jit(solution)/shard_map/ppermute | solution.py:528
  28.0 4.6 %collective-permute-start.5 = (f32[4,2,2,8,128]{4,3,2,1,0:T(8,128)S(1)}, f32[4,2,2,8,128]{4,3,2,1,0:T(8,128)S(1)}, u32[]{:S(2)}, u32[]{:S(2)}) collective-permute-start(f32[4,2,2,8,128]{4,3,2,1,0:T(8,128)S(1)} %get-tuple-element.65), channel_id=1, source_target_pairs={{0,4},{4,0},{8,12},{12,8},{16,20},{20,16},{24,28},{28,24},{1,5},{5... | collective-permute-start | bytes 196616 | tf_op jit(solution)/shard_map/ppermute | solution.py:528
  32.6 8.8 %collective-permute-start.7 = (f32[2,8,8,128]{3,2,1,0:T(8,128)S(1)}, f32[2,8,8,128]{3,2,1,0:T(8,128)S(1)}, u32[]{:S(2)}, u32[]{:S(2)}) collective-permute-start(f32[2,8,8,128]{3,2,1,0:T(8,128)S(1)} %get-tuple-element.70), channel_id=1, source_target_pairs={{0,8},{4,12},{8,16},{12,20},{16,24},{20,28},{24,0},{28,4},{1,9},{5... | collective-permute-start | bytes 196616 | tf_op jit(solution)/shard_map/ppermute | solution.py:627
  32.7 8.7 %collective-permute-start.8 = (f32[2,8,8,128]{3,2,1,0:T(8,128)S(1)}, f32[2,8,8,128]{3,2,1,0:T(8,128)S(1)}, u32[]{:S(2)}, u32[]{:S(2)}) collective-permute-start(f32[2,8,8,128]{3,2,1,0:T(8,128)S(1)} %get-tuple-element.71), channel_id=1, source_target_pairs={{0,16},{4,20},{8,24},{12,28},{16,0},{20,4},{24,8},{28,12},{1,17},{... | collective-permute-start | bytes 196616 | tf_op jit(solution)/shard_map/ppermute | solution.py:627
  35.2 6.2 %collective-permute-start.9 = (f32[2,8,8,128]{3,2,1,0:T(8,128)S(1)}, f32[2,8,8,128]{3,2,1,0:T(8,128)S(1)}, u32[]{:S(2)}, u32[]{:S(2)}) collective-permute-start(f32[2,8,8,128]{3,2,1,0:T(8,128)S(1)} %get-tuple-element.72), channel_id=1, source_target_pairs={{0,24},{4,28},{8,0},{12,4},{16,8},{20,12},{24,16},{28,20},{1,25},{... | collective-permute-start | bytes 196616 | tf_op jit(solution)/shard_map/ppermute | solution.py:627
  36.5 3.9 %collective-permute-start.10 = (f32[1,2,2,16,128]{4,3,2,1,0:T(8,128)S(1)}, f32[1,2,2,16,128]{4,3,2,1,0:T(8,128)S(1)}, u32[]{:S(2)}, u32[]{:S(2)}) collective-permute-start(f32[1,2,2,16,128]{4,3,2,1,0:T(8,128)S(1)} %get-tuple-element.68.refs_4_), channel_id=1, source_target_pairs={{0,2},{1,3},{2,0},{3,1},{4,6},{5,7},{6,4},{7,5},{8,10},{9,11},{10,... | collective-permute-start | bytes 98312 | tf_op jit(solution)/shard_map/ppermute | solution.py:528
